TPU v7x, 32 devices: a whole 2x2x4 slice. The times are simulated.
32 devices in a mesh: dp: 8 (over z, y), tensor: 4 (over x, core).
Axes of the slice: x: 2, y: 2, z: 4, core: 2. Of those that a mesh axis runs over, the one named last changes fastest.
Arguments:
- inputs: bfloat16 [8192, 2048], P(('dp', 'tensor')), may hold values from -6 to 6
- cotangent: bfloat16 [8192, 2048], P(('dp', 'tensor')), may hold values from -6 to 6
- w_query: bfloat16 [2048, 1280], P('dp', 'tensor'), may hold values from -0.125 to 0.125
- w_kv: bfloat16 [2048, 640], P('dp'), may hold values from -0.125 to 0.125
- w_out: bfloat16 [1280, 2048], P('tensor', 'dp'), may hold values from -1.25 to 1.25
- w_in: bfloat16 [2048, 2, 6144], P('dp', None, 'tensor'), may hold values from -0.125 to 0.125
- w_down: bfloat16 [6144, 2048], P('tensor', 'dp'), may hold values from -0.078125 to 0.078125
- norm_gains: bfloat16 [2, 2048], P(None, 'dp'), may hold values from 0.099609375 to 1.8984375
- head_gains: bfloat16 [2, 64], replicated, may hold values from 0.099609375 to 1.8984375
- lengths: int32 [4], replicated, may hold values from 64 to 2048, as said below
- slot_blocks: int32 [128], replicated, may hold values from 0 to 127, as said below
Outputs:
- outputs: bfloat16 [8192, 2048], P(('dp', 'tensor'))
- grad_inputs: bfloat16 [8192, 2048], P(('dp', 'tensor'))
- grad_w_query: float32 [2048, 1280], P('dp', 'tensor')
- grad_w_kv: float32 [2048, 640], P('dp')
- grad_w_out: float32 [1280, 2048], P('tensor', 'dp')
- grad_w_in: float32 [2048, 2, 6144], P('dp', None, 'tensor')
- grad_w_down: float32 [6144, 2048], P('tensor', 'dp')
- grad_norm_gains: float32 [2, 2048], P(None, 'dp')
- grad_head_gains: float32 [2, 64], replicated
Inputs may be any that keep to these rules, and one draw needn't show every extreme that they name: `lengths`: one row, drawn from the seed, has all 2048 slots live. Lengths are multiples of 64, at least 64. `slot_blocks`: each block number appears once. The slots of one dp index hold its rows in order, 4 blocks of each row, and its g-th block of a row comes from the g-th aligned group of 8 consecutive blocks of that row; every dp index holds a different block of each such group.
All inputs are finite; a program needn't handle non-finite values.
Results may differ from a plain program's by a relative error of at most 0.028.
Values may be sent and summed in bfloat16 or wider, within the bound.
No kernel may reach another device: no remote copies, remote signals or barrier semaphores. Data moves between devices by JAX's collectives and lax.ppermute only.
A program may use at most 576 MiB of HBM per device.

v0:
```python
import jax
import jax.numpy as jnp
from jax import lax
from jax.sharding import PartitionSpec as P

HEADS_KV = 5
HEAD = 64
SLOTS = 2048
STRETCH = 64


eps_norm = 1e-06
rope_base = 10000.0
neg_large = -1e30
contract_rows = (((0,), (0,)), ((), ()))
contract_cols = (((1,), (1,)), ((), ()))


def scaled_norm(value_in, gain_vec):
    return (
        value_in
        * lax.rsqrt(jnp.mean(value_in * value_in, axis=-1, keepdims=True) + eps_norm)
        * gain_vec
    )


def rotate(raw_value, gain_vec, positions, factor):
    row_total = raw_value.shape[0]
    per_head = scaled_norm(raw_value.reshape(row_total, -1, HEAD), gain_vec)
    half_head = HEAD // 2
    frequency = rope_base ** (-2.0 * jnp.arange(half_head, dtype=jnp.float32) / HEAD)
    angles = positions.astype(jnp.float32)[:, None] * frequency[None, :]
    cosine = jnp.cos(angles)[:, None, :]
    sine_tab = jnp.sin(angles)[:, None, :]
    first_half = per_head[..., :half_head]
    second = per_head[..., half_head:]
    turned = jnp.concatenate(
        [first_half * cosine - second * sine_tab, second * cosine + first_half * sine_tab], axis=-1
    )
    return (turned * factor).reshape(row_total, -1)


def silu_product(gate, up_part):
    return gate * jax.nn.sigmoid(gate) * up_part


def local(
    inputs,
    cotangent,
    w_query,
    w_kv,
    w_out,
    w_in,
    w_down,
    norm_gains,
    head_gains,
    lengths,
    slot_blocks,
):
    sp_rows = inputs.shape[0]
    dp_count = lax.axis_size("dp")
    tokens_dp = sp_rows * lax.axis_size("tensor")
    seq_count = lengths.shape[0]
    row_span = tokens_dp // seq_count
    per_row = SLOTS // STRETCH
    kv_width = w_kv.shape[1] // 2
    dp_index = lax.axis_index("dp")
    sp_start = lax.axis_index("tensor") * sp_rows
    inside = jnp.arange(STRETCH, dtype=jnp.int32)
    limits = lengths[:, None]
    blocks_here = lax.dynamic_slice_in_dim(
        slot_blocks, dp_index * (tokens_dp // STRETCH), tokens_dp // STRETCH
    )
    positions = ((blocks_here % per_row * STRETCH)[:, None] + inside[None, :]).reshape(
        seq_count, row_span
    )
    flat_pos = positions.reshape(tokens_dp)
    live_rows = (positions < limits).astype(jnp.float32).reshape(tokens_dp)
    live_sp = lax.dynamic_slice_in_dim(live_rows, sp_start, sp_rows)
    pos_sp = lax.dynamic_slice_in_dim(flat_pos, sp_start, sp_rows)
    query_all, kv_all, out_all, in_all, down_all, gains_all = (
        lax.all_gather(w_query, "dp", axis=0, tiled=True),
        lax.all_gather(w_kv, "dp", axis=0, tiled=True),
        lax.all_gather(w_out, "dp", axis=1, tiled=True),
        lax.all_gather(w_in, "dp", axis=0, tiled=True),
        lax.all_gather(w_down, "dp", axis=1, tiled=True),
        lax.all_gather(norm_gains, "dp", axis=1, tiled=True),
    )
    gain_one = gains_all[0].astype(jnp.float32)
    gain_two = gains_all[1].astype(jnp.float32)
    head_float = head_gains.astype(jnp.float32)
    inputs_f = inputs.astype(jnp.float32)
    h_one_sp = scaled_norm(inputs_f, gain_one).astype(jnp.bfloat16)
    h_one = lax.all_gather(h_one_sp, "tensor", axis=0, tiled=True)
    q_raw = jnp.dot(h_one, query_all, preferred_element_type=jnp.float32)
    kv_raw = jnp.dot(h_one, kv_all, preferred_element_type=jnp.float32)
    queries = rotate(q_raw, head_float[0], flat_pos, 0.125).astype(jnp.bfloat16)
    keys_vals = jnp.concatenate(
        [rotate(kv_raw[:, :kv_width], head_float[1], flat_pos, 1.0), kv_raw[:, kv_width:]], axis=1
    ).astype(jnp.bfloat16)
    query_rows = queries.reshape(seq_count, row_span, HEADS_KV, HEAD)

    def piece_positions(piece_rows):
        shard_count = piece_rows // tokens_dp
        piece_pos = (slot_blocks % per_row * STRETCH)[:, None] + inside[None, :]
        return (
            piece_pos.reshape(shard_count, seq_count, row_span)
            .transpose(1, 0, 2)
            .reshape(seq_count, shard_count * row_span)
        )

    def key_layout(shard_piece):
        piece_rows = shard_piece.shape[0]
        shard_count = piece_rows // tokens_dp
        key_pos = piece_positions(piece_rows)
        visible = (key_pos[:, None, :] <= positions[:, :, None]) & (
            key_pos[:, None, :] < limits[:, :, None]
        )
        laid = shard_piece.reshape(shard_count, seq_count, row_span, 2, HEADS_KV, HEAD).transpose(
            1, 0, 2, 3, 4, 5
        )
        laid = laid.reshape(seq_count, shard_count * row_span, 2, HEADS_KV, HEAD)
        return (laid[:, :, 0], laid[:, :, 1], visible[:, None])

    running_max = jnp.full((seq_count, HEADS_KV, row_span), neg_large, jnp.float32)
    key_rows, value_rows, visible = key_layout(lax.all_gather(keys_vals, "dp", axis=0, tiled=True))
    scores = jnp.einsum("rqhd,rkhd->rhqk", query_rows, key_rows, preferred_element_type=jnp.float32)
    scores = jnp.where(visible, scores, neg_large)
    new_max = jnp.maximum(running_max, jnp.max(scores, axis=-1))
    weights = jnp.where(visible, jnp.exp(scores - new_max[..., None]), 0.0)
    running_sum = jnp.sum(weights, axis=-1)
    accum = jnp.einsum(
        "rhqk,rkhd->rhqd",
        weights.astype(jnp.bfloat16),
        value_rows,
        preferred_element_type=jnp.float32,
    )
    running_max, running_sum, accum = (new_max, running_sum, accum)
    heads_f = accum / running_sum[..., None]
    log_sum = running_max + jnp.log(running_sum)
    heads_low = (
        heads_f.transpose(0, 2, 1, 3).reshape(tokens_dp, HEADS_KV * HEAD).astype(jnp.bfloat16)
    )
    attn_sp = lax.psum_scatter(
        jnp.dot(heads_low, out_all, preferred_element_type=jnp.float32).astype(jnp.bfloat16),
        "tensor",
        scatter_dimension=0,
        tiled=True,
    ).astype(jnp.float32)
    mixed = inputs_f + live_sp[:, None] * attn_sp
    h_two_sp = scaled_norm(mixed, gain_two).astype(jnp.bfloat16)
    h_two, cotangent_rows = (
        lax.all_gather(h_two_sp, "tensor", axis=0, tiled=True),
        lax.all_gather(cotangent, "tensor", axis=0, tiled=True),
    )
    gate_up = jnp.einsum("nd,dcf->ncf", h_two, in_all, preferred_element_type=jnp.float32)
    hidden = silu_product(gate_up[:, 0], gate_up[:, 1]).astype(jnp.bfloat16)
    ffn_sp = lax.psum_scatter(
        jnp.dot(hidden, down_all, preferred_element_type=jnp.float32).astype(jnp.bfloat16),
        "tensor",
        scatter_dimension=0,
        tiled=True,
    ).astype(jnp.float32)
    outputs = (mixed + live_sp[:, None] * ffn_sp).astype(jnp.bfloat16)
    d_ffn = cotangent_rows * live_rows[:, None].astype(jnp.bfloat16)
    grad_down = lax.dot_general(hidden, d_ffn, contract_rows, preferred_element_type=jnp.float32)
    d_hidden = lax.dot_general(d_ffn, down_all, contract_cols, preferred_element_type=jnp.float32)
    gate_pull = jax.vjp(silu_product, gate_up[:, 0], gate_up[:, 1])[1]
    d_gate, d_up = gate_pull(d_hidden)
    d_gate_up = jnp.stack([d_gate, d_up], axis=1).astype(jnp.bfloat16)
    grad_in = jnp.einsum("nd,ncf->dcf", h_two, d_gate_up, preferred_element_type=jnp.float32)
    d_h_two = lax.psum_scatter(
        jnp.einsum("ncf,dcf->nd", d_gate_up, in_all, preferred_element_type=jnp.float32).astype(
            jnp.bfloat16
        ),
        "tensor",
        scatter_dimension=0,
        tiled=True,
    ).astype(jnp.float32)
    norm_two_pull = jax.vjp(scaled_norm, mixed, gain_two)[1]
    d_mixed_norm, d_gain_two = norm_two_pull(d_h_two)
    d_mixed = cotangent.astype(jnp.float32) + d_mixed_norm
    d_attn = lax.all_gather(
        (live_sp[:, None] * d_mixed).astype(jnp.bfloat16), "tensor", axis=0, tiled=True
    )
    grad_out = lax.dot_general(heads_low, d_attn, contract_rows, preferred_element_type=jnp.float32)
    d_heads = lax.dot_general(
        d_attn, out_all, contract_cols, preferred_element_type=jnp.float32
    ).astype(jnp.bfloat16)
    d_head_rows = d_heads.reshape(seq_count, row_span, HEADS_KV, HEAD)
    delta = jnp.sum(heads_f * d_head_rows.astype(jnp.float32).transpose(0, 2, 1, 3), axis=-1)
    shard_piece = lax.all_gather(keys_vals, "dp", axis=0, tiled=True)
    piece_rows = shard_piece.shape[0]
    shard_count = piece_rows // tokens_dp
    key_rows, value_rows, visible = key_layout(shard_piece)
    scores = jnp.einsum("rqhd,rkhd->rhqk", query_rows, key_rows, preferred_element_type=jnp.float32)
    probs = jnp.where(visible, jnp.exp(scores - log_sum[..., None]), 0.0)
    d_values = jnp.einsum(
        "rhqk,rqhd->rkhd",
        probs.astype(jnp.bfloat16),
        d_head_rows,
        preferred_element_type=jnp.float32,
    )
    d_probs = jnp.einsum(
        "rqhd,rkhd->rhqk", d_head_rows, value_rows, preferred_element_type=jnp.float32
    )
    d_scores = (probs * (d_probs - delta[..., None])).astype(jnp.bfloat16)
    d_query = jnp.einsum("rhqk,rkhd->rqhd", d_scores, key_rows, preferred_element_type=jnp.float32)
    d_key_part = jnp.einsum(
        "rhqk,rqhd->rkhd", d_scores, query_rows, preferred_element_type=jnp.float32
    )
    both = jnp.stack([d_key_part, d_values], axis=2).reshape(
        seq_count, shard_count, row_span, 2 * HEADS_KV * HEAD
    )
    both = both.transpose(1, 0, 2, 3).reshape(piece_rows, 2 * HEADS_KV * HEAD)
    d_keys = both
    d_query, d_keys = (d_query, d_keys)
    d_kv_sp = lax.psum_scatter(d_keys, ("dp", "tensor"), scatter_dimension=0, tiled=True)
    query_pull = jax.vjp(
        lambda raw_value, gain_vec: rotate(raw_value, gain_vec, flat_pos, 0.125),
        q_raw,
        head_float[0],
    )[1]
    d_q_raw, d_q_gain = query_pull(d_query.reshape(tokens_dp, HEADS_KV * HEAD))
    kv_raw_sp = lax.dynamic_slice_in_dim(kv_raw, sp_start, sp_rows)
    key_pull = jax.vjp(
        lambda raw_value, gain_vec: rotate(raw_value, gain_vec, pos_sp, 1.0),
        kv_raw_sp[:, :kv_width],
        head_float[1],
    )[1]
    d_k_raw, d_k_gain = key_pull(d_kv_sp[:, :kv_width])
    d_kv_low = jnp.concatenate([d_k_raw, d_kv_sp[:, kv_width:]], axis=1).astype(jnp.bfloat16)
    d_q_low = d_q_raw.astype(jnp.bfloat16)
    grad_query = lax.dot_general(h_one, d_q_low, contract_rows, preferred_element_type=jnp.float32)
    grad_kv = lax.dot_general(h_one_sp, d_kv_low, contract_rows, preferred_element_type=jnp.float32)
    d_h_one = lax.psum_scatter(
        lax.dot_general(
            d_q_low, query_all, contract_cols, preferred_element_type=jnp.float32
        ).astype(jnp.bfloat16),
        "tensor",
        scatter_dimension=0,
        tiled=True,
    ).astype(jnp.float32)
    d_h_one = d_h_one + lax.dot_general(
        d_kv_low, kv_all, contract_cols, preferred_element_type=jnp.float32
    )
    norm_one_pull = jax.vjp(scaled_norm, inputs_f, gain_one)[1]
    d_inputs_norm, d_gain_one = norm_one_pull(d_h_one)
    grad_inputs = (d_mixed + d_inputs_norm).astype(jnp.bfloat16)
    grad_gains = jnp.stack([d_gain_one, d_gain_two])
    grad_heads = jnp.tile(jnp.stack([d_q_gain, d_k_gain]), (1, dp_count))
    sum_query, sum_kv, sum_out, sum_in, sum_down, sum_gains, sum_heads = (
        lax.psum_scatter(
            grad_query.astype(jnp.bfloat16), "dp", scatter_dimension=0, tiled=True
        ).astype(jnp.float32),
        lax.psum_scatter(
            grad_kv.astype(jnp.bfloat16), "dp", scatter_dimension=0, tiled=True
        ).astype(jnp.float32),
        lax.psum_scatter(
            grad_out.astype(jnp.bfloat16), "dp", scatter_dimension=1, tiled=True
        ).astype(jnp.float32),
        lax.psum_scatter(
            grad_in.astype(jnp.bfloat16), "dp", scatter_dimension=0, tiled=True
        ).astype(jnp.float32),
        lax.psum_scatter(
            grad_down.astype(jnp.bfloat16), "dp", scatter_dimension=1, tiled=True
        ).astype(jnp.float32),
        lax.psum_scatter(
            grad_gains.astype(jnp.bfloat16), "dp", scatter_dimension=1, tiled=True
        ).astype(jnp.float32),
        lax.psum_scatter(
            grad_heads.astype(jnp.bfloat16), "dp", scatter_dimension=1, tiled=True
        ).astype(jnp.float32),
    )
    sum_kv, sum_gains, sum_heads = (
        lax.psum(sum_kv.astype(jnp.bfloat16), "tensor").astype(jnp.float32),
        lax.psum(sum_gains.astype(jnp.bfloat16), "tensor").astype(jnp.float32),
        lax.psum(sum_heads.astype(jnp.bfloat16), "tensor").astype(jnp.float32),
    )
    return (
        outputs,
        grad_inputs,
        sum_query,
        sum_kv,
        sum_out,
        sum_in,
        sum_down,
        sum_gains,
        sum_heads,
    )


def solution(mesh):
    in_specs = (
        P(("dp", "tensor"), None),
        P(("dp", "tensor"), None),
        P("dp", "tensor"),
        P("dp", None),
        P("tensor", "dp"),
        P("dp", None, "tensor"),
        P("tensor", "dp"),
        P(None, "dp"),
        P(),
        P(),
        P(),
    )
    out_specs = (
        P(("dp", "tensor"), None),
        P(("dp", "tensor"), None),
        P("dp", "tensor"),
        P("dp", None),
        P("tensor", "dp"),
        P("dp", None, "tensor"),
        P("tensor", "dp"),
        P(None, "dp"),
        P(),
    )
    return jax.shard_map(local, mesh=mesh, in_specs=in_specs, out_specs=out_specs, check_vma=False)
```

profile of v0, /device:TPU:0, one launch (start us, length us, event | category | flops | bytes accessed | tf_op | source)
XLA Modules:
  0.0 2087.3 jit_solution(4328431888564727741)
XLA Ops:
  8.0 22.5 %all_gather.34 = bf16[2,2048]{1,0:T(2,128)(2,1)S(1)} all-gather(bf16[2,256]{1,0:T(2,128)(2,1)} %param.18), channel_id=1, replica_groups=mesh['dp'=8,'tensor'=4] {'dp'}, dimensions={1}, use_global_device_ids=true | all-gather | bytes 9216 | tf_op jit(solution)/shard_map/all_gather | solution.py:87
  37.3 30.3 %all-gather.15.cloned.1.call-done = bf16[2048,640]{1,0:T(8,128)(2,1)} async-done(((bf16[256,640]{1,0:T(8,128)(2,1)}), bf16[2048,640]{1,0:T(8,128)(2,1)}) %all-gather.15.cloned.1.call-update) | async-done | bytes 2621456 | tf_op jit(solution)/shard_map/all_gather | solution.py:83
  67.7 35.2 %all-gather.11.cloned.1.call-done = bf16[1024,2048]{1,0:T(8,128)(2,1)} async-done(((bf16[256,2048]{1,0:T(8,128)(2,1)}), bf16[1024,2048]{1,0:T(8,128)(2,1)}) %all-gather.11.cloned.1.call-update) | async-done | bytes 4194320 | tf_op jit(solution)/shard_map/all_gather | solution.py:94
  110.0 37.2 %all-gather.13.cloned.1.call-done = bf16[2048,320]{0,1:T(8,128)(2,1)} async-done(((bf16[256,320]{0,1:T(8,128)(2,1)}), bf16[2048,320]{0,1:T(8,128)(2,1)}) %all-gather.13.cloned.1.call-update) | async-done | bytes 1310736 | tf_op jit(solution)/shard_map/all_gather | solution.py:82
  160.4 145.0 %all-gather.17.cloned.1.call-done = bf16[8192,640]{0,1:T(8,128)(2,1)} async-done(((bf16[1024,640]{0,1:T(8,128)(2,1)}), bf16[8192,640]{0,1:T(8,128)(2,1)}) %all-gather.17.cloned.1.call-update) | async-done | bytes 10485776 | tf_op jit(solution)/shard_map/all_gather | solution.py:126
  349.6 19.2 select_reduce_fusion
  368.9 19.0 fusion.1
  387.9 19.4 fusion.48
  417.1 39.7 %reduce-scatter.17.cloned.1.call-done = bf16[256,2048]{1,0:T(8,128)(2,1)} async-done(((bf16[1024,2048]{1,0:T(8,128)(2,1)}), bf16[256,2048]{1,0:T(8,128)(2,1)}) %reduce-scatter.17.cloned.1.call-update) | async-done | bytes 1048592 | tf_op jit(solution)/shard_map/reduce_scatter | solution.py:144
  461.6 174.7 %all-gather.23.cloned.1.call-done = bf16[2048,2,1536]{2,0,1:T(8,128)(2,1)} async-done(((bf16[256,2,1536]{2,0,1:T(8,128)(2,1)}), bf16[2048,2,1536]{2,0,1:T(8,128)(2,1)}) %all-gather.23.cloned.1.call-update) | async-done | bytes 12582928 | tf_op jit(solution)/shard_map/all_gather | solution.py:85
  636.3 34.9 %all-gather.21.cloned.1.call-done = bf16[1024,2048]{1,0:T(8,128)(2,1)} async-done(((bf16[256,2048]{1,0:T(8,128)(2,1)}), bf16[1024,2048]{1,0:T(8,128)(2,1)}) %all-gather.21.cloned.1.call-update) | async-done | bytes 4194320 | tf_op jit(solution)/shard_map/all_gather | solution.py:153
  671.2 19.0 fusion.21
  707.4 102.1 %all-gather.25.cloned.1.call-done = bf16[1536,2048]{1,0:T(8,128)(2,1)} async-done(((bf16[1536,256]{1,0:T(8,128)(2,1)}), bf16[1536,2048]{1,0:T(8,128)(2,1)}) %all-gather.25.cloned.1.call-update) | async-done | bytes 6291472 | tf_op jit(solution)/shard_map/all_gather | solution.py:86
  809.4 18.7 fusion.27
  848.5 42.6 %reduce-scatter.21.cloned.1.call-done = bf16[256,2048]{1,0:T(8,128)(2,1)} async-done(((bf16[1024,2048]{1,0:T(8,128)(2,1)}), bf16[256,2048]{1,0:T(8,128)(2,1)}) %reduce-scatter.21.cloned.1.call-update) | async-done | bytes 1048592 | tf_op jit(solution)/shard_map/reduce_scatter | solution.py:172
  897.1 34.6 %all-gather.29.cloned.1.call-done = bf16[1024,2048]{1,0:T(8,128)(2,1)} async-done(((bf16[256,2048]{1,0:T(8,128)(2,1)}), bf16[1024,2048]{1,0:T(8,128)(2,1)}) %all-gather.29.cloned.1.call-update) | async-done | bytes 4194320 | tf_op jit(solution)/shard_map/all_gather | solution.py:183
  940.0 20.1 fusion.15
  960.2 26.6 %multiply_convert_fusion = bf16[4,5,256,2048]{3,2,1,0:T(8,128)(2,1)} fusion(f32[4,5,256,2048]{3,2,1,0:T(8,128)} %get-tuple-element.90, f32[4,5,256]{2,1,0:T(8,128)S(1)} %fusion.47, f32[4,5,256]{2,1,0:T(8,128)S(1)} %log_add_fusion, pred[4,256,2048]{2,1,0:T(8,128)(4,1)S(1)} %compare_and_fusion, bf16[4,2048,2,5,64]{1,4,3,0,2:T(8,128)(2,1)} %reshape.372, ...), kind=kOutput, calls=%fused_computation | convolution fusion | flops 1394606080 | bytes 70950912 | tf_op jit(solution)/shard_map/rqhd,rkhd->rhqk/dot_general | solution.py:204
  1009.5 20.6 copy.101
  1030.1 23.3 %copy.82 = f32[8,4,256,640]{3,2,1,0:T(8,128)} copy(f32[8,4,256,640]{2,0,3,1:T(8,128)} %bitcast.166) | data formatting | bytes 41943040 | tf_op jit(solution)/shard_map/transpose | solution.py:215
  1091.2 19.9 convolution_convert_fusion
  1118.9 160.1 %reduce-scatter.25.cloned.1.call-done = f32[256,640]{1,0:T(8,128)} async-done(((f32[8192,640]{1,0:T(8,128)}), f32[256,640]{1,0:T(8,128)}) %reduce-scatter.25.cloned.1.call-update) | async-done | bytes 655376 | tf_op jit(solution)/shard_map/reduce_scatter | solution.py:218
  1297.0 108.1 %reduce-scatter.35.cloned.1.call-done = bf16[1536,256]{1,0:T(8,128)(2,1)} async-done(((bf16[1536,2048]{1,0:T(8,128)(2,1)}), bf16[1536,256]{1,0:T(8,128)(2,1)}) %reduce-scatter.35.cloned.1.call-update) | async-done | bytes 786448 | tf_op jit(solution)/shard_map/reduce_scatter | solution.py:265
  1407.5 65.1 %reduce-scatter.31.cloned.1.call-done = bf16[320,256]{1,0:T(8,128)(2,1)} async-done(((bf16[320,2048]{1,0:T(8,128)(2,1)}), bf16[320,256]{1,0:T(8,128)(2,1)}) %reduce-scatter.31.cloned.1.call-update) | async-done | bytes 163856 | tf_op jit(solution)/shard_map/reduce_scatter | solution.py:259
  1474.2 65.5 %reduce-scatter.27.cloned.1.call-done = bf16[256,320]{0,1:T(8,128)(2,1)} async-done(((bf16[2048,320]{0,1:T(8,128)(2,1)}), bf16[256,320]{0,1:T(8,128)(2,1)}) %reduce-scatter.27.cloned.1.call-update) | async-done | bytes 163856 | tf_op jit(solution)/shard_map/reduce_scatter | solution.py:253
  1541.3 208.1 %reduce-scatter.33.cloned.1.call-done = bf16[256,2,1536]{2,0,1:T(8,128)(2,1)} async-done(((bf16[2048,2,1536]{2,0,1:T(8,128)(2,1)}), bf16[256,2,1536]{2,0,1:T(8,128)(2,1)}) %reduce-scatter.33.cloned.1.call-update) | async-done | bytes 1572880 | tf_op jit(solution)/shard_map/reduce_scatter | solution.py:262
  1754.8 40.6 %reduce-scatter.23.cloned.1.call-done = bf16[256,2048]{1,0:T(8,128)(2,1)} async-done(((bf16[1024,2048]{1,0:T(8,128)(2,1)}), bf16[256,2048]{1,0:T(8,128)(2,1)}) %reduce-scatter.23.cloned.1.call-update) | async-done | bytes 1048592 | tf_op jit(solution)/shard_map/reduce_scatter | solution.py:236
  1804.0 65.8 %reduce-scatter.29.cloned.1.call-done = bf16[256,640]{1,0:T(8,128)(2,1)} async-done(((bf16[2048,640]{1,0:T(8,128)(2,1)}), bf16[256,640]{1,0:T(8,128)(2,1)}) %reduce-scatter.29.cloned.1.call-update) | async-done | bytes 327696 | tf_op jit(solution)/shard_map/reduce_scatter | solution.py:256
  1869.8 45.9 %reduce-scatter.19.cloned.1.call-done = bf16[256,2048]{1,0:T(8,128)(2,1)} async-done(((bf16[1024,2048]{1,0:T(8,128)(2,1)}), bf16[256,2048]{1,0:T(8,128)(2,1)}) %reduce-scatter.19.cloned.1.call-update) | async-done | bytes 1048592 | tf_op jit(solution)/shard_map/reduce_scatter | solution.py:158
  1920.3 59.7 %reduce-scatter.39.cloned.1.call-done = bf16[64,2]{1,0:T(8,128)(2,1)} async-done(((bf16[512,2]{1,0:T(8,128)(2,1)}), bf16[64,2]{1,0:T(8,128)(2,1)}) %reduce-scatter.39.cloned.1.call-update) | async-done | bytes 272
  1980.8 64.1 %reduce-scatter.37.cloned.1.call-done = bf16[256,2]{1,0:T(8,128)(2,1)} async-done(((bf16[2048,2]{1,0:T(8,128)(2,1)}), bf16[256,2]{1,0:T(8,128)(2,1)}) %reduce-scatter.37.cloned.1.call-update) | async-done | bytes 1040
  2052.6 26.1 %all-reduce.7.cloned.1.call-done = bf16[256,640]{1,0:T(8,128)(2,1)} async-done(((bf16[256,640]{1,0:T(8,128)(2,1)}), bf16[256,640]{1,0:T(8,128)(2,1)}) %all-reduce.7.cloned.1.call-update) | async-done | bytes 327696 | tf_op jit(solution)/shard_map/psum | solution.py:276
  (260 shorter events, 258.6 us)
Async XLA Ops:
  7.2 60.5 %all-gather.15.cloned.1.call-start = ((), (), s32[]{:S(2)}) async-start(), calls=%async_computation.14 | async-start | bytes 2949120 | tf_op jit(solution)/shard_map/all_gather | solution.py:83
  7.9 95.0 %all-gather.11.cloned.1.call-start = ((), (), s32[]{:S(2)}) async-start(), calls=%async_computation.12 | async-start | bytes 5242880 | tf_op jit(solution)/shard_map/all_gather | solution.py:94
  32.5 861.9 %copy-start.23 = (f32[1,2048]{1,0:T(1,128)}, f32[1,2048]{1,0:T(1,128)S(1)}, u32[]{:S(2)}) copy-start(f32[1,2048]{1,0:T(1,128)S(1)} %get-tuple-element.82) | copy-start | bytes 24580
  35.7 111.6 %all-gather.13.cloned.1.call-start = ((), (), s32[]{:S(2)}) async-start(), calls=%async_computation.13 | async-start | bytes 1474560 | tf_op jit(solution)/shard_map/all_gather | solution.py:82
  36.4 269.0 %all-gather.17.cloned.1.call-start = ((), (), s32[]{:S(2)}) async-start(), calls=%async_computation.15 | async-start | bytes 11796480 | tf_op jit(solution)/shard_map/all_gather | solution.py:126
  155.7 252.3 %all-gather.19.cloned.1.call-start = ((), (), s32[]{:S(2)}) async-start(), calls=%async_computation.16 | async-start | bytes 1474560 | tf_op jit(solution)/shard_map/all_gather | solution.py:84
  156.3 300.5 %reduce-scatter.17.cloned.1.call-start = ((), (), s32[]{:S(2)}) async-start(), calls=%async_computation.17 | async-start | bytes 5242880 | tf_op jit(solution)/shard_map/reduce_scatter | solution.py:144
  160.4 189.2 %copy-start.11 = (bf16[1024,5,64]{0,2,1:T(8,128)(2,1)}, bf16[1024,5,64]{0,2,1:T(8,128)(2,1)S(1)}, u32[]{:S(2)}) copy-start(bf16[1024,5,64]{0,2,1:T(8,128)(2,1)S(1)} %fusion.46) | copy-start | bytes 1966084
  414.0 222.3 %all-gather.23.cloned.1.call-start = ((), (), s32[]{:S(2)}) async-start(), calls=%async_computation.19 | async-start | bytes 14155776 | tf_op jit(solution)/shard_map/all_gather | solution.py:85
  416.8 254.4 %all-gather.21.cloned.1.call-start = ((), (), s32[]{:S(2)}) async-start(), calls=%async_computation.18 | async-start | bytes 5242880 | tf_op jit(solution)/shard_map/all_gather | solution.py:153
  417.1 477.3 %copy-start.28 = (f32[256]{0:T(256)}, f32[256]{0:T(256)S(1)}, u32[]{:S(2)}) copy-start(f32[256]{0:T(256)S(1)} %dynamic_slice.13) | copy-start | bytes 3076
  458.7 435.7 %copy-start.29 = (f32[256]{0:T(256)}, f32[256]{0:T(256)S(1)}, u32[]{:S(2)}) copy-start(f32[256]{0:T(256)S(1)} %fusion.60) | copy-start | bytes 3076
  460.3 247.1 %all-gather.27.cloned.1.call-start = ((), (), s32[]{:S(2)}) async-start(), calls=%async_computation.22 | async-start | bytes 5242880 | tf_op jit(solution)/shard_map/all_gather | solution.py:154
  461.0 348.4 %all-gather.25.cloned.1.call-start = ((), (), s32[]{:S(2)}) async-start(), calls=%async_computation.20 | async-start | bytes 7077888 | tf_op jit(solution)/shard_map/all_gather | solution.py:86
  461.6 429.6 %reduce-scatter.21.cloned.1.call-start = ((), (), s32[]{:S(2)}) async-start(), calls=%async_computation.23 | async-start | bytes 5242880 | tf_op jit(solution)/shard_map/reduce_scatter | solution.py:172
  848.3 83.4 %all-gather.29.cloned.1.call-start = ((), (), s32[]{:S(2)}) async-start(), calls=%async_computation.24 | async-start | bytes 5242880 | tf_op jit(solution)/shard_map/all_gather | solution.py:183
  897.0 381.9 %reduce-scatter.25.cloned.1.call-start = ((), (), s32[]{:S(2)}) async-start(), calls=%async_computation.26 | async-start | bytes 21626880 | tf_op jit(solution)/shard_map/reduce_scatter | solution.py:218
  1053.5 351.6 %reduce-scatter.35.cloned.1.call-start = ((), (), s32[]{:S(2)}) async-start(), calls=%async_computation.32 | async-start | bytes 7077888 | tf_op jit(solution)/shard_map/reduce_scatter | solution.py:265
  1066.6 406.0 %reduce-scatter.31.cloned.1.call-start = ((), (), s32[]{:S(2)}) async-start(), calls=%async_computation.30 | async-start | bytes 1474560 | tf_op jit(solution)/shard_map/reduce_scatter | solution.py:259
  1072.5 467.2 %reduce-scatter.27.cloned.1.call-start = ((), (), s32[]{:S(2)}) async-start(), calls=%async_computation.27 | async-start | bytes 1474560 | tf_op jit(solution)/shard_map/reduce_scatter | solution.py:253
  1091.1 658.3 %reduce-scatter.33.cloned.1.call-start = ((), (), s32[]{:S(2)}) async-start(), calls=%async_computation.31 | async-start | bytes 14155776 | tf_op jit(solution)/shard_map/reduce_scatter | solution.py:262
  1111.0 684.4 %reduce-scatter.23.cloned.1.call-start = ((), (), s32[]{:S(2)}) async-start(), calls=%async_computation.25 | async-start | bytes 5242880 | tf_op jit(solution)/shard_map/reduce_scatter | solution.py:236
  1116.7 163.5 %copy-start.36 = (f32[64]{0:T(128)S(1)}, f32[64]{0:T(128)}, u32[]{:S(2)}) copy-start(f32[64]{0:T(128)} %copy-done.35) | copy-start | bytes 772
  1116.8 753.0 %reduce-scatter.29.cloned.1.call-start = ((), (), s32[]{:S(2)}) async-start(), calls=%async_computation.28 | async-start | bytes 2949120 | tf_op jit(solution)/shard_map/reduce_scatter | solution.py:256
  1117.8 164.1 %copy-start.7 = (bf16[256,2048]{1,0:T(8,128)(2,1)S(1)}, bf16[256,2048]{1,0:T(8,128)(2,1)}, u32[]{:S(2)}) copy-start(bf16[256,2048]{1,0:T(8,128)(2,1)} %fusion.32) | copy-start | bytes 3145732
  1284.4 631.3 %reduce-scatter.19.cloned.1.call-start = ((), (), s32[]{:S(2)}) async-start(), calls=%async_computation.21 | async-start | bytes 5242880 | tf_op jit(solution)/shard_map/reduce_scatter | solution.py:158
  1295.8 684.2 %reduce-scatter.39.cloned.1.call-start = ((), (), s32[]{:S(2)}) async-start(), calls=%async_computation.34 | async-start | bytes 147456
  1474.2 321.2 %copy-start.1 = (bf16[256,2048]{1,0:T(8,128)(2,1)S(1)}, bf16[256,2048]{1,0:T(8,128)(2,1)}, u32[]{:S(2)}) copy-start(bf16[256,2048]{1,0:T(8,128)(2,1)} %param.11) | copy-start | bytes 3145732
  1474.2 321.2 %copy-start.26 = (f32[1,2048]{1,0:T(1,128)S(1)}, f32[1,2048]{1,0:T(1,128)}, u32[]{:S(2)}) copy-start(f32[1,2048]{1,0:T(1,128)} %copy-done.25) | copy-start | bytes 24580
  1754.8 160.9 %copy-start.24 = (f32[1,2048]{1,0:T(1,128)S(1)}, f32[1,2048]{1,0:T(1,128)}, u32[]{:S(2)}) copy-start(f32[1,2048]{1,0:T(1,128)} %copy-done.23) | copy-start | bytes 24580
  1801.4 243.5 %reduce-scatter.37.cloned.1.call-start = ((), (), s32[]{:S(2)}) async-start(), calls=%async_computation.33 | async-start | bytes 589824
  1803.2 275.5 %all-reduce.7.cloned.1.call-start = ((), (), s32[]{:S(2)}) async-start(), calls=%async_computation.29 | async-start | bytes 655360 | tf_op jit(solution)/shard_map/psum | solution.py:276
  (39 other events, 1081.6 us)
Sparse Core Ops, SparseCore 0:
  10.2 57.4 all-gather.14
  69.8 33.0 all-gather.10
  104.9 42.2 all-gather.12
  155.8 149.5 all-gather.16
  307.3 40.4 all-gather.18
  414.1 42.7 reduce-scatter.16
  459.8 176.4 all-gather.22
  638.5 32.6 all-gather.20
  672.9 34.4 all-gather.26
  709.5 99.9 all-gather.24
  848.4 42.6 reduce-scatter.20
  897.2 34.4 all-gather.28
  1053.6 225.3 reduce-scatter.24
  1282.4 122.6 reduce-scatter.34
  1408.4 64.1 reduce-scatter.30
  1475.8 63.8 reduce-scatter.26
  1543.1 206.2 reduce-scatter.32
  1751.8 43.5 reduce-scatter.22
  1799.4 70.3 reduce-scatter.28
  1872.3 43.3 reduce-scatter.18
  1919.1 60.8 reduce-scatter.38
  1983.9 60.9 reduce-scatter.36
  2047.4 31.3 all-reduce.6
where the time goes:
time: 2100 us; the launch traced here: 2090 us
  waiting for transfers between devices  1610 us (77%)
  matrix products  245 us (12%)
  local copies, waits for them, and re-layouts  128 us (6%)
  other arithmetic  63.9 us (3%)
  blocking collectives  28.2 us (1%)
    reduce_scatter x1, waiting for transfers between devices, local(): lax.psum_scatter(grad_in.astype(jnp.bfloat16), 'dp', scatter_dimension=0,...  208 us
    all_gather x1, waiting for transfers between devices, local(): lax.all_gather(w_in, 'dp', axis=0, tiled=True)  175 us
    reduce_scatter x1, waiting for transfers between devices, local(): lax.psum_scatter(d_keys, ('dp', 'tensor'), scatter_dimension=0, tiled=True)  160 us
    all_gather x1, waiting for transfers between devices, local(): lax.all_gather(keys_vals, 'dp', axis=0, tiled=True)  145 us
    unnamed x25, waiting for transfers between devices  127 us
    reduce_scatter x1, waiting for transfers between devices, local(): lax.psum_scatter(grad_down.astype(jnp.bfloat16), 'dp', scatter_dimension=...  108 us
    all_gather x1, waiting for transfers between devices, local(): lax.all_gather(w_down, 'dp', axis=1, tiled=True)  102 us
    reduce_scatter x1, waiting for transfers between devices, local(): lax.psum_scatter(grad_kv.astype(jnp.bfloat16), 'dp', scatter_dimension=0,...  65.8 us
  transfers between devices with their start and end apart: 23, of which 22 were waited for; matrix products, arithmetic and copies ran while one was open for 12% of the time, Pallas kernels for 0%

commit v1 on v0

v1 whole, which is shorter than its diff:
```python
import functools

import jax
import jax.numpy as jnp
from jax import lax
from jax.experimental import pallas as pl
from jax.experimental.pallas import tpu as pltpu
from jax.sharding import PartitionSpec as P

HEADS_KV = 5
HEAD = 64
SLOTS = 2048
STRETCH = 64
LANES = 128
FF_CHUNKS = 3
VMEM_LIMIT = 48 * 1024 * 1024

eps_norm = 1e-06
rope_base = 10000.0
neg_large = -1e30
f32 = jnp.float32
bf16 = jnp.bfloat16
contract_rows = (((0,), (0,)), ((), ()))
contract_cols = (((1,), (1,)), ((), ()))


def dot(a, b, dims=(((1,), (0,)), ((), ()))):
    return lax.dot_general(a, b, dims, preferred_element_type=f32)


def after(value, *deps):
    return lax.optimization_barrier((value, *deps))[0]


def levels(size):
    out, bit = [], 1
    while bit < size:
        if bit > 1 and 2 * bit < size:
            out.append([bit, 2 * bit, 3 * bit])
            bit *= 4
        else:
            out.append([bit])
            bit *= 2
    return out


def swap(value, axis, mask):
    size = lax.axis_size(axis)
    return lax.ppermute(value, axis, [(i, i ^ mask) for i in range(size)])


def gather_rel(value, axis):
    pieces = {0: value}
    for masks in reversed(levels(lax.axis_size(axis))):
        pieces.update({r ^ m: swap(p, axis, m) for r, p in list(pieces.items()) for m in masks})
    return [pieces[r] for r in range(lax.axis_size(axis))]


def gather_stacked(value, axis):
    stack = value[None]
    for masks in reversed(levels(lax.axis_size(axis))):
        parts = [stack] + [swap(stack, axis, m) for m in masks]
        stack = jnp.stack(parts, axis=1).reshape((-1,) + value.shape)
    return stack


def gather_rows(value, axis):
    index = lax.axis_index(axis)
    stack = value
    size = lax.axis_size(axis)
    bit = size // 2
    at = value.ndim - 2
    while bit:
        other = swap(stack, axis, bit)
        upper = (index & bit) != 0
        stack = jnp.stack(
            [jnp.where(upper, other, stack), jnp.where(upper, stack, other)], axis=at
        )
        bit //= 2
        at += 1
    lead = value.shape[:-2]
    return stack.reshape(lead + (size,) + value.shape[-2:])


def reduce_rel(make, axis):
    size = lax.axis_size(axis)
    held = None
    keep = list(range(size))
    arrived = {}
    for masks in levels(size):
        bits = functools.reduce(lambda a, b: a | b, masks)
        rest = [r for r in keep if not r & bits]
        for m in masks:
            group = [r ^ m for r in rest]
            for r, part in zip(group, make(group)):
                total = part
                for other in arrived.get(r, ()):
                    total = total + other.astype(f32)
                arrived.setdefault(r ^ m, []).append(swap(total.astype(bf16), axis, m))
        keep = rest
    (total,) = make([0])
    for other in arrived[0]:
        total = total + other.astype(f32)
    return total


def scaled_norm(value_in, gain_vec):
    return (
        value_in
        * lax.rsqrt(jnp.mean(value_in * value_in, axis=-1, keepdims=True) + eps_norm)
        * gain_vec
    )


def silu_product(gate, up_part):
    return gate * jax.nn.sigmoid(gate) * up_part


def params(steps=1):
    return pltpu.CompilerParams(
        dimension_semantics=("arbitrary",) * steps, vmem_limit_bytes=VMEM_LIMIT
    )


def swap_halves(value):
    half = HEAD // 2
    return jnp.concatenate([value[:, half:], value[:, :half]], axis=1)


def rope_one(raw, gain, cos, sin, factor):
    scale = lax.rsqrt(jnp.mean(raw * raw, axis=-1, keepdims=True) + eps_norm)
    normed = raw * scale * gain
    return (normed * cos + swap_halves(normed) * sin) * factor


def rope_back(raw, gain, cos, sin, factor, grad):
    grad = grad * factor
    grad = grad * cos - swap_halves(grad) * sin
    scale = lax.rsqrt(jnp.mean(raw * raw, axis=-1, keepdims=True) + eps_norm)
    weighted = grad * gain
    back = scale * weighted - raw * (
        scale * scale * scale * jnp.mean(raw * weighted, axis=-1, keepdims=True)
    )
    return back, jnp.sum(grad * raw * scale, axis=0, keepdims=True)


def query_kernel(h_ref, w_ref, cos_ref, sin_ref, gain_ref, raw_ref, out_ref):
    raw = dot(h_ref[...], w_ref[0])
    raw_ref[0] = raw
    rows, blocks = out_ref.shape[0], out_ref.shape[2]
    for h in range(HEADS_KV):
        turned = rope_one(
            raw[:, h * HEAD : (h + 1) * HEAD], gain_ref[...], cos_ref[...], sin_ref[...], 0.125
        )
        wide = jnp.concatenate([turned, jnp.zeros_like(turned)], axis=1).astype(bf16)
        out_ref[:, h, :, 0] = wide.reshape(rows, blocks, STRETCH, LANES)


def key_kernel(h_ref, w_ref, cos_ref, sin_ref, gain_ref, raw_ref, out_ref):
    raw = dot(h_ref[...], w_ref[...])
    raw_ref[...] = raw
    rows, blocks = out_ref.shape[0], out_ref.shape[2]
    for h in range(HEADS_KV):
        turned = rope_one(
            raw[:, h * HEAD : (h + 1) * HEAD], gain_ref[...], cos_ref[...], sin_ref[...], 1.0
        )
        start = (HEADS_KV + h) * HEAD
        wide = jnp.concatenate([turned, raw[:, start : start + HEAD]], axis=1).astype(bf16)
        out_ref[:, h] = wide.reshape(rows, blocks, STRETCH, LANES)


def attend_kernel(q_ref, limit_ref, keypos_ref, *rest):
    pieces, (out_ref, kv, kvt) = rest[:-3], rest[-3:]
    blocks = q_ref.shape[2]
    n = len(pieces)
    group = n * STRETCH
    for r, piece in enumerate(pieces):
        for g in range(blocks):
            kv[g * group + r * STRETCH : g * group + (r + 1) * STRETCH, :] = piece[0, 0, g]
    kvt[...] = kv[...].T
    for b in range(blocks):
        span = (b + 1) * group
        q = q_ref[0, 0, b].reshape(-1, LANES)
        scores = dot(kv[:span], q, contract_cols)
        scores = jnp.where(keypos_ref[0, :span] <= limit_ref[0, b], scores, neg_large)
        top = jnp.max(scores, axis=0, keepdims=True)
        weights = jnp.exp(scores - top)
        total = jnp.sum(weights, axis=0, keepdims=True)
        heads = dot(kvt[:, :span], weights.astype(bf16)) / total
        out_ref[0, 0, b] = heads.T.astype(bf16).reshape(q_ref.shape[3:])


def attend_back_kernel(q_ref, g_ref, limit_ref, keypos_ref, *rest):
    n = (len(rest) - 4) // 2
    pieces, dq_ref, outs, (kv, kvt, acc) = rest[:n], rest[n], rest[n + 1 : -3], rest[-3:]
    blocks = q_ref.shape[2]
    group = n * STRETCH
    for r, piece in enumerate(pieces):
        for g in range(blocks):
            kv[g * group + r * STRETCH : g * group + (r + 1) * STRETCH, :] = piece[0, 0, g]
    kvt[...] = kv[...].T
    acc[...] = jnp.zeros_like(acc)
    for b in range(blocks):
        span = (b + 1) * group
        q = q_ref[0, 0, b].reshape(-1, LANES)
        grad = g_ref[0, 0, b].reshape(-1, LANES)
        scores = dot(kv[:span], q, contract_cols)
        scores = jnp.where(keypos_ref[0, :span] <= limit_ref[0, b], scores, neg_large)
        top = jnp.max(scores, axis=0, keepdims=True)
        weights = jnp.exp(scores - top)
        probs = weights * (1.0 / jnp.sum(weights, axis=0, keepdims=True))
        d_probs = dot(kv[:span], grad, contract_cols)
        delta = jnp.sum(probs * d_probs, axis=0, keepdims=True)
        d_scores = (probs * (d_probs - delta)).astype(bf16)
        dq = dot(kvt[:, :span], d_scores)
        dq_ref[0, 0, b] = dq.T.reshape(q_ref.shape[3:])
        acc[:span] += dot(d_scores, q) + dot(probs.astype(bf16), grad)
    for r, out in enumerate(outs):
        for g in range(blocks):
            out[0, 0, g] = acc[g * group + r * STRETCH : g * group + (r + 1) * STRETCH].astype(bf16)


def out_kernel(o_ref, w_ref, attn_ref, heads_ref):
    rows = heads_ref.shape[1]

    @pl.when(pl.program_id(0) == 0)
    def _():
        for s in range(heads_ref.shape[0]):
            heads_ref[s] = jnp.concatenate(
                [o_ref[:, h, :, s].reshape(rows, LANES)[:, HEAD:] for h in range(HEADS_KV)], axis=1
            )

    attn_ref[0] = sum(dot(heads_ref[s], w_ref[s, 0]) for s in range(heads_ref.shape[0]))


def heads_back_kernel(d_ref, w_ref, out_ref, acc):
    step = pl.program_id(0)

    @pl.when(step == 0)
    def _():
        acc[...] = jnp.zeros_like(acc)

    for s in range(acc.shape[0]):
        acc[s] += dot(d_ref[0], w_ref[s, 0], contract_cols)

    @pl.when(step == pl.num_programs(0) - 1)
    def _():
        rows, blocks = out_ref.shape[0], out_ref.shape[2]
        for s in range(acc.shape[0]):
            for h in range(HEADS_KV):
                part = acc[s, :, h * HEAD : (h + 1) * HEAD]
                wide = jnp.concatenate([jnp.zeros_like(part), part], axis=1).astype(bf16)
                out_ref[:, h, :, s] = wide.reshape(rows, blocks, STRETCH, LANES)


def query_back_kernel(dq_ref, raw_ref, cos_ref, sin_ref, gain_ref, out_ref, dgain_ref):
    @pl.when(pl.program_id(0) == 0)
    def _():
        dgain_ref[...] = jnp.zeros_like(dgain_ref)

    raw = raw_ref[0]
    parts = []
    for h in range(HEADS_KV):
        grad = dq_ref[:, h, :, 0].reshape(raw.shape[0], LANES)[:, :HEAD]
        back, dgain = rope_back(
            raw[:, h * HEAD : (h + 1) * HEAD],
            gain_ref[...],
            cos_ref[...],
            sin_ref[...],
            0.125,
            grad,
        )
        parts.append(back)
        dgain_ref[...] += dgain
    out_ref[0] = jnp.concatenate(parts, axis=1).astype(bf16)


def key_back_kernel(sum_ref, raw_ref, cos_ref, sin_ref, gain_ref, out_ref, dgain_ref):
    raw = raw_ref[...]
    keys, values = [], []
    total = jnp.zeros_like(dgain_ref)
    for h in range(HEADS_KV):
        both = sum_ref[:, h].reshape(raw.shape[0], LANES)
        back, dgain = rope_back(
            raw[:, h * HEAD : (h + 1) * HEAD],
            gain_ref[...],
            cos_ref[...],
            sin_ref[...],
            1.0,
            both[:, :HEAD],
        )
        keys.append(back)
        values.append(both[:, HEAD:])
        total = total + dgain
    dgain_ref[...] = total
    out_ref[...] = jnp.concatenate(keys + values, axis=1).astype(bf16)


def back_kernel(dq_ref, wq_ref, dkv_ref, wkv_ref, out_ref):
    @pl.when(pl.program_id(0) == 0)
    def _():
        out_ref[...] = dot(dkv_ref[...], wkv_ref[...], contract_cols)

    out_ref[...] += dot(dq_ref[0], wq_ref[0], contract_cols)


def whole(shape):
    return pl.BlockSpec(shape, lambda *_: (0,) * len(shape))


def local(
    inputs,
    cotangent,
    w_query,
    w_kv,
    w_out,
    w_in,
    w_down,
    norm_gains,
    head_gains,
    lengths,
    slot_blocks,
):
    sp_rows, width = inputs.shape
    n = lax.axis_size("dp")
    n_tensor = lax.axis_size("tensor")
    dp = lax.axis_index("dp")
    tensor = lax.axis_index("tensor")
    seq_count = lengths.shape[0]
    row_span = sp_rows * n_tensor // seq_count
    blocks = row_span // STRETCH
    rows = sp_rows // row_span
    per_row = SLOTS // STRETCH
    cols = width // n
    q_cols = w_query.shape[1]
    kv_cols = w_kv.shape[1]
    ff = w_down.shape[0]
    rels = jnp.arange(n, dtype=jnp.int32)

    def reorder(value):
        return jnp.concatenate(
            [lax.dynamic_slice_in_dim(value, (dp ^ r) * cols, cols, axis=1) for r in range(n)],
            axis=1,
        )

    table = slot_blocks.reshape(n, n_tensor, rows, blocks)
    mine = lax.dynamic_index_in_dim(table, tensor, axis=1, keepdims=False)[dp ^ rels]
    inside = jnp.arange(STRETCH, dtype=jnp.int32)
    key_pos = (mine % per_row * STRETCH)[..., None] + inside
    own_pos = key_pos[0]
    own_len = lengths[mine[0] // per_row][..., None]
    live = (own_pos < own_len).astype(f32).reshape(sp_rows, 1)
    limit = jnp.minimum(own_pos, own_len - 1)
    limit = jnp.broadcast_to(limit[:, :, None, None, :], (rows, blocks, 1, n_tensor, STRETCH))
    limit = limit.reshape(rows, blocks, 1, n_tensor * STRETCH)
    key_pos = key_pos.transpose(1, 2, 0, 3).reshape(rows, SLOTS, 1)
    half = HEAD // 2
    frequency = rope_base ** (-2.0 * jnp.arange(half, dtype=f32) / HEAD)
    angles = own_pos.reshape(sp_rows, 1).astype(f32) * frequency
    cosine, sine = jnp.cos(angles), jnp.sin(angles)
    cos = jnp.concatenate([cosine, cosine], axis=1)
    sin = jnp.concatenate([-sine, sine], axis=1)
    head_float = head_gains.astype(f32)
    q_gain, k_gain = head_float[0:1], head_float[1:2]

    gains = reorder(jnp.concatenate(gather_rel(norm_gains, "dp"), axis=1)).astype(f32)
    gain_one, gain_two = gains[0], gains[1]
    part = w_kv.shape[0] // n_tensor
    kv_shard = lax.dynamic_slice_in_dim(w_kv, tensor * part, part, axis=0)
    kv_all = gather_rows(gather_stacked(kv_shard, "dp"), "tensor").reshape(width, kv_cols)
    query_all = gather_stacked(gather_stacked(w_query, "dp"), "tensor").reshape(
        n_tensor, width, q_cols
    )
    out_all = gather_stacked(gather_stacked(w_out, "dp"), "tensor")

    inputs_f = inputs.astype(f32)
    h_one_sp = scaled_norm(inputs_f, gain_one).astype(bf16)
    h_one_rel = reorder(h_one_sp)

    packed = (rows, HEADS_KV, blocks, n_tensor, STRETCH, LANES)
    packed_kv = (rows, HEADS_KV, blocks, STRETCH, LANES)
    kv_raw, kv_own = pl.pallas_call(
        key_kernel,
        out_shape=(
            jax.ShapeDtypeStruct((sp_rows, kv_cols), f32),
            jax.ShapeDtypeStruct(packed_kv, bf16),
        ),
        compiler_params=pltpu.CompilerParams(vmem_limit_bytes=VMEM_LIMIT),
        name="key_value",
    )(h_one_rel, kv_all, cos, sin, k_gain)
    kv_pieces = gather_rel(kv_own, "dp")
    one_head = (sp_rows, HEAD)
    part_spec = pl.BlockSpec(
        (rows, HEADS_KV, blocks, 1, STRETCH, LANES), lambda s: (0, 0, 0, s, 0, 0)
    )
    q_raw, queries = pl.pallas_call(
        query_kernel,
        grid=(n_tensor,),
        in_specs=[
            whole((sp_rows, width)),
            pl.BlockSpec((1, width, q_cols), lambda s: (s, 0, 0)),
            whole(one_head),
            whole(one_head),
            whole((1, HEAD)),
        ],
        out_specs=(pl.BlockSpec((1, sp_rows, q_cols), lambda s: (s, 0, 0)), part_spec),
        out_shape=(
            jax.ShapeDtypeStruct((n_tensor, sp_rows, q_cols), f32),
            jax.ShapeDtypeStruct(packed, bf16),
        ),
        compiler_params=params(),
        name="query",
    )(h_one_rel, query_all, cos, sin, q_gain)

    q_spec = pl.BlockSpec(
        (1, 1, blocks, n_tensor, STRETCH, LANES), lambda i, h: (i, h, 0, 0, 0, 0)
    )
    kv_spec = pl.BlockSpec((1, 1, blocks, STRETCH, LANES), lambda i, h: (i, h, 0, 0, 0))
    limit_spec = pl.BlockSpec(
        (1, blocks, 1, n_tensor * STRETCH), lambda i, h: (i, 0, 0, 0)
    )
    pos_spec = pl.BlockSpec((1, SLOTS, 1), lambda i, h: (i, 0, 0))
    heads_packed = pl.pallas_call(
        attend_kernel,
        grid=(rows, HEADS_KV),
        in_specs=[q_spec, limit_spec, pos_spec] + [kv_spec] * n,
        out_specs=q_spec,
        out_shape=jax.ShapeDtypeStruct(packed, bf16),
        scratch_shapes=[pltpu.VMEM((SLOTS, LANES), bf16), pltpu.VMEM((LANES, SLOTS), bf16)],
        compiler_params=params(2),
        name="attend",
    )(queries, limit, key_pos, *kv_pieces)

    out_spec = pl.BlockSpec((n_tensor, 1, q_cols, cols), lambda r: (0, r, 0, 0))
    col_spec = pl.BlockSpec((1, sp_rows, cols), lambda r: (r, 0, 0))
    heads_shape = (n_tensor, sp_rows, q_cols)
    attn_rel, attn_heads = pl.pallas_call(
        out_kernel,
        grid=(n,),
        in_specs=[whole(packed), out_spec],
        out_specs=(col_spec, whole(heads_shape)),
        out_shape=(
            jax.ShapeDtypeStruct((n, sp_rows, cols), f32),
            jax.ShapeDtypeStruct(heads_shape, bf16),
        ),
        compiler_params=params(),
        name="out",
    )(heads_packed, out_all)
    attn = jnp.concatenate(
        [lax.dynamic_index_in_dim(attn_rel, dp ^ r, axis=0, keepdims=False) for r in range(n)],
        axis=1,
    )
    mixed = inputs_f + live * attn
    h_two_sp = scaled_norm(mixed, gain_two).astype(bf16)

    d_ffn_sp = cotangent * live.astype(bf16)
    d_ffn = gather_stacked(d_ffn_sp, "tensor").reshape(-1, width)
    h_two = gather_stacked(h_two_sp, "tensor").reshape(-1, width)
    down_all = lax.all_gather(w_down, "dp", axis=0).transpose(1, 0, 2).reshape(ff, width)
    ff_part = ff // FF_CHUNKS
    in_parts = [
        lax.all_gather(
            w_in[:, :, c * ff_part : (c + 1) * ff_part].reshape(cols, 2 * ff_part),
            "dp",
            axis=0,
            tiled=True,
        )
        for c in range(FF_CHUNKS)
    ]
    d_hidden = dot(d_ffn, down_all, contract_cols)

    def block_of(value, r):
        return lax.dynamic_slice_in_dim(value, (dp ^ r) * cols, cols, axis=1)

    hidden_parts, d_gate_up_parts, sum_in_parts = [], [], []
    for c in range(FF_CHUNKS):
        gate_up = dot(h_two, in_parts[c])
        gate, up = gate_up[:, :ff_part], gate_up[:, ff_part:]
        hidden_parts.append(silu_product(gate, up).astype(bf16))
        pull = jax.vjp(silu_product, gate, up)[1]
        d_gate, d_up = pull(d_hidden[:, c * ff_part : (c + 1) * ff_part])
        d_gate_up = jnp.concatenate([d_gate, d_up], axis=1).astype(bf16)
        d_gate_up_parts.append(d_gate_up)
        sum_in_parts.append(
            reduce_rel(
                lambda rs, d=d_gate_up: [dot(block_of(h_two, r), d, contract_rows) for r in rs],
                "dp",
            ).reshape(cols, 2, ff_part)
        )
    sum_in = jnp.concatenate(sum_in_parts, axis=2)
    hidden = jnp.concatenate(hidden_parts, axis=1)
    d_gate_up = jnp.concatenate(d_gate_up_parts, axis=1)
    in_all = jnp.concatenate(in_parts, axis=1)
    sum_down = reduce_rel(
        lambda rs: [dot(hidden, block_of(d_ffn, r), contract_rows) for r in rs], "dp"
    )

    def rows_of(value, s):
        return value[s * sp_rows : (s + 1) * sp_rows]

    d_h_two = reduce_rel(
        lambda ss: [dot(rows_of(d_gate_up, s), in_all, contract_cols) for s in ss], "tensor"
    )
    norm_two_pull = jax.vjp(scaled_norm, mixed, gain_two)[1]
    d_mixed_norm, d_gain_two = norm_two_pull(d_h_two)
    d_mixed = cotangent.astype(f32) + d_mixed_norm
    ffn = reduce_rel(lambda ss: [dot(rows_of(hidden, s), down_all) for s in ss], "tensor")
    outputs = (mixed + live * ffn).astype(bf16)

    d_attn_sp = (live * d_mixed).astype(bf16)
    d_attn_rel = jnp.stack([block_of(d_attn_sp, r) for r in range(n)])
    d_heads = pl.pallas_call(
        heads_back_kernel,
        grid=(n,),
        in_specs=[col_spec, out_spec],
        out_specs=whole(packed),
        out_shape=jax.ShapeDtypeStruct(packed, bf16),
        scratch_shapes=[pltpu.VMEM(heads_shape, f32)],
        compiler_params=params(),
        name="heads_back",
    )(d_attn_rel, out_all)
    d_query, *d_kv_pieces = pl.pallas_call(
        attend_back_kernel,
        grid=(rows, HEADS_KV),
        in_specs=[q_spec, q_spec, limit_spec, pos_spec] + [kv_spec] * n,
        out_specs=[q_spec] + [kv_spec] * n,
        out_shape=[jax.ShapeDtypeStruct(packed, f32)]
        + [jax.ShapeDtypeStruct(packed_kv, bf16)] * n,
        scratch_shapes=[
            pltpu.VMEM((SLOTS, LANES), bf16),
            pltpu.VMEM((LANES, SLOTS), bf16),
            pltpu.VMEM((SLOTS, LANES), f32),
        ],
        compiler_params=params(2),
        name="attend_back",
    )(queries, d_heads, limit, key_pos, *kv_pieces)
    d_kv = reduce_rel(lambda rs: [d_kv_pieces[r].astype(f32) for r in rs], "dp")
    d_q_low, d_q_gain = pl.pallas_call(
        query_back_kernel,
        grid=(n_tensor,),
        in_specs=[
            part_spec,
            pl.BlockSpec((1, sp_rows, q_cols), lambda s: (s, 0, 0)),
            whole(one_head),
            whole(one_head),
            whole((1, HEAD)),
        ],
        out_specs=(pl.BlockSpec((1, sp_rows, q_cols), lambda s: (s, 0, 0)), whole((1, HEAD))),
        out_shape=(
            jax.ShapeDtypeStruct((n_tensor, sp_rows, q_cols), bf16),
            jax.ShapeDtypeStruct((1, HEAD), f32),
        ),
        compiler_params=params(),
        name="query_back",
    )(d_query, q_raw, cos, sin, q_gain)
    d_kv_low, d_k_gain = pl.pallas_call(
        key_back_kernel,
        out_shape=(
            jax.ShapeDtypeStruct((sp_rows, kv_cols), bf16),
            jax.ShapeDtypeStruct((1, HEAD), f32),
        ),
        compiler_params=pltpu.CompilerParams(vmem_limit_bytes=VMEM_LIMIT),
        name="key_value_back",
    )(d_kv, kv_raw, cos, sin, k_gain)
    d_h_one_rel = pl.pallas_call(
        back_kernel,
        grid=(n_tensor,),
        in_specs=[
            pl.BlockSpec((1, sp_rows, q_cols), lambda s: (s, 0, 0)),
            pl.BlockSpec((1, width, q_cols), lambda s: (s, 0, 0)),
            whole((sp_rows, kv_cols)),
            whole((width, kv_cols)),
        ],
        out_specs=whole((sp_rows, width)),
        out_shape=jax.ShapeDtypeStruct((sp_rows, width), f32),
        compiler_params=params(),
        name="h_one_back",
    )(d_q_low, query_all, d_kv_low, kv_all)
    d_h_one = reorder(d_h_one_rel)
    norm_one_pull = jax.vjp(scaled_norm, inputs_f, gain_one)[1]
    d_inputs_norm, d_gain_one = norm_one_pull(d_h_one)
    grad_inputs = (d_mixed + d_inputs_norm).astype(bf16)

    h_one = gather_stacked(after(h_one_sp, h_two_sp), "tensor").reshape(-1, width)
    d_attn = gather_stacked(d_attn_sp, "tensor").reshape(-1, width)

    def to_owner(parts):
        return jnp.concatenate(
            [parts[0]] + [swap(parts[s], "tensor", s) for s in range(1, n_tensor)], axis=0
        )

    heads_mine = to_owner(attn_heads)
    d_q_mine = to_owner(d_q_low)
    kv_part = kv_cols // n_tensor
    d_kv_mine = to_owner(
        [
            lax.dynamic_slice_in_dim(d_kv_low, (tensor ^ s) * kv_part, kv_part, axis=1)
            for s in range(n_tensor)
        ]
    )
    sum_out = reduce_rel(
        lambda rs: [dot(heads_mine, block_of(d_attn, r), contract_rows) for r in rs], "dp"
    )
    sum_query = reduce_rel(
        lambda rs: [dot(block_of(h_one, r), d_q_mine, contract_rows) for r in rs], "dp"
    )
    sum_kv_part = reduce_rel(
        lambda rs: [dot(block_of(h_one, r), d_kv_mine, contract_rows) for r in rs], "dp"
    )
    sum_kv = gather_rows(sum_kv_part.astype(bf16), "tensor")
    sum_kv = sum_kv.transpose(1, 0, 2).reshape(cols, kv_cols) if False else jnp.concatenate(
        [sum_kv[s] for s in range(n_tensor)], axis=1
    )

    grad_gains = jnp.stack([d_gain_one, d_gain_two])
    small = jnp.concatenate([grad_gains, jnp.tile(jnp.concatenate([d_q_gain, d_k_gain]), (1, 2))], axis=1)
    small = sum(gather_rel(small, "tensor"))
    heads_sum = small[:, width : width + HEAD]
    sum_gains = block_of(small, 0)
    for r in range(1, n):
        sum_gains = sum_gains + swap(block_of(small, r), "dp", r)
    sum_heads = heads_sum
    for r in range(1, n):
        sum_heads = sum_heads + swap(heads_sum, "dp", r)
    return (
        outputs,
        grad_inputs,
        sum_query,
        sum_kv.astype(f32),
        sum_out,
        sum_in,
        sum_down,
        sum_gains,
        sum_heads,
    )


def solution(mesh):
    in_specs = (
        P(("dp", "tensor"), None),
        P(("dp", "tensor"), None),
        P("dp", "tensor"),
        P("dp", None),
        P("tensor", "dp"),
        P("dp", None, "tensor"),
        P("tensor", "dp"),
        P(None, "dp"),
        P(),
        P(),
        P(),
    )
    out_specs = (
        P(("dp", "tensor"), None),
        P(("dp", "tensor"), None),
        P("dp", "tensor"),
        P("dp", None),
        P("tensor", "dp"),
        P("dp", None, "tensor"),
        P("tensor", "dp"),
        P(None, "dp"),
        P(),
    )
    return jax.shard_map(local, mesh=mesh, in_specs=in_specs, out_specs=out_specs, check_vma=False)
```

time: 2100 us -> 1100 us (0.52)
  waiting for transfers between devices: 1610 us -> 487 us
  starting transfers between devices: 1.29 us -> 167 us
  matrix products: 245 us -> 147 us
  Pallas kernels: 0 us -> 94.9 us
  local copies, waits for them, and re-layouts: 128 us -> 99.5 us
  blocking collectives: 28.2 us -> 0 us
    reduce_scatter x10 -> x0, waiting for transfers between devices: 841 us -> none  [the longest x1 208 us: local(): lax.psum_scatter(grad_in.astype(jnp.bfloat16), 'dp', scatter_dimension=0,...]
    all_gather x10 -> x4, waiting for transfers between devices: 611 us -> 0.01 us  [the longest x3 0.01 us: local(): lax.all_gather(w_in[:, :, c * ff_part:(c + 1) * ff_part].reshape(cols, 2...]
    ppermute x0 -> x130, waiting for transfers between devices: none -> 486 us  [swap(): return lax.ppermute(value, axis, [(i, i ^ mask) for i in range(size)])]
    ppermute x0 -> x130, starting transfers between devices: none -> 167 us  [swap(): return lax.ppermute(value, axis, [(i, i ^ mask) for i in range(size)])]
    unnamed x25 -> x4, waiting for transfers between devices: 127 us -> 0.07 us
    dot_general x21 -> x68, matrix products: 245 us -> 147 us  [dot(): return lax.dot_general(a, b, dims, preferred_element_type=f32)]
    pallas_call x0 -> x9, Pallas kernels: none -> 94.9 us  [the longest x1 31 us: local(): pl.pallas_call(attend_back_kernel, grid=(rows, HEADS_KV), in_specs=[q_spe...]
    another operation x5 -> x28, other arithmetic: 7.03 us -> 38 us  [the longest x20 37 us: gather_stacked(): stack = jnp.stack(parts, axis=1).reshape((-1,) + value.shape)]
  transfers between devices with their start and end apart: 23 -> 134, of which waited for: 22 -> 59; matrix products, arithmetic and copies ran while one was open for 12% -> 19% of each run, Pallas kernels for 0% -> 9%
where the time goes in v1:
time: 1100 us; the launch traced here: 1090 us
  waiting for transfers between devices  487 us (44%)
  starting transfers between devices  167 us (15%)
  matrix products  147 us (13%)
  local copies, waits for them, and re-layouts  99.5 us (9%)
  Pallas kernels  94.9 us (9%)
  other arithmetic  76.7 us (7%)
  between operations  16.1 us (1%)
    ppermute x130, waiting for transfers between devices, swap(): return lax.ppermute(value, axis, [(i, i ^ mask) for i in range(size)])  486 us
    ppermute x130, starting transfers between devices, swap(): return lax.ppermute(value, axis, [(i, i ^ mask) for i in range(size)])  167 us
    dot_general x68, matrix products, dot(): return lax.dot_general(a, b, dims, preferred_element_type=f32)  147 us
    unnamed x240, local copies, waits for them, and re-layouts  52.1 us
    another operation x20, other arithmetic, gather_stacked(): stack = jnp.stack(parts, axis=1).reshape((-1,) + value.shape)  37 us
    pallas_call x1, Pallas kernels, local(): pl.pallas_call(attend_back_kernel, grid=(rows, HEADS_KV), in_specs=[q_spe...  31 us
  transfers between devices with their start and end apart: 134, of which 59 were waited for; matrix products, arithmetic and copies ran while one was open for 19% of the time, Pallas kernels for 9%

profile of v1, /device:TPU:0, one launch (start us, length us, event | category | flops | bytes accessed | tf_op | source)
XLA Modules:
  0.0 1088.3 jit_solution(13695051988117644184)
XLA Ops:
  44.2 11.4 %collective-permute-done.8 = bf16[1,256,320]{1,2,0:T(8,128)(2,1)S(1)} collective-permute-done((bf16[1,256,320]{1,2,0:T(8,128)(2,1)}, bf16[1,256,320]{1,2,0:T(8,128)(2,1)S(1)}, u32[]{:S(2)}, u32[]{:S(2)}) %collective-permute-start.8) | collective-permute-done | bytes 163872 | tf_op jit(solution)/shard_map/ppermute | solution.py:49
  56.9 9.6 collective-permute-start.14
  80.5 20.1 %collective-permute-done.29 = bf16[4,320,256]{2,1,0:T(8,128)(2,1)S(1)} collective-permute-done((bf16[4,320,256]{2,1,0:T(8,128)(2,1)S(1)}, bf16[4,320,256]{2,1,0:T(8,128)(2,1)S(1)}, u32[]{:S(2)}, u32[]{:S(2)}) %collective-permute-start.29) | collective-permute-done | bytes 655392 | tf_op jit(solution)/shard_map/ppermute | solution.py:49
  102.3 10.6 collective-permute-done.16
  114.6 49.0 %collective-permute-done.17 = bf16[8,64,640]{2,1,0:T(8,128)(2,1)S(1)} collective-permute-done((bf16[8,64,640]{2,1,0:T(8,128)(2,1)S(1)}, bf16[8,64,640]{2,1,0:T(8,128)(2,1)S(1)}, u32[]{:S(2)}, u32[]{:S(2)}) %collective-permute-start.17) | collective-permute-done | bytes 655392 | tf_op jit(solution)/shard_map/ppermute | solution.py:49
  201.0 27.9 %collective-permute-done.22.rest_4_ = bf16[1,5,4,64,128]{4,3,2,1,0:T(8,128)(2,1)S(1)} collective-permute-done((bf16[1,5,4,64,128]{4,3,2,1,0:T(8,128)(2,1)S(1)}, bf16[1,5,4,64,128]{4,3,2,1,0:T(8,128)(2,1)S(1)}, u32[]{:S(2)}, u32[]{:S(2)}) %collective-permute-start.22) | collective-permute-done | bytes 327712 | tf_op jit(solution)/shard_map/ppermute | solution.py:49
  251.4 12.9 %query.1 = (f32[4,256,320]{2,1,0:T(8,128)S(1)}, bf16[1,5,4,4,64,128]{5,4,3,2,1,0:T(8,128)(2,1)S(1)}) custom-call(bf16[256,2048]{1,0:T(8,128)(2,1)S(1)} %dynamic-slice_dynamic-update-slice_fusion.8.h_ref, bf16[4,2048,320]{2,1,0:T(8,128)(2,1)} %bitcast.229, f32[256,64]{1,0:T(8,128)S(1)} %get-tuple-element.167.cos_ref, ...), custom_call_target="tpu_custom_call" | custom-call | tf_op jit(solution)/shard_map/query/pallas_call | solution.py:396
  266.6 18.9 %attend.1.o_ref = bf16[1,5,4,4,64,128]{5,4,3,2,1,0:T(8,128)(2,1)S(1)} custom-call(bf16[1,5,4,4,64,128]{5,4,3,2,1,0:T(8,128)(2,1)} %copy-done.5, s32[1,4,1,256]{3,2,1,0:T(1,128)S(1)} %broadcast_in_dim.47.limit_ref, s32[1,2048,1]{2,1,0:T(8,128)S(1)} %reshape.430.keypos_ref, bf16[1,5,4,64,128]{4,3,2,1,0:T(8,128)(2,1)S(1)} %get-tuple-element.30.rest_0_, ...), custom_call_target="tpu_custom_call" | custom-call | tf_op jit(solution)/shard_map/attend/pallas_call | solution.py:423
  298.2 22.5 %collective-permute-done.32 = bf16[1,256,2048]{2,1,0:T(8,128)(2,1)S(1)} collective-permute-done((bf16[1,256,2048]{2,1,0:T(8,128)(2,1)S(1)}, bf16[1,256,2048]{2,1,0:T(8,128)(2,1)S(1)}, u32[]{:S(2)}, u32[]{:S(2)}) %collective-permute-start.32) | collective-permute-done | bytes 1048608 | tf_op jit(solution)/shard_map/ppermute | solution.py:49
  328.7 14.3 %collective-permute-done.49 = bf16[1,256,2048]{2,1,0:T(8,128)(2,1)} collective-permute-done((bf16[1,256,2048]{2,1,0:T(8,128)(2,1)S(1)}, bf16[1,256,2048]{2,1,0:T(8,128)(2,1)}, u32[]{:S(2)}, u32[]{:S(2)}) %collective-permute-start.49) | collective-permute-done | bytes 1048608 | tf_op jit(solution)/shard_map/ppermute | solution.py:49
  401.3 15.3 %collective-permute-done.111 = bf16[1536,256]{1,0:T(8,128)(2,1)S(1)} collective-permute-done((bf16[1536,256]{1,0:T(8,128)(2,1)S(1)}, bf16[1536,256]{1,0:T(8,128)(2,1)S(1)}, u32[]{:S(2)}, u32[]{:S(2)}) %collective-permute-start.111) | collective-permute-done | bytes 786464 | tf_op jit(solution)/shard_map/ppermute | solution.py:49
  421.0 12.4 %collective-permute-done.109 = bf16[1536,256]{1,0:T(8,128)(2,1)S(1)} collective-permute-done((bf16[1536,256]{1,0:T(8,128)(2,1)S(1)}, bf16[1536,256]{1,0:T(8,128)(2,1)S(1)}, u32[]{:S(2)}, u32[]{:S(2)}) %collective-permute-start.109) | collective-permute-done | bytes 786464 | tf_op jit(solution)/shard_map/ppermute | solution.py:49
  436.9 13.3 %collective-permute-done.107 = bf16[1536,256]{1,0:T(8,128)(2,1)S(1)} collective-permute-done((bf16[1536,256]{1,0:T(8,128)(2,1)S(1)}, bf16[1536,256]{1,0:T(8,128)(2,1)S(1)}, u32[]{:S(2)}, u32[]{:S(2)}) %collective-permute-start.107) | collective-permute-done | bytes 786464 | tf_op jit(solution)/shard_map/ppermute | solution.py:49
  467.0 25.5 %collective-permute-done.110 = bf16[1536,256]{1,0:T(8,128)(2,1)S(1)} collective-permute-done((bf16[1536,256]{1,0:T(8,128)(2,1)S(1)}, bf16[1536,256]{1,0:T(8,128)(2,1)S(1)}, u32[]{:S(2)}, u32[]{:S(2)}) %collective-permute-start.110) | collective-permute-done | bytes 786464 | tf_op jit(solution)/shard_map/ppermute | solution.py:49
  513.6 10.4 fusion.253
  555.3 9.5 convolution_convert_fusion.6
  564.8 9.5 convolution_convert_fusion.7
  586.1 14.2 %collective-permute-done.90 = bf16[256,1024]{1,0:T(8,128)(2,1)S(1)} collective-permute-done((bf16[256,1024]{1,0:T(8,128)(2,1)}, bf16[256,1024]{1,0:T(8,128)(2,1)S(1)}, u32[]{:S(2)}, u32[]{:S(2)}) %collective-permute-start.90) | collective-permute-done | bytes 524320 | tf_op jit(solution)/shard_map/ppermute | solution.py:49
  602.7 8.8 collective-permute-done.88
  625.2 8.8 collective-permute-done.97
  636.4 8.8 collective-permute-done.95
  658.1 9.6 collective-permute-done.104
  670.2 8.8 collective-permute-done.102
  697.1 9.7 add_convert_fusion
  707.3 21.4 %collective-permute-start.96 = (bf16[256,1024]{1,0:T(8,128)(2,1)}, bf16[256,1024]{1,0:T(8,128)(2,1)S(1)}, u32[]{:S(2)}, u32[]{:S(2)}) collective-permute-start(bf16[256,1024]{1,0:T(8,128)(2,1)} %add_convert_fusion.10), channel_id=1, source_target_pairs={{0,16},{4,20},{8,24},{12,28},{16,0},{20,4},{24,8},{28,12},{1,17},{... | collective-permute-start | bytes 1572872 | tf_op jit(solution)/shard_map/ppermute | solution.py:49
  728.7 30.4 %collective-permute-done.89 = bf16[256,1024]{1,0:T(8,128)(2,1)} collective-permute-done((bf16[256,1024]{1,0:T(8,128)(2,1)}, bf16[256,1024]{1,0:T(8,128)(2,1)}, u32[]{:S(2)}, u32[]{:S(2)}) %collective-permute-start.89) | collective-permute-done | bytes 524320 | tf_op jit(solution)/shard_map/ppermute | solution.py:49
  768.2 11.9 %collective-permute-done.96 = bf16[256,1024]{1,0:T(8,128)(2,1)S(1)} collective-permute-done((bf16[256,1024]{1,0:T(8,128)(2,1)}, bf16[256,1024]{1,0:T(8,128)(2,1)S(1)}, u32[]{:S(2)}, u32[]{:S(2)}) %collective-permute-start.96) | collective-permute-done | bytes 524320 | tf_op jit(solution)/shard_map/ppermute | solution.py:49
  789.0 9.5 multiply_reduce_fusion
  799.5 10.6 collective-permute-done.36
  831.0 31.0 %attend_back.1 = (f32[1,5,4,4,64,128]{5,4,3,2,1,0:T(8,128)}, bf16[1,5,4,64,128]{4,3,2,1,0:T(8,128)(2,1)S(1)}, bf16[1,5,4,64,128]{4,3,2,1,0:T(8,128)(2,1)S(1)}, b...) custom-call(bf16[1,5,4,4,64,128]{5,4,3,2,1,0:T(8,128)(2,1)} %copy-do, ...), custom_call_target="tpu_custom_call" | custom-call | tf_op jit(solution)/shard_map/attend_back/pallas_call | solution.py:522
  938.5 17.3 %collective-permute-done.58 = bf16[256,320]{0,1:T(8,128)(2,1)S(1)} collective-permute-done((bf16[256,320]{0,1:T(8,128)(2,1)S(1)}, bf16[256,320]{0,1:T(8,128)(2,1)S(1)}, u32[]{:S(2)}, u32[]{:S(2)}) %collective-permute-start.58) | collective-permute-done | bytes 163872 | tf_op jit(solution)/shard_map/ppermute | solution.py:49
  982.9 9.1 collective-permute-done.114
  (675 shorter events, 569.2 us)
Async XLA Ops:
  7.2 339.4 %all-gather.6.cloned.1.call-start = ((), (), s32[]{:S(2)}) async-start(), calls=%async_computation | async-start | bytes 4718592 | tf_op jit(solution)/shard_map/all_gather | solution.py:462
  10.6 340.8 %all-gather.8.cloned.1.call-start = ((), (), s32[]{:S(2)}) async-start(), calls=%async_computation.1 | async-start | bytes 4718592 | tf_op jit(solution)/shard_map/all_gather | solution.py:462
  11.5 344.7 %all-gather.10.cloned.1.call-start = ((), (), s32[]{:S(2)}) async-start(), calls=%async_computation.2 | async-start | bytes 4718592 | tf_op jit(solution)/shard_map/all_gather | solution.py:462
  23.5 470.6 %all-gather.12.cloned.1.call-start = ((), (), s32[]{:S(2)}) async-start(), calls=%async_computation.3 | async-start | bytes 7077888 | tf_op jit(solution)/shard_map/all_gather | solution.py:459
  69.8 115.3 %collective-permute-start.37 = (bf16[1,256,2048]{2,1,0:T(8,128)(2,1)S(1)}, bf16[1,256,2048]{2,1,0:T(8,128)(2,1)S(1)}, u32[]{:S(2)}, u32[]{:S(2)}) collective-permute-start(bf16[1,256,2048]{2,1,0:T(8,128)(2,1)S(1)} %get-tuple-element.119), channel_id=1, source_target_pairs={{0,2},{1,3},{2,0},{3,1},{4,6},{5,7},{6,4},{7,5},{8,10},{9,11},{10,... | collective-permute-start | bytes 3145736 | tf_op jit(solution)/shard_map/ppermute | solution.py:49
  78.9 84.9 %collective-permute-start.11 = (bf16[1,8,256,320]{2,3,1,0:T(8,128)(2,1)S(1)}, bf16[1,8,256,320]{2,3,1,0:T(8,128)(2,1)S(1)}, u32[]{:S(2)}, u32[]{:S(2)}) collective-permute-start(bf16[1,8,256,320]{2,3,1,0:T(8,128)(2,1)S(1)} %bitcast.243), channel_id=1, source_target_pairs={{0,2},{1,3},{2,0},{3,1},{4,6},{5,7},{6,4},{7,5},{8,10},{9,11},{10,... | collective-permute-start | bytes 3932168 | tf_op jit(solution)/shard_map/ppermute | solution.py:49
  100.7 66.5 %collective-permute-start.30 = (bf16[1,8,320,256]{3,2,1,0:T(8,128)(2,1)S(1)}, bf16[1,8,320,256]{3,2,1,0:T(8,128)(2,1)S(1)}, u32[]{:S(2)}, u32[]{:S(2)}) collective-permute-start(bf16[1,8,320,256]{3,2,1,0:T(8,128)(2,1)S(1)} %bitcast.241), channel_id=1, source_target_pairs={{0,2},{1,3},{2,0},{3,1},{4,6},{5,7},{6,4},{7,5},{8,10},{9,11},{10,... | collective-permute-start | bytes 3932168 | tf_op jit(solution)/shard_map/ppermute | solution.py:49
  113.0 50.6 %collective-permute-start.17 = (bf16[8,64,640]{2,1,0:T(8,128)(2,1)S(1)}, bf16[8,64,640]{2,1,0:T(8,128)(2,1)S(1)}, u32[]{:S(2)}, u32[]{:S(2)}) collective-permute-start(bf16[8,64,640]{2,1,0:T(8,128)(2,1)S(1)} %bitcast.305), channel_id=1, source_target_pairs={{0,2},{1,3},{2,0},{3,1},{4,6},{5,7},{6,4},{7,5},{8,10},{9,11},{10,... | collective-permute-start | bytes 1966088 | tf_op jit(solution)/shard_map/ppermute | solution.py:49
  166.5 64.4 %collective-permute-start.12 = (bf16[2,8,256,320]{2,3,1,0:T(8,128)(2,1)}, bf16[2,8,256,320]{2,3,1,0:T(8,128)(2,1)}, u32[]{:S(2)}, u32[]{:S(2)}) collective-permute-start(bf16[2,8,256,320]{2,3,1,0:T(8,128)(2,1)} %get-tuple-element.103), channel_id=1, source_target_pairs={{0,1},{1,0},{2,3},{3,2},{4,5},{5,4},{6,7},{7,6},{8,9},{9,8},{10,11... | collective-permute-start | bytes 7864328 | tf_op jit(solution)/shard_map/ppermute | solution.py:49
  169.9 75.8 %collective-permute-start.31 = (bf16[2,8,320,256]{3,2,1,0:T(8,128)(2,1)}, bf16[2,8,320,256]{3,2,1,0:T(8,128)(2,1)}, u32[]{:S(2)}, u32[]{:S(2)}) collective-permute-start(bf16[2,8,320,256]{3,2,1,0:T(8,128)(2,1)} %get-tuple-element.99), channel_id=1, source_target_pairs={{0,1},{1,0},{2,3},{3,2},{4,5},{5,4},{6,7},{7,6},{8,9},{9,8},{10,11... | collective-permute-start | bytes 7864328 | tf_op jit(solution)/shard_map/ppermute | solution.py:49
  200.1 66.5 %collective-permute-start.19 = (bf16[1,5,4,64,128]{4,3,2,1,0:T(8,128)(2,1)S(1)}, bf16[1,5,4,64,128]{4,3,2,1,0:T(8,128)(2,1)}, u32[]{:S(2)}, u32[]{:S(2)}) collective-permute-start(bf16[1,5,4,64,128]{4,3,2,1,0:T(8,128)(2,1)S(1)} %get-tuple-element.30.rest_0_), channel_id=1, source_target_pairs={{0,4},{4,0},{8,12},{12,8},{16,20},{20,16},{24,28},{28,24},{1,5},{5... | collective-permute-start | bytes 983048 | tf_op jit(solution)/shard_map/ppermute | solution.py:49
  245.7 77.4 %collective-permute-start.38 = (bf16[2,256,2048]{2,1,0:T(8,128)(2,1)}, bf16[2,256,2048]{2,1,0:T(8,128)(2,1)}, u32[]{:S(2)}, u32[]{:S(2)}) collective-permute-start(bf16[2,256,2048]{2,1,0:T(8,128)(2,1)} %get-tuple-element.110), channel_id=1, source_target_pairs={{0,1},{1,0},{2,3},{3,2},{4,5},{5,4},{6,7},{7,6},{8,9},{9,8},{10,11... | collective-permute-start | bytes 6291464 | tf_op jit(solution)/shard_map/ppermute | solution.py:49
  296.4 46.6 %collective-permute-start.49 = (bf16[1,256,2048]{2,1,0:T(8,128)(2,1)S(1)}, bf16[1,256,2048]{2,1,0:T(8,128)(2,1)}, u32[]{:S(2)}, u32[]{:S(2)}) collective-permute-start(bf16[1,256,2048]{2,1,0:T(8,128)(2,1)S(1)} %bitcast.233), channel_id=1, source_target_pairs={{0,2},{1,3},{2,0},{3,1},{4,6},{5,7},{6,4},{7,5},{8,10},{9,11},{10,... | collective-permute-start | bytes 3145736 | tf_op jit(solution)/shard_map/ppermute | solution.py:49
  346.6 106.3 %collective-permute-start.50 = (bf16[2,256,2048]{2,1,0:T(8,128)(2,1)}, bf16[2,256,2048]{2,1,0:T(8,128)(2,1)}, u32[]{:S(2)}, u32[]{:S(2)}) collective-permute-start(bf16[2,256,2048]{2,1,0:T(8,128)(2,1)} %get-tuple-element.108), channel_id=1, source_target_pairs={{0,1},{1,0},{2,3},{3,2},{4,5},{5,4},{6,7},{7,6},{8,9},{9,8},{10,11... | collective-permute-start | bytes 6291464 | tf_op jit(solution)/shard_map/ppermute | solution.py:49
  397.9 52.3 %collective-permute-start.107 = (bf16[1536,256]{1,0:T(8,128)(2,1)S(1)}, bf16[1536,256]{1,0:T(8,128)(2,1)S(1)}, u32[]{:S(2)}, u32[]{:S(2)}) collective-permute-start(bf16[1536,256]{1,0:T(8,128)(2,1)S(1)} %convolution_convert_fusion.2), channel_id=1, source_target_pairs={{0,4},{4,0},{8,12},{12,8},{16,20},{20,16},{24,28},{28,24},{1,5},{5... | collective-permute-start | bytes 2359304 | tf_op jit(solution)/shard_map/ppermute | solution.py:49
  399.7 67.3 %collective-permute-start.106 = (bf16[1536,256]{1,0:T(8,128)(2,1)S(1)}, bf16[1536,256]{1,0:T(8,128)(2,1)S(1)}, u32[]{:S(2)}, u32[]{:S(2)}) collective-permute-start(bf16[1536,256]{1,0:T(8,128)(2,1)S(1)} %convolution_convert_fusion.3), channel_id=1, source_target_pairs={{0,4},{4,0},{8,12},{12,8},{16,20},{20,16},{24,28},{28,24},{1,5},{5... | collective-permute-start | bytes 2359304 | tf_op jit(solution)/shard_map/ppermute | solution.py:49
  417.6 49.4 %collective-permute-start.112 = (bf16[1536,256]{1,0:T(8,128)(2,1)S(1)}, bf16[1536,256]{1,0:T(8,128)(2,1)S(1)}, u32[]{:S(2)}, u32[]{:S(2)}) collective-permute-start(bf16[1536,256]{1,0:T(8,128)(2,1)S(1)} %add_convert_fusion.3), channel_id=1, source_target_pairs={{0,24},{4,28},{8,16},{12,20},{16,8},{20,12},{24,0},{28,4},{1,25},{... | collective-permute-start | bytes 2359304 | tf_op jit(solution)/shard_map/ppermute | solution.py:49
  434.4 58.1 %collective-permute-start.110 = (bf16[1536,256]{1,0:T(8,128)(2,1)S(1)}, bf16[1536,256]{1,0:T(8,128)(2,1)S(1)}, u32[]{:S(2)}, u32[]{:S(2)}) collective-permute-start(bf16[1536,256]{1,0:T(8,128)(2,1)S(1)} %add_convert_fusion.4), channel_id=1, source_target_pairs={{0,16},{4,20},{8,24},{12,28},{16,0},{20,4},{24,8},{28,12},{1,17},{... | collective-permute-start | bytes 2359304 | tf_op jit(solution)/shard_map/ppermute | solution.py:49
  574.3 132.5 %collective-permute-start.35 = (bf16[256,2048]{1,0:T(8,128)(2,1)}, bf16[256,2048]{1,0:T(8,128)(2,1)}, u32[]{:S(2)}, u32[]{:S(2)}) collective-permute-start(bf16[256,2048]{1,0:T(8,128)(2,1)} %convolution_convert_fusion.4), channel_id=1, source_target_pairs={{0,1},{1,0},{2,3},{3,2},{4,5},{5,4},{6,7},{7,6},{8,9},{9,8},{10,11... | collective-permute-start | bytes 3145736 | tf_op jit(solution)/shard_map/ppermute | solution.py:49
  574.3 117.4 %collective-permute-start.85 = (bf16[256,1024]{1,0:T(8,128)(2,1)S(1)}, bf16[256,1024]{1,0:T(8,128)(2,1)}, u32[]{:S(2)}, u32[]{:S(2)}) collective-permute-start(bf16[256,1024]{1,0:T(8,128)(2,1)S(1)} %convolution_convert_fusion.19), channel_id=1, source_target_pairs={{0,4},{4,0},{8,12},{12,8},{16,20},{20,16},{24,28},{28,24},{1,5},{5... | collective-permute-start | bytes 1572872 | tf_op jit(solution)/shard_map/ppermute | solution.py:49
  577.2 45.5 %collective-permute-start.86 = (bf16[256,1024]{1,0:T(8,128)(2,1)}, bf16[256,1024]{1,0:T(8,128)(2,1)S(1)}, u32[]{:S(2)}, u32[]{:S(2)}) collective-permute-start(bf16[256,1024]{1,0:T(8,128)(2,1)} %convolution_convert_fusion.18), channel_id=1, source_target_pairs={{0,4},{4,0},{8,12},{12,8},{16,20},{20,16},{24,28},{28,24},{1,5},{5... | collective-permute-start | bytes 1572872 | tf_op jit(solution)/shard_map/ppermute | solution.py:49
  691.8 67.3 %collective-permute-start.89 = (bf16[256,1024]{1,0:T(8,128)(2,1)}, bf16[256,1024]{1,0:T(8,128)(2,1)}, u32[]{:S(2)}, u32[]{:S(2)}) collective-permute-start(bf16[256,1024]{1,0:T(8,128)(2,1)} %add_convert_fusion.13), channel_id=1, source_target_pairs={{0,16},{4,20},{8,24},{12,28},{16,0},{20,4},{24,8},{28,12},{1,17},{... | collective-permute-start | bytes 1572872 | tf_op jit(solution)/shard_map/ppermute | solution.py:49
  692.8 66.4 %collective-permute-start.87 = (bf16[256,1024]{1,0:T(8,128)(2,1)}, bf16[256,1024]{1,0:T(8,128)(2,1)}, u32[]{:S(2)}, u32[]{:S(2)}) collective-permute-start(bf16[256,1024]{1,0:T(8,128)(2,1)} %add_convert_fusion.14), channel_id=1, source_target_pairs={{0,8},{4,12},{8,0},{12,4},{16,24},{20,28},{24,16},{28,20},{1,9},{5... | collective-permute-start | bytes 1572872 | tf_op jit(solution)/shard_map/ppermute | solution.py:49
  706.9 78.7 %collective-permute-start.39 = (bf16[256,2048]{1,0:T(8,128)(2,1)}, bf16[256,2048]{1,0:T(8,128)(2,1)S(1)}, u32[]{:S(2)}, u32[]{:S(2)}) collective-permute-start(bf16[256,2048]{1,0:T(8,128)(2,1)} %convolution_convert_fusion.7), channel_id=1, source_target_pairs={{0,1},{1,0},{2,3},{3,2},{4,5},{5,4},{6,7},{7,6},{8,9},{9,8},{10,11... | collective-permute-start | bytes 3145736 | tf_op jit(solution)/shard_map/ppermute | solution.py:49
  706.9 61.3 %collective-permute-start.98 = (bf16[256,1024]{1,0:T(8,128)(2,1)}, bf16[256,1024]{1,0:T(8,128)(2,1)S(1)}, u32[]{:S(2)}, u32[]{:S(2)}) collective-permute-start(bf16[256,1024]{1,0:T(8,128)(2,1)} %add_convert_fusion.9), channel_id=1, source_target_pairs={{0,24},{4,28},{8,16},{12,20},{16,8},{20,12},{24,0},{28,4},{1,25},{... | collective-permute-start | bytes 1572872 | tf_op jit(solution)/shard_map/ppermute | solution.py:49
  707.3 72.9 %collective-permute-start.96 = (bf16[256,1024]{1,0:T(8,128)(2,1)}, bf16[256,1024]{1,0:T(8,128)(2,1)S(1)}, u32[]{:S(2)}, u32[]{:S(2)}) collective-permute-start(bf16[256,1024]{1,0:T(8,128)(2,1)} %add_convert_fusion.10), channel_id=1, source_target_pairs={{0,16},{4,20},{8,24},{12,28},{16,0},{20,4},{24,8},{28,12},{1,17},{... | collective-permute-start | bytes 1572872 | tf_op jit(solution)/shard_map/ppermute | solution.py:49
  780.1 92.2 %collective-permute-start.99 = (bf16[256,1024]{1,0:T(8,128)(2,1)}, bf16[256,1024]{1,0:T(8,128)(2,1)}, u32[]{:S(2)}, u32[]{:S(2)}) collective-permute-start(bf16[256,1024]{1,0:T(8,128)(2,1)} %convolution_convert_fusion.11), channel_id=1, source_target_pairs={{0,4},{4,0},{8,12},{12,8},{16,20},{20,16},{24,28},{28,24},{1,5},{5... | collective-permute-start | bytes 1572872 | tf_op jit(solution)/shard_map/ppermute | solution.py:49
  781.7 92.2 %collective-permute-start.105 = (bf16[256,1024]{1,0:T(8,128)(2,1)}, bf16[256,1024]{1,0:T(8,128)(2,1)}, u32[]{:S(2)}, u32[]{:S(2)}) collective-permute-start(bf16[256,1024]{1,0:T(8,128)(2,1)} %add_convert_fusion.6), channel_id=1, source_target_pairs={{0,24},{4,28},{8,16},{12,20},{16,8},{20,12},{24,0},{28,4},{1,25},{... | collective-permute-start | bytes 1572872 | tf_op jit(solution)/shard_map/ppermute | solution.py:49
  785.6 88.6 %collective-permute-start.103 = (bf16[256,1024]{1,0:T(8,128)(2,1)}, bf16[256,1024]{1,0:T(8,128)(2,1)}, u32[]{:S(2)}, u32[]{:S(2)}) collective-permute-start(bf16[256,1024]{1,0:T(8,128)(2,1)} %add_convert_fusion.7), channel_id=1, source_target_pairs={{0,16},{4,20},{8,24},{12,28},{16,0},{20,4},{24,8},{28,12},{1,17},{... | collective-permute-start | bytes 1572872 | tf_op jit(solution)/shard_map/ppermute | solution.py:49
  798.5 75.8 %collective-permute-start.101 = (bf16[256,1024]{1,0:T(8,128)(2,1)}, bf16[256,1024]{1,0:T(8,128)(2,1)S(1)}, u32[]{:S(2)}, u32[]{:S(2)}) collective-permute-start(bf16[256,1024]{1,0:T(8,128)(2,1)} %add_convert_fusion.8), channel_id=1, source_target_pairs={{0,8},{4,12},{8,0},{12,4},{16,24},{20,28},{24,16},{28,20},{1,9},{5... | collective-permute-start | bytes 1572872 | tf_op jit(solution)/shard_map/ppermute | solution.py:49
  886.4 82.6 %collective-permute-start.42 = (bf16[1,5,4,64,128]{4,3,2,1,0:T(8,128)(2,1)S(1)}, bf16[1,5,4,64,128]{4,3,2,1,0:T(8,128)(2,1)S(1)}, u32[]{:S(2)}, u32[]{:S(2)}) collective-permute-start(bf16[1,5,4,64,128]{4,3,2,1,0:T(8,128)(2,1)S(1)} %get-tuple-element.36), channel_id=1, source_target_pairs={{0,4},{4,0},{8,12},{12,8},{16,20},{20,16},{24,28},{28,24},{1,5},{5... | collective-permute-start | bytes 983048 | tf_op jit(solution)/shard_map/ppermute | solution.py:49
  921.5 47.5 %collective-permute-start.44 = (bf16[1,5,4,64,128]{4,3,2,1,0:T(8,128)(2,1)S(1)}, bf16[1,5,4,64,128]{4,3,2,1,0:T(8,128)(2,1)S(1)}, u32[]{:S(2)}, u32[]{:S(2)}) collective-permute-start(bf16[1,5,4,64,128]{4,3,2,1,0:T(8,128)(2,1)S(1)} %add_convert_fusion.17), channel_id=1, source_target_pairs={{0,8},{4,12},{8,0},{12,4},{16,24},{20,28},{24,16},{28,20},{1,9},{5... | collective-permute-start | bytes 983048 | tf_op jit(solution)/shard_map/ppermute | solution.py:49
  (198 other events, 3874.2 us)
Sparse Core Ops, SparseCore 0:
  10.7 118.6 all-gather.5
  131.5 91.6 all-gather.7
  225.3 75.0 all-gather.9
  323.1 138.7 all-gather.11

commit v2 on v1

v2 whole, which is shorter than its diff:
```python
import functools

import jax
import jax.numpy as jnp
from jax import lax
from jax.experimental import layout
from jax.experimental import pallas as pl
from jax.experimental.pallas import tpu as pltpu
from jax.sharding import PartitionSpec as P

HEADS_KV = 5
HEAD = 64
SLOTS = 2048
STRETCH = 64
LANES = 128
FF_PARTS = (1, 1, 1, 1, 1, 1)
VMEM_LIMIT = 48 * 1024 * 1024
SMALL = pl.CostEstimate(flops=1000, bytes_accessed=1000, transcendentals=0)

eps_norm = 1e-06
rope_base = 10000.0
neg_large = -1e30
f32 = jnp.float32
bf16 = jnp.bfloat16
contract_rows = (((0,), (0,)), ((), ()))
contract_cols = (((1,), (1,)), ((), ()))


def dot(a, b, dims=(((1,), (0,)), ((), ()))):
    return lax.dot_general(a, b, dims, preferred_element_type=f32)


def after(value, *deps):
    return lax.optimization_barrier((value, *deps))[0]


def masks_of(axis):
    size = lax.axis_size(axis)
    bits = [1 << i for i in range(1, size.bit_length() - 1)]
    return bits + [1]


def order_of(axis):
    order = [0]
    for mask in masks_of(axis):
        order = order + [r ^ mask for r in order]
    return order


def swap(value, axis, mask):
    size = lax.axis_size(axis)
    return lax.ppermute(value, axis, [(i, i ^ mask) for i in range(size)])


def join(first, second):
    both = jnp.concatenate([first, second], axis=0)
    return layout.with_layout_constraint(both, layout.Layout(tuple(range(both.ndim))))


def gather(value, axis):
    stack = value[None]
    for mask in masks_of(axis):
        stack = join(stack, swap(stack, axis, mask))
    return stack


def gather_rows(value, axis):
    index = lax.axis_index(axis)
    stack = value
    size = lax.axis_size(axis)
    bit = size // 2
    at = value.ndim - 2
    while bit:
        other = swap(stack, axis, bit)
        upper = (index & bit) != 0
        stack = jnp.stack(
            [jnp.where(upper, other, stack), jnp.where(upper, stack, other)], axis=at
        )
        bit //= 2
        at += 1
    return stack.reshape(value.shape[:-2] + (size,) + value.shape[-2:])


def scatter(make, axis):
    half = lax.axis_size(axis)
    arrived = []
    for mask in reversed(masks_of(axis)):
        half //= 2
        sent = make(half, 2 * half, [x[half : 2 * half] for x in arrived], bf16)
        arrived = [x[:half] for x in arrived] + [swap(sent, axis, mask)]
    return make(0, 1, arrived, f32)[0]


def phases():
    masks = masks_of("dp")
    return [masks[:1], masks[1:-1], masks[-1:]]


class Item:
    late = ()

    def bring(self, value, axis, mask):
        got = swap(value, axis, mask)
        return after(got, *self.late) if self.late else got


class Gather(Item):
    def __init__(self, value):
        self.stack, self.halves, self.phase = value[None], None, 0

    def value(self):
        return self.stack

    def advance(self, value):
        for mask in phases()[self.phase]:
            got = self.bring(value, "dp", mask)
            self.halves = (value, got)
            value = join(value, got)
        self.stack = value
        self.phase += 1
        return got

    def pieces(self):
        half = order_of("dp")[: lax.axis_size("dp") // 2]
        return [(x, [r ^ m for r in half]) for x, m in zip(self.halves, (0, masks_of("dp")[-1]))]


class GatherLate(Item):
    def __init__(self, value):
        self.parts, self.phase = [(value[None], [0])], 0

    def value(self):
        return self.parts[max(self.phase - 2, 0)][0]

    def advance(self, value):
        masks = masks_of("dp")
        masks = [masks[-1:], masks[:1], masks[1:-1], masks[1:-1]][self.phase]
        at = max(self.phase - 2, 0)
        places = self.parts[at][1]
        for mask in masks:
            got = self.bring(value, "dp", mask)
            halves = [(value, places), (got, [r ^ mask for r in places])]
            places = places + halves[1][1]
            if mask != masks[-1] or self.phase == 0:
                value = join(value, got)
        if self.phase == 0:
            self.parts = [(value, places)]
        elif self.phase == 1:
            self.parts = halves
        elif self.phase == 2:
            self.parts, self.first = [None, self.parts[1]], halves
        else:
            self.parts = self.first + halves
        self.phase += 1
        return got

    def pieces(self):
        return self.parts


class Scatter(Item):
    def __init__(self, make):
        self.make, self.half, self.arrived, self.phase = make, lax.axis_size("dp"), [], 2

    def value(self):
        half = self.half // 2
        return self.make(half, 2 * half, [x[half : 2 * half] for x in self.arrived], bf16)

    def advance(self, value):
        for k, mask in enumerate(reversed(phases()[self.phase])):
            if k:
                value = self.value()
            self.half //= 2
            got = self.bring(value, "dp", mask)
            self.arrived = [x[: self.half] for x in self.arrived] + [got]
        self.phase -= 1
        return got

    def result(self):
        return self.make(0, 1, self.arrived, f32)[0]


class TensorGather(Item):
    def __init__(self, value):
        self.stack, self.masks = value[None], masks_of("tensor")

    def value(self):
        return self.stack

    def advance(self, value):
        got = self.bring(value, "tensor", self.masks[0])
        self.stack, self.masks = join(value, got), self.masks[1:]
        return got


class PairRows(Item):
    def __init__(self, value):
        self.stack = value

    def value(self):
        return self.stack

    def advance(self, value):
        got = self.bring(value, "tensor", 1)
        upper = (lax.axis_index("tensor") & 1) != 0
        self.stack = jnp.stack(
            [jnp.where(upper, got, value), jnp.where(upper, value, got)], axis=value.ndim - 2
        )
        return got


class TensorScatter(Item):
    def __init__(self, sums):
        self.sums, self.masks, self.arrived = sums, masks_of("tensor")[::-1], []

    def value(self):
        half = 1 << (len(self.masks) - 1)
        if half == self.sums[1].shape[0]:
            return self.sums[1]
        return plus(
            self.sums[0][half : 2 * half].astype(f32),
            [x[half : 2 * half] for x in self.arrived],
            bf16,
        )

    def advance(self, value):
        self.arrived.append(self.bring(value, "tensor", self.masks[0]))
        self.masks = self.masks[1:]
        return self.arrived[-1]

    def terms(self):
        return [self.sums[0], *self.arrived]


class TensorExchange(Item):
    def __init__(self, stack):
        self.stack, self.masks = stack[:, None], masks_of("tensor")

    def value(self):
        return self.stack[1::2]

    def advance(self, value):
        got = self.bring(value, "tensor", self.masks[0])
        self.stack = jnp.concatenate([self.stack[0::2], got], axis=1)
        self.masks = self.masks[1:]
        return got

    def rows(self):
        return self.stack.reshape((-1,) + self.stack.shape[3:])


class Direct(Item):
    def __init__(self, parts):
        self.parts = parts

    def value(self):
        return jnp.stack(self.parts)

    def advance(self, value):
        order = order_of("tensor")
        got = [value[0]] + [
            self.bring(value[p], "tensor", order[p]) for p in range(1, len(order))
        ]
        self.all = jnp.concatenate(got, axis=0)
        return self.all

    def rows(self):
        return self.all


class Rounds:
    def __init__(self):
        self.done = []

    def go(self, *items, ends=(), during=()):
        done = list(ends)
        for item in items:
            value = item.value()
            if self.done:
                value = after(value, *self.done)
            item.late = during
            done.append(item.advance(value))
        self.done = done


def plus(total, arrived, kind):
    for other in arrived:
        total = total + other.astype(f32)
    return total.astype(kind)


def scaled_norm(value_in, gain_vec):
    return (
        value_in
        * lax.rsqrt(jnp.mean(value_in * value_in, axis=-1, keepdims=True) + eps_norm)
        * gain_vec
    )


def silu_product(gate, up_part):
    return gate * jax.nn.sigmoid(gate) * up_part


def params(steps=1):
    return pltpu.CompilerParams(
        dimension_semantics=("arbitrary",) * steps, vmem_limit_bytes=VMEM_LIMIT
    )


def swap_halves(value):
    half = HEAD // 2
    return jnp.concatenate([value[:, half:], value[:, :half]], axis=1)


def rope_one(raw, gain, cos, sin, factor):
    scale = lax.rsqrt(jnp.mean(raw * raw, axis=-1, keepdims=True) + eps_norm)
    normed = raw * scale * gain
    return (normed * cos + swap_halves(normed) * sin) * factor


def rope_back(raw, gain, cos, sin, factor, grad):
    grad = grad * factor
    grad = grad * cos - swap_halves(grad) * sin
    scale = lax.rsqrt(jnp.mean(raw * raw, axis=-1, keepdims=True) + eps_norm)
    weighted = grad * gain
    back = scale * weighted - raw * (
        scale * scale * scale * jnp.mean(raw * weighted, axis=-1, keepdims=True)
    )
    return back, jnp.sum(grad * raw * scale, axis=0, keepdims=True)


def query_kernel(h_ref, w_ref, cos_ref, sin_ref, gain_ref, raw_ref, out_ref):
    cols = w_ref.shape[3]
    raw = sum(
        dot(h_ref[:, r * cols : (r + 1) * cols], w_ref[0, r], contract_cols)
        for r in range(w_ref.shape[1])
    )
    raw_ref[0] = raw
    rows, blocks = out_ref.shape[0], out_ref.shape[2]
    for h in range(HEADS_KV):
        turned = rope_one(
            raw[:, h * HEAD : (h + 1) * HEAD], gain_ref[...], cos_ref[...], sin_ref[...], 0.125
        )
        wide = jnp.concatenate([turned, jnp.zeros_like(turned)], axis=1).astype(bf16)
        out_ref[:, h, :, 0] = wide.reshape(rows, blocks, STRETCH, LANES)


def key_kernel(h_ref, w_ref, cos_ref, sin_ref, gain_ref, raw_ref, out_ref):
    raw = dot(h_ref[...], w_ref[...])
    raw_ref[...] = raw
    rows, blocks = out_ref.shape[0], out_ref.shape[2]
    for h in range(HEADS_KV):
        turned = rope_one(
            raw[:, h * HEAD : (h + 1) * HEAD], gain_ref[...], cos_ref[...], sin_ref[...], 1.0
        )
        start = (HEADS_KV + h) * HEAD
        wide = jnp.concatenate([turned, raw[:, start : start + HEAD]], axis=1).astype(bf16)
        out_ref[:, h] = wide.reshape(rows, blocks, STRETCH, LANES)


def load_keys(halves, kv, kvt):
    places = [(half, i) for half in halves for i in range(half.shape[0])]
    group = len(places) * STRETCH
    for g in range(halves[0].shape[3]):
        for r, (half, i) in enumerate(places):
            start = g * group + r * STRETCH
            kv[start : start + STRETCH, :] = half[i, 0, 0, g]
    kvt[...] = kv[...].T
    return group


def attend_kernel(q_ref, limit_ref, keypos_ref, low_ref, high_ref, out_ref, kv, kvt):
    blocks = q_ref.shape[2]
    group = load_keys((low_ref, high_ref), kv, kvt)
    for b in range(blocks):
        span = (b + 1) * group
        q = q_ref[0, 0, b].reshape(-1, LANES)
        scores = dot(kv[:span], q, contract_cols)
        scores = jnp.where(keypos_ref[0, :span] <= limit_ref[0, b], scores, neg_large)
        top = jnp.max(scores, axis=0, keepdims=True)
        weights = jnp.exp(scores - top)
        total = jnp.sum(weights, axis=0, keepdims=True)
        heads = dot(kvt[:, :span], weights.astype(bf16)) / total
        out_ref[0, 0, b] = heads.T.astype(bf16).reshape(q_ref.shape[3:])


def attend_back_kernel(
    q_ref, g_ref, limit_ref, keypos_ref, low_ref, high_ref, dq_ref, dlow_ref, dhigh_ref, kv, kvt, acc
):
    blocks = q_ref.shape[2]
    group = load_keys((low_ref, high_ref), kv, kvt)
    acc[...] = jnp.zeros_like(acc)
    for b in range(blocks):
        span = (b + 1) * group
        q = q_ref[0, 0, b].reshape(-1, LANES)
        grad = g_ref[0, 0, b].reshape(-1, LANES)
        scores = dot(kv[:span], q, contract_cols)
        scores = jnp.where(keypos_ref[0, :span] <= limit_ref[0, b], scores, neg_large)
        top = jnp.max(scores, axis=0, keepdims=True)
        weights = jnp.exp(scores - top)
        probs = weights * (1.0 / jnp.sum(weights, axis=0, keepdims=True))
        d_probs = dot(kv[:span], grad, contract_cols)
        delta = jnp.sum(probs * d_probs, axis=0, keepdims=True)
        d_scores = (probs * (d_probs - delta)).astype(bf16)
        dq = dot(kvt[:, :span], d_scores)
        dq_ref[0, 0, b] = dq.T.reshape(q_ref.shape[3:])
        acc[:span] += dot(d_scores, q) + dot(probs.astype(bf16), grad)
    count = dlow_ref.shape[0]
    for out, first in ((dlow_ref, 0), (dhigh_ref, count)):
        for r in range(count):
            for g in range(blocks):
                start = g * group + (first + r) * STRETCH
                out[r, 0, 0, g] = acc[start : start + STRETCH].astype(bf16)


def out_kernel(o_ref, w_ref, x_ref, live_ref, gain_ref, mixed_ref, h_ref, heads_ref):
    rows = heads_ref.shape[1]
    heads = jnp.concatenate(
        [o_ref[:, h, :, 0].reshape(rows, LANES)[:, HEAD:] for h in range(HEADS_KV)], axis=1
    )
    heads_ref[0] = heads
    cols = w_ref.shape[3]

    @pl.when(pl.program_id(0) == 0)
    def _():
        mixed_ref[...] = jnp.zeros_like(mixed_ref)

    for r in range(w_ref.shape[1]):
        mixed_ref[:, r * cols : (r + 1) * cols] += dot(heads, w_ref[0, r])

    @pl.when(pl.program_id(0) == pl.num_programs(0) - 1)
    def _():
        mixed = x_ref[...].astype(f32) + live_ref[...] * mixed_ref[...]
        mixed_ref[...] = mixed
        h_ref[...] = scaled_norm(mixed, gain_ref[...]).astype(bf16)


def norm_back(value, gain, grad):
    scale = lax.rsqrt(jnp.mean(value * value, axis=-1, keepdims=True) + eps_norm)
    weighted = grad * gain
    inner = jnp.mean(value * weighted, axis=-1, keepdims=True)
    back = scale * weighted - value * (scale * scale * scale * inner)
    return back, jnp.sum(grad * value * scale, axis=0, keepdims=True)


def mixed_back_kernel(mixed_ref, cot_ref, gain_ref, live_ref, *rest):
    terms, (d_mixed_ref, d_attn_ref, dgain_ref) = rest[:-3], rest[-3:]
    grad = sum(ref[0].astype(f32) for ref in terms)
    back, dgain_ref[...] = norm_back(mixed_ref[...], gain_ref[...], grad)
    d_mixed = cot_ref[...].astype(f32) + back
    d_mixed_ref[...] = d_mixed
    d_attn_ref[...] = (live_ref[...] * d_mixed).astype(bf16)


def heads_back_kernel(d_ref, w_ref, out_ref):
    cols = w_ref.shape[3]
    grad = sum(
        dot(d_ref[:, r * cols : (r + 1) * cols], w_ref[0, r], contract_cols)
        for r in range(w_ref.shape[1])
    )
    rows, blocks = out_ref.shape[0], out_ref.shape[2]
    for h in range(HEADS_KV):
        part = grad[:, h * HEAD : (h + 1) * HEAD]
        wide = jnp.concatenate([jnp.zeros_like(part), part], axis=1).astype(bf16)
        out_ref[:, h, :, 0] = wide.reshape(rows, blocks, STRETCH, LANES)


def query_back_kernel(dq_ref, raw_ref, cos_ref, sin_ref, gain_ref, out_ref, dgain_ref):
    @pl.when(pl.program_id(0) == 0)
    def _():
        dgain_ref[...] = jnp.zeros_like(dgain_ref)

    raw = raw_ref[0]
    parts = []
    for h in range(HEADS_KV):
        grad = dq_ref[:, h, :, 0].reshape(raw.shape[0], LANES)[:, :HEAD]
        back, dgain = rope_back(
            raw[:, h * HEAD : (h + 1) * HEAD],
            gain_ref[...],
            cos_ref[...],
            sin_ref[...],
            0.125,
            grad,
        )
        parts.append(back)
        dgain_ref[...] += dgain
    out_ref[0] = jnp.concatenate(parts, axis=1).astype(bf16)


def key_back_kernel(sum_ref, raw_ref, cos_ref, sin_ref, gain_ref, out_ref, dgain_ref):
    raw = raw_ref[...]
    keys, values = [], []
    total = jnp.zeros_like(dgain_ref)
    for h in range(HEADS_KV):
        both = sum_ref[:, h].reshape(raw.shape[0], LANES)
        back, dgain = rope_back(
            raw[:, h * HEAD : (h + 1) * HEAD],
            gain_ref[...],
            cos_ref[...],
            sin_ref[...],
            1.0,
            both[:, :HEAD],
        )
        keys.append(back)
        values.append(both[:, HEAD:])
        total = total + dgain
    dgain_ref[...] = total
    out_ref[...] = jnp.concatenate(keys + values, axis=1).astype(bf16)


def back_kernel(
    dq_ref, wq_ref, dkv_ref, wkv_ref, x_ref, gain_ref, d_mixed_ref, out_ref, dgain_ref, acc
):
    @pl.when(pl.program_id(0) == 0)
    def _():
        acc[...] = dot(dkv_ref[...], wkv_ref[...], contract_cols)

    cols = wq_ref.shape[3]
    for r in range(wq_ref.shape[1]):
        acc[:, r * cols : (r + 1) * cols] += dot(dq_ref[0], wq_ref[0, r])

    @pl.when(pl.program_id(0) == pl.num_programs(0) - 1)
    def _():
        back, dgain_ref[...] = norm_back(x_ref[...].astype(f32), gain_ref[...], acc[...])
        out_ref[...] = (d_mixed_ref[...] + back).astype(bf16)


def shards_kernel(in_ref, down_ref, query_ref, *refs):
    parts, query_out_ref = refs[:-1], refs[-1]
    ff = down_ref.shape[0]
    start = 0
    for ref in parts:
        part = ref.shape[1] // 3
        ref[:, :part] = in_ref[:, start : start + part]
        ref[:, part : 2 * part] = in_ref[:, ff + start : ff + start + part]
        ref[:, 2 * part :] = down_ref[start : start + part, :].T
        start += part
    query_out_ref[...] = query_ref[...].T


def columns_kernel(order, back, index_ref, *refs):
    count = len(refs) // 2
    index = index_ref[0]
    size = len(order)
    for x_ref, o_ref in zip(refs[:count], refs[count:]):
        cols = x_ref.shape[1] // size

        def pick(value, places):
            return jnp.concatenate(
                [value[:, p * cols : (p + 1) * cols] for p in places], axis=1
            )

        value = x_ref[...].astype(f32)
        if back:
            value = pick(value, [order.index(i) for i in range(size)])
        bit = 1
        while bit < size:
            value = jnp.where(
                (index & bit) != 0, pick(value, [i ^ bit for i in range(size)]), value
            )
            bit *= 2
        if not back:
            value = pick(value, order)
        o_ref[...] = value.astype(o_ref.dtype)


def pick_columns(ref, places, cols):
    if places == list(range(places[0], places[0] + len(places))):
        return ref[:, places[0] * cols : (places[-1] + 1) * cols]
    return jnp.concatenate([ref[:, p * cols : (p + 1) * cols] for p in places], axis=1)


def hidden_kernel(all_places, h_ref, d_ref, *refs):
    pieces, (hidden_ref, d_gate_up_ref, turned_ref) = refs[:-3], refs[-3:]
    part = hidden_ref.shape[1]
    gate_up = d_hidden = None
    for places, ref in zip(all_places, pieces):
        cols = ref.shape[0] // len(places)
        first = dot(pick_columns(h_ref, places, cols), ref[:, : 2 * part])
        second = dot(pick_columns(d_ref, places, cols), ref[:, 2 * part :])
        gate_up = first if gate_up is None else gate_up + first
        d_hidden = second if d_hidden is None else d_hidden + second
    gate, up = gate_up[:, :part], gate_up[:, part:]
    sig = jax.nn.sigmoid(gate)
    swish = gate * sig
    hidden = (swish * up).astype(bf16)
    d_gate = (d_hidden * up * (sig + swish * (1.0 - sig))).astype(bf16)
    d_up = (d_hidden * swish).astype(bf16)
    hidden_ref[...] = hidden
    d_gate_up_ref[:, :part] = d_gate
    d_gate_up_ref[:, part:] = d_up
    turned_ref[:part] = d_gate.T
    turned_ref[part : 2 * part] = d_up.T
    turned_ref[2 * part :] = hidden.T


def grads_kernel(h_ref, d_ref, turned_ref, low_ref, high_ref):
    split = turned_ref.shape[0] // 3 * 2
    first = dot(turned_ref[:split], h_ref[...]).astype(bf16)
    second = dot(turned_ref[split:], d_ref[...]).astype(bf16)
    low = pl.program_id(0) < pl.num_programs(0) // 2
    for out_ref, here in ((low_ref, low), (high_ref, jnp.logical_not(low))):

        @pl.when(here)
        def _(out_ref=out_ref):
            out_ref[0, :split] = first
            out_ref[0, split:] = second


def back_sum_kernel(all_places, *refs):
    count = len(all_places)
    half = refs[-1].shape[1] // 2
    totals = [None, None]
    at = count
    for c, pieces in enumerate(all_places):
        terms = [dot(refs[c][...], refs[at + i][...], contract_cols) for i in range(len(pieces))]
        at += len(pieces)
        if len(pieces) > 2:
            blocks = {}
            for places, term in zip(pieces, terms):
                cols = term.shape[1] // len(places)
                for i, p in enumerate(places):
                    blocks[p] = term[:, i * cols : (i + 1) * cols]
            middle = len(blocks) // 2
            terms = [
                jnp.concatenate([blocks[side * middle + i] for i in range(middle)], axis=1)
                for side in range(2)
            ]
        totals = [t if old is None else old + t for old, t in zip(totals, terms)]
    low = pl.program_id(0) < pl.num_programs(0) // 2
    for out_ref, here in ((refs[-2], low), (refs[-1], jnp.logical_not(low))):

        @pl.when(here)
        def _(out_ref=out_ref):
            for side in range(2):
                out_ref[:, side * half : (side + 1) * half] = totals[side].astype(bf16)


def whole(shape):
    return pl.BlockSpec(shape, lambda *_: (0,) * len(shape))


def local(
    inputs,
    cotangent,
    w_query,
    w_kv,
    w_out,
    w_in,
    w_down,
    norm_gains,
    head_gains,
    lengths,
    slot_blocks,
):
    sp_rows, width = inputs.shape
    n = lax.axis_size("dp")
    n_tensor = lax.axis_size("tensor")
    dp = lax.axis_index("dp")
    tensor = lax.axis_index("tensor")
    seq_count = lengths.shape[0]
    row_span = sp_rows * n_tensor // seq_count
    blocks = row_span // STRETCH
    rows = sp_rows // row_span
    per_row = SLOTS // STRETCH
    cols = width // n
    q_cols = w_query.shape[1]
    kv_cols = w_kv.shape[1]
    ff = w_down.shape[0]
    order = order_of("dp")
    tensor_order = order_of("tensor")
    rels = jnp.array(order, jnp.int32)

    def columns(back, *values):
        return pl.pallas_call(
            functools.partial(columns_kernel, tuple(order), back),
            in_specs=[pl.BlockSpec(memory_space=pltpu.SMEM)]
            + [pl.BlockSpec(memory_space=pltpu.VMEM)] * len(values),
            out_shape=[jax.ShapeDtypeStruct(v.shape, bf16) for v in values],
            compiler_params=pltpu.CompilerParams(vmem_limit_bytes=VMEM_LIMIT),
            cost_estimate=SMALL,
        name="columns",
        )(dp.reshape(1), *values)

    table = slot_blocks.reshape(n, n_tensor, rows, blocks)
    mine = lax.dynamic_index_in_dim(table, tensor, axis=1, keepdims=False)[dp ^ rels]
    inside = jnp.arange(STRETCH, dtype=jnp.int32)
    key_pos = (mine % per_row * STRETCH)[..., None] + inside
    own_pos = key_pos[0]
    own_len = lengths[mine[0] // per_row][..., None]
    live = (own_pos < own_len).astype(f32).reshape(sp_rows, 1)
    limit = jnp.minimum(own_pos, own_len - 1)
    limit = jnp.broadcast_to(limit[:, :, None, None, :], (rows, blocks, 1, n_tensor, STRETCH))
    limit = limit.reshape(rows, blocks, 1, n_tensor * STRETCH)
    key_pos = key_pos.transpose(1, 2, 0, 3).reshape(rows, SLOTS, 1)
    half = HEAD // 2
    frequency = rope_base ** (-2.0 * jnp.arange(half, dtype=f32) / HEAD)
    angles = own_pos.reshape(sp_rows, 1).astype(f32) * frequency
    cosine, sine = jnp.cos(angles), jnp.sin(angles)
    cos = jnp.concatenate([cosine, cosine], axis=1)
    sin = jnp.concatenate([-sine, sine], axis=1)
    head_float = head_gains.astype(f32)
    q_gain, k_gain = head_float[0:1], head_float[1:2]

    inputs, cotangent = columns(False, inputs, cotangent)
    inputs_f = inputs.astype(f32)
    part = w_kv.shape[0] // 2
    kv_shard = lax.dynamic_slice_in_dim(w_kv, (tensor & 1) * part, part, axis=0)
    unit = ff // sum(FF_PARTS)
    sizes = [size * unit for size in FF_PARTS]
    *shards, query_shard = pl.pallas_call(
        shards_kernel,
        out_shape=[jax.ShapeDtypeStruct((cols, 3 * part), bf16) for part in sizes]
        + [jax.ShapeDtypeStruct((q_cols, cols), bf16)],
        compiler_params=pltpu.CompilerParams(vmem_limit_bytes=VMEM_LIMIT),
        cost_estimate=SMALL,
        name="shards",
    )(w_in.reshape(cols, 2 * ff), w_down, w_query)
    link = Rounds()
    g_kv, g_gains = Gather(kv_shard), Gather(norm_gains)
    g_query, g_out = Gather(query_shard), Gather(w_out)
    g_ff = [Gather(x) for x in shards[:-1]] + [GatherLate(shards[-1])]
    link.go(g_kv, g_query, g_gains)
    link.go(g_kv, g_gains, g_out, g_ff[0])
    link.go(g_kv, g_gains, g_query)
    gains = g_gains.stack.transpose(1, 0, 2).reshape(2, width).astype(f32)
    gain_one, gain_two = gains[0], gains[1]
    h_one = scaled_norm(inputs_f, gain_one).astype(bf16)
    t_kv = PairRows(g_kv.stack)
    link.go(t_kv, g_query, g_out, g_ff[5])
    t_query = TensorGather(g_query.stack)
    kv_all = t_kv.stack.reshape(width, kv_cols)
    t_d_ffn = TensorGather(cotangent * live.astype(bf16))

    packed = (rows, HEADS_KV, blocks, n_tensor, STRETCH, LANES)
    packed_kv = (rows, HEADS_KV, blocks, STRETCH, LANES)
    both_spec = pl.BlockSpec((1, n, q_cols, cols), lambda s: (s, 0, 0, 0))
    kv_raw, kv_own = pl.pallas_call(
        key_kernel,
        out_shape=(
            jax.ShapeDtypeStruct((sp_rows, kv_cols), f32),
            jax.ShapeDtypeStruct(packed_kv, bf16),
        ),
        compiler_params=pltpu.CompilerParams(vmem_limit_bytes=VMEM_LIMIT),
        cost_estimate=SMALL,
        name="key_value",
    )(h_one, kv_all, cos, sin, k_gain)
    g_keys = Gather(kv_own)
    link.go(t_query, g_out, g_ff[0], g_keys)
    t_out = TensorGather(g_out.stack)
    link.go(t_query, t_out, g_keys, g_ff[0], g_ff[1])
    query_all = t_query.stack
    one_head = (sp_rows, HEAD)
    part_spec = pl.BlockSpec(
        (rows, HEADS_KV, blocks, 1, STRETCH, LANES), lambda s: (0, 0, 0, s, 0, 0)
    )
    q_raw, queries = pl.pallas_call(
        query_kernel,
        grid=(n_tensor,),
        in_specs=[
            whole((sp_rows, width)),
            both_spec,
            whole(one_head),
            whole(one_head),
            whole((1, HEAD)),
        ],
        out_specs=(pl.BlockSpec((1, sp_rows, q_cols), lambda s: (s, 0, 0)), part_spec),
        out_shape=(
            jax.ShapeDtypeStruct((n_tensor, sp_rows, q_cols), f32),
            jax.ShapeDtypeStruct(packed, bf16),
        ),
        compiler_params=params(),
        cost_estimate=SMALL,
        name="query",
    )(h_one, query_all, cos, sin, q_gain)
    link.go(t_out, t_d_ffn, g_keys, g_ff[1], g_ff[2], during=[queries])
    out_all = t_out.stack
    kv_halves = g_keys.halves
    q_spec = pl.BlockSpec(
        (1, 1, blocks, n_tensor, STRETCH, LANES), lambda i, h: (i, h, 0, 0, 0, 0)
    )
    kv_spec = pl.BlockSpec(
        (n // 2, 1, 1, blocks, STRETCH, LANES), lambda i, h: (0, i, h, 0, 0, 0)
    )
    limit_spec = pl.BlockSpec(
        (1, blocks, 1, n_tensor * STRETCH), lambda i, h: (i, 0, 0, 0)
    )
    pos_spec = pl.BlockSpec((1, SLOTS, 1), lambda i, h: (i, 0, 0))
    heads_packed = pl.pallas_call(
        attend_kernel,
        grid=(rows, HEADS_KV),
        in_specs=[q_spec, limit_spec, pos_spec] + [kv_spec] * 2,
        out_specs=q_spec,
        out_shape=jax.ShapeDtypeStruct(packed, bf16),
        scratch_shapes=[pltpu.VMEM((SLOTS, LANES), bf16), pltpu.VMEM((LANES, SLOTS), bf16)],
        compiler_params=params(2),
        cost_estimate=SMALL,
        name="attend",
    )(queries, limit, key_pos, *kv_halves)

    heads_shape = (n_tensor, sp_rows, q_cols)
    head_spec = pl.BlockSpec((1, sp_rows, q_cols), lambda s: (s, 0, 0))
    square = whole((sp_rows, width))
    mixed, h_two_own, attn_heads = pl.pallas_call(
        out_kernel,
        grid=(n_tensor,),
        in_specs=[part_spec, both_spec, square, whole((sp_rows, 1)), whole((1, width))],
        out_specs=(square, square, head_spec),
        out_shape=(
            jax.ShapeDtypeStruct((sp_rows, width), f32),
            jax.ShapeDtypeStruct((sp_rows, width), bf16),
            jax.ShapeDtypeStruct(heads_shape, bf16),
        ),
        compiler_params=params(),
        cost_estimate=SMALL,
        name="out",
    )(heads_packed, out_all, inputs, live, gain_two[None])
    t_heads = TensorExchange(attn_heads)

    t_h_two = TensorGather(h_two_own)
    t_h_one = TensorGather(h_one)
    rows_all = sp_rows * n_tensor
    link.go(t_d_ffn, g_ff[1], g_ff[2], g_ff[3], during=[h_two_own])
    d_ffn = t_d_ffn.stack.reshape(-1, width)
    link.go(t_h_two, g_ff[2], g_ff[3], g_ff[4])
    link.go(t_h_two, t_h_one, g_ff[3], g_ff[4], g_ff[5])
    h_two = t_h_two.stack.reshape(-1, width)
    row_spec = pl.BlockSpec((sp_rows, width), lambda i: (i, 0))
    row_block = lambda span: pl.BlockSpec((sp_rows, span), lambda i: (i, 0))
    weights, hiddens, d_gate_ups, turned = [], [], [], []

    def hidden_part(g, part):
        pieces = [
            (x.reshape(len(rs) * cols, 3 * part), [order.index(r) for r in rs])
            for x, rs in g.pieces()
        ]
        weights.append(pieces)
        hidden, d_gate_up, flipped = pl.pallas_call(
            functools.partial(hidden_kernel, [places for _, places in pieces]),
            grid=(n_tensor,),
            in_specs=[row_spec, row_spec] + [whole(x.shape) for x, _ in pieces],
            out_specs=(
                row_block(part),
                row_block(2 * part),
                pl.BlockSpec((3 * part, sp_rows), lambda i: (0, i)),
            ),
            out_shape=(
                jax.ShapeDtypeStruct((rows_all, part), bf16),
                jax.ShapeDtypeStruct((rows_all, 2 * part), bf16),
                jax.ShapeDtypeStruct((3 * part, rows_all), bf16),
            ),
            compiler_params=params(),
            cost_estimate=SMALL,
        name="hidden",
        )(h_two, d_ffn, *[x for x, _ in pieces])
        hiddens.append(hidden)
        d_gate_ups.append(d_gate_up)
        turned.append(flipped)

    def grads_of(flipped):
        wide = flipped.shape[0]
        count = width // 256
        low_spec = pl.BlockSpec((1, wide, 256), lambda j: (jnp.minimum(j, count // 2 - 1), 0, 0))
        high_spec = pl.BlockSpec((1, wide, 256), lambda j: (jnp.maximum(j - count // 2, 0), 0, 0))
        block = pl.BlockSpec((rows_all, 256), lambda j: (0, j))
        halves = pl.pallas_call(
            grads_kernel,
            grid=(count,),
            in_specs=[block, block, whole(flipped.shape)],
            out_specs=(low_spec, high_spec),
            out_shape=[jax.ShapeDtypeStruct((count // 2, wide, 256), bf16)] * 2,
            compiler_params=params(),
            cost_estimate=SMALL,
            name="weight_grads",
        )(h_two, d_ffn, flipped)
        if cols != 256:
            halves = [
                x.reshape(count // 2, wide, 256 // cols, cols)
                .transpose(0, 2, 1, 3)
                .reshape(n // 2, wide, cols)
                for x in halves
            ]

        def make(begin, end, arrived, kind):
            if begin >= n // 2:
                return halves[1]
            return plus(halves[0][begin:end].astype(f32), arrived, kind)

        return Scatter(make), halves[1]

    s_ff, sent = [], []

    def add_grads(c):
        item, first = grads_of(turned[c])
        s_ff.append(item)
        sent.append(first)

    def back_sum(parts, down):
        def weight_spec(x, w):
            span = x.shape[1]
            at = (w.shape[1] - span) // span if down else 0
            return pl.BlockSpec(
                (w.shape[0], span), lambda i: (0, at), pipeline_mode=pl.Buffered(1)
            )

        return pl.pallas_call(
            functools.partial(
                back_sum_kernel, [[places for _, places in pieces] for pieces in weights]
            ),
            grid=(n_tensor,),
            in_specs=[row_block(x.shape[1]) for x in parts]
            + [weight_spec(x, w) for x, pieces in zip(parts, weights) for w, _ in pieces],
            out_specs=(
                pl.BlockSpec((sp_rows, width), lambda i: (jnp.minimum(i, n_tensor // 2 - 1), 0)),
                pl.BlockSpec((sp_rows, width), lambda i: (jnp.maximum(i - n_tensor // 2, 0), 0)),
            ),
            out_shape=[jax.ShapeDtypeStruct((rows_all // 2, width), bf16)] * 2,
            compiler_params=params(),
            cost_estimate=SMALL,
            name="back_sum",
        )(*parts, *[w for pieces in weights for w, _ in pieces])

    def row_sums(parts, down):
        return TensorScatter(
            [x.reshape(n_tensor // 2, sp_rows, width) for x in back_sum(parts, down)]
        )

    hidden_part(g_ff[0], sizes[0])
    hidden_part(g_ff[1], sizes[1])
    add_grads(0)
    link.go(t_h_one, t_heads, g_ff[4], g_ff[5], during=[*turned, *sent])
    h_one_all = t_h_one.stack.reshape(-1, width)
    hidden_part(g_ff[2], sizes[2])
    hidden_part(g_ff[3], sizes[3])
    add_grads(1)
    add_grads(2)
    link.go(t_heads, s_ff[0], g_ff[5], during=[*turned[2:], *sent[1:]])
    hidden_part(g_ff[4], sizes[4])
    hidden_part(g_ff[5], sizes[5])
    t_back = row_sums(d_gate_ups, False)
    link.go(s_ff[1], s_ff[0], during=t_back.sums)
    add_grads(3)
    add_grads(4)
    t_ffn = row_sums(hiddens, True)
    link.go(t_back, s_ff[2], s_ff[1], s_ff[0], during=[*t_ffn.sums, *sent[3:]])
    add_grads(5)
    link.go(t_back, t_ffn, s_ff[3], s_ff[2], s_ff[1], during=sent[5:])
    first_spec = pl.BlockSpec((1, sp_rows, width), lambda i: (0, 0, 0))
    back_terms = t_back.terms()
    d_mixed, d_attn_own, d_gain_two = pl.pallas_call(
        mixed_back_kernel,
        grid=(1,),
        in_specs=[square, square, whole((1, width)), whole((sp_rows, 1))]
        + [first_spec] * len(back_terms),
        out_specs=(square, square, whole((1, width))),
        out_shape=(
            jax.ShapeDtypeStruct((sp_rows, width), f32),
            jax.ShapeDtypeStruct((sp_rows, width), bf16),
            jax.ShapeDtypeStruct((1, width), f32),
        ),
        compiler_params=params(),
        cost_estimate=SMALL,
        name="mixed_back",
    )(mixed, cotangent, gain_two[None], live, *back_terms)

    d_heads = pl.pallas_call(
        heads_back_kernel,
        grid=(n_tensor,),
        in_specs=[whole((sp_rows, width)), both_spec],
        out_specs=part_spec,
        out_shape=jax.ShapeDtypeStruct(packed, bf16),
        compiler_params=params(),
        cost_estimate=SMALL,
        name="heads_back",
    )(d_attn_own, out_all)
    d_query, d_low, d_high = pl.pallas_call(
        attend_back_kernel,
        grid=(rows, HEADS_KV),
        in_specs=[q_spec, q_spec, limit_spec, pos_spec] + [kv_spec] * 2,
        out_specs=[q_spec] + [kv_spec] * 2,
        out_shape=[jax.ShapeDtypeStruct(packed, f32)]
        + [jax.ShapeDtypeStruct((n // 2,) + packed_kv, bf16)] * 2,
        scratch_shapes=[
            pltpu.VMEM((SLOTS, LANES), bf16),
            pltpu.VMEM((LANES, SLOTS), bf16),
            pltpu.VMEM((SLOTS, LANES), f32),
        ],
        compiler_params=params(2),
        cost_estimate=SMALL,
        name="attend_back",
    )(queries, d_heads, limit, key_pos, *kv_halves)

    def key_grads(begin, end, arrived, kind):
        if begin >= n // 2:
            return d_high
        return plus(d_low[begin:end].astype(f32), arrived, kind)

    s_keys = Scatter(key_grads)
    t_attn = TensorGather(d_attn_own)
    d_q_low, d_q_gain = pl.pallas_call(
        query_back_kernel,
        grid=(n_tensor,),
        in_specs=[part_spec, head_spec, whole(one_head), whole(one_head), whole((1, HEAD))],
        out_specs=(head_spec, whole((1, HEAD))),
        out_shape=(
            jax.ShapeDtypeStruct(heads_shape, bf16),
            jax.ShapeDtypeStruct((1, HEAD), f32),
        ),
        compiler_params=params(),
        cost_estimate=SMALL,
        name="query_back",
    )(d_query, q_raw, cos, sin, q_gain)

    def product(left, right):
        def make(begin, end, arrived, kind):
            rows_here = left[:, begin * cols : end * cols]
            total = dot(rows_here, right, contract_rows).reshape(end - begin, cols, -1)
            return plus(total, arrived, kind)

        return make

    t_query_back = TensorExchange(d_q_low)
    link.go(t_ffn, s_ff[4], s_ff[3], s_ff[2], during=[d_query])
    link.go(t_attn, t_query_back, s_keys, s_ff[4], s_ff[3], during=[d_q_low])
    ffn = sum(x[0].astype(f32) for x in t_ffn.terms())
    (outputs,) = columns(True, (mixed + live * ffn).astype(bf16))
    link.go(t_attn, t_query_back, s_keys, s_ff[5], s_ff[4], during=[outputs])
    d_attn = t_attn.stack.reshape(-1, width)
    s_out = Scatter(product(d_attn, t_heads.rows()))
    s_query = Scatter(product(h_one_all, t_query_back.rows()))
    link.go(s_keys, s_out)
    d_kv = s_keys.result()
    d_kv_low, d_k_gain = pl.pallas_call(
        key_back_kernel,
        out_shape=(
            jax.ShapeDtypeStruct((sp_rows, kv_cols), bf16),
            jax.ShapeDtypeStruct((1, HEAD), f32),
        ),
        compiler_params=pltpu.CompilerParams(vmem_limit_bytes=VMEM_LIMIT),
        cost_estimate=SMALL,
        name="key_value_back",
    )(d_kv, kv_raw, cos, sin, k_gain)
    kv_part = kv_cols // n_tensor
    t_kv_back = Direct(
        [
            lax.dynamic_slice_in_dim(d_kv_low, (tensor ^ s) * kv_part, kv_part, axis=1)
            for s in tensor_order
        ]
    )
    grad_rel, d_gain_one = pl.pallas_call(
        back_kernel,
        grid=(n_tensor,),
        in_specs=[
            head_spec,
            both_spec,
            whole((sp_rows, kv_cols)),
            whole((width, kv_cols)),
            square,
            whole((1, width)),
            square,
        ],
        out_specs=(square, whole((1, width))),
        out_shape=(
            jax.ShapeDtypeStruct((sp_rows, width), bf16),
            jax.ShapeDtypeStruct((1, width), f32),
        ),
        scratch_shapes=[pltpu.VMEM((sp_rows, width), f32)],
        compiler_params=params(),
        cost_estimate=SMALL,
        name="h_one_back",
    )(d_q_low, query_all, d_kv_low, kv_all, inputs, gain_one[None], d_mixed)
    link.go(t_kv_back, s_query, s_out, during=[grad_rel])
    (grad_inputs,) = columns(True, grad_rel)

    gain_parts = jnp.concatenate([d_gain_one, d_gain_two]).reshape(2, n, cols)
    gain_parts = gain_parts.transpose(1, 0, 2).reshape(n, 2 * cols)
    head_parts = jnp.broadcast_to(
        jnp.concatenate([d_q_gain, d_k_gain]).reshape(1, 2 * HEAD), (n, 2 * HEAD)
    )
    small_parts = jnp.concatenate([gain_parts, head_parts], axis=1)
    extra = -(-small_parts.shape[1] // kv_part)
    small_parts = jnp.pad(
        small_parts, ((0, 0), (0, extra * kv_part - small_parts.shape[1]))
    ).reshape(n, extra, kv_part)
    kv_product = product(h_one_all, t_kv_back.rows())

    def kv_grads(begin, end, arrived, kind):
        own = jnp.concatenate([kv_product(begin, end, [], f32), small_parts[begin:end]], axis=1)
        return plus(own, arrived, kind)

    s_kv = Scatter(kv_grads)
    link.go(s_kv, s_query, s_out)
    link.go(s_kv, s_query, s_ff[5])
    link.go(s_kv, s_ff[5])
    sum_kv = s_kv.result()
    t_small = TensorGather(sum_kv[cols:])
    t_sums = TensorGather(sum_kv[:cols].astype(bf16))
    link.go(t_small, t_sums)
    link.go(t_small, t_sums)
    small = jnp.sum(t_small.stack, axis=0).reshape(-1)
    sum_gains = small[: 2 * cols].reshape(2, cols)
    sum_heads = small[2 * cols : 2 * cols + 2 * HEAD].reshape(2, HEAD)
    stack = t_sums.stack
    sum_kv = jnp.concatenate(
        [
            lax.dynamic_index_in_dim(
                stack, places[i], axis=0, keepdims=False
            )
            for places in [jnp.argsort(tensor ^ jnp.array(tensor_order, jnp.int32))]
            for i in range(n_tensor)
        ],
        axis=1,
    )
    sum_out = s_out.result().T
    sum_query = s_query.result()
    sums = [s.result() for s in s_ff]
    sum_in = jnp.concatenate(
        [x[: 2 * part].reshape(2, part, cols) for part, x in zip(sizes, sums)], axis=1
    ).transpose(2, 0, 1)
    sum_down = jnp.concatenate([x[2 * part :] for part, x in zip(sizes, sums)], axis=0)
    return (
        outputs,
        grad_inputs,
        sum_query,
        sum_kv.astype(f32),
        sum_out,
        sum_in,
        sum_down,
        sum_gains,
        sum_heads,
    )


def solution(mesh):
    in_specs = (
        P(("dp", "tensor"), None),
        P(("dp", "tensor"), None),
        P("dp", "tensor"),
        P("dp", None),
        P("tensor", "dp"),
        P("dp", None, "tensor"),
        P("tensor", "dp"),
        P(None, "dp"),
        P(),
        P(),
        P(),
    )
    out_specs = (
        P(("dp", "tensor"), None),
        P(("dp", "tensor"), None),
        P("dp", "tensor"),
        P("dp", None),
        P("tensor", "dp"),
        P("dp", None, "tensor"),
        P("tensor", "dp"),
        P(None, "dp"),
        P(),
    )
    return jax.shard_map(local, mesh=mesh, in_specs=in_specs, out_specs=out_specs, check_vma=False)
```

time: 1100 us -> 936 us (0.85)
  Pallas kernels: 94.9 us -> 237 us
  matrix products: 147 us -> 17.8 us
  waiting for transfers between devices: 487 us -> 358 us
  starting transfers between devices: 167 us -> 85.7 us
  other arithmetic: 76.7 us -> 99.6 us
  local copies, waits for them, and re-layouts: 99.5 us -> 116 us
    pallas_call x3 -> x22, Pallas kernels: 20.7 us -> 164 us  [the longest x6 56.1 us: grads_of(): pl.pallas_call(grads_kernel, grid=(count,), in_specs=[block, block, whole...]
    dot_general x68 -> x12, matrix products: 147 us -> 17.8 us  [dot(): return lax.dot_general(a, b, dims, preferred_element_type=f32)]
    ppermute x130 -> x92, waiting for transfers between devices: 486 us -> 358 us  [swap(): return lax.ppermute(value, axis, [(i, i ^ mask) for i in range(size)])]
    ppermute x130 -> x92, starting transfers between devices: 167 us -> 85.7 us  [swap(): return lax.ppermute(value, axis, [(i, i ^ mask) for i in range(size)])]
    another operation x28 -> x3, other arithmetic: 38 us -> 0.64 us  [the longest x2 0.52 us: advance(): jnp.stack([jnp.where(upper, got, value), jnp.where(upper, value, got)], a...]
    concatenate x5 -> x42, other arithmetic: 6.51 us -> 42.2 us  [the longest x34 37 us: join(): both = jnp.concatenate([first, second], axis=0)]
    convert_element_type x10 -> x23, other arithmetic: 9.44 us -> 37.7 us  [the longest x18 34 us: plus(): return total.astype(kind)]
    dot_general x0 -> x8, local copies, waits for them, and re-layouts: none -> 20.1 us  [dot(): return lax.dot_general(a, b, dims, preferred_element_type=f32)]
  transfers between devices with their start and end apart: 134 -> 92, of which waited for: 59 -> 36; matrix products, arithmetic and copies ran while one was open for 19% -> 19% of each run, Pallas kernels for 9% -> 26%
where the time goes in v2:
time: 936 us; the launch traced here: 925 us
  waiting for transfers between devices  358 us (38%)
  Pallas kernels  237 us (25%)
  local copies, waits for them, and re-layouts  116 us (12%)
  other arithmetic  99.6 us (11%)
  starting transfers between devices  85.7 us (9%)
  matrix products  17.8 us (2%)
  between operations  10.9 us (1%)
    ppermute x92, waiting for transfers between devices, swap(): return lax.ppermute(value, axis, [(i, i ^ mask) for i in range(size)])  358 us
    ppermute x92, starting transfers between devices, swap(): return lax.ppermute(value, axis, [(i, i ^ mask) for i in range(size)])  85.7 us
    unnamed x357, local copies, waits for them, and re-layouts  68.8 us
    pallas_call x6, Pallas kernels, grads_of(): pl.pallas_call(grads_kernel, grid=(count,), in_specs=[block, block, whole...  56.1 us
    pallas_call x6, Pallas kernels, hidden_part(): pl.pallas_call(functools.partial(hidden_kernel, [places for _, places in...  45.1 us
    concatenate x34, other arithmetic, join(): both = jnp.concatenate([first, second], axis=0)  37 us
    convert_element_type x18, other arithmetic, plus(): return total.astype(kind)  34 us
    pallas_call x2, Pallas kernels, back_sum(): pl.pallas_call(functools.partial(back_sum_kernel, [[places for _, places...  32.6 us
  transfers between devices with their start and end apart: 92, of which 36 were waited for; matrix products, arithmetic and copies ran while one was open for 19% of the time, Pallas kernels for 26%

profile of v2, /device:TPU:0, one launch (start us, length us, event | category | flops | bytes accessed | tf_op | source)
XLA Modules:
  0.0 925.0 jit_solution(13864375063330075266)
XLA Ops:
  46.0 12.7 %collective-permute-done.9 = bf16[4,128,640]{2,1,0:T(8,128)(2,1)S(1)} collective-permute-done((bf16[4,128,640]{2,1,0:T(8,128)(2,1)S(1)}, bf16[4,128,640]{2,1,0:T(8,128)(2,1)S(1)}, u32[]{:S(2)}, u32[]{:S(2)}) %collective-permute-start.9) | collective-permute-done | bytes 655392 | tf_op jit(solution)/shard_map/ppermute | solution.py:52
  66.0 14.1 %collective-permute-done.10 = bf16[4,320,256]{2,1,0:T(8,128)(2,1)S(1)} collective-permute-done((bf16[4,320,256]{2,1,0:T(8,128)(2,1)S(1)}, bf16[4,320,256]{2,1,0:T(8,128)(2,1)S(1)}, u32[]{:S(2)}, u32[]{:S(2)}) %collective-permute-start.10) | collective-permute-done | bytes 655392 | tf_op jit(solution)/shard_map/ppermute | solution.py:52
  95.5 22.1 %collective-permute-done.14 = bf16[1,8,320,256]{3,2,1,0:T(8,128)(2,1)} collective-permute-done((bf16[1,8,320,256]{3,2,1,0:T(8,128)(2,1)S(1)}, bf16[1,8,320,256]{3,2,1,0:T(8,128)(2,1)}, u32[]{:S(2)}, u32[]{:S(2)}) %collective-permute-start.14) | collective-permute-done | bytes 1310752 | tf_op jit(solution)/shard_map/ppermute | solution.py:52
  131.1 28.4 %collective-permute-done.20 = bf16[1,8,320,256]{3,2,1,0:T(8,128)(2,1)S(1)} collective-permute-done((bf16[1,8,320,256]{3,2,1,0:T(8,128)(2,1)S(1)}, bf16[1,8,320,256]{3,2,1,0:T(8,128)(2,1)S(1)}, u32[]{:S(2)}, u32[]{:S(2)}) %collective-permute-start.20) | collective-permute-done | bytes 1310752 | tf_op jit(solution)/shard_map/ppermute | solution.py:52
  177.2 12.7 %query.1 = (f32[4,256,320]{2,1,0:T(8,128)S(1)}, bf16[1,5,4,4,64,128]{5,4,3,2,1,0:T(8,128)(2,1)S(1)}) custom-call(bf16[256,2048]{1,0:T(8,128)(2,1)S(1)} %copy-done.13, bf16[4,8,320,256]{3,2,1,0:T(8,128)(2,1)} %copy-done.101, f32[256,64]{1,0:T(8,128)S(1)} %get-tuple-element.438.cos_ref, f32[256,64]{1,0:T(8,128)S(1)} %get-tuple-element.439.sin_ref, ...), custom_call_target="tpu_custom_call" | custom-call | flops 1000 | bytes 1000 | tf_op jit(solution)/shard_map/query/pallas_call | solution.py:757
  189.9 8.8 collective-permute-done.27
  198.7 10.4 %collective-permute-done.26 = bf16[2,256,768]{2,1,0:T(8,128)(2,1)} collective-permute-done((bf16[2,256,768]{2,1,0:T(8,128)(2,1)}, bf16[2,256,768]{2,1,0:T(8,128)(2,1)}, u32[]{:S(2)}, u32[]{:S(2)}) %collective-permute-start.26) | collective-permute-done | bytes 786464 | tf_op jit(solution)/shard_map/ppermute | solution.py:52
  226.1 18.8 %attend.1.o_ref = bf16[1,5,4,4,64,128]{5,4,3,2,1,0:T(8,128)(2,1)S(1)} custom-call(bf16[1,5,4,4,64,128]{5,4,3,2,1,0:T(8,128)(2,1)S(1)} %copy-done.21, s32[1,4,1,256]{3,2,1,0:T(1,128)S(1)} %broadcast_in_dim.96.limit_ref, s32[1,2048,1]{2,1,0:T(8,128)S(1)} %copy-done.10, bf16[4,1,5,4,64,128]{5,4,3,2,1,0:T(8,128)(2,1)S(1)} %copy-done.9, ...), custom_call_target="tpu_custom_call" | custom-call | flops 1000 | bytes 1000 | tf_op jit(solution)/shard_map/attend/pallas_call | solution.py:789
  263.9 19.6 %collective-permute-done.32 = bf16[1,256,2048]{2,1,0:T(8,128)(2,1)S(1)} collective-permute-done((bf16[1,256,2048]{2,1,0:T(8,128)(2,1)S(1)}, bf16[1,256,2048]{2,1,0:T(8,128)(2,1)S(1)}, u32[]{:S(2)}, u32[]{:S(2)}) %collective-permute-start.32) | collective-permute-done | bytes 1048608 | tf_op jit(solution)/shard_map/ppermute | solution.py:52
  286.6 11.2 %collective-permute-done.34 = bf16[2,256,768]{2,1,0:T(8,128)(2,1)S(1)} collective-permute-done((bf16[2,256,768]{2,1,0:T(8,128)(2,1)S(1)}, bf16[2,256,768]{2,1,0:T(8,128)(2,1)S(1)}, u32[]{:S(2)}, u32[]{:S(2)}) %collective-permute-start.34) | collective-permute-done | bytes 786464 | tf_op jit(solution)/shard_map/ppermute | solution.py:52
  303.6 21.8 %collective-permute-done.39 = bf16[1,256,2048]{2,1,0:T(8,128)(2,1)S(1)} collective-permute-done((bf16[1,256,2048]{2,1,0:T(8,128)(2,1)S(1)}, bf16[1,256,2048]{2,1,0:T(8,128)(2,1)S(1)}, u32[]{:S(2)}, u32[]{:S(2)}) %collective-permute-start.39) | collective-permute-done | bytes 1048608 | tf_op jit(solution)/shard_map/ppermute | solution.py:52
  326.9 9.7 %collective-permute-done.40 = bf16[2,256,768]{2,1,0:T(8,128)(2,1)S(1)} collective-permute-done((bf16[2,256,768]{2,1,0:T(8,128)(2,1)S(1)}, bf16[2,256,768]{2,1,0:T(8,128)(2,1)S(1)}, u32[]{:S(2)}, u32[]{:S(2)}) %collective-permute-start.40) | collective-permute-done | bytes 786464 | tf_op jit(solution)/shard_map/ppermute | solution.py:52
  358.0 9.6 %weight_grads.6 = (bf16[4,768,256]{2,1,0:T(8,128)(2,1)S(1)}, bf16[4,768,256]{2,1,0:T(8,128)(2,1)}) custom-call(bf16[1024,2048]{1,0:T(8,128)(2,1)} %bitcast.286, bf16[1024,2048]{1,0:T(8,128)(2,1)} %bitcast.274, bf16[768,1024]{1,0:T(8,128)(2,1)S(1)} %get-tuple-element.270.turned_ref), custom_call_target="tpu_custom_call" | custom-call | flops 1000 | bytes 1000 | tf_op jit(solution)/shard_map/weight_grads/pallas_call | solution.py:866
  382.4 9.1 weight_grads.7
  399.2 9.6 %weight_grads.8 = (bf16[4,768,256]{2,1,0:T(8,128)(2,1)S(1)}, bf16[4,768,256]{2,1,0:T(8,128)(2,1)}) custom-call(bf16[1024,2048]{1,0:T(8,128)(2,1)} %bitcast.290, bf16[1024,2048]{1,0:T(8,128)(2,1)} %bitcast.278, bf16[768,1024]{1,0:T(8,128)(2,1)S(1)} %get-tuple-element.283.turned_ref), custom_call_target="tpu_custom_call" | custom-call | flops 1000 | bytes 1000 | tf_op jit(solution)/shard_map/weight_grads/pallas_call | solution.py:866
  436.2 9.2 weight_grads.9
  455.5 9.3 %weight_grads.10 = (bf16[4,768,256]{2,1,0:T(8,128)(2,1)S(1)}, bf16[4,768,256]{2,1,0:T(8,128)(2,1)}) custom-call(bf16[1024,2048]{1,0:T(8,128)(2,1)} %bitcast.294, bf16[1024,2048]{1,0:T(8,128)(2,1)} %bitcast.282, bf16[768,1024]{1,0:T(8,128)(2,1)S(1)} %get-tuple-element.310.turned_ref), custom_call_target="tpu_custom_call" | custom-call | flops 1000 | bytes 1000 | tf_op jit(solution)/shard_map/weight_grads/pallas_call | solution.py:866
  464.8 8.1 hidden.11
  473.9 20.6 %back_sum.3 = (bf16[512,2048]{1,0:T(8,128)(2,1)}, bf16[512,2048]{1,0:T(8,128)(2,1)}) custom-call(bf16[1024,512]{1,0:T(8,128)(2,1)S(1)} %copy-done.54, bf16[1024,512]{1,0:T(8,128)(2,1)S(1)} %copy-done.56, bf16[1024,512]{1,0:T(8,128)(2,1)} %copy-done.57, bf16[1024,512]{1,0:T(8,128)(2,1)} %copy-done.58, bf16[1024,512]{1,0:T(8,128)(2,1)} %copy-done.61, ...), custom_call_target="tpu_custom_call" | custom-call | flops 1000 | bytes 1000 | tf_op jit(solution)/shard_map/back_sum/pallas_call | solution.py:906
  518.8 9.3 %weight_grads.11 = (bf16[4,768,256]{2,1,0:T(8,128)(2,1)S(1)}, bf16[4,768,256]{2,1,0:T(8,128)(2,1)}) custom-call(bf16[1024,2048]{1,0:T(8,128)(2,1)} %bitcast.296, bf16[1024,2048]{1,0:T(8,128)(2,1)} %bitcast.284, bf16[768,1024]{1,0:T(8,128)(2,1)S(1)} %copy-done.33), custom_call_target="tpu_custom_call" | custom-call | flops 1000 | bytes 1000 | tf_op jit(solution)/shard_map/weight_grads/pallas_call | solution.py:866
  529.3 12.0 %back_sum.2 = (bf16[512,2048]{1,0:T(8,128)(2,1)}, bf16[512,2048]{1,0:T(8,128)(2,1)}) custom-call(bf16[1024,256]{1,0:T(8,128)(2,1)S(1)} %copy-done.69, bf16[1024,256]{1,0:T(8,128)(2,1)S(1)} %copy-done.71, bf16[1024,256]{1,0:T(8,128)(2,1)S(1)} %copy-done.73, bf16[1024,256]{1,0:T(8,128)(2,1)S(1)} %copy-done.75, bf16[1024,256]{1,0:T(8,128)(2,1)S(1)} %copy-done.77, ...), custom_call_target="tpu_custom_call" | custom-call | flops 1000 | bytes 1000 | tf_op jit(solution)/shard_map/back_sum/pallas_call | solution.py:906
  572.2 19.0 %collective-permute-done.57 = bf16[2,768,256]{2,1,0:T(8,128)(2,1)} collective-permute-done((bf16[2,768,256]{2,1,0:T(8,128)(2,1)}, bf16[2,768,256]{2,1,0:T(8,128)(2,1)}, u32[]{:S(2)}, u32[]{:S(2)}) %collective-permute-start.57) | collective-permute-done | bytes 786464 | tf_op jit(solution)/shard_map/ppermute | solution.py:52
  616.1 30.7 %attend_back.1 = (f32[1,5,4,4,64,128]{5,4,3,2,1,0:T(8,128)}, bf16[4,1,5,4,64,128]{5,4,3,2,1,0:T(8,128)(2,1)S(1)}, bf16[4,1,5,4,64,128]{5,4,3,2,1,0:T(8,128)(2,1)}) custom-call(bf16[1,5,4,4,64,128]{5,4,3,2,1,0:T(8,128)(2,1)S(1)} %copy-done.22, bf16[1,5,4,4,64,128]{5,4,3,2,1,0:T(8,128)(2,1)} %copy-done.23, s32[1,4,1,256]{3,2,1,0:T(1,128)S(1)} %copy-done.94, ...), custom_call_target="tpu_custom_call" | custom-call | flops 1000 | bytes 1000 | tf_op jit(solution)/shard_map/attend_back/pallas_call | solution.py:976
  669.9 21.3 %collective-permute-done.60 = bf16[4,768,256]{2,1,0:T(8,128)(2,1)} collective-permute-done((bf16[4,768,256]{2,1,0:T(8,128)(2,1)}, bf16[4,768,256]{2,1,0:T(8,128)(2,1)}, u32[]{:S(2)}, u32[]{:S(2)}) %collective-permute-start.60) | collective-permute-done | bytes 1572896 | tf_op jit(solution)/shard_map/ppermute | solution.py:52
  713.5 17.5 %collective-permute-done.66 = bf16[2,768,256]{2,1,0:T(8,128)(2,1)} collective-permute-done((bf16[2,768,256]{2,1,0:T(8,128)(2,1)}, bf16[2,768,256]{2,1,0:T(8,128)(2,1)}, u32[]{:S(2)}, u32[]{:S(2)}) %collective-permute-start.66) | collective-permute-done | bytes 786464 | tf_op jit(solution)/shard_map/ppermute | solution.py:52
  743.7 9.2 collective-permute-done.72
  761.8 8.7 collective-permute-done.68
  798.5 8.7 h_one_back.1
  819.5 11.6 %collective-permute-done.79 = bf16[2,256,320]{1,2,0:T(8,128)(2,1)S(1)} collective-permute-done((bf16[2,256,320]{1,2,0:T(8,128)(2,1)S(1)}, bf16[2,256,320]{1,2,0:T(8,128)(2,1)S(1)}, u32[]{:S(2)}, u32[]{:S(2)}) %collective-permute-start.79) | collective-permute-done | bytes 327712 | tf_op jit(solution)/shard_map/ppermute | solution.py:52
  841.4 9.9 %collective-permute-done.80 = bf16[2,256,320]{1,2,0:T(8,128)(2,1)S(1)} collective-permute-done((bf16[2,256,320]{1,2,0:T(8,128)(2,1)S(1)}, bf16[2,256,320]{1,2,0:T(8,128)(2,1)S(1)}, u32[]{:S(2)}, u32[]{:S(2)}) %collective-permute-start.80) | collective-permute-done | bytes 327712 | tf_op jit(solution)/shard_map/ppermute | solution.py:52
  857.6 40.7 %collective-permute-done.84 = bf16[2,260,160]{2,1,0:T(8,128)(2,1)S(1)} collective-permute-done((bf16[2,260,160]{2,1,0:T(8,128)(2,1)}, bf16[2,260,160]{2,1,0:T(8,128)(2,1)S(1)}, u32[]{:S(2)}, u32[]{:S(2)}) %collective-permute-start.84) | collective-permute-done | bytes 166432 | tf_op jit(solution)/shard_map/ppermute | solution.py:52
  905.2 9.4 %collective-permute-done.86 = bf16[1,260,160]{2,1,0:T(8,128)(2,1)S(1)} collective-permute-done((bf16[1,260,160]{2,1,0:T(8,128)(2,1)S(1)}, bf16[1,260,160]{2,1,0:T(8,128)(2,1)S(1)}, u32[]{:S(2)}, u32[]{:S(2)}) %collective-permute-start.86) | collective-permute-done | bytes 83232 | tf_op jit(solution)/shard_map/ppermute | solution.py:52
  (719 shorter events, 440.2 us)
Async XLA Ops:
  124.3 39.3 %collective-permute-start.18 = (bf16[2,8,320,256]{3,2,1,0:T(8,128)(2,1)S(1)}, bf16[2,8,320,256]{3,2,1,0:T(8,128)(2,1)S(1)}, u32[]{:S(2)}, u32[]{:S(2)}) collective-permute-start(bf16[2,8,320,256]{3,2,1,0:T(8,128)(2,1)S(1)} %pad_maximum_fusion.4), channel_id=1, source_target_pairs={{0,1},{1,0},{2,3},{3,2},{4,5},{5,4},{6,7},{7,6},{8,9},{9,8},{10,11... | collective-permute-start | bytes 7864328 | tf_op jit(solution)/shard_map/ppermute | solution.py:52
  165.1 47.1 %collective-permute-start.24 = (bf16[2,8,320,256]{3,2,1,0:T(8,128)(2,1)}, bf16[2,8,320,256]{3,2,1,0:T(8,128)(2,1)}, u32[]{:S(2)}, u32[]{:S(2)}) collective-permute-start(bf16[2,8,320,256]{3,2,1,0:T(8,128)(2,1)} %pad_maximum_fusion.6), channel_id=1, source_target_pairs={{0,1},{1,0},{2,3},{3,2},{4,5},{5,4},{6,7},{7,6},{8,9},{9,8},{10,11... | collective-permute-start | bytes 7864328 | tf_op jit(solution)/shard_map/ppermute | solution.py:52
  169.6 39.5 %collective-permute-start.25 = (bf16[1,256,2048]{2,1,0:T(8,128)(2,1)}, bf16[1,256,2048]{2,1,0:T(8,128)(2,1)}, u32[]{:S(2)}, u32[]{:S(2)}) collective-permute-start(bf16[1,256,2048]{2,1,0:T(8,128)(2,1)} %multiply_bitcast_fusion), channel_id=1, source_target_pairs={{0,2},{1,3},{2,0},{3,1},{4,6},{5,7},{6,4},{7,5},{8,10},{9,11},{10,... | collective-permute-start | bytes 3145736 | tf_op jit(solution)/shard_map/ppermute | solution.py:52
  170.1 42.1 %collective-permute-start.23 = (bf16[4,1,5,4,64,128]{5,4,3,2,1,0:T(8,128)(2,1)S(1)}, bf16[4,1,5,4,64,128]{5,4,3,2,1,0:T(8,128)(2,1)S(1)}, u32[]{:S(2)}, u32[]{:S(2)}) collective-permute-start(bf16[4,1,5,4,64,128]{5,4,3,2,1,0:T(8,128)(2,1)S(1)} %pad_maximum_fusion.17.low_ref), channel_id=1, source_target_pairs={{0,4},{4,0},{8,12},{12,8},{16,20},{20,16},{24,28},{28,24},{1,5},{5... | collective-permute-start | bytes 3932168 | tf_op jit(solution)/shard_map/ppermute | solution.py:52
  212.2 46.0 %collective-permute-start.28 = (bf16[2,256,2048]{2,1,0:T(8,128)(2,1)}, bf16[2,256,2048]{2,1,0:T(8,128)(2,1)}, u32[]{:S(2)}, u32[]{:S(2)}) collective-permute-start(bf16[2,256,2048]{2,1,0:T(8,128)(2,1)} %pad_maximum_fusion.7), channel_id=1, source_target_pairs={{0,1},{1,0},{2,3},{3,2},{4,5},{5,4},{6,7},{7,6},{8,9},{9,8},{10,11... | collective-permute-start | bytes 6291464 | tf_op jit(solution)/shard_map/ppermute | solution.py:52
  215.3 42.8 %collective-permute-start.29 = (bf16[4,256,768]{2,1,0:T(8,128)(2,1)}, bf16[4,256,768]{2,1,0:T(8,128)(2,1)}, u32[]{:S(2)}, u32[]{:S(2)}) collective-permute-start(bf16[4,256,768]{2,1,0:T(8,128)(2,1)} %pad_maximum_fusion.12), channel_id=1, source_target_pairs={{0,4},{4,0},{8,12},{12,8},{16,20},{20,16},{24,28},{28,24},{1,5},{5... | collective-permute-start | bytes 4718600 | tf_op jit(solution)/shard_map/ppermute | solution.py:52
  217.5 39.1 %collective-permute-start.30 = (bf16[2,256,768]{2,1,0:T(8,128)(2,1)}, bf16[2,256,768]{2,1,0:T(8,128)(2,1)}, u32[]{:S(2)}, u32[]{:S(2)}) collective-permute-start(bf16[2,256,768]{2,1,0:T(8,128)(2,1)} %pad_maximum_fusion.22), channel_id=1, source_target_pairs={{0,16},{4,20},{8,24},{12,28},{16,0},{20,4},{24,8},{28,12},{1,17},{... | collective-permute-start | bytes 2359304 | tf_op jit(solution)/shard_map/ppermute | solution.py:52
  217.5 39.1 %collective-permute-start.31 = (bf16[1,256,768]{2,1,0:T(8,128)(2,1)}, bf16[1,256,768]{2,1,0:T(8,128)(2,1)}, u32[]{:S(2)}, u32[]{:S(2)}) collective-permute-start(bf16[1,256,768]{2,1,0:T(8,128)(2,1)} %bitcast.25), channel_id=1, source_target_pairs={{0,8},{4,12},{8,0},{12,4},{16,24},{20,28},{24,16},{28,20},{1,9},{5... | collective-permute-start | bytes 1179656 | tf_op jit(solution)/shard_map/ppermute | solution.py:52
  258.2 39.6 %collective-permute-start.33 = (bf16[4,256,768]{2,1,0:T(8,128)(2,1)S(1)}, bf16[4,256,768]{2,1,0:T(8,128)(2,1)S(1)}, u32[]{:S(2)}, u32[]{:S(2)}) collective-permute-start(bf16[4,256,768]{2,1,0:T(8,128)(2,1)S(1)} %pad_maximum_fusion.13), channel_id=1, source_target_pairs={{0,4},{4,0},{8,12},{12,8},{16,20},{20,16},{24,28},{28,24},{1,5},{5... | collective-permute-start | bytes 4718600 | tf_op jit(solution)/shard_map/ppermute | solution.py:52
  298.9 39.9 %collective-permute-start.36 = (bf16[2,256,2048]{2,1,0:T(8,128)(2,1)S(1)}, bf16[2,256,2048]{2,1,0:T(8,128)(2,1)S(1)}, u32[]{:S(2)}, u32[]{:S(2)}) collective-permute-start(bf16[2,256,2048]{2,1,0:T(8,128)(2,1)S(1)} %pad_maximum_fusion.8), channel_id=1, source_target_pairs={{0,1},{1,0},{2,3},{3,2},{4,5},{5,4},{6,7},{7,6},{8,9},{9,8},{10,11... | collective-permute-start | bytes 6291464 | tf_op jit(solution)/shard_map/ppermute | solution.py:52
  299.1 39.7 %collective-permute-start.37 = (bf16[4,256,768]{2,1,0:T(8,128)(2,1)S(1)}, bf16[4,256,768]{2,1,0:T(8,128)(2,1)S(1)}, u32[]{:S(2)}, u32[]{:S(2)}) collective-permute-start(bf16[4,256,768]{2,1,0:T(8,128)(2,1)S(1)} %pad_maximum_fusion.14), channel_id=1, source_target_pairs={{0,4},{4,0},{8,12},{12,8},{16,20},{20,16},{24,28},{28,24},{1,5},{5... | collective-permute-start | bytes 4718600 | tf_op jit(solution)/shard_map/ppermute | solution.py:52
  338.9 38.4 %collective-permute-start.43 = (bf16[2,256,2048]{2,1,0:T(8,128)(2,1)}, bf16[2,256,2048]{2,1,0:T(8,128)(2,1)}, u32[]{:S(2)}, u32[]{:S(2)}) collective-permute-start(bf16[2,256,2048]{2,1,0:T(8,128)(2,1)} %pad_maximum_fusion.9), channel_id=1, source_target_pairs={{0,1},{1,0},{2,3},{3,2},{4,5},{5,4},{6,7},{7,6},{8,9},{9,8},{10,11... | collective-permute-start | bytes 6291464 | tf_op jit(solution)/shard_map/ppermute | solution.py:52
  377.3 43.9 %collective-permute-start.47 = (bf16[4,768,256]{2,1,0:T(8,128)(2,1)}, bf16[4,768,256]{2,1,0:T(8,128)(2,1)}, u32[]{:S(2)}, u32[]{:S(2)}) collective-permute-start(bf16[4,768,256]{2,1,0:T(8,128)(2,1)} %get-tuple-element.300), channel_id=1, source_target_pairs={{0,4},{4,0},{8,12},{12,8},{16,20},{20,16},{24,28},{28,24},{1,5},{5... | collective-permute-start | bytes 4718600 | tf_op jit(solution)/shard_map/ppermute | solution.py:52
  378.0 42.3 %collective-permute-start.45 = (bf16[2,256,768]{2,1,0:T(8,128)(2,1)S(1)}, bf16[2,256,768]{2,1,0:T(8,128)(2,1)S(1)}, u32[]{:S(2)}, u32[]{:S(2)}) collective-permute-start(bf16[2,256,768]{2,1,0:T(8,128)(2,1)S(1)} %collective-permute-done.40), channel_id=1, source_target_pairs={{0,16},{4,20},{8,24},{12,28},{16,0},{20,4},{24,8},{28,12},{1,17},{... | collective-permute-start | bytes 2359304 | tf_op jit(solution)/shard_map/ppermute | solution.py:52
  382.4 37.9 %collective-permute-start.46 = (bf16[1,2,256,320]{3,2,0,1:T(8,128)(2,1)}, bf16[1,2,256,320]{3,2,0,1:T(8,128)(2,1)S(1)}, u32[]{:S(2)}, u32[]{:S(2)}) collective-permute-start(bf16[1,2,256,320]{3,2,0,1:T(8,128)(2,1)} %fusion.25), channel_id=1, source_target_pairs={{0,1},{1,0},{2,3},{3,2},{4,5},{5,4},{6,7},{7,6},{8,9},{9,8},{10,11... | collective-permute-start | bytes 983048 | tf_op jit(solution)/shard_map/ppermute | solution.py:52
  421.2 73.3 %collective-permute-start.48 = (bf16[4,768,256]{2,1,0:T(8,128)(2,1)}, bf16[4,768,256]{2,1,0:T(8,128)(2,1)}, u32[]{:S(2)}, u32[]{:S(2)}) collective-permute-start(bf16[4,768,256]{2,1,0:T(8,128)(2,1)} %get-tuple-element.302), channel_id=1, source_target_pairs={{0,4},{4,0},{8,12},{12,8},{16,20},{20,16},{24,28},{28,24},{1,5},{5... | collective-permute-start | bytes 4718600 | tf_op jit(solution)/shard_map/ppermute | solution.py:52
  424.9 69.6 %collective-permute-start.49 = (bf16[2,768,256]{2,1,0:T(8,128)(2,1)}, bf16[2,768,256]{2,1,0:T(8,128)(2,1)}, u32[]{:S(2)}, u32[]{:S(2)}) collective-permute-start(bf16[2,768,256]{2,1,0:T(8,128)(2,1)} %add_convert_fusion.5), channel_id=1, source_target_pairs={{0,16},{4,20},{8,24},{12,28},{16,0},{20,4},{24,8},{28,12},{1,17},{... | collective-permute-start | bytes 2359304 | tf_op jit(solution)/shard_map/ppermute | solution.py:52
  494.5 52.0 %collective-permute-start.50 = (bf16[2,256,2048]{2,1,0:T(8,128)(2,1)}, bf16[2,256,2048]{2,1,0:T(8,128)(2,1)}, u32[]{:S(2)}, u32[]{:S(2)}) collective-permute-start(bf16[2,256,2048]{2,1,0:T(8,128)(2,1)} %bitcast.350), channel_id=1, source_target_pairs={{0,1},{1,0},{2,3},{3,2},{4,5},{5,4},{6,7},{7,6},{8,9},{9,8},{10,11... | collective-permute-start | bytes 6291464 | tf_op jit(solution)/shard_map/ppermute | solution.py:52
  497.2 49.4 %collective-permute-start.51 = (bf16[4,768,256]{2,1,0:T(8,128)(2,1)}, bf16[4,768,256]{2,1,0:T(8,128)(2,1)}, u32[]{:S(2)}, u32[]{:S(2)}) collective-permute-start(bf16[4,768,256]{2,1,0:T(8,128)(2,1)} %get-tuple-element.313), channel_id=1, source_target_pairs={{0,4},{4,0},{8,12},{12,8},{16,20},{20,16},{24,28},{28,24},{1,5},{5... | collective-permute-start | bytes 4718600 | tf_op jit(solution)/shard_map/ppermute | solution.py:52
  507.1 38.0 %collective-permute-start.52 = (bf16[2,768,256]{2,1,0:T(8,128)(2,1)}, bf16[2,768,256]{2,1,0:T(8,128)(2,1)}, u32[]{:S(2)}, u32[]{:S(2)}) collective-permute-start(bf16[2,768,256]{2,1,0:T(8,128)(2,1)} %add_convert_fusion.4), channel_id=1, source_target_pairs={{0,16},{4,20},{8,24},{12,28},{16,0},{20,4},{24,8},{28,12},{1,17},{... | collective-permute-start | bytes 2359304 | tf_op jit(solution)/shard_map/ppermute | solution.py:52
  546.6 62.6 %collective-permute-start.54 = (bf16[2,256,2048]{2,1,0:T(8,128)(2,1)}, bf16[2,256,2048]{2,1,0:T(8,128)(2,1)}, u32[]{:S(2)}, u32[]{:S(2)}) collective-permute-start(bf16[2,256,2048]{2,1,0:T(8,128)(2,1)} %bitcast.349), channel_id=1, source_target_pairs={{0,1},{1,0},{2,3},{3,2},{4,5},{5,4},{6,7},{7,6},{8,9},{9,8},{10,11... | collective-permute-start | bytes 6291464 | tf_op jit(solution)/shard_map/ppermute | solution.py:52
  549.0 57.8 %collective-permute-start.56 = (bf16[4,768,256]{2,1,0:T(8,128)(2,1)}, bf16[4,768,256]{2,1,0:T(8,128)(2,1)}, u32[]{:S(2)}, u32[]{:S(2)}) collective-permute-start(bf16[4,768,256]{2,1,0:T(8,128)(2,1)} %get-tuple-element.326), channel_id=1, source_target_pairs={{0,4},{4,0},{8,12},{12,8},{16,20},{20,16},{24,28},{28,24},{1,5},{5... | collective-permute-start | bytes 4718600 | tf_op jit(solution)/shard_map/ppermute | solution.py:52
  554.9 37.7 %collective-permute-start.55 = (bf16[1,256,2048]{2,1,0:T(8,128)(2,1)}, bf16[1,256,2048]{2,1,0:T(8,128)(2,1)S(1)}, u32[]{:S(2)}, u32[]{:S(2)}) collective-permute-start(bf16[1,256,2048]{2,1,0:T(8,128)(2,1)} %fusion.6), channel_id=1, source_target_pairs={{0,2},{1,3},{2,0},{3,1},{4,6},{5,7},{6,4},{7,5},{8,10},{9,11},{10,... | collective-permute-start | bytes 3145736 | tf_op jit(solution)/shard_map/ppermute | solution.py:52
  609.2 49.5 %collective-permute-start.62 = (bf16[1,768,256]{2,1,0:T(8,128)(2,1)S(1)}, bf16[1,768,256]{2,1,0:T(8,128)(2,1)S(1)}, u32[]{:S(2)}, u32[]{:S(2)}) collective-permute-start(bf16[1,768,256]{2,1,0:T(8,128)(2,1)S(1)} %add_convert_fusion.10), channel_id=1, source_target_pairs={{0,8},{4,12},{8,0},{12,4},{16,24},{20,28},{24,16},{28,20},{1,9},{5... | collective-permute-start | bytes 1179656 | tf_op jit(solution)/shard_map/ppermute | solution.py:52
  612.0 53.7 %collective-permute-start.61 = (bf16[2,768,256]{2,1,0:T(8,128)(2,1)}, bf16[2,768,256]{2,1,0:T(8,128)(2,1)}, u32[]{:S(2)}, u32[]{:S(2)}) collective-permute-start(bf16[2,768,256]{2,1,0:T(8,128)(2,1)} %add_convert_fusion.2), channel_id=1, source_target_pairs={{0,16},{4,20},{8,24},{12,28},{16,0},{20,4},{24,8},{28,12},{1,17},{... | collective-permute-start | bytes 2359304 | tf_op jit(solution)/shard_map/ppermute | solution.py:52
  614.5 52.6 %collective-permute-start.59 = (bf16[1,256,2048]{2,1,0:T(8,128)(2,1)}, bf16[1,256,2048]{2,1,0:T(8,128)(2,1)}, u32[]{:S(2)}, u32[]{:S(2)}) collective-permute-start(bf16[1,256,2048]{2,1,0:T(8,128)(2,1)} %fusion.7), channel_id=1, source_target_pairs={{0,2},{1,3},{2,0},{3,1},{4,6},{5,7},{6,4},{7,5},{8,10},{9,11},{10,... | collective-permute-start | bytes 3145736 | tf_op jit(solution)/shard_map/ppermute | solution.py:52
  693.1 37.9 %collective-permute-start.64 = (bf16[1,256,2048]{2,1,0:T(8,128)(2,1)S(1)}, bf16[1,256,2048]{2,1,0:T(8,128)(2,1)}, u32[]{:S(2)}, u32[]{:S(2)}) collective-permute-start(bf16[1,256,2048]{2,1,0:T(8,128)(2,1)S(1)} %bitcast.248), channel_id=1, source_target_pairs={{0,2},{1,3},{2,0},{3,1},{4,6},{5,7},{6,4},{7,5},{8,10},{9,11},{10,... | collective-permute-start | bytes 3145736 | tf_op jit(solution)/shard_map/ppermute | solution.py:52
  693.7 40.0 %collective-permute-start.63 = (bf16[4,1,5,4,64,128]{5,4,3,2,1,0:T(8,128)(2,1)}, bf16[4,1,5,4,64,128]{5,4,3,2,1,0:T(8,128)(2,1)}, u32[]{:S(2)}, u32[]{:S(2)}) collective-permute-start(bf16[4,1,5,4,64,128]{5,4,3,2,1,0:T(8,128)(2,1)} %get-tuple-element.348), channel_id=1, source_target_pairs={{0,4},{4,0},{8,12},{12,8},{16,20},{20,16},{24,28},{28,24},{1,5},{5... | collective-permute-start | bytes 3932168 | tf_op jit(solution)/shard_map/ppermute | solution.py:52
  733.7 41.0 %collective-permute-start.69 = (bf16[2,256,2048]{2,1,0:T(8,128)(2,1)}, bf16[2,256,2048]{2,1,0:T(8,128)(2,1)}, u32[]{:S(2)}, u32[]{:S(2)}) collective-permute-start(bf16[2,256,2048]{2,1,0:T(8,128)(2,1)} %pad_maximum_fusion.10), channel_id=1, source_target_pairs={{0,1},{1,0},{2,3},{3,2},{4,5},{5,4},{6,7},{7,6},{8,9},{9,8},{10,11... | collective-permute-start | bytes 6291464 | tf_op jit(solution)/shard_map/ppermute | solution.py:52
  851.3 48.1 %collective-permute-start.85 = (bf16[2,768,256]{2,1,0:T(8,128)(2,1)}, bf16[2,768,256]{2,1,0:T(8,128)(2,1)S(1)}, u32[]{:S(2)}, u32[]{:S(2)}) collective-permute-start(bf16[2,768,256]{2,1,0:T(8,128)(2,1)} %add_convert_fusion), channel_id=1, source_target_pairs={{0,16},{4,20},{8,24},{12,28},{16,0},{20,4},{24,8},{28,12},{1,17},{... | collective-permute-start | bytes 2359304 | tf_op jit(solution)/shard_map/ppermute | solution.py:52
  853.5 44.9 %collective-permute-start.84 = (bf16[2,260,160]{2,1,0:T(8,128)(2,1)}, bf16[2,260,160]{2,1,0:T(8,128)(2,1)S(1)}, u32[]{:S(2)}, u32[]{:S(2)}) collective-permute-start(bf16[2,260,160]{2,1,0:T(8,128)(2,1)} %fusion.17), channel_id=1, source_target_pairs={{0,16},{4,20},{8,24},{12,28},{16,0},{20,4},{24,8},{28,12},{1,17},{... | collective-permute-start | bytes 499208 | tf_op jit(solution)/shard_map/ppermute | solution.py:52
  856.4 44.2 %collective-permute-start.83 = (bf16[1,256,320]{1,2,0:T(8,128)(2,1)}, bf16[1,256,320]{1,2,0:T(8,128)(2,1)}, u32[]{:S(2)}, u32[]{:S(2)}) collective-permute-start(bf16[1,256,320]{1,2,0:T(8,128)(2,1)} %add_convert_fusion.17), channel_id=1, source_target_pairs={{0,8},{4,12},{8,0},{12,4},{16,24},{20,28},{24,16},{28,20},{1,9},{5... | collective-permute-start | bytes 491528 | tf_op jit(solution)/shard_map/ppermute | solution.py:52
  (229 other events, 3642.3 us)

commit v3 on v2

--- a/solution.py
+++ b/solution.py
@@ -538,30 +538,53 @@
     query_out_ref[...] = query_ref[...].T
 
 
-def columns_kernel(order, back, index_ref, *refs):
-    count = len(refs) // 2
-    index = index_ref[0]
+def turn_columns(order, back, index, value):
     size = len(order)
-    for x_ref, o_ref in zip(refs[:count], refs[count:]):
-        cols = x_ref.shape[1] // size
-
-        def pick(value, places):
-            return jnp.concatenate(
-                [value[:, p * cols : (p + 1) * cols] for p in places], axis=1
-            )
-
-        value = x_ref[...].astype(f32)
-        if back:
-            value = pick(value, [order.index(i) for i in range(size)])
-        bit = 1
-        while bit < size:
-            value = jnp.where(
-                (index & bit) != 0, pick(value, [i ^ bit for i in range(size)]), value
-            )
-            bit *= 2
-        if not back:
-            value = pick(value, order)
-        o_ref[...] = value.astype(o_ref.dtype)
+    cols = value.shape[1] // size
+
+    def pick(value, places):
+        return jnp.concatenate([value[:, p * cols : (p + 1) * cols] for p in places], axis=1)
+
+    if back:
+        value = pick(value, [order.index(i) for i in range(size)])
+    bit = 1
+    while bit < size:
+        value = jnp.where((index & bit) != 0, pick(value, [i ^ bit for i in range(size)]), value)
+        bit *= 2
+    return value if back else pick(value, order)
+
+
+def enter_kernel(order, index_ref, x_ref, cot_ref, live_ref, x_out, cot_out, d_ffn_out):
+    x_out[...] = turn_columns(order, False, index_ref[0], x_ref[...].astype(f32)).astype(bf16)
+    cot = turn_columns(order, False, index_ref[0], cot_ref[...].astype(f32))
+    cot_out[...] = cot.astype(bf16)
+    d_ffn_out[...] = (cot * live_ref[...]).astype(bf16)
+
+
+def leave_kernel(order, index_ref, x_ref, out_ref):
+    value = x_ref[...].astype(f32)
+    out_ref[...] = turn_columns(order, True, index_ref[0], value).astype(bf16)
+
+
+def finish_kernel(order, index_ref, mixed_ref, live_ref, *rest):
+    terms, out_ref = rest[:-1], rest[-1]
+    ffn = sum(ref[0].astype(f32) for ref in terms)
+    value = mixed_ref[...] + live_ref[...] * ffn
+    out_ref[...] = turn_columns(order, True, index_ref[0], value).astype(bf16)
+
+
+def product_kernel(left_ref, right_ref, low_ref, high_ref, turned):
+    @pl.when(pl.program_id(0) == 0)
+    def _():
+        turned[...] = right_ref[...].T
+
+    out = dot(turned[...], left_ref[...]).astype(bf16)
+    low = pl.program_id(0) < pl.num_programs(0) // 2
+    for out_ref, here in ((low_ref, low), (high_ref, jnp.logical_not(low))):
+
+        @pl.when(here)
+        def _(out_ref=out_ref):
+            out_ref[0] = out
 
 
 def pick_columns(ref, places, cols):
@@ -599,12 +622,14 @@
     first = dot(turned_ref[:split], h_ref[...]).astype(bf16)
     second = dot(turned_ref[split:], d_ref[...]).astype(bf16)
     low = pl.program_id(0) < pl.num_programs(0) // 2
+    span = low_ref.shape[2]
     for out_ref, here in ((low_ref, low), (high_ref, jnp.logical_not(low))):
 
         @pl.when(here)
         def _(out_ref=out_ref):
-            out_ref[0, :split] = first
-            out_ref[0, split:] = second
+            for p in range(out_ref.shape[0]):
+                out_ref[p, :split] = first[:, p * span : (p + 1) * span]
+                out_ref[p, split:] = second[:, p * span : (p + 1) * span]
 
 
 def back_sum_kernel(all_places, *refs):
@@ -671,16 +696,17 @@
     tensor_order = order_of("tensor")
     rels = jnp.array(order, jnp.int32)
 
-    def columns(back, *values):
+    smem = pl.BlockSpec(memory_space=pltpu.SMEM)
+
+    def call(kernel, out_shape, name, *args, specs=None):
         return pl.pallas_call(
-            functools.partial(columns_kernel, tuple(order), back),
-            in_specs=[pl.BlockSpec(memory_space=pltpu.SMEM)]
-            + [pl.BlockSpec(memory_space=pltpu.VMEM)] * len(values),
-            out_shape=[jax.ShapeDtypeStruct(v.shape, bf16) for v in values],
+            kernel,
+            in_specs=specs,
+            out_shape=out_shape,
             compiler_params=pltpu.CompilerParams(vmem_limit_bytes=VMEM_LIMIT),
             cost_estimate=SMALL,
-        name="columns",
-        )(dp.reshape(1), *values)
+            name=name,
+        )(*args)
 
     table = slot_blocks.reshape(n, n_tensor, rows, blocks)
     mine = lax.dynamic_index_in_dim(table, tensor, axis=1, keepdims=False)[dp ^ rels]
@@ -702,7 +728,19 @@
     head_float = head_gains.astype(f32)
     q_gain, k_gain = head_float[0:1], head_float[1:2]
 
-    inputs, cotangent = columns(False, inputs, cotangent)
+    vmem = pl.BlockSpec(memory_space=pltpu.VMEM)
+    index = dp.reshape(1)
+    low_square = jax.ShapeDtypeStruct((sp_rows, width), bf16)
+    inputs, cotangent, d_ffn_own = call(
+        functools.partial(enter_kernel, tuple(order)),
+        [low_square] * 3,
+        "enter",
+        index,
+        inputs,
+        cotangent,
+        live,
+        specs=[smem, vmem, vmem, vmem],
+    )
     inputs_f = inputs.astype(f32)
     part = w_kv.shape[0] // 2
     kv_shard = lax.dynamic_slice_in_dim(w_kv, (tensor & 1) * part, part, axis=0)
@@ -721,8 +759,8 @@
     g_query, g_out = Gather(query_shard), Gather(w_out)
     g_ff = [Gather(x) for x in shards[:-1]] + [GatherLate(shards[-1])]
     link.go(g_kv, g_query, g_gains)
-    link.go(g_kv, g_gains, g_out, g_ff[0])
-    link.go(g_kv, g_gains, g_query)
+    link.go(g_kv, g_gains, g_out)
+    link.go(g_kv, g_gains, g_query, g_ff[0])
     gains = g_gains.stack.transpose(1, 0, 2).reshape(2, width).astype(f32)
     gain_one, gain_two = gains[0], gains[1]
     h_one = scaled_norm(inputs_f, gain_one).astype(bf16)
@@ -730,7 +768,7 @@
     link.go(t_kv, g_query, g_out, g_ff[5])
     t_query = TensorGather(g_query.stack)
     kv_all = t_kv.stack.reshape(width, kv_cols)
-    t_d_ffn = TensorGather(cotangent * live.astype(bf16))
+    t_d_ffn = TensorGather(d_ffn_own)
 
     packed = (rows, HEADS_KV, blocks, n_tensor, STRETCH, LANES)
     packed_kv = (rows, HEADS_KV, blocks, STRETCH, LANES)
@@ -825,8 +863,9 @@
     link.go(t_h_two, g_ff[2], g_ff[3], g_ff[4])
     link.go(t_h_two, t_h_one, g_ff[3], g_ff[4], g_ff[5])
     h_two = t_h_two.stack.reshape(-1, width)
-    row_spec = pl.BlockSpec((sp_rows, width), lambda i: (i, 0))
-    row_block = lambda span: pl.BlockSpec((sp_rows, span), lambda i: (i, 0))
+    steps = n_tensor // 2
+    row_block = lambda span: pl.BlockSpec((rows_all // steps, span), lambda i: (i, 0))
+    row_spec = row_block(width)
     weights, hiddens, d_gate_ups, turned = [], [], [], []
 
     def hidden_part(g, part):
@@ -837,12 +876,12 @@
         weights.append(pieces)
         hidden, d_gate_up, flipped = pl.pallas_call(
             functools.partial(hidden_kernel, [places for _, places in pieces]),
-            grid=(n_tensor,),
+            grid=(steps,),
             in_specs=[row_spec, row_spec] + [whole(x.shape) for x, _ in pieces],
             out_specs=(
                 row_block(part),
                 row_block(2 * part),
-                pl.BlockSpec((3 * part, sp_rows), lambda i: (0, i)),
+                pl.BlockSpec((3 * part, rows_all // steps), lambda i: (0, i)),
             ),
             out_shape=(
                 jax.ShapeDtypeStruct((rows_all, part), bf16),
@@ -857,15 +896,24 @@
         d_gate_ups.append(d_gate_up)
         turned.append(flipped)
 
+    def split_places(halves, wide):
+        if cols == 256:
+            return halves
+        return [
+            x.reshape(-1, wide, 256 // cols, cols).transpose(0, 2, 1, 3).reshape(n // 2, wide, cols)
+            for x in halves
+        ]
+
     def grads_of(flipped):
         wide = flipped.shape[0]
         count = width // 256
-        low_spec = pl.BlockSpec((1, wide, 256), lambda j: (jnp.minimum(j, count // 2 - 1), 0, 0))
-        high_spec = pl.BlockSpec((1, wide, 256), lambda j: (jnp.maximum(j - count // 2, 0), 0, 0))
-        block = pl.BlockSpec((rows_all, 256), lambda j: (0, j))
+        grid = width // 512
+        low_spec = pl.BlockSpec((2, wide, 256), lambda j: (jnp.minimum(j, grid // 2 - 1), 0, 0))
+        high_spec = pl.BlockSpec((2, wide, 256), lambda j: (jnp.maximum(j - grid // 2, 0), 0, 0))
+        block = pl.BlockSpec((rows_all, 512), lambda j: (0, j))
         halves = pl.pallas_call(
             grads_kernel,
-            grid=(count,),
+            grid=(grid,),
             in_specs=[block, block, whole(flipped.shape)],
             out_specs=(low_spec, high_spec),
             out_shape=[jax.ShapeDtypeStruct((count // 2, wide, 256), bf16)] * 2,
@@ -873,13 +921,7 @@
             cost_estimate=SMALL,
             name="weight_grads",
         )(h_two, d_ffn, flipped)
-        if cols != 256:
-            halves = [
-                x.reshape(count // 2, wide, 256 // cols, cols)
-                .transpose(0, 2, 1, 3)
-                .reshape(n // 2, wide, cols)
-                for x in halves
-            ]
+        halves = split_places(halves, wide)
 
         def make(begin, end, arrived, kind):
             if begin >= n // 2:
@@ -891,7 +933,7 @@
     s_ff, sent = [], []
 
     def add_grads(c):
-        item, first = grads_of(turned[c])
+        item, first = grads_of(after(turned[c], *link.done) if c > 2 else turned[c])
         s_ff.append(item)
         sent.append(first)
 
@@ -907,12 +949,16 @@
             functools.partial(
                 back_sum_kernel, [[places for _, places in pieces] for pieces in weights]
             ),
-            grid=(n_tensor,),
+            grid=(steps,),
             in_specs=[row_block(x.shape[1]) for x in parts]
             + [weight_spec(x, w) for x, pieces in zip(parts, weights) for w, _ in pieces],
             out_specs=(
-                pl.BlockSpec((sp_rows, width), lambda i: (jnp.minimum(i, n_tensor // 2 - 1), 0)),
-                pl.BlockSpec((sp_rows, width), lambda i: (jnp.maximum(i - n_tensor // 2, 0), 0)),
+                pl.BlockSpec(
+                    (rows_all // steps, width), lambda i: (jnp.minimum(i, steps // 2 - 1), 0)
+                ),
+                pl.BlockSpec(
+                    (rows_all // steps, width), lambda i: (jnp.maximum(i - steps // 2, 0), 0)
+                ),
             ),
             out_shape=[jax.ShapeDtypeStruct((rows_all // 2, width), bf16)] * 2,
             compiler_params=params(),
@@ -940,11 +986,10 @@
     t_back = row_sums(d_gate_ups, False)
     link.go(s_ff[1], s_ff[0], during=t_back.sums)
     add_grads(3)
-    add_grads(4)
     t_ffn = row_sums(hiddens, True)
     link.go(t_back, s_ff[2], s_ff[1], s_ff[0], during=[*t_ffn.sums, *sent[3:]])
-    add_grads(5)
-    link.go(t_back, t_ffn, s_ff[3], s_ff[2], s_ff[1], during=sent[5:])
+    add_grads(4)
+    link.go(t_back, t_ffn, s_ff[3], s_ff[2], s_ff[1], during=sent[4:])
     first_spec = pl.BlockSpec((1, sp_rows, width), lambda i: (0, 0, 0))
     back_terms = t_back.terms()
     d_mixed, d_attn_own, d_gain_two = pl.pallas_call(
@@ -1012,23 +1057,52 @@
     )(d_query, q_raw, cos, sin, q_gain)
 
     def product(left, right):
+        wide = right.shape[1]
+        count = width // 256
+        halves = pl.pallas_call(
+            product_kernel,
+            grid=(count,),
+            in_specs=[pl.BlockSpec((rows_all, 256), lambda j: (0, j)), whole(right.shape)],
+            out_specs=(
+                pl.BlockSpec((1, wide, 256), lambda j: (jnp.minimum(j, count // 2 - 1), 0, 0)),
+                pl.BlockSpec((1, wide, 256), lambda j: (jnp.maximum(j - count // 2, 0), 0, 0)),
+            ),
+            out_shape=[jax.ShapeDtypeStruct((count // 2, wide, 256), bf16)] * 2,
+            scratch_shapes=[pltpu.VMEM((wide, rows_all), bf16)],
+            compiler_params=params(),
+            cost_estimate=SMALL,
+            name="product",
+        )(left, right)
+        return split_places(halves, wide)
+
+    def sum_of(halves):
         def make(begin, end, arrived, kind):
-            rows_here = left[:, begin * cols : end * cols]
-            total = dot(rows_here, right, contract_rows).reshape(end - begin, cols, -1)
-            return plus(total, arrived, kind)
-
-        return make
+            if begin >= n // 2:
+                return halves[1]
+            return plus(halves[0][begin:end].astype(f32), arrived, kind)
+
+        return Scatter(make)
 
     t_query_back = TensorExchange(d_q_low)
     link.go(t_ffn, s_ff[4], s_ff[3], s_ff[2], during=[d_query])
-    link.go(t_attn, t_query_back, s_keys, s_ff[4], s_ff[3], during=[d_q_low])
-    ffn = sum(x[0].astype(f32) for x in t_ffn.terms())
-    (outputs,) = columns(True, (mixed + live * ffn).astype(bf16))
+    add_grads(5)
+    link.go(t_attn, t_query_back, s_keys, s_ff[4], s_ff[3], during=[d_q_low, sent[5]])
+    ffn_terms = t_ffn.terms()
+    outputs = pl.pallas_call(
+        functools.partial(finish_kernel, tuple(order)),
+        grid=(1,),
+        in_specs=[smem, square, whole((sp_rows, 1))] + [first_spec] * len(ffn_terms),
+        out_specs=square,
+        out_shape=low_square,
+        compiler_params=params(),
+        cost_estimate=SMALL,
+        name="finish",
+    )(index, mixed, live, *ffn_terms)
     link.go(t_attn, t_query_back, s_keys, s_ff[5], s_ff[4], during=[outputs])
     d_attn = t_attn.stack.reshape(-1, width)
-    s_out = Scatter(product(d_attn, t_heads.rows()))
-    s_query = Scatter(product(h_one_all, t_query_back.rows()))
-    link.go(s_keys, s_out)
+    s_out = sum_of(product(d_attn, t_heads.rows()))
+    s_query = sum_of(product(h_one_all, t_query_back.rows()))
+    link.go(s_keys, s_out, s_query, s_ff[5])
     d_kv = s_keys.result()
     d_kv_low, d_k_gain = pl.pallas_call(
         key_back_kernel,
@@ -1069,50 +1143,53 @@
         cost_estimate=SMALL,
         name="h_one_back",
     )(d_q_low, query_all, d_kv_low, kv_all, inputs, gain_one[None], d_mixed)
-    link.go(t_kv_back, s_query, s_out, during=[grad_rel])
-    (grad_inputs,) = columns(True, grad_rel)
-
-    gain_parts = jnp.concatenate([d_gain_one, d_gain_two]).reshape(2, n, cols)
-    gain_parts = gain_parts.transpose(1, 0, 2).reshape(n, 2 * cols)
-    head_parts = jnp.broadcast_to(
-        jnp.concatenate([d_q_gain, d_k_gain]).reshape(1, 2 * HEAD), (n, 2 * HEAD)
-    )
+    link.go(t_kv_back, s_out, during=[grad_rel])
+    grad_inputs = call(
+        functools.partial(leave_kernel, tuple(order)),
+        low_square,
+        "leave",
+        index,
+        grad_rel,
+        specs=[smem, vmem],
+    )
+
+    gain_parts = jnp.concatenate([d_gain_one, d_gain_two]).reshape(2, n, cols).transpose(1, 0, 2)
+    head_rows = max(2 * HEAD // cols, 1)
+    head_parts = jnp.concatenate([d_q_gain, d_k_gain]).reshape(1, -1)
+    head_parts = jnp.pad(head_parts, ((0, 0), (0, head_rows * cols - 2 * HEAD)))
+    head_parts = jnp.broadcast_to(head_parts.reshape(1, head_rows, cols), (n, head_rows, cols))
     small_parts = jnp.concatenate([gain_parts, head_parts], axis=1)
-    extra = -(-small_parts.shape[1] // kv_part)
-    small_parts = jnp.pad(
-        small_parts, ((0, 0), (0, extra * kv_part - small_parts.shape[1]))
-    ).reshape(n, extra, kv_part)
-    kv_product = product(h_one_all, t_kv_back.rows())
+    kv_halves_back = product(h_one_all, t_kv_back.rows())
 
     def kv_grads(begin, end, arrived, kind):
-        own = jnp.concatenate([kv_product(begin, end, [], f32), small_parts[begin:end]], axis=1)
+        side = begin // (n // 2)
+        own = kv_halves_back[side][begin - side * n // 2 : end - side * n // 2]
+        own = jnp.concatenate([own.astype(f32), small_parts[begin:end]], axis=1)
         return plus(own, arrived, kind)
 
     s_kv = Scatter(kv_grads)
-    link.go(s_kv, s_query, s_out)
-    link.go(s_kv, s_query, s_ff[5])
-    link.go(s_kv, s_ff[5])
+    link.go(s_kv, s_query, s_out, s_ff[5])
+    link.go(s_kv, s_query)
+    link.go(s_kv)
     sum_kv = s_kv.result()
-    t_small = TensorGather(sum_kv[cols:])
-    t_sums = TensorGather(sum_kv[:cols].astype(bf16))
+    t_small = TensorGather(sum_kv[kv_part:])
+    t_sums = TensorGather(sum_kv[:kv_part].astype(bf16))
     link.go(t_small, t_sums)
     link.go(t_small, t_sums)
-    small = jnp.sum(t_small.stack, axis=0).reshape(-1)
-    sum_gains = small[: 2 * cols].reshape(2, cols)
-    sum_heads = small[2 * cols : 2 * cols + 2 * HEAD].reshape(2, HEAD)
+    small = jnp.sum(t_small.stack, axis=0)
+    sum_gains = small[:2]
+    sum_heads = small[2:].reshape(-1)[: 2 * HEAD].reshape(2, HEAD)
     stack = t_sums.stack
+    places = jnp.argsort(tensor ^ jnp.array(tensor_order, jnp.int32))
     sum_kv = jnp.concatenate(
         [
-            lax.dynamic_index_in_dim(
-                stack, places[i], axis=0, keepdims=False
-            )
-            for places in [jnp.argsort(tensor ^ jnp.array(tensor_order, jnp.int32))]
+            lax.dynamic_index_in_dim(stack, places[i], axis=0, keepdims=False)
             for i in range(n_tensor)
         ],
-        axis=1,
-    )
-    sum_out = s_out.result().T
-    sum_query = s_query.result()
+        axis=0,
+    ).T
+    sum_out = s_out.result()
+    sum_query = s_query.result().T
     sums = [s.result() for s in s_ff]
     sum_in = jnp.concatenate(
         [x[: 2 * part].reshape(2, part, cols) for part, x in zip(sizes, sums)], axis=1

time: 936 us -> 817 us (0.87)
  waiting for transfers between devices: 358 us -> 278 us
  local copies, waits for them, and re-layouts: 116 us -> 82.7 us
  matrix products: 17.8 us -> 0 us
    ppermute x92, waiting for transfers between devices: 358 us -> 278 us  [swap(): return lax.ppermute(value, axis, [(i, i ^ mask) for i in range(size)])]
    dot_general x8 -> x0, local copies, waits for them, and re-layouts: 20.1 us -> none  [dot(): return lax.dot_general(a, b, dims, preferred_element_type=f32)]
    dot_general x12 -> x0, matrix products: 17.8 us -> none  [dot(): return lax.dot_general(a, b, dims, preferred_element_type=f32)]
    unnamed x357 -> x336, local copies, waits for them, and re-layouts: 68.8 us -> 56.5 us
    pallas_call x9 -> x12, Pallas kernels: 59.3 us -> 68 us  [the longest x6 43.4 us: grads_of(): pl.pallas_call(grads_kernel, grid=(grid,), in_specs=[block, block, whole(...]
    convert_element_type x18 -> x22, other arithmetic: 34 us -> 37.6 us  [plus(): return total.astype(kind)]
  transfers between devices with their start and end apart: 92 -> 92, of which waited for: 36 -> 38; matrix products, arithmetic and copies ran while one was open for 19% -> 18% of each run, Pallas kernels for 26% -> 30%
where the time goes in v3:
time: 817 us; the launch traced here: 806 us
  waiting for transfers between devices  278 us (34%)
  Pallas kernels  245 us (30%)
  other arithmetic  104 us (13%)
  starting transfers between devices  87.5 us (11%)
  local copies, waits for them, and re-layouts  82.7 us (10%)
  between operations  10.7 us (1%)
    ppermute x92, waiting for transfers between devices, swap(): return lax.ppermute(value, axis, [(i, i ^ mask) for i in range(size)])  278 us
    ppermute x92, starting transfers between devices, swap(): return lax.ppermute(value, axis, [(i, i ^ mask) for i in range(size)])  87.5 us
    unnamed x336, local copies, waits for them, and re-layouts  56.5 us
    pallas_call x6, Pallas kernels, grads_of(): pl.pallas_call(grads_kernel, grid=(grid,), in_specs=[block, block, whole(...  43.4 us
    pallas_call x6, Pallas kernels, hidden_part(): pl.pallas_call(functools.partial(hidden_kernel, [places for _, places in...  43.1 us
    concatenate x34, other arithmetic, join(): both = jnp.concatenate([first, second], axis=0)  39.3 us
    convert_element_type x22, other arithmetic, plus(): return total.astype(kind)  37.6 us
    pallas_call x2, Pallas kernels, back_sum(): pl.pallas_call(functools.partial(back_sum_kernel, [[places for _, places...  33.2 us
  transfers between devices with their start and end apart: 92, of which 38 were waited for; matrix products, arithmetic and copies ran while one was open for 18% of the time, Pallas kernels for 30%

profile of v3, /device:TPU:0, one launch (start us, length us, event | category | flops | bytes accessed | tf_op | source)
XLA Modules:
  0.0 806.5 jit_solution(8474195727222852548)
XLA Ops:
  23.1 11.2 %collective-permute-done.4 = bf16[2,128,640]{2,1,0:T(8,128)(2,1)S(1)} collective-permute-done((bf16[2,128,640]{2,1,0:T(8,128)(2,1)S(1)}, bf16[2,128,640]{2,1,0:T(8,128)(2,1)S(1)}, u32[]{:S(2)}, u32[]{:S(2)}) %collective-permute-start.4) | collective-permute-done | bytes 327712 | tf_op jit(solution)/shard_map/ppermute | solution.py:52
  61.4 15.0 %collective-permute-done.10 = bf16[4,320,256]{2,1,0:T(8,128)(2,1)S(1)} collective-permute-done((bf16[4,320,256]{2,1,0:T(8,128)(2,1)S(1)}, bf16[4,320,256]{2,1,0:T(8,128)(2,1)S(1)}, u32[]{:S(2)}, u32[]{:S(2)}) %collective-permute-start.10) | collective-permute-done | bytes 655392 | tf_op jit(solution)/shard_map/ppermute | solution.py:52
  95.7 17.4 %collective-permute-done.14 = bf16[1,8,320,256]{3,2,1,0:T(8,128)(2,1)S(1)} collective-permute-done((bf16[1,8,320,256]{3,2,1,0:T(8,128)(2,1)S(1)}, bf16[1,8,320,256]{3,2,1,0:T(8,128)(2,1)S(1)}, u32[]{:S(2)}, u32[]{:S(2)}) %collective-permute-start.14) | collective-permute-done | bytes 1310752 | tf_op jit(solution)/shard_map/ppermute | solution.py:52
  113.4 9.1 %collective-permute-done.16 = bf16[2,256,768]{2,1,0:T(8,128)(2,1)S(1)} collective-permute-done((bf16[2,256,768]{2,1,0:T(8,128)(2,1)S(1)}, bf16[2,256,768]{2,1,0:T(8,128)(2,1)S(1)}, u32[]{:S(2)}, u32[]{:S(2)}) %collective-permute-start.16) | collective-permute-done | bytes 786464 | tf_op jit(solution)/shard_map/ppermute | solution.py:52
  127.1 27.9 %collective-permute-done.20 = bf16[1,8,320,256]{3,2,1,0:T(8,128)(2,1)S(1)} collective-permute-done((bf16[1,8,320,256]{3,2,1,0:T(8,128)(2,1)S(1)}, bf16[1,8,320,256]{3,2,1,0:T(8,128)(2,1)S(1)}, u32[]{:S(2)}, u32[]{:S(2)}) %collective-permute-start.20) | collective-permute-done | bytes 1310752 | tf_op jit(solution)/shard_map/ppermute | solution.py:52
  167.6 12.7 %query.1 = (f32[4,256,320]{2,1,0:T(8,128)S(1)}, bf16[1,5,4,4,64,128]{5,4,3,2,1,0:T(8,128)(2,1)S(1)}) custom-call(bf16[256,2048]{1,0:T(8,128)(2,1)S(1)} %fusion.2.h_ref, bf16[4,8,320,256]{3,2,1,0:T(8,128)(2,1)} %copy-done.109, f32[256,64]{1,0:T(8,128)S(1)} %get-tuple-element.472.cos_ref, f32[256,64]{1,0:T(8,128)S(1)} %get-tuple-element.473.sin_ref, ...), custom_call_target="tpu_custom_call" | custom-call | flops 1000 | bytes 1000 | tf_op jit(solution)/shard_map/query/pallas_call | solution.py:795
  180.3 8.0 collective-permute-done.27
  188.3 10.7 %collective-permute-done.26 = bf16[2,256,768]{2,1,0:T(8,128)(2,1)} collective-permute-done((bf16[2,256,768]{2,1,0:T(8,128)(2,1)}, bf16[2,256,768]{2,1,0:T(8,128)(2,1)}, u32[]{:S(2)}, u32[]{:S(2)}) %collective-permute-start.26) | collective-permute-done | bytes 786464 | tf_op jit(solution)/shard_map/ppermute | solution.py:52
  216.7 18.6 %attend.1.o_ref = bf16[1,5,4,4,64,128]{5,4,3,2,1,0:T(8,128)(2,1)S(1)} custom-call(bf16[1,5,4,4,64,128]{5,4,3,2,1,0:T(8,128)(2,1)S(1)} %copy-done.19, s32[1,4,1,256]{3,2,1,0:T(1,128)S(1)} %broadcast_in_dim.93.limit_ref, s32[1,2048,1]{2,1,0:T(8,128)S(1)} %copy-done.10, bf16[4,1,5,4,64,128]{5,4,3,2,1,0:T(8,128)(2,1)S(1)} %copy-done.9, ...), custom_call_target="tpu_custom_call" | custom-call | flops 1000 | bytes 1000 | tf_op jit(solution)/shard_map/attend/pallas_call | solution.py:827
  239.6 7.4 out.1
  254.7 19.0 %collective-permute-done.32 = bf16[1,256,2048]{2,1,0:T(8,128)(2,1)S(1)} collective-permute-done((bf16[1,256,2048]{2,1,0:T(8,128)(2,1)S(1)}, bf16[1,256,2048]{2,1,0:T(8,128)(2,1)S(1)}, u32[]{:S(2)}, u32[]{:S(2)}) %collective-permute-start.32) | collective-permute-done | bytes 1048608 | tf_op jit(solution)/shard_map/ppermute | solution.py:52
  277.1 10.9 %collective-permute-done.34 = bf16[2,256,768]{2,1,0:T(8,128)(2,1)S(1)} collective-permute-done((bf16[2,256,768]{2,1,0:T(8,128)(2,1)S(1)}, bf16[2,256,768]{2,1,0:T(8,128)(2,1)S(1)}, u32[]{:S(2)}, u32[]{:S(2)}) %collective-permute-start.34) | collective-permute-done | bytes 786464 | tf_op jit(solution)/shard_map/ppermute | solution.py:52
  293.7 22.2 %collective-permute-done.39 = bf16[1,256,2048]{2,1,0:T(8,128)(2,1)S(1)} collective-permute-done((bf16[1,256,2048]{2,1,0:T(8,128)(2,1)S(1)}, bf16[1,256,2048]{2,1,0:T(8,128)(2,1)S(1)}, u32[]{:S(2)}, u32[]{:S(2)}) %collective-permute-start.39) | collective-permute-done | bytes 1048608 | tf_op jit(solution)/shard_map/ppermute | solution.py:52
  317.4 10.7 %collective-permute-done.38 = bf16[2,256,768]{2,1,0:T(8,128)(2,1)S(1)} collective-permute-done((bf16[2,256,768]{2,1,0:T(8,128)(2,1)S(1)}, bf16[2,256,768]{2,1,0:T(8,128)(2,1)S(1)}, u32[]{:S(2)}, u32[]{:S(2)}) %collective-permute-start.38) | collective-permute-done | bytes 786464 | tf_op jit(solution)/shard_map/ppermute | solution.py:52
  340.3 7.2 hidden.6
  348.3 7.3 weight_grads.6
  356.7 7.3 hidden.7
  376.0 7.4 hidden.8
  385.2 7.3 weight_grads.8
  415.6 7.6 hidden.11
  424.3 20.7 %back_sum.3 = (bf16[512,2048]{1,0:T(8,128)(2,1)}, bf16[512,2048]{1,0:T(8,128)(2,1)}) custom-call(bf16[1024,512]{1,0:T(8,128)(2,1)S(1)} %get-tuple-element.300.refs_0_, bf16[1024,512]{1,0:T(8,128)(2,1)S(1)} %copy-done.57, bf16[1024,512]{1,0:T(8,128)(2,1)} %copy-done.58, bf16[1024,512]{1,0:T(8,128)(2,1)} %copy-done.59, bf16[1024,512]{1,0:T(8,128)(2,1)} %copy-done.60, ...), custom_call_target="tpu_custom_call" | custom-call | flops 1000 | bytes 1000 | tf_op jit(solution)/shard_map/back_sum/pallas_call | solution.py:948
  472.7 12.5 %back_sum.2 = (bf16[512,2048]{1,0:T(8,128)(2,1)}, bf16[512,2048]{1,0:T(8,128)(2,1)}) custom-call(bf16[1024,256]{1,0:T(8,128)(2,1)S(1)} %copy-done.76, bf16[1024,256]{1,0:T(8,128)(2,1)S(1)} %copy-done.78, bf16[1024,256]{1,0:T(8,128)(2,1)S(1)} %copy-done.80, bf16[1024,256]{1,0:T(8,128)(2,1)S(1)} %copy-done.82, bf16[1024,256]{1,0:T(8,128)(2,1)S(1)} %copy-done.84, ...), custom_call_target="tpu_custom_call" | custom-call | flops 1000 | bytes 1000 | tf_op jit(solution)/shard_map/back_sum/pallas_call | solution.py:948
  485.2 7.3 weight_grads.9
  511.6 7.4 weight_grads.10
  521.1 15.8 %collective-permute-done.57 = bf16[2,768,256]{2,1,0:T(8,128)(2,1)} collective-permute-done((bf16[2,768,256]{2,1,0:T(8,128)(2,1)}, bf16[2,768,256]{2,1,0:T(8,128)(2,1)}, u32[]{:S(2)}, u32[]{:S(2)}) %collective-permute-start.57) | collective-permute-done | bytes 786464 | tf_op jit(solution)/shard_map/ppermute | solution.py:52
  567.4 30.9 %attend_back.1 = (f32[1,5,4,4,64,128]{5,4,3,2,1,0:T(8,128)}, bf16[4,1,5,4,64,128]{5,4,3,2,1,0:T(8,128)(2,1)S(1)}, bf16[4,1,5,4,64,128]{5,4,3,2,1,0:T(8,128)(2,1)S(1)}) custom-call(bf16[1,5,4,4,64,128]{5,4,3,2,1,0:T(8,128)(2,1)S(1)} %copy-done.20, bf16[1,5,4,4,64,128]{5,4,3,2,1,0:T(8,128)(2,1)} %copy-done.21, s32[1,4,1,256]{3,2,1,0:T(1,128)S(1)} %copy-done.99, ...), custom_call_target="tpu_custom_call" | custom-call | flops 1000 | bytes 1000 | tf_op jit(solution)/shard_map/attend_back/pallas_call | solution.py:1021
  630.5 7.5 weight_grads.11
  638.1 8.0 collective-permute-done.65
  665.6 7.3 product.3
  684.0 11.0 %collective-permute-done.68 = bf16[2,1,5,4,64,128]{5,4,3,2,1,0:T(8,128)(2,1)} collective-permute-done((bf16[2,1,5,4,64,128]{5,4,3,2,1,0:T(8,128)(2,1)}, bf16[2,1,5,4,64,128]{5,4,3,2,1,0:T(8,128)(2,1)}, u32[]{:S(2)}, u32[]{:S(2)}) %collective-permute-start.68) | collective-permute-done | bytes 655392 | tf_op jit(solution)/shard_map/ppermute | solution.py:52
  706.3 7.2 product.4
  718.6 8.4 %h_one_back.1 = (bf16[256,2048]{1,0:T(8,128)(2,1)S(1)}, f32[1,2048]{1,0:T(1,128)S(1)}) custom-call(bf16[4,256,320]{2,1,0:T(8,128)(2,1)S(1)} %copy-done.31, bf16[4,8,320,256]{3,2,1,0:T(8,128)(2,1)} %copy-done.109, bf16[256,640]{1,0:T(8,128)(2,1)S(1)} %get-tuple-element.384.dkv_ref, bf16[2048,640]{1,0:T(8,128)(2,1)} %bitcast.174, ...), custom_call_target="tpu_custom_call" | custom-call | flops 1000 | bytes 1000 | tf_op jit(solution)/shard_map/h_one_back/pallas_call | solution.py:1124
  (674 shorter events, 406.8 us)
Async XLA Ops:
  122.5 37.0 %collective-permute-start.18 = (bf16[2,8,320,256]{3,2,1,0:T(8,128)(2,1)S(1)}, bf16[2,8,320,256]{3,2,1,0:T(8,128)(2,1)S(1)}, u32[]{:S(2)}, u32[]{:S(2)}) collective-permute-start(bf16[2,8,320,256]{3,2,1,0:T(8,128)(2,1)S(1)} %pad_maximum_fusion.4), channel_id=1, source_target_pairs={{0,1},{1,0},{2,3},{3,2},{4,5},{5,4},{6,7},{7,6},{8,9},{9,8},{10,11... | collective-permute-start | bytes 7864328 | tf_op jit(solution)/shard_map/ppermute | solution.py:52
  122.7 36.9 %collective-permute-start.21 = (bf16[4,256,768]{2,1,0:T(8,128)(2,1)S(1)}, bf16[4,256,768]{2,1,0:T(8,128)(2,1)S(1)}, u32[]{:S(2)}, u32[]{:S(2)}) collective-permute-start(bf16[4,256,768]{2,1,0:T(8,128)(2,1)S(1)} %pad_maximum_fusion.11), channel_id=1, source_target_pairs={{0,4},{4,0},{8,12},{12,8},{16,20},{20,16},{24,28},{28,24},{1,5},{5... | collective-permute-start | bytes 4718600 | tf_op jit(solution)/shard_map/ppermute | solution.py:52
  159.6 42.2 %collective-permute-start.24 = (bf16[2,8,320,256]{3,2,1,0:T(8,128)(2,1)}, bf16[2,8,320,256]{3,2,1,0:T(8,128)(2,1)}, u32[]{:S(2)}, u32[]{:S(2)}) collective-permute-start(bf16[2,8,320,256]{3,2,1,0:T(8,128)(2,1)} %pad_maximum_fusion.6), channel_id=1, source_target_pairs={{0,1},{1,0},{2,3},{3,2},{4,5},{5,4},{6,7},{7,6},{8,9},{9,8},{10,11... | collective-permute-start | bytes 7864328 | tf_op jit(solution)/shard_map/ppermute | solution.py:52
  159.6 39.4 %collective-permute-start.25 = (bf16[1,256,2048]{2,1,0:T(8,128)(2,1)S(1)}, bf16[1,256,2048]{2,1,0:T(8,128)(2,1)}, u32[]{:S(2)}, u32[]{:S(2)}) collective-permute-start(bf16[1,256,2048]{2,1,0:T(8,128)(2,1)S(1)} %bitcast.194), channel_id=1, source_target_pairs={{0,2},{1,3},{2,0},{3,1},{4,6},{5,7},{6,4},{7,5},{8,10},{9,11},{10,... | collective-permute-start | bytes 3145736 | tf_op jit(solution)/shard_map/ppermute | solution.py:52
  160.3 41.4 %collective-permute-start.23 = (bf16[4,1,5,4,64,128]{5,4,3,2,1,0:T(8,128)(2,1)S(1)}, bf16[4,1,5,4,64,128]{5,4,3,2,1,0:T(8,128)(2,1)S(1)}, u32[]{:S(2)}, u32[]{:S(2)}) collective-permute-start(bf16[4,1,5,4,64,128]{5,4,3,2,1,0:T(8,128)(2,1)S(1)} %pad_maximum_fusion.17.low_ref), channel_id=1, source_target_pairs={{0,4},{4,0},{8,12},{12,8},{16,20},{20,16},{24,28},{28,24},{1,5},{5... | collective-permute-start | bytes 3932168 | tf_op jit(solution)/shard_map/ppermute | solution.py:52
  201.8 46.8 %collective-permute-start.28 = (bf16[2,256,2048]{2,1,0:T(8,128)(2,1)}, bf16[2,256,2048]{2,1,0:T(8,128)(2,1)}, u32[]{:S(2)}, u32[]{:S(2)}) collective-permute-start(bf16[2,256,2048]{2,1,0:T(8,128)(2,1)} %pad_maximum_fusion.7), channel_id=1, source_target_pairs={{0,1},{1,0},{2,3},{3,2},{4,5},{5,4},{6,7},{7,6},{8,9},{9,8},{10,11... | collective-permute-start | bytes 6291464 | tf_op jit(solution)/shard_map/ppermute | solution.py:52
  205.5 43.1 %collective-permute-start.29 = (bf16[4,256,768]{2,1,0:T(8,128)(2,1)}, bf16[4,256,768]{2,1,0:T(8,128)(2,1)}, u32[]{:S(2)}, u32[]{:S(2)}) collective-permute-start(bf16[4,256,768]{2,1,0:T(8,128)(2,1)} %pad_maximum_fusion.12), channel_id=1, source_target_pairs={{0,4},{4,0},{8,12},{12,8},{16,20},{20,16},{24,28},{28,24},{1,5},{5... | collective-permute-start | bytes 4718600 | tf_op jit(solution)/shard_map/ppermute | solution.py:52
  208.3 38.7 %collective-permute-start.30 = (bf16[2,256,768]{2,1,0:T(8,128)(2,1)}, bf16[2,256,768]{2,1,0:T(8,128)(2,1)}, u32[]{:S(2)}, u32[]{:S(2)}) collective-permute-start(bf16[2,256,768]{2,1,0:T(8,128)(2,1)} %pad_maximum_fusion.22), channel_id=1, source_target_pairs={{0,16},{4,20},{8,24},{12,28},{16,0},{20,4},{24,8},{28,12},{1,17},{... | collective-permute-start | bytes 2359304 | tf_op jit(solution)/shard_map/ppermute | solution.py:52
  208.3 38.7 %collective-permute-start.31 = (bf16[1,256,768]{2,1,0:T(8,128)(2,1)S(1)}, bf16[1,256,768]{2,1,0:T(8,128)(2,1)}, u32[]{:S(2)}, u32[]{:S(2)}) collective-permute-start(bf16[1,256,768]{2,1,0:T(8,128)(2,1)S(1)} %bitcast.203), channel_id=1, source_target_pairs={{0,8},{4,12},{8,0},{12,4},{16,24},{20,28},{24,16},{28,20},{1,9},{5... | collective-permute-start | bytes 1179656 | tf_op jit(solution)/shard_map/ppermute | solution.py:52
  248.6 39.4 %collective-permute-start.33 = (bf16[4,256,768]{2,1,0:T(8,128)(2,1)S(1)}, bf16[4,256,768]{2,1,0:T(8,128)(2,1)S(1)}, u32[]{:S(2)}, u32[]{:S(2)}) collective-permute-start(bf16[4,256,768]{2,1,0:T(8,128)(2,1)S(1)} %pad_maximum_fusion.13), channel_id=1, source_target_pairs={{0,4},{4,0},{8,12},{12,8},{16,20},{20,16},{24,28},{28,24},{1,5},{5... | collective-permute-start | bytes 4718600 | tf_op jit(solution)/shard_map/ppermute | solution.py:52
  289.1 39.1 %collective-permute-start.36 = (bf16[2,256,2048]{2,1,0:T(8,128)(2,1)S(1)}, bf16[2,256,2048]{2,1,0:T(8,128)(2,1)S(1)}, u32[]{:S(2)}, u32[]{:S(2)}) collective-permute-start(bf16[2,256,2048]{2,1,0:T(8,128)(2,1)S(1)} %pad_maximum_fusion.8), channel_id=1, source_target_pairs={{0,1},{1,0},{2,3},{3,2},{4,5},{5,4},{6,7},{7,6},{8,9},{9,8},{10,11... | collective-permute-start | bytes 6291464 | tf_op jit(solution)/shard_map/ppermute | solution.py:52
  289.3 39.0 %collective-permute-start.37 = (bf16[4,256,768]{2,1,0:T(8,128)(2,1)S(1)}, bf16[4,256,768]{2,1,0:T(8,128)(2,1)S(1)}, u32[]{:S(2)}, u32[]{:S(2)}) collective-permute-start(bf16[4,256,768]{2,1,0:T(8,128)(2,1)S(1)} %pad_maximum_fusion.14), channel_id=1, source_target_pairs={{0,4},{4,0},{8,12},{12,8},{16,20},{20,16},{24,28},{28,24},{1,5},{5... | collective-permute-start | bytes 4718600 | tf_op jit(solution)/shard_map/ppermute | solution.py:52
  329.4 38.0 %collective-permute-start.43 = (bf16[2,256,2048]{2,1,0:T(8,128)(2,1)}, bf16[2,256,2048]{2,1,0:T(8,128)(2,1)}, u32[]{:S(2)}, u32[]{:S(2)}) collective-permute-start(bf16[2,256,2048]{2,1,0:T(8,128)(2,1)} %pad_maximum_fusion.9), channel_id=1, source_target_pairs={{0,1},{1,0},{2,3},{3,2},{4,5},{5,4},{6,7},{7,6},{8,9},{9,8},{10,11... | collective-permute-start | bytes 6291464 | tf_op jit(solution)/shard_map/ppermute | solution.py:52
  329.6 37.9 %collective-permute-start.41 = (bf16[4,256,768]{2,1,0:T(8,128)(2,1)S(1)}, bf16[4,256,768]{2,1,0:T(8,128)(2,1)}, u32[]{:S(2)}, u32[]{:S(2)}) collective-permute-start(bf16[4,256,768]{2,1,0:T(8,128)(2,1)S(1)} %pad_maximum_fusion.15), channel_id=1, source_target_pairs={{0,4},{4,0},{8,12},{12,8},{16,20},{20,16},{24,28},{28,24},{1,5},{5... | collective-permute-start | bytes 4718600 | tf_op jit(solution)/shard_map/ppermute | solution.py:52
  330.5 36.9 %collective-permute-start.42 = (bf16[2,256,768]{2,1,0:T(8,128)(2,1)S(1)}, bf16[2,256,768]{2,1,0:T(8,128)(2,1)S(1)}, u32[]{:S(2)}, u32[]{:S(2)}) collective-permute-start(bf16[2,256,768]{2,1,0:T(8,128)(2,1)S(1)} %pad_maximum_fusion.25), channel_id=1, source_target_pairs={{0,16},{4,20},{8,24},{12,28},{16,0},{20,4},{24,8},{28,12},{1,17},{... | collective-permute-start | bytes 2359304 | tf_op jit(solution)/shard_map/ppermute | solution.py:52
  367.4 37.3 %collective-permute-start.47 = (bf16[4,768,256]{2,1,0:T(8,128)(2,1)}, bf16[4,768,256]{2,1,0:T(8,128)(2,1)}, u32[]{:S(2)}, u32[]{:S(2)}) collective-permute-start(bf16[4,768,256]{2,1,0:T(8,128)(2,1)} %get-tuple-element.309), channel_id=1, source_target_pairs={{0,4},{4,0},{8,12},{12,8},{16,20},{20,16},{24,28},{28,24},{1,5},{5... | collective-permute-start | bytes 4718600 | tf_op jit(solution)/shard_map/ppermute | solution.py:52
  404.7 40.4 %collective-permute-start.48 = (bf16[4,768,256]{2,1,0:T(8,128)(2,1)S(1)}, bf16[4,768,256]{2,1,0:T(8,128)(2,1)S(1)}, u32[]{:S(2)}, u32[]{:S(2)}) collective-permute-start(bf16[4,768,256]{2,1,0:T(8,128)(2,1)S(1)} %get-tuple-element.311), channel_id=1, source_target_pairs={{0,4},{4,0},{8,12},{12,8},{16,20},{20,16},{24,28},{28,24},{1,5},{5... | collective-permute-start | bytes 4718600 | tf_op jit(solution)/shard_map/ppermute | solution.py:52
  407.8 37.2 %collective-permute-start.49 = (bf16[2,768,256]{2,1,0:T(8,128)(2,1)}, bf16[2,768,256]{2,1,0:T(8,128)(2,1)}, u32[]{:S(2)}, u32[]{:S(2)}) collective-permute-start(bf16[2,768,256]{2,1,0:T(8,128)(2,1)} %add_convert_fusion.5), channel_id=1, source_target_pairs={{0,16},{4,20},{8,24},{12,28},{16,0},{20,4},{24,8},{28,12},{1,17},{... | collective-permute-start | bytes 2359304 | tf_op jit(solution)/shard_map/ppermute | solution.py:52
  446.3 46.3 %collective-permute-start.50 = (bf16[2,256,2048]{2,1,0:T(8,128)(2,1)}, bf16[2,256,2048]{2,1,0:T(8,128)(2,1)}, u32[]{:S(2)}, u32[]{:S(2)}) collective-permute-start(bf16[2,256,2048]{2,1,0:T(8,128)(2,1)} %bitcast.271), channel_id=1, source_target_pairs={{0,1},{1,0},{2,3},{3,2},{4,5},{5,4},{6,7},{7,6},{8,9},{9,8},{10,11... | collective-permute-start | bytes 6291464 | tf_op jit(solution)/shard_map/ppermute | solution.py:52
  446.3 46.3 %collective-permute-start.51 = (bf16[4,768,256]{2,1,0:T(8,128)(2,1)}, bf16[4,768,256]{2,1,0:T(8,128)(2,1)}, u32[]{:S(2)}, u32[]{:S(2)}) collective-permute-start(bf16[4,768,256]{2,1,0:T(8,128)(2,1)} %get-tuple-element.321), channel_id=1, source_target_pairs={{0,4},{4,0},{8,12},{12,8},{16,20},{20,16},{24,28},{28,24},{1,5},{5... | collective-permute-start | bytes 4718600 | tf_op jit(solution)/shard_map/ppermute | solution.py:52
  453.0 39.6 %collective-permute-start.52 = (bf16[2,768,256]{2,1,0:T(8,128)(2,1)}, bf16[2,768,256]{2,1,0:T(8,128)(2,1)}, u32[]{:S(2)}, u32[]{:S(2)}) collective-permute-start(bf16[2,768,256]{2,1,0:T(8,128)(2,1)} %add_convert_fusion.4), channel_id=1, source_target_pairs={{0,16},{4,20},{8,24},{12,28},{16,0},{20,4},{24,8},{28,12},{1,17},{... | collective-permute-start | bytes 2359304 | tf_op jit(solution)/shard_map/ppermute | solution.py:52
  492.5 46.6 %collective-permute-start.54 = (bf16[2,256,2048]{2,1,0:T(8,128)(2,1)}, bf16[2,256,2048]{2,1,0:T(8,128)(2,1)}, u32[]{:S(2)}, u32[]{:S(2)}) collective-permute-start(bf16[2,256,2048]{2,1,0:T(8,128)(2,1)} %bitcast.46), channel_id=1, source_target_pairs={{0,1},{1,0},{2,3},{3,2},{4,5},{5,4},{6,7},{7,6},{8,9},{9,8},{10,11... | collective-permute-start | bytes 6291464 | tf_op jit(solution)/shard_map/ppermute | solution.py:52
  499.8 37.2 %collective-permute-start.57 = (bf16[2,768,256]{2,1,0:T(8,128)(2,1)}, bf16[2,768,256]{2,1,0:T(8,128)(2,1)}, u32[]{:S(2)}, u32[]{:S(2)}) collective-permute-start(bf16[2,768,256]{2,1,0:T(8,128)(2,1)} %add_convert_fusion.3), channel_id=1, source_target_pairs={{0,16},{4,20},{8,24},{12,28},{16,0},{20,4},{24,8},{28,12},{1,17},{... | collective-permute-start | bytes 2359304 | tf_op jit(solution)/shard_map/ppermute | solution.py:52
  500.4 38.7 %collective-permute-start.56 = (bf16[4,768,256]{2,1,0:T(8,128)(2,1)}, bf16[4,768,256]{2,1,0:T(8,128)(2,1)}, u32[]{:S(2)}, u32[]{:S(2)}) collective-permute-start(bf16[4,768,256]{2,1,0:T(8,128)(2,1)} %get-tuple-element.335), channel_id=1, source_target_pairs={{0,4},{4,0},{8,12},{12,8},{16,20},{20,16},{24,28},{28,24},{1,5},{5... | collective-permute-start | bytes 4718600 | tf_op jit(solution)/shard_map/ppermute | solution.py:52
  539.2 75.4 %collective-permute-start.60 = (bf16[4,768,256]{2,1,0:T(8,128)(2,1)}, bf16[4,768,256]{2,1,0:T(8,128)(2,1)}, u32[]{:S(2)}, u32[]{:S(2)}) collective-permute-start(bf16[4,768,256]{2,1,0:T(8,128)(2,1)} %get-tuple-element.351), channel_id=1, source_target_pairs={{0,4},{4,0},{8,12},{12,8},{16,20},{20,16},{24,28},{28,24},{1,5},{5... | collective-permute-start | bytes 4718600 | tf_op jit(solution)/shard_map/ppermute | solution.py:52
  542.7 71.9 %collective-permute-start.59 = (bf16[1,256,2048]{2,1,0:T(8,128)(2,1)}, bf16[1,256,2048]{2,1,0:T(8,128)(2,1)}, u32[]{:S(2)}, u32[]{:S(2)}) collective-permute-start(bf16[1,256,2048]{2,1,0:T(8,128)(2,1)} %fusion.4), channel_id=1, source_target_pairs={{0,2},{1,3},{2,0},{3,1},{4,6},{5,7},{6,4},{7,5},{8,10},{9,11},{10,... | collective-permute-start | bytes 3145736 | tf_op jit(solution)/shard_map/ppermute | solution.py:52
  546.3 63.6 %collective-permute-start.62 = (bf16[1,768,256]{2,1,0:T(8,128)(2,1)}, bf16[1,768,256]{2,1,0:T(8,128)(2,1)}, u32[]{:S(2)}, u32[]{:S(2)}) collective-permute-start(bf16[1,768,256]{2,1,0:T(8,128)(2,1)} %add_convert_fusion.10), channel_id=1, source_target_pairs={{0,8},{4,12},{8,0},{12,4},{16,24},{20,28},{24,16},{28,20},{1,9},{5... | collective-permute-start | bytes 1179656 | tf_op jit(solution)/shard_map/ppermute | solution.py:52
  546.3 68.3 %collective-permute-start.61 = (bf16[2,768,256]{2,1,0:T(8,128)(2,1)}, bf16[2,768,256]{2,1,0:T(8,128)(2,1)}, u32[]{:S(2)}, u32[]{:S(2)}) collective-permute-start(bf16[2,768,256]{2,1,0:T(8,128)(2,1)} %add_convert_fusion.2), channel_id=1, source_target_pairs={{0,16},{4,20},{8,24},{12,28},{16,0},{20,4},{24,8},{28,12},{1,17},{... | collective-permute-start | bytes 2359304 | tf_op jit(solution)/shard_map/ppermute | solution.py:52
  614.6 37.9 %collective-permute-start.64 = (bf16[1,256,2048]{2,1,0:T(8,128)(2,1)}, bf16[1,256,2048]{2,1,0:T(8,128)(2,1)}, u32[]{:S(2)}, u32[]{:S(2)}) collective-permute-start(bf16[1,256,2048]{2,1,0:T(8,128)(2,1)} %bitcast.189), channel_id=1, source_target_pairs={{0,2},{1,3},{2,0},{3,1},{4,6},{5,7},{6,4},{7,5},{8,10},{9,11},{10,... | collective-permute-start | bytes 3145736 | tf_op jit(solution)/shard_map/ppermute | solution.py:52
  618.1 37.3 %collective-permute-start.63 = (bf16[4,1,5,4,64,128]{5,4,3,2,1,0:T(8,128)(2,1)}, bf16[4,1,5,4,64,128]{5,4,3,2,1,0:T(8,128)(2,1)}, u32[]{:S(2)}, u32[]{:S(2)}) collective-permute-start(bf16[4,1,5,4,64,128]{5,4,3,2,1,0:T(8,128)(2,1)} %copy-done.106), channel_id=1, source_target_pairs={{0,4},{4,0},{8,12},{12,8},{16,20},{20,16},{24,28},{28,24},{1,5},{5... | collective-permute-start | bytes 3932168 | tf_op jit(solution)/shard_map/ppermute | solution.py:52
  655.3 43.1 %collective-permute-start.69 = (bf16[2,256,2048]{2,1,0:T(8,128)(2,1)}, bf16[2,256,2048]{2,1,0:T(8,128)(2,1)}, u32[]{:S(2)}, u32[]{:S(2)}) collective-permute-start(bf16[2,256,2048]{2,1,0:T(8,128)(2,1)} %pad_maximum_fusion.10), channel_id=1, source_target_pairs={{0,1},{1,0},{2,3},{3,2},{4,5},{5,4},{6,7},{7,6},{8,9},{9,8},{10,11... | collective-permute-start | bytes 6291464 | tf_op jit(solution)/shard_map/ppermute | solution.py:52
  658.5 37.8 %collective-permute-start.71 = (bf16[4,768,256]{2,1,0:T(8,128)(2,1)}, bf16[4,768,256]{2,1,0:T(8,128)(2,1)}, u32[]{:S(2)}, u32[]{:S(2)}) collective-permute-start(bf16[4,768,256]{2,1,0:T(8,128)(2,1)} %get-tuple-element.378), channel_id=1, source_target_pairs={{0,4},{4,0},{8,12},{12,8},{16,20},{20,16},{24,28},{28,24},{1,5},{5... | collective-permute-start | bytes 4718600 | tf_op jit(solution)/shard_map/ppermute | solution.py:52
  (220 other events, 3375.6 us)

commit v4 on v3

--- a/solution.py
+++ b/solution.py
@@ -14,6 +14,7 @@
 STRETCH = 64
 LANES = 128
 FF_PARTS = (1, 1, 1, 1, 1, 1)
+FF_LAST = len(FF_PARTS) - 1
 VMEM_LIMIT = 48 * 1024 * 1024
 SMALL = pl.CostEstimate(flops=1000, bytes_accessed=1000, transcendentals=0)
 
@@ -123,6 +124,63 @@
     def pieces(self):
         half = order_of("dp")[: lax.axis_size("dp") // 2]
         return [(x, [r ^ m for r in half]) for x, m in zip(self.halves, (0, masks_of("dp")[-1]))]
+
+
+class GatherSoon(Item):
+    def __init__(self, value):
+        self.stack, self.phase = value[None], 0
+
+    def value(self):
+        return self.stack
+
+    def advance(self, value):
+        order = order_of("dp")
+        if self.phase:
+            got = [self.bring(value, "dp", masks_of("dp")[-1])]
+        else:
+            got = [self.bring(value, "dp", r) for r in order[1 : len(order) // 2]]
+        both = jnp.concatenate([value, *got], axis=0)
+        self.stack = layout.with_layout_constraint(both, layout.Layout(tuple(range(both.ndim))))
+        self.phase += 1
+        return got
+
+
+class ScatterSoon(Item):
+    def __init__(self, low, high):
+        self.low, self.high, self.phase = low, high, 0
+
+    def value(self):
+        if self.phase == 0:
+            return self.high
+        self.total = self.low.astype(f32) + self.first.astype(f32)
+        return self.total[1:].astype(bf16)
+
+    def advance(self, value):
+        order = order_of("dp")
+        self.phase += 1
+        if self.phase == 1:
+            self.first = self.bring(value, "dp", order[len(order) // 2])
+            return self.first
+        self.rest = [
+            self.bring(value[p - 1], "dp", order[p]) for p in range(1, len(order) // 2)
+        ]
+        return self.rest
+
+    def result(self):
+        return self.total[0] + sum(x.astype(f32) for x in self.rest)
+
+
+class TensorAll(Item):
+    def __init__(self, value):
+        self.own = value
+
+    def value(self):
+        return self.own
+
+    def advance(self, value):
+        got = [self.bring(value, "tensor", r) for r in order_of("tensor")[1:]]
+        self.stack = jnp.stack([value, *got])
+        return got
 
 
 class GatherLate(Item):
@@ -161,6 +219,7 @@
 class Scatter(Item):
     def __init__(self, make):
         self.make, self.half, self.arrived, self.phase = make, lax.axis_size("dp"), [], 2
+        self.raw = []
 
     def value(self):
         half = self.half // 2
@@ -173,6 +232,7 @@
             self.half //= 2
             got = self.bring(value, "dp", mask)
             self.arrived = [x[: self.half] for x in self.arrived] + [got]
+            self.raw.append(got)
         self.phase -= 1
         return got
 
@@ -189,8 +249,12 @@
 
     def advance(self, value):
         got = self.bring(value, "tensor", self.masks[0])
+        self.halves = (value, got)
         self.stack, self.masks = join(value, got), self.masks[1:]
         return got
+
+    def rows(self):
+        return [x.reshape(-1, x.shape[-1]) for x in self.halves]
 
 
 class PairRows(Item):
@@ -232,6 +296,22 @@
         return [self.sums[0], *self.arrived]
 
 
+class TensorDirect(Item):
+    def __init__(self, parts):
+        self.parts = list(parts)
+
+    def value(self):
+        return self.parts
+
+    def advance(self, value):
+        order = order_of("tensor")
+        self.got = [self.bring(value[p], "tensor", order[p]) for p in range(1, len(order))]
+        return self.got
+
+    def terms(self):
+        return [x[None] for x in [self.parts[0], *self.got]]
+
+
 class TensorExchange(Item):
     def __init__(self, stack):
         self.stack, self.masks = stack[:, None], masks_of("tensor")
@@ -279,7 +359,8 @@
             if self.done:
                 value = after(value, *self.done)
             item.late = during
-            done.append(item.advance(value))
+            got = item.advance(value)
+            done += got if isinstance(got, list) else [got]
         self.done = done
 
 
@@ -384,9 +465,8 @@
         out_ref[0, 0, b] = heads.T.astype(bf16).reshape(q_ref.shape[3:])
 
 
-def attend_back_kernel(
-    q_ref, g_ref, limit_ref, keypos_ref, low_ref, high_ref, dq_ref, dlow_ref, dhigh_ref, kv, kvt, acc
-):
+def attend_back_kernel(q_ref, g_ref, limit_ref, keypos_ref, low_ref, high_ref, *rest):
+    dq_ref, dlow_ref, dhigh_ref, kv, kvt, acc = rest[-6:]
     blocks = q_ref.shape[2]
     group = load_keys((low_ref, high_ref), kv, kvt)
     acc[...] = jnp.zeros_like(acc)
@@ -413,20 +493,22 @@
                 out[r, 0, 0, g] = acc[start : start + STRETCH].astype(bf16)
 
 
-def out_kernel(o_ref, w_ref, x_ref, live_ref, gain_ref, mixed_ref, h_ref, heads_ref):
+def out_kernel(o_ref, w_low, w_high, x_ref, live_ref, gain_ref, mixed_ref, h_ref, heads_ref):
     rows = heads_ref.shape[1]
     heads = jnp.concatenate(
         [o_ref[:, h, :, 0].reshape(rows, LANES)[:, HEAD:] for h in range(HEADS_KV)], axis=1
     )
     heads_ref[0] = heads
-    cols = w_ref.shape[3]
+    cols = w_low.shape[3]
+    low = pl.program_id(0) < pl.num_programs(0) // 2
 
     @pl.when(pl.program_id(0) == 0)
     def _():
         mixed_ref[...] = jnp.zeros_like(mixed_ref)
 
-    for r in range(w_ref.shape[1]):
-        mixed_ref[:, r * cols : (r + 1) * cols] += dot(heads, w_ref[0, r])
+    for r in range(w_low.shape[1]):
+        here = jnp.where(low, w_low[0, r], w_high[0, r])
+        mixed_ref[:, r * cols : (r + 1) * cols] += dot(heads, here)
 
     @pl.when(pl.program_id(0) == pl.num_programs(0) - 1)
     def _():
@@ -452,11 +534,16 @@
     d_attn_ref[...] = (live_ref[...] * d_mixed).astype(bf16)
 
 
-def heads_back_kernel(d_ref, w_ref, out_ref):
-    cols = w_ref.shape[3]
+def heads_back_kernel(d_ref, w_low, w_high, out_ref):
+    cols = w_low.shape[3]
+    low = pl.program_id(0) < pl.num_programs(0) // 2
     grad = sum(
-        dot(d_ref[:, r * cols : (r + 1) * cols], w_ref[0, r], contract_cols)
-        for r in range(w_ref.shape[1])
+        dot(
+            d_ref[:, r * cols : (r + 1) * cols],
+            jnp.where(low, w_low[0, r], w_high[0, r]),
+            contract_cols,
+        )
+        for r in range(w_low.shape[1])
     )
     rows, blocks = out_ref.shape[0], out_ref.shape[2]
     for h in range(HEADS_KV):
@@ -525,8 +612,11 @@
         out_ref[...] = (d_mixed_ref[...] + back).astype(bf16)
 
 
-def shards_kernel(in_ref, down_ref, query_ref, *refs):
-    parts, query_out_ref = refs[:-1], refs[-1]
+def turn_kernel(x_ref, out_ref):
+    out_ref[...] = x_ref[...].T
+
+
+def shards_kernel(in_ref, down_ref, *parts):
     ff = down_ref.shape[0]
     start = 0
     for ref in parts:
@@ -535,7 +625,6 @@
         ref[:, part : 2 * part] = in_ref[:, ff + start : ff + start + part]
         ref[:, 2 * part :] = down_ref[start : start + part, :].T
         start += part
-    query_out_ref[...] = query_ref[...].T
 
 
 def turn_columns(order, back, index, value):
@@ -573,34 +662,39 @@
     out_ref[...] = turn_columns(order, True, index_ref[0], value).astype(bf16)
 
 
-def product_kernel(left_ref, right_ref, low_ref, high_ref, turned):
+def product_kernel(left_low, left_high, right_ref, low_ref, high_ref, turned):
     @pl.when(pl.program_id(0) == 0)
     def _():
         turned[...] = right_ref[...].T
 
-    out = dot(turned[...], left_ref[...]).astype(bf16)
+    out = halves_product(turned[...], left_low, left_high).astype(bf16)
     low = pl.program_id(0) < pl.num_programs(0) // 2
+    span = low_ref.shape[2]
     for out_ref, here in ((low_ref, low), (high_ref, jnp.logical_not(low))):
 
         @pl.when(here)
         def _(out_ref=out_ref):
-            out_ref[0] = out
-
-
-def pick_columns(ref, places, cols):
+            for p in range(out_ref.shape[0]):
+                out_ref[p] = out[:, p * span : (p + 1) * span]
+
+
+def pick_columns(value, places, cols):
     if places == list(range(places[0], places[0] + len(places))):
-        return ref[:, places[0] * cols : (places[-1] + 1) * cols]
-    return jnp.concatenate([ref[:, p * cols : (p + 1) * cols] for p in places], axis=1)
-
-
-def hidden_kernel(all_places, h_ref, d_ref, *refs):
+        return value[:, places[0] * cols : (places[-1] + 1) * cols]
+    return jnp.concatenate([value[:, p * cols : (p + 1) * cols] for p in places], axis=1)
+
+
+def hidden_kernel(all_places, h_low, h_high, d_low, d_high, *refs):
     pieces, (hidden_ref, d_gate_up_ref, turned_ref) = refs[:-3], refs[-3:]
     part = hidden_ref.shape[1]
+    low = pl.program_id(0) < pl.num_programs(0) // 2
+    h = jnp.where(low, h_low[...], h_high[...])
+    d = jnp.where(low, d_low[...], d_high[...])
     gate_up = d_hidden = None
     for places, ref in zip(all_places, pieces):
         cols = ref.shape[0] // len(places)
-        first = dot(pick_columns(h_ref, places, cols), ref[:, : 2 * part])
-        second = dot(pick_columns(d_ref, places, cols), ref[:, 2 * part :])
+        first = dot(pick_columns(h, places, cols), ref[:, : 2 * part])
+        second = dot(pick_columns(d, places, cols), ref[:, 2 * part :])
         gate_up = first if gate_up is None else gate_up + first
         d_hidden = second if d_hidden is None else d_hidden + second
     gate, up = gate_up[:, :part], gate_up[:, part:]
@@ -617,10 +711,15 @@
     turned_ref[2 * part :] = hidden.T
 
 
-def grads_kernel(h_ref, d_ref, turned_ref, low_ref, high_ref):
+def halves_product(left, low_ref, high_ref):
+    middle = low_ref.shape[0]
+    return dot(left[:, :middle], low_ref[...]) + dot(left[:, middle:], high_ref[...])
+
+
+def grads_kernel(h_low, h_high, d_low, d_high, turned_ref, low_ref, high_ref):
     split = turned_ref.shape[0] // 3 * 2
-    first = dot(turned_ref[:split], h_ref[...]).astype(bf16)
-    second = dot(turned_ref[split:], d_ref[...]).astype(bf16)
+    first = halves_product(turned_ref[:split], h_low, h_high).astype(bf16)
+    second = halves_product(turned_ref[split:], d_low, d_high).astype(bf16)
     low = pl.program_id(0) < pl.num_programs(0) // 2
     span = low_ref.shape[2]
     for out_ref, here in ((low_ref, low), (high_ref, jnp.logical_not(low))):
@@ -630,6 +729,19 @@
             for p in range(out_ref.shape[0]):
                 out_ref[p, :split] = first[:, p * span : (p + 1) * span]
                 out_ref[p, split:] = second[:, p * span : (p + 1) * span]
+
+
+def collect_kernel(count, each, *refs):
+    in_ref, down_ref = refs[-2:]
+    part = down_ref.shape[0]
+    for c in range(count):
+
+        @pl.when(pl.program_id(0) == c)
+        def _(c=c):
+            total = sum(ref[0].astype(f32) for ref in refs[c * each : (c + 1) * each])
+            in_ref[:, 0, :] = total[:part].T
+            in_ref[:, 1, :] = total[part : 2 * part].T
+            down_ref[...] = total[2 * part :]
 
 
 def back_sum_kernel(all_places, *refs):
@@ -652,13 +764,18 @@
                 for side in range(2)
             ]
         totals = [t if old is None else old + t for old, t in zip(totals, terms)]
-    low = pl.program_id(0) < pl.num_programs(0) // 2
-    for out_ref, here in ((refs[-2], low), (refs[-1], jnp.logical_not(low))):
-
-        @pl.when(here)
-        def _(out_ref=out_ref):
-            for side in range(2):
-                out_ref[:, side * half : (side + 1) * half] = totals[side].astype(bf16)
+    outs = refs[at:]
+    span = outs[0].shape[0]
+    rows = totals[0].shape[0]
+    each = max(rows // span, 1)
+    for step in range(len(outs) // each):
+
+        @pl.when(pl.program_id(0) == step)
+        def _(step=step):
+            for i in range(each):
+                for side in range(2):
+                    block = totals[side][i * span : (i + 1) * span].astype(bf16)
+                    outs[step * each + i][:, side * half : (side + 1) * half] = block
 
 
 def whole(shape):
@@ -746,26 +863,28 @@
     kv_shard = lax.dynamic_slice_in_dim(w_kv, (tensor & 1) * part, part, axis=0)
     unit = ff // sum(FF_PARTS)
     sizes = [size * unit for size in FF_PARTS]
-    *shards, query_shard = pl.pallas_call(
+    query_shard = call(
+        turn_kernel, jax.ShapeDtypeStruct((q_cols, cols), bf16), "turn", w_query, specs=[vmem]
+    )
+    shards = call(
         shards_kernel,
-        out_shape=[jax.ShapeDtypeStruct((cols, 3 * part), bf16) for part in sizes]
-        + [jax.ShapeDtypeStruct((q_cols, cols), bf16)],
-        compiler_params=pltpu.CompilerParams(vmem_limit_bytes=VMEM_LIMIT),
-        cost_estimate=SMALL,
-        name="shards",
-    )(w_in.reshape(cols, 2 * ff), w_down, w_query)
+        [jax.ShapeDtypeStruct((cols, 3 * part), bf16) for part in sizes],
+        "shards",
+        w_in.reshape(cols, 2 * ff),
+        w_down,
+        specs=[vmem, vmem],
+    )
     link = Rounds()
-    g_kv, g_gains = Gather(kv_shard), Gather(norm_gains)
+    g_kv, g_gains = GatherSoon(kv_shard), Gather(norm_gains)
     g_query, g_out = Gather(query_shard), Gather(w_out)
     g_ff = [Gather(x) for x in shards[:-1]] + [GatherLate(shards[-1])]
-    link.go(g_kv, g_query, g_gains)
-    link.go(g_kv, g_gains, g_out)
-    link.go(g_kv, g_gains, g_query, g_ff[0])
+    link.go(g_kv, g_gains, g_query)
+    link.go(g_kv, g_gains, g_query, g_out, g_ff[0])
+    t_kv = PairRows(g_kv.stack)
+    link.go(t_kv, g_gains, g_query, g_out)
     gains = g_gains.stack.transpose(1, 0, 2).reshape(2, width).astype(f32)
     gain_one, gain_two = gains[0], gains[1]
     h_one = scaled_norm(inputs_f, gain_one).astype(bf16)
-    t_kv = PairRows(g_kv.stack)
-    link.go(t_kv, g_query, g_out, g_ff[5])
     t_query = TensorGather(g_query.stack)
     kv_all = t_kv.stack.reshape(width, kv_cols)
     t_d_ffn = TensorGather(d_ffn_own)
@@ -773,6 +892,14 @@
     packed = (rows, HEADS_KV, blocks, n_tensor, STRETCH, LANES)
     packed_kv = (rows, HEADS_KV, blocks, STRETCH, LANES)
     both_spec = pl.BlockSpec((1, n, q_cols, cols), lambda s: (s, 0, 0, 0))
+    half_specs = [
+        pl.BlockSpec(
+            (1, n, q_cols, cols), lambda s: (jnp.minimum(s, n_tensor // 2 - 1), 0, 0, 0)
+        ),
+        pl.BlockSpec(
+            (1, n, q_cols, cols), lambda s: (jnp.maximum(s - n_tensor // 2, 0), 0, 0, 0)
+        ),
+    ]
     kv_raw, kv_own = pl.pallas_call(
         key_kernel,
         out_shape=(
@@ -784,7 +911,7 @@
         name="key_value",
     )(h_one, kv_all, cos, sin, k_gain)
     g_keys = Gather(kv_own)
-    link.go(t_query, g_out, g_ff[0], g_keys)
+    link.go(t_query, g_out, g_ff[5], g_ff[0], g_keys)
     t_out = TensorGather(g_out.stack)
     link.go(t_query, t_out, g_keys, g_ff[0], g_ff[1])
     query_all = t_query.stack
@@ -811,8 +938,7 @@
         cost_estimate=SMALL,
         name="query",
     )(h_one, query_all, cos, sin, q_gain)
-    link.go(t_out, t_d_ffn, g_keys, g_ff[1], g_ff[2], during=[queries])
-    out_all = t_out.stack
+    link.go(t_out, t_d_ffn, g_keys, g_ff[1], g_ff[2], during=[queries, key_pos])
     kv_halves = g_keys.halves
     q_spec = pl.BlockSpec(
         (1, 1, blocks, n_tensor, STRETCH, LANES), lambda i, h: (i, h, 0, 0, 0, 0)
@@ -842,7 +968,13 @@
     mixed, h_two_own, attn_heads = pl.pallas_call(
         out_kernel,
         grid=(n_tensor,),
-        in_specs=[part_spec, both_spec, square, whole((sp_rows, 1)), whole((1, width))],
+        in_specs=[
+            part_spec,
+            *half_specs,
+            square,
+            whole((sp_rows, 1)),
+            whole((1, width)),
+        ],
         out_specs=(square, square, head_spec),
         out_shape=(
             jax.ShapeDtypeStruct((sp_rows, width), f32),
@@ -852,20 +984,21 @@
         compiler_params=params(),
         cost_estimate=SMALL,
         name="out",
-    )(heads_packed, out_all, inputs, live, gain_two[None])
+    )(heads_packed, *t_out.halves, inputs, live, gain_two[None])
     t_heads = TensorExchange(attn_heads)
 
     t_h_two = TensorGather(h_two_own)
     t_h_one = TensorGather(h_one)
     rows_all = sp_rows * n_tensor
     link.go(t_d_ffn, g_ff[1], g_ff[2], g_ff[3], during=[h_two_own])
-    d_ffn = t_d_ffn.stack.reshape(-1, width)
+    d_ffn = t_d_ffn.rows()
     link.go(t_h_two, g_ff[2], g_ff[3], g_ff[4])
     link.go(t_h_two, t_h_one, g_ff[3], g_ff[4], g_ff[5])
-    h_two = t_h_two.stack.reshape(-1, width)
+    h_two = t_h_two.rows()
     steps = n_tensor // 2
     row_block = lambda span: pl.BlockSpec((rows_all // steps, span), lambda i: (i, 0))
-    row_spec = row_block(width)
+    low_rows = pl.BlockSpec((sp_rows, width), lambda i: (jnp.minimum(i, n_tensor // 2 - 1), 0))
+    high_rows = pl.BlockSpec((sp_rows, width), lambda i: (jnp.maximum(i - n_tensor // 2, 0), 0))
     weights, hiddens, d_gate_ups, turned = [], [], [], []
 
     def hidden_part(g, part):
@@ -876,12 +1009,12 @@
         weights.append(pieces)
         hidden, d_gate_up, flipped = pl.pallas_call(
             functools.partial(hidden_kernel, [places for _, places in pieces]),
-            grid=(steps,),
-            in_specs=[row_spec, row_spec] + [whole(x.shape) for x, _ in pieces],
+            grid=(n_tensor,),
+            in_specs=[low_rows, high_rows] * 2 + [whole(x.shape) for x, _ in pieces],
             out_specs=(
-                row_block(part),
-                row_block(2 * part),
-                pl.BlockSpec((3 * part, rows_all // steps), lambda i: (0, i)),
+                pl.BlockSpec((sp_rows, part), lambda i: (i, 0)),
+                pl.BlockSpec((sp_rows, 2 * part), lambda i: (i, 0)),
+                pl.BlockSpec((3 * part, sp_rows), lambda i: (0, i)),
             ),
             out_shape=(
                 jax.ShapeDtypeStruct((rows_all, part), bf16),
@@ -891,7 +1024,7 @@
             compiler_params=params(),
             cost_estimate=SMALL,
         name="hidden",
-        )(h_two, d_ffn, *[x for x, _ in pieces])
+        )(*h_two, *d_ffn, *[x for x, _ in pieces])
         hiddens.append(hidden)
         d_gate_ups.append(d_gate_up)
         turned.append(flipped)
@@ -910,17 +1043,17 @@
         grid = width // 512
         low_spec = pl.BlockSpec((2, wide, 256), lambda j: (jnp.minimum(j, grid // 2 - 1), 0, 0))
         high_spec = pl.BlockSpec((2, wide, 256), lambda j: (jnp.maximum(j - grid // 2, 0), 0, 0))
-        block = pl.BlockSpec((rows_all, 512), lambda j: (0, j))
+        block = pl.BlockSpec((rows_all // 2, 512), lambda j: (0, j))
         halves = pl.pallas_call(
             grads_kernel,
             grid=(grid,),
-            in_specs=[block, block, whole(flipped.shape)],
+            in_specs=[block] * 4 + [whole(flipped.shape)],
             out_specs=(low_spec, high_spec),
             out_shape=[jax.ShapeDtypeStruct((count // 2, wide, 256), bf16)] * 2,
             compiler_params=params(),
             cost_estimate=SMALL,
             name="weight_grads",
-        )(h_two, d_ffn, flipped)
+        )(*h_two, *d_ffn, flipped)
         halves = split_places(halves, wide)
 
         def make(begin, end, arrived, kind):
@@ -928,16 +1061,18 @@
                 return halves[1]
             return plus(halves[0][begin:end].astype(f32), arrived, kind)
 
+        lows.append(halves[0])
         return Scatter(make), halves[1]
 
-    s_ff, sent = [], []
+    s_ff, sent, lows = [], [], []
 
     def add_grads(c):
         item, first = grads_of(after(turned[c], *link.done) if c > 2 else turned[c])
         s_ff.append(item)
         sent.append(first)
 
-    def back_sum(parts, down):
+    def back_sum(parts, down, pieces):
+        span = rows_all // pieces
         def weight_spec(x, w):
             span = x.shape[1]
             at = (w.shape[1] - span) // span if down else 0
@@ -952,44 +1087,33 @@
             grid=(steps,),
             in_specs=[row_block(x.shape[1]) for x in parts]
             + [weight_spec(x, w) for x, pieces in zip(parts, weights) for w, _ in pieces],
-            out_specs=(
-                pl.BlockSpec(
-                    (rows_all // steps, width), lambda i: (jnp.minimum(i, steps // 2 - 1), 0)
-                ),
-                pl.BlockSpec(
-                    (rows_all // steps, width), lambda i: (jnp.maximum(i - steps // 2, 0), 0)
-                ),
-            ),
-            out_shape=[jax.ShapeDtypeStruct((rows_all // 2, width), bf16)] * 2,
+            out_specs=[whole((span, width))] * pieces,
+            out_shape=[jax.ShapeDtypeStruct((span, width), bf16)] * pieces,
             compiler_params=params(),
             cost_estimate=SMALL,
             name="back_sum",
         )(*parts, *[w for pieces in weights for w, _ in pieces])
 
-    def row_sums(parts, down):
-        return TensorScatter(
-            [x.reshape(n_tensor // 2, sp_rows, width) for x in back_sum(parts, down)]
-        )
-
     hidden_part(g_ff[0], sizes[0])
     hidden_part(g_ff[1], sizes[1])
+    hidden_part(g_ff[2], sizes[2])
     add_grads(0)
     link.go(t_h_one, t_heads, g_ff[4], g_ff[5], during=[*turned, *sent])
-    h_one_all = t_h_one.stack.reshape(-1, width)
-    hidden_part(g_ff[2], sizes[2])
+    h_one_all = t_h_one.rows()
     hidden_part(g_ff[3], sizes[3])
+    hidden_part(g_ff[4], sizes[4])
     add_grads(1)
     add_grads(2)
-    link.go(t_heads, s_ff[0], g_ff[5], during=[*turned[2:], *sent[1:]])
-    hidden_part(g_ff[4], sizes[4])
+    link.go(t_heads, s_ff[0], g_ff[5], during=[*turned[3:], *sent[1:]])
     hidden_part(g_ff[5], sizes[5])
-    t_back = row_sums(d_gate_ups, False)
-    link.go(s_ff[1], s_ff[0], during=t_back.sums)
+    t_back = TensorDirect(back_sum(d_gate_ups, False, n_tensor))
+    link.go(s_ff[1], s_ff[0], during=t_back.parts)
     add_grads(3)
-    t_ffn = row_sums(hiddens, True)
-    link.go(t_back, s_ff[2], s_ff[1], s_ff[0], during=[*t_ffn.sums, *sent[3:]])
     add_grads(4)
-    link.go(t_back, t_ffn, s_ff[3], s_ff[2], s_ff[1], during=sent[4:])
+    t_ffn = TensorScatter(
+        [x.reshape(n_tensor // 2, sp_rows, width) for x in back_sum(hiddens, True, 2)]
+    )
+    link.go(t_back, s_ff[2], s_ff[1], during=[*t_ffn.sums, *sent[3:]])
     first_spec = pl.BlockSpec((1, sp_rows, width), lambda i: (0, 0, 0))
     back_terms = t_back.terms()
     d_mixed, d_attn_own, d_gain_two = pl.pallas_call(
@@ -1011,29 +1135,42 @@
     d_heads = pl.pallas_call(
         heads_back_kernel,
         grid=(n_tensor,),
-        in_specs=[whole((sp_rows, width)), both_spec],
+        in_specs=[whole((sp_rows, width)), *half_specs],
         out_specs=part_spec,
         out_shape=jax.ShapeDtypeStruct(packed, bf16),
         compiler_params=params(),
         cost_estimate=SMALL,
         name="heads_back",
-    )(d_attn_own, out_all)
-    d_query, d_low, d_high = pl.pallas_call(
-        attend_back_kernel,
-        grid=(rows, HEADS_KV),
-        in_specs=[q_spec, q_spec, limit_spec, pos_spec] + [kv_spec] * 2,
-        out_specs=[q_spec] + [kv_spec] * 2,
-        out_shape=[jax.ShapeDtypeStruct(packed, f32)]
-        + [jax.ShapeDtypeStruct((n // 2,) + packed_kv, bf16)] * 2,
-        scratch_shapes=[
-            pltpu.VMEM((SLOTS, LANES), bf16),
-            pltpu.VMEM((LANES, SLOTS), bf16),
-            pltpu.VMEM((SLOTS, LANES), f32),
-        ],
-        compiler_params=params(2),
-        cost_estimate=SMALL,
-        name="attend_back",
-    )(queries, d_heads, limit, key_pos, *kv_halves)
+    )(d_attn_own, *t_out.halves)
+    def attend_back(first, count, grads, *held):
+        shift = lambda spec: pl.BlockSpec(
+            spec.block_shape, lambda i, h: spec.index_map(i, h + first)
+        )
+        q_part, kv_part = shift(q_spec), shift(kv_spec)
+        return pl.pallas_call(
+            attend_back_kernel,
+            grid=(rows, count),
+            in_specs=[q_part, q_part, limit_spec, pos_spec]
+            + [kv_part] * 2
+            + [pl.BlockSpec(memory_space=pl.ANY)] * len(held),
+            out_specs=[q_part] + [kv_part] * 2,
+            out_shape=[jax.ShapeDtypeStruct(packed, f32)]
+            + [jax.ShapeDtypeStruct((n // 2,) + packed_kv, bf16)] * 2,
+            scratch_shapes=[
+                pltpu.VMEM((SLOTS, LANES), bf16),
+                pltpu.VMEM((LANES, SLOTS), bf16),
+                pltpu.VMEM((SLOTS, LANES), f32),
+            ],
+            input_output_aliases={6 + i: i for i in range(len(held))},
+            compiler_params=params(2),
+            cost_estimate=SMALL,
+            name="attend_back",
+        )(queries, grads, limit, key_pos, *kv_halves, *held)
+
+    held = attend_back(0, 3, d_heads)
+    t_attn = TensorGather(d_attn_own)
+    link.go(t_ffn, s_ff[3], s_ff[2], s_ff[0], s_ff[1], during=held)
+    d_query, d_low, d_high = attend_back(3, HEADS_KV - 3, after(d_heads, *link.done), *held)
 
     def key_grads(begin, end, arrived, kind):
         if begin >= n // 2:
@@ -1041,7 +1178,6 @@
         return plus(d_low[begin:end].astype(f32), arrived, kind)
 
     s_keys = Scatter(key_grads)
-    t_attn = TensorGather(d_attn_own)
     d_q_low, d_q_gain = pl.pallas_call(
         query_back_kernel,
         grid=(n_tensor,),
@@ -1059,20 +1195,22 @@
     def product(left, right):
         wide = right.shape[1]
         count = width // 256
+        grid = width // 512
         halves = pl.pallas_call(
             product_kernel,
-            grid=(count,),
-            in_specs=[pl.BlockSpec((rows_all, 256), lambda j: (0, j)), whole(right.shape)],
+            grid=(grid,),
+            in_specs=[pl.BlockSpec((rows_all // 2, 512), lambda j: (0, j))] * 2
+            + [whole(right.shape)],
             out_specs=(
-                pl.BlockSpec((1, wide, 256), lambda j: (jnp.minimum(j, count // 2 - 1), 0, 0)),
-                pl.BlockSpec((1, wide, 256), lambda j: (jnp.maximum(j - count // 2, 0), 0, 0)),
+                pl.BlockSpec((2, wide, 256), lambda j: (jnp.minimum(j, grid // 2 - 1), 0, 0)),
+                pl.BlockSpec((2, wide, 256), lambda j: (jnp.maximum(j - grid // 2, 0), 0, 0)),
             ),
             out_shape=[jax.ShapeDtypeStruct((count // 2, wide, 256), bf16)] * 2,
             scratch_shapes=[pltpu.VMEM((wide, rows_all), bf16)],
             compiler_params=params(),
             cost_estimate=SMALL,
             name="product",
-        )(left, right)
+        )(*left, right)
         return split_places(halves, wide)
 
     def sum_of(halves):
@@ -1084,9 +1222,9 @@
         return Scatter(make)
 
     t_query_back = TensorExchange(d_q_low)
-    link.go(t_ffn, s_ff[4], s_ff[3], s_ff[2], during=[d_query])
+    link.go(t_attn, s_ff[4], s_ff[3], s_ff[2], during=[d_q_low])
     add_grads(5)
-    link.go(t_attn, t_query_back, s_keys, s_ff[4], s_ff[3], during=[d_q_low, sent[5]])
+    link.go(t_attn, t_query_back, s_keys, s_ff[4], t_ffn, during=[sent[5]])
     ffn_terms = t_ffn.terms()
     outputs = pl.pallas_call(
         functools.partial(finish_kernel, tuple(order)),
@@ -1098,11 +1236,12 @@
         cost_estimate=SMALL,
         name="finish",
     )(index, mixed, live, *ffn_terms)
-    link.go(t_attn, t_query_back, s_keys, s_ff[5], s_ff[4], during=[outputs])
-    d_attn = t_attn.stack.reshape(-1, width)
-    s_out = sum_of(product(d_attn, t_heads.rows()))
+    d_attn = t_attn.rows()
+    out_halves = product(d_attn, t_heads.rows())
+    link.go(t_query_back, s_keys, s_ff[5], s_ff[3], s_ff[4], during=[*out_halves, outputs])
+    s_out = sum_of(out_halves)
     s_query = sum_of(product(h_one_all, t_query_back.rows()))
-    link.go(s_keys, s_out, s_query, s_ff[5])
+    link.go(s_keys, s_out, s_ff[5], during=[s_query.value()])
     d_kv = s_keys.result()
     d_kv_low, d_k_gain = pl.pallas_call(
         key_back_kernel,
@@ -1143,7 +1282,32 @@
         cost_estimate=SMALL,
         name="h_one_back",
     )(d_q_low, query_all, d_kv_low, kv_all, inputs, gain_one[None], d_mixed)
-    link.go(t_kv_back, s_out, during=[grad_rel])
+    def collect(first, last, *held):
+        terms = [[lows[c], *s_ff[c].raw] for c in range(first, last)]
+        flat = [x for group in terms for x in group]
+        if not held:
+            flat[0] = after(flat[0], *link.done)
+        return pl.pallas_call(
+            functools.partial(collect_kernel, len(terms), len(terms[0])),
+            grid=(len(terms),),
+            in_specs=[pl.BlockSpec((1,) + x.shape[1:], lambda i: (0, 0, 0)) for x in flat]
+            + [pl.BlockSpec(memory_space=pl.ANY)] * len(held),
+            out_specs=(
+                pl.BlockSpec((cols, 2, unit), lambda i: (0, 0, first + i)),
+                pl.BlockSpec((unit, cols), lambda i: (first + i, 0)),
+            ),
+            out_shape=(
+                jax.ShapeDtypeStruct((cols, 2, ff), f32),
+                jax.ShapeDtypeStruct((ff, cols), f32),
+            ),
+            input_output_aliases={len(flat) + i: i for i in range(len(held))},
+            compiler_params=params(),
+            cost_estimate=SMALL,
+            name="collect",
+        )(*flat, *held)
+
+    early_sums = collect(0, FF_LAST)
+    link.go(t_kv_back, s_out, s_query, during=[grad_rel, *early_sums])
     grad_inputs = call(
         functools.partial(leave_kernel, tuple(order)),
         low_square,
@@ -1161,40 +1325,36 @@
     small_parts = jnp.concatenate([gain_parts, head_parts], axis=1)
     kv_halves_back = product(h_one_all, t_kv_back.rows())
 
-    def kv_grads(begin, end, arrived, kind):
-        side = begin // (n // 2)
-        own = kv_halves_back[side][begin - side * n // 2 : end - side * n // 2]
-        own = jnp.concatenate([own.astype(f32), small_parts[begin:end]], axis=1)
-        return plus(own, arrived, kind)
-
-    s_kv = Scatter(kv_grads)
+    def with_small(side):
+        begin = side * n // 2
+        small_here = small_parts[begin : begin + n // 2].astype(bf16)
+        return jnp.concatenate([kv_halves_back[side], small_here], axis=1)
+
+    s_kv = ScatterSoon(with_small(0), with_small(1))
     link.go(s_kv, s_query, s_out, s_ff[5])
-    link.go(s_kv, s_query)
-    link.go(s_kv)
-    sum_kv = s_kv.result()
-    t_small = TensorGather(sum_kv[kv_part:])
-    t_sums = TensorGather(sum_kv[:kv_part].astype(bf16))
-    link.go(t_small, t_sums)
-    link.go(t_small, t_sums)
-    small = jnp.sum(t_small.stack, axis=0)
+    sum_in, sum_down = collect(FF_LAST, len(sizes), *early_sums)
+    link.go(s_kv, s_query, during=[sum_in, sum_down])
+    t_sums = TensorAll(s_kv.result().astype(bf16))
+    link.go(t_sums)
+    stack = t_sums.stack
+    small = jnp.sum(stack[:, kv_part:].astype(f32), axis=0)
+    stack = stack[:, :kv_part]
     sum_gains = small[:2]
     sum_heads = small[2:].reshape(-1)[: 2 * HEAD].reshape(2, HEAD)
-    stack = t_sums.stack
-    places = jnp.argsort(tensor ^ jnp.array(tensor_order, jnp.int32))
+    inverse = jnp.array([tensor_order.index(i) for i in range(n_tensor)], jnp.int32)
+    places = [
+        lax.dynamic_index_in_dim(inverse, tensor ^ i, axis=0, keepdims=False)
+        for i in range(n_tensor)
+    ]
     sum_kv = jnp.concatenate(
         [
             lax.dynamic_index_in_dim(stack, places[i], axis=0, keepdims=False)
             for i in range(n_tensor)
         ],
         axis=0,
-    ).T
+    ).T.astype(f32)
     sum_out = s_out.result()
     sum_query = s_query.result().T
-    sums = [s.result() for s in s_ff]
-    sum_in = jnp.concatenate(
-        [x[: 2 * part].reshape(2, part, cols) for part, x in zip(sizes, sums)], axis=1
-    ).transpose(2, 0, 1)
-    sum_down = jnp.concatenate([x[2 * part :] for part, x in zip(sizes, sums)], axis=0)
     return (
         outputs,
         grad_inputs,

time: 817 us -> 792 us (0.969)
  other arithmetic: 104 us -> 65.4 us
  local copies, waits for them, and re-layouts: 82.7 us -> 57.4 us
  waiting for transfers between devices: 278 us -> 299 us
  Pallas kernels: 245 us -> 259 us
    ppermute x92 -> x94, waiting for transfers between devices: 278 us -> 299 us  [swap(): return lax.ppermute(value, axis, [(i, i ^ mask) for i in range(size)])]
    concatenate x34 -> x25, other arithmetic: 39.3 us -> 19.9 us  [join(): both = jnp.concatenate([first, second], axis=0)]
    unnamed x336 -> x310, local copies, waits for them, and re-layouts: 56.5 us -> 45.1 us
    add x7 -> x1, other arithmetic: 9.02 us -> 0.07 us  [value(): self.total = self.low.astype(f32) + self.first.astype(f32)]
    reshape x6 -> x0, local copies, waits for them, and re-layouts: 8.57 us -> none  [local(): x[:2 * part].reshape(2, part, cols)]
    convert_element_type x22 -> x19, other arithmetic: 37.6 us -> 29.3 us  [plus(): return total.astype(kind)]
    pallas_call x12 -> x14, Pallas kernels: 100 us -> 105 us  [the longest x6 43.1 us: grads_of(): pl.pallas_call(grads_kernel, grid=(grid,), in_specs=[block] * 4 + [whole(...]
    ppermute x92 -> x94, starting transfers between devices: 87.5 us -> 89.1 us  [swap(): return lax.ppermute(value, axis, [(i, i ^ mask) for i in range(size)])]
  transfers between devices with their start and end apart: 92 -> 94, of which waited for: 38 -> 36; matrix products, arithmetic and copies ran while one was open for 18% -> 10% of each run, Pallas kernels for 30% -> 33%
where the time goes in v4:
time: 792 us; the launch traced here: 781 us
  waiting for transfers between devices  299 us (38%)
  Pallas kernels  259 us (33%)
  starting transfers between devices  89.1 us (11%)
  other arithmetic  65.4 us (8%)
  local copies, waits for them, and re-layouts  57.4 us (7%)
  between operations  10.7 us (1%)
    ppermute x94, waiting for transfers between devices, swap(): return lax.ppermute(value, axis, [(i, i ^ mask) for i in range(size)])  299 us
    ppermute x94, starting transfers between devices, swap(): return lax.ppermute(value, axis, [(i, i ^ mask) for i in range(size)])  89.1 us
    pallas_call x6, Pallas kernels, hidden_part(): pl.pallas_call(functools.partial(hidden_kernel, [places for _, places in...  49 us
    unnamed x310, local copies, waits for them, and re-layouts  45.1 us
    pallas_call x6, Pallas kernels, grads_of(): pl.pallas_call(grads_kernel, grid=(grid,), in_specs=[block] * 4 + [whole(...  43.1 us
    pallas_call x2, Pallas kernels, back_sum(): pl.pallas_call(functools.partial(back_sum_kernel, [[places for _, places...  33 us
    pallas_call x2, Pallas kernels, attend_back(): pl.pallas_call(attend_back_kernel, grid=(rows, count), in_specs=[q_part,...  32.9 us
    convert_element_type x19, other arithmetic, plus(): return total.astype(kind)  29.3 us
  transfers between devices with their start and end apart: 94, of which 36 were waited for; matrix products, arithmetic and copies ran while one was open for 10% of the time, Pallas kernels for 33%

profile of v4, /device:TPU:0, one launch (start us, length us, event | category | flops | bytes accessed | tf_op | source)
XLA Modules:
  0.0 781.0 jit_solution(8297663935939782887)
XLA Ops:
  41.3 13.5 %collective-permute-done.5 = bf16[2,2,256]{2,1,0:T(2,128)(2,1)S(1)} collective-permute-done((bf16[2,2,256]{2,1,0:T(2,128)(2,1)S(1)}, bf16[2,2,256]{2,1,0:T(2,128)(2,1)S(1)}, u32[]{:S(2)}, u32[]{:S(2)}) %collective-permute-start.5) | collective-permute-done | bytes 2080 | tf_op jit(solution)/shard_map/ppermute | solution.py:53
  60.9 13.5 %collective-permute-done.10 = bf16[4,2,256]{2,1,0:T(2,128)(2,1)S(1)} collective-permute-done((bf16[4,2,256]{2,1,0:T(2,128)(2,1)S(1)}, bf16[4,2,256]{2,1,0:T(2,128)(2,1)S(1)}, u32[]{:S(2)}, u32[]{:S(2)}) %collective-permute-start.10) | collective-permute-done | bytes 4128 | tf_op jit(solution)/shard_map/ppermute | solution.py:53
  88.6 18.4 %collective-permute-done.14 = bf16[1,8,320,256]{3,2,1,0:T(8,128)(2,1)S(1)} collective-permute-done((bf16[1,8,320,256]{3,2,1,0:T(8,128)(2,1)S(1)}, bf16[1,8,320,256]{3,2,1,0:T(8,128)(2,1)S(1)}, u32[]{:S(2)}, u32[]{:S(2)}) %collective-permute-start.14) | collective-permute-done | bytes 1310752 | tf_op jit(solution)/shard_map/ppermute | solution.py:53
  107.3 10.0 %collective-permute-done.17 = bf16[2,256,768]{2,1,0:T(8,128)(2,1)} collective-permute-done((bf16[2,256,768]{2,1,0:T(8,128)(2,1)S(1)}, bf16[2,256,768]{2,1,0:T(8,128)(2,1)}, u32[]{:S(2)}, u32[]{:S(2)}) %collective-permute-start.17) | collective-permute-done | bytes 786464 | tf_op jit(solution)/shard_map/ppermute | solution.py:53
  122.2 28.5 %collective-permute-done.21 = bf16[1,8,320,256]{3,2,1,0:T(8,128)(2,1)S(1)} collective-permute-done((bf16[1,8,320,256]{3,2,1,0:T(8,128)(2,1)S(1)}, bf16[1,8,320,256]{3,2,1,0:T(8,128)(2,1)S(1)}, u32[]{:S(2)}, u32[]{:S(2)}) %collective-permute-start.21) | collective-permute-done | bytes 1310752 | tf_op jit(solution)/shard_map/ppermute | solution.py:53
  167.3 12.7 %query.1 = (f32[4,256,320]{2,1,0:T(8,128)S(1)}, bf16[1,5,4,4,64,128]{5,4,3,2,1,0:T(8,128)(2,1)S(1)}) custom-call(bf16[256,2048]{1,0:T(8,128)(2,1)S(1)} %copy-done.17, bf16[4,8,320,256]{3,2,1,0:T(8,128)(2,1)} %copy-done.127, f32[256,64]{1,0:T(8,128)S(1)} %get-tuple-element.503.cos_ref, f32[256,64]{1,0:T(8,128)S(1)} %get-tuple-element.504.sin_ref, ...), custom_call_target="tpu_custom_call" | custom-call | flops 1000 | bytes 1000 | tf_op jit(solution)/shard_map/query/pallas_call | solution.py:922
  185.4 10.0 %collective-permute-done.27 = bf16[2,256,768]{2,1,0:T(8,128)(2,1)} collective-permute-done((bf16[2,256,768]{2,1,0:T(8,128)(2,1)}, bf16[2,256,768]{2,1,0:T(8,128)(2,1)}, u32[]{:S(2)}, u32[]{:S(2)}) %collective-permute-start.27) | collective-permute-done | bytes 786464 | tf_op jit(solution)/shard_map/ppermute | solution.py:53
  216.2 18.8 %attend.1.o_ref = bf16[1,5,4,4,64,128]{5,4,3,2,1,0:T(8,128)(2,1)S(1)} custom-call(bf16[1,5,4,4,64,128]{5,4,3,2,1,0:T(8,128)(2,1)S(1)} %copy-done.12, s32[1,4,1,256]{3,2,1,0:T(1,128)S(1)} %copy-done.112, s32[1,2048,1]{2,1,0:T(8,128)S(1)} %copy-done.9, bf16[4,1,5,4,64,128]{5,4,3,2,1,0:T(8,128)(2,1)} %pad_maximum_fusion.13.low_ref, ...), custom_call_target="tpu_custom_call" | custom-call | flops 1000 | bytes 1000 | tf_op jit(solution)/shard_map/attend/pallas_call | solution.py:953
  235.0 7.8 %out.1 = (f32[256,2048]{1,0:T(8,128)}, bf16[256,2048]{1,0:T(8,128)(2,1)S(1)}, bf16[4,256,320]{2,1,0:T(8,128)(2,1)S(1)}) custom-call(bf16[1,5,4,4,64,128]{5,4,3,2,1,0:T(8,128)(2,1)S(1)} %attend.1.o_ref, bf16[2,8,320,256]{3,2,1,0:T(8,128)(2,1)} %pad_maximum_fusion.2.w_low, bf16[2,8,320,256]{3,2,1,0:T(8,128)(2,1)} %collective-permute-done.25.w_high, ...), custom_call_target="tpu_custom_call" | custom-call | flops 1000 | bytes 1000 | tf_op jit(solution)/shard_map/out/pallas_call | solution.py:968
  249.7 20.2 %collective-permute-done.33 = bf16[1,256,2048]{2,1,0:T(8,128)(2,1)S(1)} collective-permute-done((bf16[1,256,2048]{2,1,0:T(8,128)(2,1)S(1)}, bf16[1,256,2048]{2,1,0:T(8,128)(2,1)S(1)}, u32[]{:S(2)}, u32[]{:S(2)}) %collective-permute-start.33) | collective-permute-done | bytes 1048608 | tf_op jit(solution)/shard_map/ppermute | solution.py:53
  272.8 11.2 %collective-permute-done.35 = bf16[2,256,768]{2,1,0:T(8,128)(2,1)S(1)} collective-permute-done((bf16[2,256,768]{2,1,0:T(8,128)(2,1)S(1)}, bf16[2,256,768]{2,1,0:T(8,128)(2,1)S(1)}, u32[]{:S(2)}, u32[]{:S(2)}) %collective-permute-start.35) | collective-permute-done | bytes 786464 | tf_op jit(solution)/shard_map/ppermute | solution.py:53
  289.8 22.4 %collective-permute-done.40 = bf16[1,256,2048]{2,1,0:T(8,128)(2,1)S(1)} collective-permute-done((bf16[1,256,2048]{2,1,0:T(8,128)(2,1)S(1)}, bf16[1,256,2048]{2,1,0:T(8,128)(2,1)S(1)}, u32[]{:S(2)}, u32[]{:S(2)}) %collective-permute-start.40) | collective-permute-done | bytes 1048608 | tf_op jit(solution)/shard_map/ppermute | solution.py:53
  312.4 11.5 %collective-permute-done.39 = bf16[2,256,768]{2,1,0:T(8,128)(2,1)S(1)} collective-permute-done((bf16[2,256,768]{2,1,0:T(8,128)(2,1)S(1)}, bf16[2,256,768]{2,1,0:T(8,128)(2,1)S(1)}, u32[]{:S(2)}, u32[]{:S(2)}) %collective-permute-start.39) | collective-permute-done | bytes 786464 | tf_op jit(solution)/shard_map/ppermute | solution.py:53
  329.2 7.8 %hidden.6 = (bf16[1024,256]{1,0:T(8,128)(2,1)S(1)}, bf16[1024,512]{1,0:T(8,128)(2,1)S(1)}, bf16[768,1024]{1,0:T(8,128)(2,1)S(1)}) custom-call(bf16[512,2048]{1,0:T(8,128)(2,1)} %bitcast.206, bf16[512,2048]{1,0:T(8,128)(2,1)} %bitcast.218, bf16[512,2048]{1,0:T(8,128)(2,1)} %bitcast.29.d_low, bf16[512,2048]{1,0:T(8,128)(2,1)} %bitcast.30.d_high, ...), custom_call_target="tpu_custom_call" | custom-call | flops 1000 | bytes 1000 | tf_op jit(solution)/shard_map/hidden/pallas_call | solution.py:1010
  347.2 8.2 %hidden.8 = (bf16[1024,256]{1,0:T(8,128)(2,1)S(1)}, bf16[1024,512]{1,0:T(8,128)(2,1)S(1)}, bf16[768,1024]{1,0:T(8,128)(2,1)S(1)}) custom-call(bf16[512,2048]{1,0:T(8,128)(2,1)} %bitcast.208, bf16[512,2048]{1,0:T(8,128)(2,1)} %bitcast.220, bf16[512,2048]{1,0:T(8,128)(2,1)} %bitcast.29.d_low, bf16[512,2048]{1,0:T(8,128)(2,1)} %bitcast.30.d_high, ...), custom_call_target="tpu_custom_call" | custom-call | flops 1000 | bytes 1000 | tf_op jit(solution)/shard_map/hidden/pallas_call | solution.py:1010
  356.6 8.8 %hidden.7 = (bf16[1024,256]{1,0:T(8,128)(2,1)S(1)}, bf16[1024,512]{1,0:T(8,128)(2,1)S(1)}, bf16[768,1024]{1,0:T(8,128)(2,1)S(1)}) custom-call(bf16[512,2048]{1,0:T(8,128)(2,1)} %bitcast.209, bf16[512,2048]{1,0:T(8,128)(2,1)} %bitcast.221, bf16[512,2048]{1,0:T(8,128)(2,1)} %bitcast.29.d_low, bf16[512,2048]{1,0:T(8,128)(2,1)} %bitcast.30.d_high, ...), custom_call_target="tpu_custom_call" | custom-call | flops 1000 | bytes 1000 | tf_op jit(solution)/shard_map/hidden/pallas_call | solution.py:1010
  390.4 7.8 hidden.9
  399.2 8.4 %hidden.10 = (bf16[1024,256]{1,0:T(8,128)(2,1)S(1)}, bf16[1024,512]{1,0:T(8,128)(2,1)S(1)}, bf16[768,1024]{1,0:T(8,128)(2,1)S(1)}) custom-call(bf16[512,2048]{1,0:T(8,128)(2,1)} %bitcast.213, bf16[512,2048]{1,0:T(8,128)(2,1)} %bitcast.225, bf16[512,2048]{1,0:T(8,128)(2,1)} %bitcast.29.d_low, bf16[512,2048]{1,0:T(8,128)(2,1)} %bitcast.30.d_high, ...), custom_call_target="tpu_custom_call" | custom-call | flops 1000 | bytes 1000 | tf_op jit(solution)/shard_map/hidden/pallas_call | solution.py:1010
  411.6 8.0 %hidden.11 = (bf16[1024,256]{1,0:T(8,128)(2,1)S(1)}, bf16[1024,512]{1,0:T(8,128)(2,1)S(1)}, bf16[768,1024]{1,0:T(8,128)(2,1)}) custom-call(bf16[512,2048]{1,0:T(8,128)(2,1)} %bitcast.214, bf16[512,2048]{1,0:T(8,128)(2,1)} %bitcast.226, bf16[512,2048]{1,0:T(8,128)(2,1)} %bitcast.29.d_low, bf16[512,2048]{1,0:T(8,128)(2,1)} %bitcast.30.d_high, ...), custom_call_target="tpu_custom_call" | custom-call | flops 1000 | bytes 1000 | tf_op jit(solution)/shard_map/hidden/pallas_call | solution.py:1010
  421.8 20.9 %back_sum.3 = (bf16[256,2048]{1,0:T(8,128)(2,1)S(1)}, bf16[256,2048]{1,0:T(8,128)(2,1)}, bf16[256,2048]{1,0:T(8,128)(2,1)}, bf16[256,2048]{1,0:T(8,128)(2,1)}) custom-call(bf16[1024,512]{1,0:T(8,128)(2,1)} %copy-done.70, bf16[1024,512]{1,0:T(8,128)(2,1)} %copy-done.72, bf16[1024,512]{1,0:T(8,128)(2,1)} %copy-done.71, bf16[1024,512]{1,0:T(8,128)(2,1)} %copy-done.73, ...), custom_call_target="tpu_custom_call" | custom-call | flops 1000 | bytes 1000 | tf_op jit(solution)/shard_map/back_sum/pallas_call | solution.py:1083
  452.8 12.1 %back_sum.2 = (bf16[512,2048]{1,0:T(8,128)(2,1)}, bf16[512,2048]{1,0:T(8,128)(2,1)}) custom-call(bf16[1024,256]{1,0:T(8,128)(2,1)S(1)} %copy-done.90, bf16[1024,256]{1,0:T(8,128)(2,1)S(1)} %copy-done.94, bf16[1024,256]{1,0:T(8,128)(2,1)S(1)} %copy-done.92, bf16[1024,256]{1,0:T(8,128)(2,1)S(1)} %get-tuple-element.286.refs_3_, ...), custom_call_target="tpu_custom_call" | custom-call | flops 1000 | bytes 1000 | tf_op jit(solution)/shard_map/back_sum/pallas_call | solution.py:1083
  473.8 7.6 weight_grads.10
  481.5 7.5 collective-permute-done.55.refs_6_
  517.5 19.2 %attend_back.2 = (f32[1,5,4,4,64,128]{5,4,3,2,1,0:T(8,128)}, bf16[4,1,5,4,64,128]{5,4,3,2,1,0:T(8,128)(2,1)S(1)}, bf16[4,1,5,4,64,128]{5,4,3,2,1,0:T(8,128)(2,1)S(1)}) custom-call(bf16[1,5,4,4,64,128]{5,4,3,2,1,0:T(8,128)(2,1)S(1)} %copy-done.13, bf16[1,5,4,4,64,128]{5,4,3,2,1,0:T(8,128)(2,1)} %copy-done.14, s32[1,4,1,256]{3,2,1,0:T(1,128)S(1)} %copy-done.113, ...), custom_call_target="tpu_custom_call" | custom-call | flops 1000 | bytes 1000 | tf_op jit(solution)/shard_map/attend_back/pallas_call | solution.py:1150
  545.5 13.7 %attend_back.3 = (f32[1,5,4,4,64,128]{5,4,3,2,1,0:T(8,128)}, bf16[4,1,5,4,64,128]{5,4,3,2,1,0:T(8,128)(2,1)S(1)}, bf16[4,1,5,4,64,128]{5,4,3,2,1,0:T(8,128)(2,1)S(1)}) custom-call(bf16[1,5,4,4,64,128]{5,4,3,2,1,0:T(8,128)(2,1)S(1)} %copy-done.13, ...), custom_call_target="tpu_custom_call", output_to_operand_aliasing={{0}: (6, {}), {1}: (7, {}), {2}: (8, {})} | custom-call | flops 1000 | bytes 1000 | tf_op jit(solution)/shard_map/attend_back/pallas_call | solution.py:1150
  568.9 8.4 %collective-permute-done.63.refs_14_ = bf16[2,768,256]{2,1,0:T(8,128)(2,1)} collective-permute-done((bf16[2,768,256]{2,1,0:T(8,128)(2,1)}, bf16[2,768,256]{2,1,0:T(8,128)(2,1)}, u32[]{:S(2)}, u32[]{:S(2)}) %collective-permute-start.63) | collective-permute-done | bytes 786464 | tf_op jit(solution)/shard_map/ppermute | solution.py:53
  594.4 21.9 %collective-permute-done.68 = bf16[2,1,256,320]{3,2,0,1:T(8,128)(2,1)S(1)} collective-permute-done((bf16[2,1,256,320]{3,2,0,1:T(8,128)(2,1)S(1)}, bf16[2,1,256,320]{3,2,0,1:T(8,128)(2,1)S(1)}, u32[]{:S(2)}, u32[]{:S(2)}) %collective-permute-start.68) | collective-permute-done | bytes 327712 | tf_op jit(solution)/shard_map/ppermute | solution.py:53
  654.2 9.8 %collective-permute-done.74.refs_19_ = bf16[1,768,256]{2,1,0:T(8,128)(2,1)} collective-permute-done((bf16[1,768,256]{2,1,0:T(8,128)(2,1)}, bf16[1,768,256]{2,1,0:T(8,128)(2,1)}, u32[]{:S(2)}, u32[]{:S(2)}) %collective-permute-start.74) | collective-permute-done | bytes 393248 | tf_op jit(solution)/shard_map/ppermute | solution.py:53
  679.9 8.5 %h_one_back.1 = (bf16[256,2048]{1,0:T(8,128)(2,1)S(1)}, f32[1,2048]{1,0:T(1,128)S(1)}) custom-call(bf16[4,256,320]{2,1,0:T(8,128)(2,1)S(1)} %copy-done.45, bf16[4,8,320,256]{3,2,1,0:T(8,128)(2,1)} %copy-done.127, bf16[256,640]{1,0:T(8,128)(2,1)S(1)} %get-tuple-element.408.dkv_ref, bf16[2048,640]{1,0:T(8,128)(2,1)} %bitcast.160, ...), custom_call_target="tpu_custom_call" | custom-call | flops 1000 | bytes 1000 | tf_op jit(solution)/shard_map/h_one_back/pallas_call | solution.py:1263
  690.3 19.8 %collective-permute-done.77.refs_2_ = bf16[2,768,256]{2,1,0:T(8,128)(2,1)} collective-permute-done((bf16[2,768,256]{2,1,0:T(8,128)(2,1)}, bf16[2,768,256]{2,1,0:T(8,128)(2,1)}, u32[]{:S(2)}, u32[]{:S(2)}) %collective-permute-start.77) | collective-permute-done | bytes 786464 | tf_op jit(solution)/shard_map/ppermute | solution.py:53
  727.0 10.6 %collective-permute-done.82 = bf16[2,320,256]{2,1,0:T(8,128)(2,1)S(1)} collective-permute-done((bf16[2,320,256]{2,1,0:T(8,128)(2,1)S(1)}, bf16[2,320,256]{2,1,0:T(8,128)(2,1)S(1)}, u32[]{:S(2)}, u32[]{:S(2)}) %collective-permute-start.82) | collective-permute-done | bytes 327712 | tf_op jit(solution)/shard_map/ppermute | solution.py:53
  749.1 8.3 %collective-permute-done.83 = bf16[2,320,256]{2,1,0:T(8,128)(2,1)S(1)} collective-permute-done((bf16[2,320,256]{2,1,0:T(8,128)(2,1)S(1)}, bf16[2,320,256]{2,1,0:T(8,128)(2,1)S(1)}, u32[]{:S(2)}, u32[]{:S(2)}) %collective-permute-start.83) | collective-permute-done | bytes 327712 | tf_op jit(solution)/shard_map/ppermute | solution.py:53
  (622 shorter events, 354.5 us)
Async XLA Ops:
  117.3 38.2 %collective-permute-start.19 = (bf16[2,8,320,256]{3,2,1,0:T(8,128)(2,1)S(1)}, bf16[2,8,320,256]{3,2,1,0:T(8,128)(2,1)S(1)}, u32[]{:S(2)}, u32[]{:S(2)}) collective-permute-start(bf16[2,8,320,256]{3,2,1,0:T(8,128)(2,1)S(1)} %pad_maximum_fusion), channel_id=1, source_target_pairs={{0,1},{1,0},{2,3},{3,2},{4,5},{5,4},{6,7},{7,6},{8,9},{9,8},{10,11... | collective-permute-start | bytes 7864328 | tf_op jit(solution)/shard_map/ppermute | solution.py:53
  118.6 36.9 %collective-permute-start.22 = (bf16[4,256,768]{2,1,0:T(8,128)(2,1)S(1)}, bf16[4,256,768]{2,1,0:T(8,128)(2,1)S(1)}, u32[]{:S(2)}, u32[]{:S(2)}) collective-permute-start(bf16[4,256,768]{2,1,0:T(8,128)(2,1)S(1)} %pad_maximum_fusion.7), channel_id=1, source_target_pairs={{0,4},{4,0},{8,12},{12,8},{16,20},{20,16},{24,28},{28,24},{1,5},{5... | collective-permute-start | bytes 4718600 | tf_op jit(solution)/shard_map/ppermute | solution.py:53
  155.5 43.0 %collective-permute-start.25 = (bf16[2,8,320,256]{3,2,1,0:T(8,128)(2,1)}, bf16[2,8,320,256]{3,2,1,0:T(8,128)(2,1)}, u32[]{:S(2)}, u32[]{:S(2)}) collective-permute-start(bf16[2,8,320,256]{3,2,1,0:T(8,128)(2,1)} %pad_maximum_fusion.2.w_low), channel_id=1, source_target_pairs={{0,1},{1,0},{2,3},{3,2},{4,5},{5,4},{6,7},{7,6},{8,9},{9,8},{10,11... | collective-permute-start | bytes 7864328 | tf_op jit(solution)/shard_map/ppermute | solution.py:53
  155.6 39.8 %collective-permute-start.26 = (bf16[1,256,2048]{2,1,0:T(8,128)(2,1)}, bf16[1,256,2048]{2,1,0:T(8,128)(2,1)}, u32[]{:S(2)}, u32[]{:S(2)}) collective-permute-start(bf16[1,256,2048]{2,1,0:T(8,128)(2,1)} %bitcast.23), channel_id=1, source_target_pairs={{0,2},{1,3},{2,0},{3,1},{4,6},{5,7},{6,4},{7,5},{8,10},{9,11},{10,... | collective-permute-start | bytes 3145736 | tf_op jit(solution)/shard_map/ppermute | solution.py:53
  157.9 40.6 %collective-permute-start.24 = (bf16[4,1,5,4,64,128]{5,4,3,2,1,0:T(8,128)(2,1)}, bf16[4,1,5,4,64,128]{5,4,3,2,1,0:T(8,128)(2,1)}, u32[]{:S(2)}, u32[]{:S(2)}) collective-permute-start(bf16[4,1,5,4,64,128]{5,4,3,2,1,0:T(8,128)(2,1)} %pad_maximum_fusion.13.low_ref), channel_id=1, source_target_pairs={{0,4},{4,0},{8,12},{12,8},{16,20},{20,16},{24,28},{28,24},{1,5},{5... | collective-permute-start | bytes 3932168 | tf_op jit(solution)/shard_map/ppermute | solution.py:53
  198.5 46.0 %collective-permute-start.29 = (bf16[2,256,2048]{2,1,0:T(8,128)(2,1)}, bf16[2,256,2048]{2,1,0:T(8,128)(2,1)}, u32[]{:S(2)}, u32[]{:S(2)}) collective-permute-start(bf16[2,256,2048]{2,1,0:T(8,128)(2,1)} %pad_maximum_fusion.3), channel_id=1, source_target_pairs={{0,1},{1,0},{2,3},{3,2},{4,5},{5,4},{6,7},{7,6},{8,9},{9,8},{10,11... | collective-permute-start | bytes 6291464 | tf_op jit(solution)/shard_map/ppermute | solution.py:53
  201.2 43.2 %collective-permute-start.30 = (bf16[4,256,768]{2,1,0:T(8,128)(2,1)}, bf16[4,256,768]{2,1,0:T(8,128)(2,1)}, u32[]{:S(2)}, u32[]{:S(2)}) collective-permute-start(bf16[4,256,768]{2,1,0:T(8,128)(2,1)} %pad_maximum_fusion.8), channel_id=1, source_target_pairs={{0,4},{4,0},{8,12},{12,8},{16,20},{20,16},{24,28},{28,24},{1,5},{5... | collective-permute-start | bytes 4718600 | tf_op jit(solution)/shard_map/ppermute | solution.py:53
  204.4 38.5 %collective-permute-start.31 = (bf16[2,256,768]{2,1,0:T(8,128)(2,1)}, bf16[2,256,768]{2,1,0:T(8,128)(2,1)}, u32[]{:S(2)}, u32[]{:S(2)}) collective-permute-start(bf16[2,256,768]{2,1,0:T(8,128)(2,1)} %pad_maximum_fusion.18), channel_id=1, source_target_pairs={{0,16},{4,20},{8,24},{12,28},{16,0},{20,4},{24,8},{28,12},{1,17},{... | collective-permute-start | bytes 2359304 | tf_op jit(solution)/shard_map/ppermute | solution.py:53
  244.5 39.5 %collective-permute-start.34 = (bf16[4,256,768]{2,1,0:T(8,128)(2,1)S(1)}, bf16[4,256,768]{2,1,0:T(8,128)(2,1)S(1)}, u32[]{:S(2)}, u32[]{:S(2)}) collective-permute-start(bf16[4,256,768]{2,1,0:T(8,128)(2,1)S(1)} %pad_maximum_fusion.9), channel_id=1, source_target_pairs={{0,4},{4,0},{8,12},{12,8},{16,20},{20,16},{24,28},{28,24},{1,5},{5... | collective-permute-start | bytes 4718600 | tf_op jit(solution)/shard_map/ppermute | solution.py:53
  285.1 39.0 %collective-permute-start.37 = (bf16[2,256,2048]{2,1,0:T(8,128)(2,1)S(1)}, bf16[2,256,2048]{2,1,0:T(8,128)(2,1)S(1)}, u32[]{:S(2)}, u32[]{:S(2)}) collective-permute-start(bf16[2,256,2048]{2,1,0:T(8,128)(2,1)S(1)} %pad_maximum_fusion.4), channel_id=1, source_target_pairs={{0,1},{1,0},{2,3},{3,2},{4,5},{5,4},{6,7},{7,6},{8,9},{9,8},{10,11... | collective-permute-start | bytes 6291464 | tf_op jit(solution)/shard_map/ppermute | solution.py:53
  285.3 38.8 %collective-permute-start.38 = (bf16[4,256,768]{2,1,0:T(8,128)(2,1)S(1)}, bf16[4,256,768]{2,1,0:T(8,128)(2,1)S(1)}, u32[]{:S(2)}, u32[]{:S(2)}) collective-permute-start(bf16[4,256,768]{2,1,0:T(8,128)(2,1)S(1)} %pad_maximum_fusion.10), channel_id=1, source_target_pairs={{0,4},{4,0},{8,12},{12,8},{16,20},{20,16},{24,28},{28,24},{1,5},{5... | collective-permute-start | bytes 4718600 | tf_op jit(solution)/shard_map/ppermute | solution.py:53
  325.3 42.2 %collective-permute-start.44 = (bf16[2,256,2048]{2,1,0:T(8,128)(2,1)S(1)}, bf16[2,256,2048]{2,1,0:T(8,128)(2,1)}, u32[]{:S(2)}, u32[]{:S(2)}) collective-permute-start(bf16[2,256,2048]{2,1,0:T(8,128)(2,1)S(1)} %pad_maximum_fusion.5), channel_id=1, source_target_pairs={{0,1},{1,0},{2,3},{3,2},{4,5},{5,4},{6,7},{7,6},{8,9},{9,8},{10,11... | collective-permute-start | bytes 6291464 | tf_op jit(solution)/shard_map/ppermute | solution.py:53
  325.4 42.0 %collective-permute-start.42 = (bf16[4,256,768]{2,1,0:T(8,128)(2,1)S(1)}, bf16[4,256,768]{2,1,0:T(8,128)(2,1)}, u32[]{:S(2)}, u32[]{:S(2)}) collective-permute-start(bf16[4,256,768]{2,1,0:T(8,128)(2,1)S(1)} %pad_maximum_fusion.11), channel_id=1, source_target_pairs={{0,4},{4,0},{8,12},{12,8},{16,20},{20,16},{24,28},{28,24},{1,5},{5... | collective-permute-start | bytes 4718600 | tf_op jit(solution)/shard_map/ppermute | solution.py:53
  326.4 41.0 %collective-permute-start.43 = (bf16[2,256,768]{2,1,0:T(8,128)(2,1)S(1)}, bf16[2,256,768]{2,1,0:T(8,128)(2,1)S(1)}, u32[]{:S(2)}, u32[]{:S(2)}) collective-permute-start(bf16[2,256,768]{2,1,0:T(8,128)(2,1)S(1)} %pad_maximum_fusion.21), channel_id=1, source_target_pairs={{0,16},{4,20},{8,24},{12,28},{16,0},{20,4},{24,8},{28,12},{1,17},{... | collective-permute-start | bytes 2359304 | tf_op jit(solution)/shard_map/ppermute | solution.py:53
  327.8 39.6 %collective-permute-start.45 = (bf16[2,1,256,320]{3,2,0,1:T(8,128)(2,1)}, bf16[2,1,256,320]{3,2,0,1:T(8,128)(2,1)}, u32[]{:S(2)}, u32[]{:S(2)}) collective-permute-start(bf16[2,1,256,320]{3,2,0,1:T(8,128)(2,1)} %get-tuple-element.302), channel_id=1, source_target_pairs={{0,2},{1,3},{2,0},{3,1},{4,6},{5,7},{6,4},{7,5},{8,10},{9,11},{10,... | collective-permute-start | bytes 983048 | tf_op jit(solution)/shard_map/ppermute | solution.py:53
  367.4 41.3 %collective-permute-start.48 = (bf16[4,768,256]{2,1,0:T(8,128)(2,1)}, bf16[4,768,256]{2,1,0:T(8,128)(2,1)}, u32[]{:S(2)}, u32[]{:S(2)}) collective-permute-start(bf16[4,768,256]{2,1,0:T(8,128)(2,1)} %get-tuple-element.325), channel_id=1, source_target_pairs={{0,4},{4,0},{8,12},{12,8},{16,20},{20,16},{24,28},{28,24},{1,5},{5... | collective-permute-start | bytes 4718600 | tf_op jit(solution)/shard_map/ppermute | solution.py:53
  368.6 40.2 %collective-permute-start.46 = (bf16[2,256,768]{2,1,0:T(8,128)(2,1)S(1)}, bf16[2,256,768]{2,1,0:T(8,128)(2,1)S(1)}, u32[]{:S(2)}, u32[]{:S(2)}) collective-permute-start(bf16[2,256,768]{2,1,0:T(8,128)(2,1)S(1)} %collective-permute-done.41), channel_id=1, source_target_pairs={{0,16},{4,20},{8,24},{12,28},{16,0},{20,4},{24,8},{28,12},{1,17},{... | collective-permute-start | bytes 2359304 | tf_op jit(solution)/shard_map/ppermute | solution.py:53
  408.8 39.4 %collective-permute-start.49 = (bf16[4,768,256]{2,1,0:T(8,128)(2,1)}, bf16[4,768,256]{2,1,0:T(8,128)(2,1)}, u32[]{:S(2)}, u32[]{:S(2)}) collective-permute-start(bf16[4,768,256]{2,1,0:T(8,128)(2,1)} %get-tuple-element.327), channel_id=1, source_target_pairs={{0,4},{4,0},{8,12},{12,8},{16,20},{20,16},{24,28},{28,24},{1,5},{5... | collective-permute-start | bytes 4718600 | tf_op jit(solution)/shard_map/ppermute | solution.py:53
  411.1 37.0 %collective-permute-start.50 = (bf16[2,768,256]{2,1,0:T(8,128)(2,1)S(1)}, bf16[2,768,256]{2,1,0:T(8,128)(2,1)S(1)}, u32[]{:S(2)}, u32[]{:S(2)}) collective-permute-start(bf16[2,768,256]{2,1,0:T(8,128)(2,1)S(1)} %add_convert_fusion.5), channel_id=1, source_target_pairs={{0,16},{4,20},{8,24},{12,28},{16,0},{20,4},{24,8},{28,12},{1,17},{... | collective-permute-start | bytes 2359304 | tf_op jit(solution)/shard_map/ppermute | solution.py:53
  448.2 47.4 %collective-permute-start.54 = (bf16[4,768,256]{2,1,0:T(8,128)(2,1)}, bf16[4,768,256]{2,1,0:T(8,128)(2,1)}, u32[]{:S(2)}, u32[]{:S(2)}) collective-permute-start(bf16[4,768,256]{2,1,0:T(8,128)(2,1)} %copy-done.120), channel_id=1, source_target_pairs={{0,4},{4,0},{8,12},{12,8},{16,20},{20,16},{24,28},{28,24},{1,5},{5... | collective-permute-start | bytes 4718600 | tf_op jit(solution)/shard_map/ppermute | solution.py:53
  449.2 46.4 %collective-permute-start.51 = (bf16[256,2048]{1,0:T(8,128)(2,1)}, bf16[256,2048]{1,0:T(8,128)(2,1)}, u32[]{:S(2)}, u32[]{:S(2)}) collective-permute-start(bf16[256,2048]{1,0:T(8,128)(2,1)} %get-tuple-element.332), channel_id=1, source_target_pairs={{0,2},{1,3},{2,0},{3,1},{4,6},{5,7},{6,4},{7,5},{8,10},{9,11},{10,... | collective-permute-start | bytes 3145736 | tf_op jit(solution)/shard_map/ppermute | solution.py:53
  449.9 45.7 %collective-permute-start.52 = (bf16[256,2048]{1,0:T(8,128)(2,1)}, bf16[256,2048]{1,0:T(8,128)(2,1)}, u32[]{:S(2)}, u32[]{:S(2)}) collective-permute-start(bf16[256,2048]{1,0:T(8,128)(2,1)} %get-tuple-element.338), channel_id=1, source_target_pairs={{0,1},{1,0},{2,3},{3,2},{4,5},{5,4},{6,7},{7,6},{8,9},{9,8},{10,11... | collective-permute-start | bytes 3145736 | tf_op jit(solution)/shard_map/ppermute | solution.py:53
  449.9 45.7 %collective-permute-start.53 = (bf16[256,2048]{1,0:T(8,128)(2,1)}, bf16[256,2048]{1,0:T(8,128)(2,1)}, u32[]{:S(2)}, u32[]{:S(2)}) collective-permute-start(bf16[256,2048]{1,0:T(8,128)(2,1)} %get-tuple-element.340), channel_id=1, source_target_pairs={{0,3},{1,2},{2,1},{3,0},{4,7},{5,6},{6,5},{7,4},{8,11},{9,10},{10,... | collective-permute-start | bytes 3145736 | tf_op jit(solution)/shard_map/ppermute | solution.py:53
  495.6 41.8 %collective-permute-start.56 = (bf16[2,256,2048]{2,1,0:T(8,128)(2,1)}, bf16[2,256,2048]{2,1,0:T(8,128)(2,1)}, u32[]{:S(2)}, u32[]{:S(2)}) collective-permute-start(bf16[2,256,2048]{2,1,0:T(8,128)(2,1)} %bitcast.256), channel_id=1, source_target_pairs={{0,1},{1,0},{2,3},{3,2},{4,5},{5,4},{6,7},{7,6},{8,9},{9,8},{10,11... | collective-permute-start | bytes 6291464 | tf_op jit(solution)/shard_map/ppermute | solution.py:53
  496.7 40.6 %collective-permute-start.57 = (bf16[4,768,256]{2,1,0:T(8,128)(2,1)}, bf16[4,768,256]{2,1,0:T(8,128)(2,1)}, u32[]{:S(2)}, u32[]{:S(2)}) collective-permute-start(bf16[4,768,256]{2,1,0:T(8,128)(2,1)} %copy-done.121), channel_id=1, source_target_pairs={{0,4},{4,0},{8,12},{12,8},{16,20},{20,16},{24,28},{28,24},{1,5},{5... | collective-permute-start | bytes 4718600 | tf_op jit(solution)/shard_map/ppermute | solution.py:53
  499.0 38.3 %collective-permute-start.58 = (bf16[2,768,256]{2,1,0:T(8,128)(2,1)S(1)}, bf16[2,768,256]{2,1,0:T(8,128)(2,1)S(1)}, u32[]{:S(2)}, u32[]{:S(2)}) collective-permute-start(bf16[2,768,256]{2,1,0:T(8,128)(2,1)S(1)} %add_convert_fusion.3), channel_id=1, source_target_pairs={{0,16},{4,20},{8,24},{12,28},{16,0},{20,4},{24,8},{28,12},{1,17},{... | collective-permute-start | bytes 2359304 | tf_op jit(solution)/shard_map/ppermute | solution.py:53
  537.4 41.4 %collective-permute-start.62 = (bf16[4,768,256]{2,1,0:T(8,128)(2,1)}, bf16[4,768,256]{2,1,0:T(8,128)(2,1)}, u32[]{:S(2)}, u32[]{:S(2)}) collective-permute-start(bf16[4,768,256]{2,1,0:T(8,128)(2,1)} %get-tuple-element.369), channel_id=1, source_target_pairs={{0,4},{4,0},{8,12},{12,8},{16,20},{20,16},{24,28},{28,24},{1,5},{5... | collective-permute-start | bytes 4718600 | tf_op jit(solution)/shard_map/ppermute | solution.py:53
  538.6 38.8 %collective-permute-start.61 = (bf16[1,256,2048]{2,1,0:T(8,128)(2,1)S(1)}, bf16[1,256,2048]{2,1,0:T(8,128)(2,1)}, u32[]{:S(2)}, u32[]{:S(2)}) collective-permute-start(bf16[1,256,2048]{2,1,0:T(8,128)(2,1)S(1)} %bitcast.178), channel_id=1, source_target_pairs={{0,2},{1,3},{2,0},{3,1},{4,6},{5,7},{6,4},{7,5},{8,10},{9,11},{10,... | collective-permute-start | bytes 3145736 | tf_op jit(solution)/shard_map/ppermute | solution.py:53
  578.8 44.3 %collective-permute-start.67 = (bf16[2,256,2048]{2,1,0:T(8,128)(2,1)S(1)}, bf16[2,256,2048]{2,1,0:T(8,128)(2,1)}, u32[]{:S(2)}, u32[]{:S(2)}) collective-permute-start(bf16[2,256,2048]{2,1,0:T(8,128)(2,1)S(1)} %pad_maximum_fusion.6), channel_id=1, source_target_pairs={{0,1},{1,0},{2,3},{3,2},{4,5},{5,4},{6,7},{7,6},{8,9},{9,8},{10,11... | collective-permute-start | bytes 6291464 | tf_op jit(solution)/shard_map/ppermute | solution.py:53
  578.9 44.2 %collective-permute-start.66 = (bf16[4,1,5,4,64,128]{5,4,3,2,1,0:T(8,128)(2,1)S(1)}, bf16[4,1,5,4,64,128]{5,4,3,2,1,0:T(8,128)(2,1)}, u32[]{:S(2)}, u32[]{:S(2)}) collective-permute-start(bf16[4,1,5,4,64,128]{5,4,3,2,1,0:T(8,128)(2,1)S(1)} %copy-done.69), channel_id=1, source_target_pairs={{0,4},{4,0},{8,12},{12,8},{16,20},{20,16},{24,28},{28,24},{1,5},{5... | collective-permute-start | bytes 3932168 | tf_op jit(solution)/shard_map/ppermute | solution.py:53
  582.6 40.5 %collective-permute-start.65 = (bf16[1,256,2048]{2,1,0:T(8,128)(2,1)}, bf16[1,256,2048]{2,1,0:T(8,128)(2,1)}, u32[]{:S(2)}, u32[]{:S(2)}) collective-permute-start(bf16[1,256,2048]{2,1,0:T(8,128)(2,1)} %fusion.3), channel_id=1, source_target_pairs={{0,2},{1,3},{2,0},{3,1},{4,6},{5,7},{6,4},{7,5},{8,10},{9,11},{10,... | collective-permute-start | bytes 3145736 | tf_op jit(solution)/shard_map/ppermute | solution.py:53
  623.0 42.2 %collective-permute-start.72 = (bf16[4,768,256]{2,1,0:T(8,128)(2,1)}, bf16[4,768,256]{2,1,0:T(8,128)(2,1)}, u32[]{:S(2)}, u32[]{:S(2)}) collective-permute-start(bf16[4,768,256]{2,1,0:T(8,128)(2,1)} %get-tuple-element.398), channel_id=1, source_target_pairs={{0,4},{4,0},{8,12},{12,8},{16,20},{20,16},{24,28},{28,24},{1,5},{5... | collective-permute-start | bytes 4718600 | tf_op jit(solution)/shard_map/ppermute | solution.py:53
  (215 other events, 3578.8 us)

commit v5 on v4

--- a/solution.py
+++ b/solution.py
@@ -878,10 +878,10 @@
     g_kv, g_gains = GatherSoon(kv_shard), Gather(norm_gains)
     g_query, g_out = Gather(query_shard), Gather(w_out)
     g_ff = [Gather(x) for x in shards[:-1]] + [GatherLate(shards[-1])]
-    link.go(g_kv, g_gains, g_query)
-    link.go(g_kv, g_gains, g_query, g_out, g_ff[0])
+    link.go(g_kv, g_gains, g_query, during=[d_ffn_own, cos, sin, limit, *shards])
+    link.go(g_kv, g_gains, g_query, g_out)
     t_kv = PairRows(g_kv.stack)
-    link.go(t_kv, g_gains, g_query, g_out)
+    link.go(t_kv, g_gains, g_query, g_out, g_ff[0])
     gains = g_gains.stack.transpose(1, 0, 2).reshape(2, width).astype(f32)
     gain_one, gain_two = gains[0], gains[1]
     h_one = scaled_norm(inputs_f, gain_one).astype(bf16)
@@ -1240,9 +1240,10 @@
     out_halves = product(d_attn, t_heads.rows())
     link.go(t_query_back, s_keys, s_ff[5], s_ff[3], s_ff[4], during=[*out_halves, outputs])
     s_out = sum_of(out_halves)
-    s_query = sum_of(product(h_one_all, t_query_back.rows()))
-    link.go(s_keys, s_out, s_ff[5], during=[s_query.value()])
+    link.go(s_keys, s_out, s_ff[5])
     d_kv = s_keys.result()
+    query_halves = product(h_one_all, after(t_query_back.rows(), d_kv))
+    s_query = sum_of(query_halves)
     d_kv_low, d_k_gain = pl.pallas_call(
         key_back_kernel,
         out_shape=(
@@ -1286,7 +1287,7 @@
         terms = [[lows[c], *s_ff[c].raw] for c in range(first, last)]
         flat = [x for group in terms for x in group]
         if not held:
-            flat[0] = after(flat[0], *link.done)
+            flat[0] = after(flat[0], grad_rel)
         return pl.pallas_call(
             functools.partial(collect_kernel, len(terms), len(terms[0])),
             grid=(len(terms),),
@@ -1307,7 +1308,8 @@
         )(*flat, *held)
 
     early_sums = collect(0, FF_LAST)
-    link.go(t_kv_back, s_out, s_query, during=[grad_rel, *early_sums])
+    link.done += [*query_halves, *early_sums, grad_rel]
+    link.go(t_kv_back, s_out, s_query)
     grad_inputs = call(
         functools.partial(leave_kernel, tuple(order)),
         low_square,
@@ -1341,9 +1343,8 @@
     stack = stack[:, :kv_part]
     sum_gains = small[:2]
     sum_heads = small[2:].reshape(-1)[: 2 * HEAD].reshape(2, HEAD)
-    inverse = jnp.array([tensor_order.index(i) for i in range(n_tensor)], jnp.int32)
     places = [
-        lax.dynamic_index_in_dim(inverse, tensor ^ i, axis=0, keepdims=False)
+        sum((((tensor ^ i) // mask) & 1) << k for k, mask in enumerate(masks_of("tensor")))
         for i in range(n_tensor)
     ]
     sum_kv = jnp.concatenate(

time: 792 us -> 763 us (0.963)
  waiting for transfers between devices: 299 us -> 283 us
    ppermute x94, waiting for transfers between devices: 299 us -> 283 us  [swap(): return lax.ppermute(value, axis, [(i, i ^ mask) for i in range(size)])]
    unnamed x310 -> x302, local copies, waits for them, and re-layouts: 45.1 us -> 46.3 us
  transfers between devices with their start and end apart: 94 -> 94, of which waited for: 36 -> 40; matrix products, arithmetic and copies ran while one was open for 10% -> 9% of each run, Pallas kernels for 33% -> 35%
where the time goes in v5:
time: 763 us; the launch traced here: 752 us
  waiting for transfers between devices  283 us (37%)
  Pallas kernels  260 us (34%)
  starting transfers between devices  92.6 us (12%)
  other arithmetic  59.8 us (8%)
  local copies, waits for them, and re-layouts  53.6 us (7%)
    ppermute x94, waiting for transfers between devices, swap(): return lax.ppermute(value, axis, [(i, i ^ mask) for i in range(size)])  283 us
    ppermute x94, starting transfers between devices, swap(): return lax.ppermute(value, axis, [(i, i ^ mask) for i in range(size)])  92.6 us
    pallas_call x6, Pallas kernels, hidden_part(): pl.pallas_call(functools.partial(hidden_kernel, [places for _, places in...  50 us
    unnamed x302, local copies, waits for them, and re-layouts  46.3 us
    pallas_call x6, Pallas kernels, grads_of(): pl.pallas_call(grads_kernel, grid=(grid,), in_specs=[block] * 4 + [whole(...  41.8 us
    pallas_call x2, Pallas kernels, back_sum(): pl.pallas_call(functools.partial(back_sum_kernel, [[places for _, places...  33.4 us
    pallas_call x2, Pallas kernels, attend_back(): pl.pallas_call(attend_back_kernel, grid=(rows, count), in_specs=[q_part,...  33 us
    convert_element_type x19, other arithmetic, plus(): return total.astype(kind)  25.2 us
  transfers between devices with their start and end apart: 94, of which 40 were waited for; matrix products, arithmetic and copies ran while one was open for 9% of the time, Pallas kernels for 35%

profile of v5, /device:TPU:0, one launch (start us, length us, event | category | flops | bytes accessed | tf_op | source)
XLA Modules:
  0.0 752.1 jit_solution(10123435656486161039)
XLA Ops:
  28.4 10.0 %collective-permute-done.6 = bf16[4,128,640]{2,1,0:T(8,128)(2,1)S(1)} collective-permute-done((bf16[4,128,640]{2,1,0:T(8,128)(2,1)S(1)}, bf16[4,128,640]{2,1,0:T(8,128)(2,1)S(1)}, u32[]{:S(2)}, u32[]{:S(2)}) %collective-permute-start.6) | collective-permute-done | bytes 655392 | tf_op jit(solution)/shard_map/ppermute | solution.py:53
  47.8 10.7 %collective-permute-done.9 = bf16[4,2,256]{2,1,0:T(2,128)(2,1)S(1)} collective-permute-done((bf16[4,2,256]{2,1,0:T(2,128)(2,1)S(1)}, bf16[4,2,256]{2,1,0:T(2,128)(2,1)S(1)}, u32[]{:S(2)}, u32[]{:S(2)}) %collective-permute-start.9) | collective-permute-done | bytes 4128 | tf_op jit(solution)/shard_map/ppermute | solution.py:53
  76.4 16.6 %collective-permute-done.14 = bf16[1,8,320,256]{3,2,1,0:T(8,128)(2,1)S(1)} collective-permute-done((bf16[1,8,320,256]{3,2,1,0:T(8,128)(2,1)S(1)}, bf16[1,8,320,256]{3,2,1,0:T(8,128)(2,1)S(1)}, u32[]{:S(2)}, u32[]{:S(2)}) %collective-permute-start.14) | collective-permute-done | bytes 1310752 | tf_op jit(solution)/shard_map/ppermute | solution.py:53
  95.1 7.6 %collective-permute-done.17 = bf16[2,256,768]{2,1,0:T(8,128)(2,1)S(1)} collective-permute-done((bf16[2,256,768]{2,1,0:T(8,128)(2,1)S(1)}, bf16[2,256,768]{2,1,0:T(8,128)(2,1)S(1)}, u32[]{:S(2)}, u32[]{:S(2)}) %collective-permute-start.17) | collective-permute-done | bytes 786464 | tf_op jit(solution)/shard_map/ppermute | solution.py:53
  108.5 27.1 %collective-permute-done.21 = bf16[1,8,320,256]{3,2,1,0:T(8,128)(2,1)S(1)} collective-permute-done((bf16[1,8,320,256]{3,2,1,0:T(8,128)(2,1)S(1)}, bf16[1,8,320,256]{3,2,1,0:T(8,128)(2,1)S(1)}, u32[]{:S(2)}, u32[]{:S(2)}) %collective-permute-start.21) | collective-permute-done | bytes 1310752 | tf_op jit(solution)/shard_map/ppermute | solution.py:53
  152.9 12.8 %query.1 = (f32[4,256,320]{2,1,0:T(8,128)S(1)}, bf16[1,5,4,4,64,128]{5,4,3,2,1,0:T(8,128)(2,1)S(1)}) custom-call(bf16[256,2048]{1,0:T(8,128)(2,1)S(1)} %copy-done.17, bf16[4,8,320,256]{3,2,1,0:T(8,128)(2,1)} %copy-done.126, f32[256,64]{1,0:T(8,128)S(1)} %get-tuple-element.495.cos_ref, f32[256,64]{1,0:T(8,128)S(1)} %get-tuple-element.496.sin_ref, ...), custom_call_target="tpu_custom_call" | custom-call | flops 1000 | bytes 1000 | tf_op jit(solution)/shard_map/query/pallas_call | solution.py:922
  170.1 11.4 %collective-permute-done.27 = bf16[2,256,768]{2,1,0:T(8,128)(2,1)} collective-permute-done((bf16[2,256,768]{2,1,0:T(8,128)(2,1)}, bf16[2,256,768]{2,1,0:T(8,128)(2,1)}, u32[]{:S(2)}, u32[]{:S(2)}) %collective-permute-start.27) | collective-permute-done | bytes 786464 | tf_op jit(solution)/shard_map/ppermute | solution.py:53
  195.7 18.8 %attend.1.o_ref = bf16[1,5,4,4,64,128]{5,4,3,2,1,0:T(8,128)(2,1)S(1)} custom-call(bf16[1,5,4,4,64,128]{5,4,3,2,1,0:T(8,128)(2,1)S(1)} %copy-done.12, s32[1,4,1,256]{3,2,1,0:T(1,128)S(1)} %broadcast_in_dim.96.limit_ref, s32[1,2048,1]{2,1,0:T(8,128)S(1)} %copy-done.9, bf16[4,1,5,4,64,128]{5,4,3,2,1,0:T(8,128)(2,1)} %pad_maximum_fusion.13.low_ref, ...), custom_call_target="tpu_custom_call" | custom-call | flops 1000 | bytes 1000 | tf_op jit(solution)/shard_map/attend/pallas_call | solution.py:953
  214.5 7.8 %out.1 = (f32[256,2048]{1,0:T(8,128)}, bf16[256,2048]{1,0:T(8,128)(2,1)S(1)}, bf16[4,256,320]{2,1,0:T(8,128)(2,1)S(1)}) custom-call(bf16[1,5,4,4,64,128]{5,4,3,2,1,0:T(8,128)(2,1)S(1)} %attend.1.o_ref, bf16[2,8,320,256]{3,2,1,0:T(8,128)(2,1)} %pad_maximum_fusion.2.w_low, bf16[2,8,320,256]{3,2,1,0:T(8,128)(2,1)} %collective-permute-done.25.w_high, ...), custom_call_target="tpu_custom_call" | custom-call | flops 1000 | bytes 1000 | tf_op jit(solution)/shard_map/out/pallas_call | solution.py:968
  235.2 19.1 %collective-permute-done.33 = bf16[1,256,2048]{2,1,0:T(8,128)(2,1)S(1)} collective-permute-done((bf16[1,256,2048]{2,1,0:T(8,128)(2,1)S(1)}, bf16[1,256,2048]{2,1,0:T(8,128)(2,1)S(1)}, u32[]{:S(2)}, u32[]{:S(2)}) %collective-permute-start.33) | collective-permute-done | bytes 1048608 | tf_op jit(solution)/shard_map/ppermute | solution.py:53
  257.2 11.4 %collective-permute-done.35 = bf16[2,256,768]{2,1,0:T(8,128)(2,1)S(1)} collective-permute-done((bf16[2,256,768]{2,1,0:T(8,128)(2,1)S(1)}, bf16[2,256,768]{2,1,0:T(8,128)(2,1)S(1)}, u32[]{:S(2)}, u32[]{:S(2)}) %collective-permute-start.35) | collective-permute-done | bytes 786464 | tf_op jit(solution)/shard_map/ppermute | solution.py:53
  273.7 22.5 %collective-permute-done.40 = bf16[1,256,2048]{2,1,0:T(8,128)(2,1)S(1)} collective-permute-done((bf16[1,256,2048]{2,1,0:T(8,128)(2,1)S(1)}, bf16[1,256,2048]{2,1,0:T(8,128)(2,1)S(1)}, u32[]{:S(2)}, u32[]{:S(2)}) %collective-permute-start.40) | collective-permute-done | bytes 1048608 | tf_op jit(solution)/shard_map/ppermute | solution.py:53
  296.5 11.8 %collective-permute-done.39 = bf16[2,256,768]{2,1,0:T(8,128)(2,1)S(1)} collective-permute-done((bf16[2,256,768]{2,1,0:T(8,128)(2,1)S(1)}, bf16[2,256,768]{2,1,0:T(8,128)(2,1)S(1)}, u32[]{:S(2)}, u32[]{:S(2)}) %collective-permute-start.39) | collective-permute-done | bytes 786464 | tf_op jit(solution)/shard_map/ppermute | solution.py:53
  313.4 7.9 %hidden.6 = (bf16[1024,256]{1,0:T(8,128)(2,1)S(1)}, bf16[1024,512]{1,0:T(8,128)(2,1)S(1)}, bf16[768,1024]{1,0:T(8,128)(2,1)S(1)}) custom-call(bf16[512,2048]{1,0:T(8,128)(2,1)} %bitcast.200, bf16[512,2048]{1,0:T(8,128)(2,1)} %bitcast.212, bf16[512,2048]{1,0:T(8,128)(2,1)} %bitcast.29.d_low, bf16[512,2048]{1,0:T(8,128)(2,1)} %bitcast.30.d_high, ...), custom_call_target="tpu_custom_call" | custom-call | flops 1000 | bytes 1000 | tf_op jit(solution)/shard_map/hidden/pallas_call | solution.py:1010
  331.8 8.4 %hidden.8 = (bf16[1024,256]{1,0:T(8,128)(2,1)S(1)}, bf16[1024,512]{1,0:T(8,128)(2,1)S(1)}, bf16[768,1024]{1,0:T(8,128)(2,1)S(1)}) custom-call(bf16[512,2048]{1,0:T(8,128)(2,1)} %bitcast.202, bf16[512,2048]{1,0:T(8,128)(2,1)} %bitcast.214, bf16[512,2048]{1,0:T(8,128)(2,1)} %bitcast.29.d_low, bf16[512,2048]{1,0:T(8,128)(2,1)} %bitcast.30.d_high, ...), custom_call_target="tpu_custom_call" | custom-call | flops 1000 | bytes 1000 | tf_op jit(solution)/shard_map/hidden/pallas_call | solution.py:1010
  341.4 8.8 %hidden.7 = (bf16[1024,256]{1,0:T(8,128)(2,1)S(1)}, bf16[1024,512]{1,0:T(8,128)(2,1)S(1)}, bf16[768,1024]{1,0:T(8,128)(2,1)S(1)}) custom-call(bf16[512,2048]{1,0:T(8,128)(2,1)} %bitcast.203, bf16[512,2048]{1,0:T(8,128)(2,1)} %bitcast.215, bf16[512,2048]{1,0:T(8,128)(2,1)} %bitcast.29.d_low, bf16[512,2048]{1,0:T(8,128)(2,1)} %bitcast.30.d_high, ...), custom_call_target="tpu_custom_call" | custom-call | flops 1000 | bytes 1000 | tf_op jit(solution)/shard_map/hidden/pallas_call | solution.py:1010
  364.7 7.5 %weight_grads.8 = (bf16[4,768,256]{2,1,0:T(8,128)(2,1)S(1)}, bf16[4,768,256]{2,1,0:T(8,128)(2,1)S(1)}) custom-call(bf16[512,2048]{1,0:T(8,128)(2,1)} %bitcast.205, bf16[512,2048]{1,0:T(8,128)(2,1)} %bitcast.217, bf16[512,2048]{1,0:T(8,128)(2,1)} %bitcast.29.d_low, bf16[512,2048]{1,0:T(8,128)(2,1)} %bitcast.30.d_high, bf16[768,1024]{1,0:T(8,128)(2,1)S(1)} %copy-done.63), custom_call_target="tpu_custom_call" | custom-call | flops 1000 | bytes 1000 | tf_op jit(solution)/shard_map/weight_grads/pallas_call | solution.py:1047
  374.6 8.0 %hidden.9 = (bf16[1024,256]{1,0:T(8,128)(2,1)S(1)}, bf16[1024,512]{1,0:T(8,128)(2,1)S(1)}, bf16[768,1024]{1,0:T(8,128)(2,1)S(1)}) custom-call(bf16[512,2048]{1,0:T(8,128)(2,1)} %bitcast.206, bf16[512,2048]{1,0:T(8,128)(2,1)} %bitcast.218, bf16[512,2048]{1,0:T(8,128)(2,1)} %bitcast.29.d_low, bf16[512,2048]{1,0:T(8,128)(2,1)} %bitcast.30.d_high, ...), custom_call_target="tpu_custom_call" | custom-call | flops 1000 | bytes 1000 | tf_op jit(solution)/shard_map/hidden/pallas_call | solution.py:1010
  383.7 8.6 %hidden.10 = (bf16[1024,256]{1,0:T(8,128)(2,1)S(1)}, bf16[1024,512]{1,0:T(8,128)(2,1)S(1)}, bf16[768,1024]{1,0:T(8,128)(2,1)S(1)}) custom-call(bf16[512,2048]{1,0:T(8,128)(2,1)} %bitcast.207, bf16[512,2048]{1,0:T(8,128)(2,1)} %bitcast.219, bf16[512,2048]{1,0:T(8,128)(2,1)} %bitcast.29.d_low, bf16[512,2048]{1,0:T(8,128)(2,1)} %bitcast.30.d_high, ...), custom_call_target="tpu_custom_call" | custom-call | flops 1000 | bytes 1000 | tf_op jit(solution)/shard_map/hidden/pallas_call | solution.py:1010
  396.6 8.3 %hidden.11 = (bf16[1024,256]{1,0:T(8,128)(2,1)S(1)}, bf16[1024,512]{1,0:T(8,128)(2,1)S(1)}, bf16[768,1024]{1,0:T(8,128)(2,1)}) custom-call(bf16[512,2048]{1,0:T(8,128)(2,1)} %bitcast.208, bf16[512,2048]{1,0:T(8,128)(2,1)} %bitcast.220, bf16[512,2048]{1,0:T(8,128)(2,1)} %bitcast.29.d_low, bf16[512,2048]{1,0:T(8,128)(2,1)} %bitcast.30.d_high, ...), custom_call_target="tpu_custom_call" | custom-call | flops 1000 | bytes 1000 | tf_op jit(solution)/shard_map/hidden/pallas_call | solution.py:1010
  407.1 20.8 %back_sum.3 = (bf16[256,2048]{1,0:T(8,128)(2,1)S(1)}, bf16[256,2048]{1,0:T(8,128)(2,1)}, bf16[256,2048]{1,0:T(8,128)(2,1)}, bf16[256,2048]{1,0:T(8,128)(2,1)}) custom-call(bf16[1024,512]{1,0:T(8,128)(2,1)} %copy-done.70, bf16[1024,512]{1,0:T(8,128)(2,1)} %copy-done.72, bf16[1024,512]{1,0:T(8,128)(2,1)} %copy-done.71, bf16[1024,512]{1,0:T(8,128)(2,1)} %copy-done.73, ...), custom_call_target="tpu_custom_call" | custom-call | flops 1000 | bytes 1000 | tf_op jit(solution)/shard_map/back_sum/pallas_call | solution.py:1083
  437.1 12.6 %back_sum.2 = (bf16[512,2048]{1,0:T(8,128)(2,1)}, bf16[512,2048]{1,0:T(8,128)(2,1)}) custom-call(bf16[1024,256]{1,0:T(8,128)(2,1)S(1)} %copy-done.90, bf16[1024,256]{1,0:T(8,128)(2,1)S(1)} %copy-done.94, bf16[1024,256]{1,0:T(8,128)(2,1)S(1)} %copy-done.92, bf16[1024,256]{1,0:T(8,128)(2,1)S(1)} %get-tuple-element.289.refs_3_, ...), custom_call_target="tpu_custom_call" | custom-call | flops 1000 | bytes 1000 | tf_op jit(solution)/shard_map/back_sum/pallas_call | solution.py:1083
  458.5 7.6 %weight_grads.10 = (bf16[4,768,256]{2,1,0:T(8,128)(2,1)S(1)}, bf16[4,768,256]{2,1,0:T(8,128)(2,1)}) custom-call(bf16[512,2048]{1,0:T(8,128)(2,1)} %bitcast.210, bf16[512,2048]{1,0:T(8,128)(2,1)} %bitcast.222, bf16[512,2048]{1,0:T(8,128)(2,1)} %bitcast.29.d_low, bf16[512,2048]{1,0:T(8,128)(2,1)} %bitcast.30.d_high, bf16[768,1024]{1,0:T(8,128)(2,1)S(1)} %copy-done.61), custom_call_target="tpu_custom_call" | custom-call | flops 1000 | bytes 1000 | tf_op jit(solution)/shard_map/weight_grads/pallas_call | solution.py:1047
  473.0 8.0 %collective-permute-done.53 = bf16[256,2048]{1,0:T(8,128)(2,1)} collective-permute-done((bf16[256,2048]{1,0:T(8,128)(2,1)}, bf16[256,2048]{1,0:T(8,128)(2,1)}, u32[]{:S(2)}, u32[]{:S(2)}) %collective-permute-start.53) | collective-permute-done | bytes 1048608 | tf_op jit(solution)/shard_map/ppermute | solution.py:53
  501.8 19.2 %attend_back.2 = (f32[1,5,4,4,64,128]{5,4,3,2,1,0:T(8,128)}, bf16[4,1,5,4,64,128]{5,4,3,2,1,0:T(8,128)(2,1)S(1)}, bf16[4,1,5,4,64,128]{5,4,3,2,1,0:T(8,128)(2,1)S(1)}) custom-call(bf16[1,5,4,4,64,128]{5,4,3,2,1,0:T(8,128)(2,1)S(1)} %copy-done.13, bf16[1,5,4,4,64,128]{5,4,3,2,1,0:T(8,128)(2,1)} %copy-done.14, s32[1,4,1,256]{3,2,1,0:T(1,128)S(1)} %copy-done.109, ...), custom_call_target="tpu_custom_call" | custom-call | flops 1000 | bytes 1000 | tf_op jit(solution)/shard_map/attend_back/pallas_call | solution.py:1150
  528.3 13.7 %attend_back.3 = (f32[1,5,4,4,64,128]{5,4,3,2,1,0:T(8,128)}, bf16[4,1,5,4,64,128]{5,4,3,2,1,0:T(8,128)(2,1)S(1)}, bf16[4,1,5,4,64,128]{5,4,3,2,1,0:T(8,128)(2,1)S(1)}) custom-call(bf16[1,5,4,4,64,128]{5,4,3,2,1,0:T(8,128)(2,1)S(1)} %copy-done.13, ...), custom_call_target="tpu_custom_call", output_to_operand_aliasing={{0}: (6, {}), {1}: (7, {}), {2}: (8, {})} | custom-call | flops 1000 | bytes 1000 | tf_op jit(solution)/shard_map/attend_back/pallas_call | solution.py:1150
  552.0 7.9 %collective-permute-done.63.refs_14_ = bf16[2,768,256]{2,1,0:T(8,128)(2,1)} collective-permute-done((bf16[2,768,256]{2,1,0:T(8,128)(2,1)S(1)}, bf16[2,768,256]{2,1,0:T(8,128)(2,1)}, u32[]{:S(2)}, u32[]{:S(2)}) %collective-permute-start.63) | collective-permute-done | bytes 786464 | tf_op jit(solution)/shard_map/ppermute | solution.py:53
  577.1 21.9 %collective-permute-done.68 = bf16[2,1,256,320]{3,2,0,1:T(8,128)(2,1)S(1)} collective-permute-done((bf16[2,1,256,320]{3,2,0,1:T(8,128)(2,1)S(1)}, bf16[2,1,256,320]{3,2,0,1:T(8,128)(2,1)S(1)}, u32[]{:S(2)}, u32[]{:S(2)}) %collective-permute-start.68) | collective-permute-done | bytes 327712 | tf_op jit(solution)/shard_map/ppermute | solution.py:53
  634.8 11.7 %collective-permute-done.74.refs_19_ = bf16[1,768,256]{2,1,0:T(8,128)(2,1)} collective-permute-done((bf16[1,768,256]{2,1,0:T(8,128)(2,1)}, bf16[1,768,256]{2,1,0:T(8,128)(2,1)}, u32[]{:S(2)}, u32[]{:S(2)}) %collective-permute-start.74) | collective-permute-done | bytes 393248 | tf_op jit(solution)/shard_map/ppermute | solution.py:53
  661.5 8.7 %h_one_back.1 = (bf16[256,2048]{1,0:T(8,128)(2,1)S(1)}, f32[1,2048]{1,0:T(1,128)S(1)}) custom-call(bf16[4,256,320]{2,1,0:T(8,128)(2,1)S(1)} %copy-done.45, bf16[4,8,320,256]{3,2,1,0:T(8,128)(2,1)} %copy-done.126, bf16[256,640]{1,0:T(8,128)(2,1)S(1)} %get-tuple-element.409.dkv_ref, bf16[2048,640]{1,0:T(8,128)(2,1)} %bitcast.156, ...), custom_call_target="tpu_custom_call" | custom-call | flops 1000 | bytes 1000 | tf_op jit(solution)/shard_map/h_one_back/pallas_call | solution.py:1264
  701.0 7.7 %collective-permute-done.82 = bf16[2,320,256]{2,1,0:T(8,128)(2,1)S(1)} collective-permute-done((bf16[2,320,256]{2,1,0:T(8,128)(2,1)S(1)}, bf16[2,320,256]{2,1,0:T(8,128)(2,1)S(1)}, u32[]{:S(2)}, u32[]{:S(2)}) %collective-permute-start.82) | collective-permute-done | bytes 327712 | tf_op jit(solution)/shard_map/ppermute | solution.py:53
  720.3 8.2 %collective-permute-done.83 = bf16[2,320,256]{2,1,0:T(8,128)(2,1)S(1)} collective-permute-done((bf16[2,320,256]{2,1,0:T(8,128)(2,1)S(1)}, bf16[2,320,256]{2,1,0:T(8,128)(2,1)S(1)}, u32[]{:S(2)}, u32[]{:S(2)}) %collective-permute-start.83) | collective-permute-done | bytes 327712 | tf_op jit(solution)/shard_map/ppermute | solution.py:53
  (613 shorter events, 355.8 us)
Async XLA Ops:
  102.7 37.1 %collective-permute-start.19 = (bf16[2,8,320,256]{3,2,1,0:T(8,128)(2,1)S(1)}, bf16[2,8,320,256]{3,2,1,0:T(8,128)(2,1)S(1)}, u32[]{:S(2)}, u32[]{:S(2)}) collective-permute-start(bf16[2,8,320,256]{3,2,1,0:T(8,128)(2,1)S(1)} %pad_maximum_fusion), channel_id=1, source_target_pairs={{0,1},{1,0},{2,3},{3,2},{4,5},{5,4},{6,7},{7,6},{8,9},{9,8},{10,11... | collective-permute-start | bytes 7864328 | tf_op jit(solution)/shard_map/ppermute | solution.py:53
  102.9 36.9 %collective-permute-start.22 = (bf16[4,256,768]{2,1,0:T(8,128)(2,1)S(1)}, bf16[4,256,768]{2,1,0:T(8,128)(2,1)S(1)}, u32[]{:S(2)}, u32[]{:S(2)}) collective-permute-start(bf16[4,256,768]{2,1,0:T(8,128)(2,1)S(1)} %pad_maximum_fusion.7), channel_id=1, source_target_pairs={{0,4},{4,0},{8,12},{12,8},{16,20},{20,16},{24,28},{28,24},{1,5},{5... | collective-permute-start | bytes 4718600 | tf_op jit(solution)/shard_map/ppermute | solution.py:53
  139.8 44.9 %collective-permute-start.25 = (bf16[2,8,320,256]{3,2,1,0:T(8,128)(2,1)}, bf16[2,8,320,256]{3,2,1,0:T(8,128)(2,1)}, u32[]{:S(2)}, u32[]{:S(2)}) collective-permute-start(bf16[2,8,320,256]{3,2,1,0:T(8,128)(2,1)} %pad_maximum_fusion.2.w_low), channel_id=1, source_target_pairs={{0,1},{1,0},{2,3},{3,2},{4,5},{5,4},{6,7},{7,6},{8,9},{9,8},{10,11... | collective-permute-start | bytes 7864328 | tf_op jit(solution)/shard_map/ppermute | solution.py:53
  139.8 41.7 %collective-permute-start.26 = (bf16[1,256,2048]{2,1,0:T(8,128)(2,1)}, bf16[1,256,2048]{2,1,0:T(8,128)(2,1)}, u32[]{:S(2)}, u32[]{:S(2)}) collective-permute-start(bf16[1,256,2048]{2,1,0:T(8,128)(2,1)} %bitcast.23), channel_id=1, source_target_pairs={{0,2},{1,3},{2,0},{3,1},{4,6},{5,7},{6,4},{7,5},{8,10},{9,11},{10,... | collective-permute-start | bytes 3145736 | tf_op jit(solution)/shard_map/ppermute | solution.py:53
  142.1 42.6 %collective-permute-start.24 = (bf16[4,1,5,4,64,128]{5,4,3,2,1,0:T(8,128)(2,1)}, bf16[4,1,5,4,64,128]{5,4,3,2,1,0:T(8,128)(2,1)}, u32[]{:S(2)}, u32[]{:S(2)}) collective-permute-start(bf16[4,1,5,4,64,128]{5,4,3,2,1,0:T(8,128)(2,1)} %pad_maximum_fusion.13.low_ref), channel_id=1, source_target_pairs={{0,4},{4,0},{8,12},{12,8},{16,20},{20,16},{24,28},{28,24},{1,5},{5... | collective-permute-start | bytes 3932168 | tf_op jit(solution)/shard_map/ppermute | solution.py:53
  144.5 37.0 %collective-permute-start.27 = (bf16[2,256,768]{2,1,0:T(8,128)(2,1)}, bf16[2,256,768]{2,1,0:T(8,128)(2,1)}, u32[]{:S(2)}, u32[]{:S(2)}) collective-permute-start(bf16[2,256,768]{2,1,0:T(8,128)(2,1)} %pad_maximum_fusion.17), channel_id=1, source_target_pairs={{0,16},{4,20},{8,24},{12,28},{16,0},{20,4},{24,8},{28,12},{1,17},{... | collective-permute-start | bytes 2359304 | tf_op jit(solution)/shard_map/ppermute | solution.py:53
  184.7 43.2 %collective-permute-start.29 = (bf16[2,256,2048]{2,1,0:T(8,128)(2,1)}, bf16[2,256,2048]{2,1,0:T(8,128)(2,1)}, u32[]{:S(2)}, u32[]{:S(2)}) collective-permute-start(bf16[2,256,2048]{2,1,0:T(8,128)(2,1)} %pad_maximum_fusion.3), channel_id=1, source_target_pairs={{0,1},{1,0},{2,3},{3,2},{4,5},{5,4},{6,7},{7,6},{8,9},{9,8},{10,11... | collective-permute-start | bytes 6291464 | tf_op jit(solution)/shard_map/ppermute | solution.py:53
  187.4 40.4 %collective-permute-start.30 = (bf16[4,256,768]{2,1,0:T(8,128)(2,1)}, bf16[4,256,768]{2,1,0:T(8,128)(2,1)}, u32[]{:S(2)}, u32[]{:S(2)}) collective-permute-start(bf16[4,256,768]{2,1,0:T(8,128)(2,1)} %pad_maximum_fusion.8), channel_id=1, source_target_pairs={{0,4},{4,0},{8,12},{12,8},{16,20},{20,16},{24,28},{28,24},{1,5},{5... | collective-permute-start | bytes 4718600 | tf_op jit(solution)/shard_map/ppermute | solution.py:53
  227.8 40.8 %collective-permute-start.34 = (bf16[4,256,768]{2,1,0:T(8,128)(2,1)S(1)}, bf16[4,256,768]{2,1,0:T(8,128)(2,1)S(1)}, u32[]{:S(2)}, u32[]{:S(2)}) collective-permute-start(bf16[4,256,768]{2,1,0:T(8,128)(2,1)S(1)} %pad_maximum_fusion.9), channel_id=1, source_target_pairs={{0,4},{4,0},{8,12},{12,8},{16,20},{20,16},{24,28},{28,24},{1,5},{5... | collective-permute-start | bytes 4718600 | tf_op jit(solution)/shard_map/ppermute | solution.py:53
  269.8 39.0 %collective-permute-start.37 = (bf16[2,256,2048]{2,1,0:T(8,128)(2,1)S(1)}, bf16[2,256,2048]{2,1,0:T(8,128)(2,1)S(1)}, u32[]{:S(2)}, u32[]{:S(2)}) collective-permute-start(bf16[2,256,2048]{2,1,0:T(8,128)(2,1)S(1)} %pad_maximum_fusion.4), channel_id=1, source_target_pairs={{0,1},{1,0},{2,3},{3,2},{4,5},{5,4},{6,7},{7,6},{8,9},{9,8},{10,11... | collective-permute-start | bytes 6291464 | tf_op jit(solution)/shard_map/ppermute | solution.py:53
  270.0 38.8 %collective-permute-start.38 = (bf16[4,256,768]{2,1,0:T(8,128)(2,1)S(1)}, bf16[4,256,768]{2,1,0:T(8,128)(2,1)S(1)}, u32[]{:S(2)}, u32[]{:S(2)}) collective-permute-start(bf16[4,256,768]{2,1,0:T(8,128)(2,1)S(1)} %pad_maximum_fusion.10), channel_id=1, source_target_pairs={{0,4},{4,0},{8,12},{12,8},{16,20},{20,16},{24,28},{28,24},{1,5},{5... | collective-permute-start | bytes 4718600 | tf_op jit(solution)/shard_map/ppermute | solution.py:53
  271.9 36.9 %collective-permute-start.41 = (bf16[2,256,768]{2,1,0:T(8,128)(2,1)S(1)}, bf16[2,256,768]{2,1,0:T(8,128)(2,1)S(1)}, u32[]{:S(2)}, u32[]{:S(2)}) collective-permute-start(bf16[2,256,768]{2,1,0:T(8,128)(2,1)S(1)} %pad_maximum_fusion.21), channel_id=1, source_target_pairs={{0,8},{4,12},{8,0},{12,4},{16,24},{20,28},{24,16},{28,20},{1,9},{5... | collective-permute-start | bytes 2359304 | tf_op jit(solution)/shard_map/ppermute | solution.py:53
  309.9 42.2 %collective-permute-start.44 = (bf16[2,256,2048]{2,1,0:T(8,128)(2,1)S(1)}, bf16[2,256,2048]{2,1,0:T(8,128)(2,1)}, u32[]{:S(2)}, u32[]{:S(2)}) collective-permute-start(bf16[2,256,2048]{2,1,0:T(8,128)(2,1)S(1)} %pad_maximum_fusion.5), channel_id=1, source_target_pairs={{0,1},{1,0},{2,3},{3,2},{4,5},{5,4},{6,7},{7,6},{8,9},{9,8},{10,11... | collective-permute-start | bytes 6291464 | tf_op jit(solution)/shard_map/ppermute | solution.py:53
  310.1 42.0 %collective-permute-start.42 = (bf16[4,256,768]{2,1,0:T(8,128)(2,1)S(1)}, bf16[4,256,768]{2,1,0:T(8,128)(2,1)}, u32[]{:S(2)}, u32[]{:S(2)}) collective-permute-start(bf16[4,256,768]{2,1,0:T(8,128)(2,1)S(1)} %pad_maximum_fusion.11), channel_id=1, source_target_pairs={{0,4},{4,0},{8,12},{12,8},{16,20},{20,16},{24,28},{28,24},{1,5},{5... | collective-permute-start | bytes 4718600 | tf_op jit(solution)/shard_map/ppermute | solution.py:53
  311.1 41.0 %collective-permute-start.43 = (bf16[2,256,768]{2,1,0:T(8,128)(2,1)S(1)}, bf16[2,256,768]{2,1,0:T(8,128)(2,1)S(1)}, u32[]{:S(2)}, u32[]{:S(2)}) collective-permute-start(bf16[2,256,768]{2,1,0:T(8,128)(2,1)S(1)} %pad_maximum_fusion.21), channel_id=1, source_target_pairs={{0,16},{4,20},{8,24},{12,28},{16,0},{20,4},{24,8},{28,12},{1,17},{... | collective-permute-start | bytes 2359304 | tf_op jit(solution)/shard_map/ppermute | solution.py:53
  312.0 40.1 %collective-permute-start.45 = (bf16[2,1,256,320]{3,2,0,1:T(8,128)(2,1)}, bf16[2,1,256,320]{3,2,0,1:T(8,128)(2,1)}, u32[]{:S(2)}, u32[]{:S(2)}) collective-permute-start(bf16[2,1,256,320]{3,2,0,1:T(8,128)(2,1)} %get-tuple-element.305), channel_id=1, source_target_pairs={{0,2},{1,3},{2,0},{3,1},{4,6},{5,7},{6,4},{7,5},{8,10},{9,11},{10,... | collective-permute-start | bytes 983048 | tf_op jit(solution)/shard_map/ppermute | solution.py:53
  352.2 41.3 %collective-permute-start.48 = (bf16[4,768,256]{2,1,0:T(8,128)(2,1)}, bf16[4,768,256]{2,1,0:T(8,128)(2,1)}, u32[]{:S(2)}, u32[]{:S(2)}) collective-permute-start(bf16[4,768,256]{2,1,0:T(8,128)(2,1)} %copy-done.119), channel_id=1, source_target_pairs={{0,4},{4,0},{8,12},{12,8},{16,20},{20,16},{24,28},{28,24},{1,5},{5... | collective-permute-start | bytes 4718600 | tf_op jit(solution)/shard_map/ppermute | solution.py:53
  353.1 40.4 %collective-permute-start.46 = (bf16[2,256,768]{2,1,0:T(8,128)(2,1)S(1)}, bf16[2,256,768]{2,1,0:T(8,128)(2,1)S(1)}, u32[]{:S(2)}, u32[]{:S(2)}) collective-permute-start(bf16[2,256,768]{2,1,0:T(8,128)(2,1)S(1)} %collective-permute-done.41), channel_id=1, source_target_pairs={{0,16},{4,20},{8,24},{12,28},{16,0},{20,4},{24,8},{28,12},{1,17},{... | collective-permute-start | bytes 2359304 | tf_op jit(solution)/shard_map/ppermute | solution.py:53
  393.5 40.0 %collective-permute-start.49 = (bf16[4,768,256]{2,1,0:T(8,128)(2,1)}, bf16[4,768,256]{2,1,0:T(8,128)(2,1)S(1)}, u32[]{:S(2)}, u32[]{:S(2)}) collective-permute-start(bf16[4,768,256]{2,1,0:T(8,128)(2,1)} %copy-done.120), channel_id=1, source_target_pairs={{0,4},{4,0},{8,12},{12,8},{16,20},{20,16},{24,28},{28,24},{1,5},{5... | collective-permute-start | bytes 4718600 | tf_op jit(solution)/shard_map/ppermute | solution.py:53
  396.4 37.1 %collective-permute-start.50 = (bf16[2,768,256]{2,1,0:T(8,128)(2,1)S(1)}, bf16[2,768,256]{2,1,0:T(8,128)(2,1)S(1)}, u32[]{:S(2)}, u32[]{:S(2)}) collective-permute-start(bf16[2,768,256]{2,1,0:T(8,128)(2,1)S(1)} %add_convert_fusion.5), channel_id=1, source_target_pairs={{0,16},{4,20},{8,24},{12,28},{16,0},{20,4},{24,8},{28,12},{1,17},{... | collective-permute-start | bytes 2359304 | tf_op jit(solution)/shard_map/ppermute | solution.py:53
  433.5 47.5 %collective-permute-start.54 = (bf16[4,768,256]{2,1,0:T(8,128)(2,1)S(1)}, bf16[4,768,256]{2,1,0:T(8,128)(2,1)}, u32[]{:S(2)}, u32[]{:S(2)}) collective-permute-start(bf16[4,768,256]{2,1,0:T(8,128)(2,1)S(1)} %copy-done.117), channel_id=1, source_target_pairs={{0,4},{4,0},{8,12},{12,8},{16,20},{20,16},{24,28},{28,24},{1,5},{5... | collective-permute-start | bytes 4718600 | tf_op jit(solution)/shard_map/ppermute | solution.py:53
  434.6 46.4 %collective-permute-start.51 = (bf16[256,2048]{1,0:T(8,128)(2,1)}, bf16[256,2048]{1,0:T(8,128)(2,1)}, u32[]{:S(2)}, u32[]{:S(2)}) collective-permute-start(bf16[256,2048]{1,0:T(8,128)(2,1)} %get-tuple-element.335), channel_id=1, source_target_pairs={{0,2},{1,3},{2,0},{3,1},{4,6},{5,7},{6,4},{7,5},{8,10},{9,11},{10,... | collective-permute-start | bytes 3145736 | tf_op jit(solution)/shard_map/ppermute | solution.py:53
  435.4 45.6 %collective-permute-start.52 = (bf16[256,2048]{1,0:T(8,128)(2,1)}, bf16[256,2048]{1,0:T(8,128)(2,1)}, u32[]{:S(2)}, u32[]{:S(2)}) collective-permute-start(bf16[256,2048]{1,0:T(8,128)(2,1)} %get-tuple-element.341), channel_id=1, source_target_pairs={{0,1},{1,0},{2,3},{3,2},{4,5},{5,4},{6,7},{7,6},{8,9},{9,8},{10,11... | collective-permute-start | bytes 3145736 | tf_op jit(solution)/shard_map/ppermute | solution.py:53
  435.4 45.6 %collective-permute-start.53 = (bf16[256,2048]{1,0:T(8,128)(2,1)}, bf16[256,2048]{1,0:T(8,128)(2,1)}, u32[]{:S(2)}, u32[]{:S(2)}) collective-permute-start(bf16[256,2048]{1,0:T(8,128)(2,1)} %get-tuple-element.343), channel_id=1, source_target_pairs={{0,3},{1,2},{2,1},{3,0},{4,7},{5,6},{6,5},{7,4},{8,11},{9,10},{10,... | collective-permute-start | bytes 3145736 | tf_op jit(solution)/shard_map/ppermute | solution.py:53
  481.0 41.1 %collective-permute-start.56 = (bf16[2,256,2048]{2,1,0:T(8,128)(2,1)}, bf16[2,256,2048]{2,1,0:T(8,128)(2,1)}, u32[]{:S(2)}, u32[]{:S(2)}) collective-permute-start(bf16[2,256,2048]{2,1,0:T(8,128)(2,1)} %bitcast.250), channel_id=1, source_target_pairs={{0,1},{1,0},{2,3},{3,2},{4,5},{5,4},{6,7},{7,6},{8,9},{9,8},{10,11... | collective-permute-start | bytes 6291464 | tf_op jit(solution)/shard_map/ppermute | solution.py:53
  482.1 39.9 %collective-permute-start.57 = (bf16[4,768,256]{2,1,0:T(8,128)(2,1)}, bf16[4,768,256]{2,1,0:T(8,128)(2,1)S(1)}, u32[]{:S(2)}, u32[]{:S(2)}) collective-permute-start(bf16[4,768,256]{2,1,0:T(8,128)(2,1)} %copy-done.118), channel_id=1, source_target_pairs={{0,4},{4,0},{8,12},{12,8},{16,20},{20,16},{24,28},{28,24},{1,5},{5... | collective-permute-start | bytes 4718600 | tf_op jit(solution)/shard_map/ppermute | solution.py:53
  484.5 37.5 %collective-permute-start.58 = (bf16[2,768,256]{2,1,0:T(8,128)(2,1)S(1)}, bf16[2,768,256]{2,1,0:T(8,128)(2,1)S(1)}, u32[]{:S(2)}, u32[]{:S(2)}) collective-permute-start(bf16[2,768,256]{2,1,0:T(8,128)(2,1)S(1)} %add_convert_fusion.3), channel_id=1, source_target_pairs={{0,16},{4,20},{8,24},{12,28},{16,0},{20,4},{24,8},{28,12},{1,17},{... | collective-permute-start | bytes 2359304 | tf_op jit(solution)/shard_map/ppermute | solution.py:53
  522.1 39.3 %collective-permute-start.62 = (bf16[4,768,256]{2,1,0:T(8,128)(2,1)}, bf16[4,768,256]{2,1,0:T(8,128)(2,1)}, u32[]{:S(2)}, u32[]{:S(2)}) collective-permute-start(bf16[4,768,256]{2,1,0:T(8,128)(2,1)} %get-tuple-element.372), channel_id=1, source_target_pairs={{0,4},{4,0},{8,12},{12,8},{16,20},{20,16},{24,28},{28,24},{1,5},{5... | collective-permute-start | bytes 4718600 | tf_op jit(solution)/shard_map/ppermute | solution.py:53
  561.4 44.2 %collective-permute-start.67 = (bf16[2,256,2048]{2,1,0:T(8,128)(2,1)S(1)}, bf16[2,256,2048]{2,1,0:T(8,128)(2,1)}, u32[]{:S(2)}, u32[]{:S(2)}) collective-permute-start(bf16[2,256,2048]{2,1,0:T(8,128)(2,1)S(1)} %pad_maximum_fusion.6), channel_id=1, source_target_pairs={{0,1},{1,0},{2,3},{3,2},{4,5},{5,4},{6,7},{7,6},{8,9},{9,8},{10,11... | collective-permute-start | bytes 6291464 | tf_op jit(solution)/shard_map/ppermute | solution.py:53
  561.5 44.1 %collective-permute-start.66 = (bf16[4,1,5,4,64,128]{5,4,3,2,1,0:T(8,128)(2,1)S(1)}, bf16[4,1,5,4,64,128]{5,4,3,2,1,0:T(8,128)(2,1)}, u32[]{:S(2)}, u32[]{:S(2)}) collective-permute-start(bf16[4,1,5,4,64,128]{5,4,3,2,1,0:T(8,128)(2,1)S(1)} %copy-done.69), channel_id=1, source_target_pairs={{0,4},{4,0},{8,12},{12,8},{16,20},{20,16},{24,28},{28,24},{1,5},{5... | collective-permute-start | bytes 3932168 | tf_op jit(solution)/shard_map/ppermute | solution.py:53
  565.2 40.4 %collective-permute-start.65 = (bf16[1,256,2048]{2,1,0:T(8,128)(2,1)}, bf16[1,256,2048]{2,1,0:T(8,128)(2,1)}, u32[]{:S(2)}, u32[]{:S(2)}) collective-permute-start(bf16[1,256,2048]{2,1,0:T(8,128)(2,1)} %fusion.3), channel_id=1, source_target_pairs={{0,2},{1,3},{2,0},{3,1},{4,6},{5,7},{6,4},{7,5},{8,10},{9,11},{10,... | collective-permute-start | bytes 3145736 | tf_op jit(solution)/shard_map/ppermute | solution.py:53
  605.6 42.3 %collective-permute-start.72 = (bf16[4,768,256]{2,1,0:T(8,128)(2,1)}, bf16[4,768,256]{2,1,0:T(8,128)(2,1)}, u32[]{:S(2)}, u32[]{:S(2)}) collective-permute-start(bf16[4,768,256]{2,1,0:T(8,128)(2,1)} %get-tuple-element.401), channel_id=1, source_target_pairs={{0,4},{4,0},{8,12},{12,8},{16,20},{20,16},{24,28},{28,24},{1,5},{5... | collective-permute-start | bytes 4718600 | tf_op jit(solution)/shard_map/ppermute | solution.py:53
  (211 other events, 3764.7 us)

commit v6 on v5

--- a/solution.py
+++ b/solution.py
@@ -990,9 +990,9 @@
     t_h_two = TensorGather(h_two_own)
     t_h_one = TensorGather(h_one)
     rows_all = sp_rows * n_tensor
-    link.go(t_d_ffn, g_ff[1], g_ff[2], g_ff[3], during=[h_two_own])
+    link.go(g_ff[1], g_ff[2], g_ff[3], during=[h_two_own], ends=[t_d_ffn.stack])
+    link.go(t_h_two, t_d_ffn, g_ff[2], g_ff[3], g_ff[4])
     d_ffn = t_d_ffn.rows()
-    link.go(t_h_two, g_ff[2], g_ff[3], g_ff[4])
     link.go(t_h_two, t_h_one, g_ff[3], g_ff[4], g_ff[5])
     h_two = t_h_two.rows()
     steps = n_tensor // 2
@@ -1224,23 +1224,12 @@
     t_query_back = TensorExchange(d_q_low)
     link.go(t_attn, s_ff[4], s_ff[3], s_ff[2], during=[d_q_low])
     add_grads(5)
-    link.go(t_attn, t_query_back, s_keys, s_ff[4], t_ffn, during=[sent[5]])
-    ffn_terms = t_ffn.terms()
-    outputs = pl.pallas_call(
-        functools.partial(finish_kernel, tuple(order)),
-        grid=(1,),
-        in_specs=[smem, square, whole((sp_rows, 1))] + [first_spec] * len(ffn_terms),
-        out_specs=square,
-        out_shape=low_square,
-        compiler_params=params(),
-        cost_estimate=SMALL,
-        name="finish",
-    )(index, mixed, live, *ffn_terms)
+    link.go(t_attn, t_query_back, s_keys, s_ff[4], s_ff[3], during=[sent[5]])
     d_attn = t_attn.rows()
     out_halves = product(d_attn, t_heads.rows())
-    link.go(t_query_back, s_keys, s_ff[5], s_ff[3], s_ff[4], during=[*out_halves, outputs])
+    link.go(t_query_back, s_keys, s_ff[5], s_ff[4], during=out_halves)
     s_out = sum_of(out_halves)
-    link.go(s_keys, s_out, s_ff[5])
+    link.go(s_keys, s_out, s_ff[5], t_ffn)
     d_kv = s_keys.result()
     query_halves = product(h_one_all, after(t_query_back.rows(), d_kv))
     s_query = sum_of(query_halves)
@@ -1309,7 +1298,18 @@
 
     early_sums = collect(0, FF_LAST)
     link.done += [*query_halves, *early_sums, grad_rel]
-    link.go(t_kv_back, s_out, s_query)
+    ffn_terms = t_ffn.terms()
+    outputs = pl.pallas_call(
+        functools.partial(finish_kernel, tuple(order)),
+        grid=(1,),
+        in_specs=[smem, square, whole((sp_rows, 1))] + [first_spec] * len(ffn_terms),
+        out_specs=square,
+        out_shape=low_square,
+        compiler_params=params(),
+        cost_estimate=SMALL,
+        name="finish",
+    )(index, mixed, live, *ffn_terms)
+    link.go(t_kv_back, s_out, s_query, during=[outputs])
     grad_inputs = call(
         functools.partial(leave_kernel, tuple(order)),
         low_square,

time: 763 us -> 754 us (0.988)
    unnamed x302 -> x277, local copies, waits for them, and re-layouts: 46.3 us -> 40.3 us
    concatenate x25 -> x24, other arithmetic: 18.7 us -> 15.4 us  [join(): both = jnp.concatenate([first, second], axis=0)]
  transfers between devices with their start and end apart: 94 -> 94, of which waited for: 40 -> 40; matrix products, arithmetic and copies ran while one was open for 9% -> 10% of each run, Pallas kernels for 35% -> 35%
where the time goes in v6:
time: 754 us; the launch traced here: 743 us
  waiting for transfers between devices  280 us (37%)
  Pallas kernels  256 us (34%)
  starting transfers between devices  94 us (12%)
  other arithmetic  59.8 us (8%)
  local copies, waits for them, and re-layouts  50 us (7%)
    ppermute x94, waiting for transfers between devices, swap(): return lax.ppermute(value, axis, [(i, i ^ mask) for i in range(size)])  280 us
    ppermute x94, starting transfers between devices, swap(): return lax.ppermute(value, axis, [(i, i ^ mask) for i in range(size)])  94 us
    pallas_call x6, Pallas kernels, hidden_part(): pl.pallas_call(functools.partial(hidden_kernel, [places for _, places in...  49.3 us
    pallas_call x6, Pallas kernels, grads_of(): pl.pallas_call(grads_kernel, grid=(grid,), in_specs=[block] * 4 + [whole(...  40.9 us
    unnamed x277, local copies, waits for them, and re-layouts  40.3 us
    pallas_call x2, Pallas kernels, back_sum(): pl.pallas_call(functools.partial(back_sum_kernel, [[places for _, places...  32.9 us
    pallas_call x2, Pallas kernels, attend_back(): pl.pallas_call(attend_back_kernel, grid=(rows, count), in_specs=[q_part,...  32.7 us
    convert_element_type x19, other arithmetic, plus(): return total.astype(kind)  26.3 us
  transfers between devices with their start and end apart: 94, of which 40 were waited for; matrix products, arithmetic and copies ran while one was open for 10% of the time, Pallas kernels for 35%

profile of v6, /device:TPU:0, one launch (start us, length us, event | category | flops | bytes accessed | tf_op | source)
XLA Modules:
  0.0 743.1 jit_solution(4443965417733044043)
XLA Ops:
  31.9 9.1 %collective-permute-done.6 = bf16[4,128,640]{2,1,0:T(8,128)(2,1)S(1)} collective-permute-done((bf16[4,128,640]{2,1,0:T(8,128)(2,1)S(1)}, bf16[4,128,640]{2,1,0:T(8,128)(2,1)S(1)}, u32[]{:S(2)}, u32[]{:S(2)}) %collective-permute-start.6) | collective-permute-done | bytes 655392 | tf_op jit(solution)/shard_map/ppermute | solution.py:53
  51.1 10.9 %collective-permute-done.9 = bf16[4,2,256]{2,1,0:T(2,128)(2,1)S(1)} collective-permute-done((bf16[4,2,256]{2,1,0:T(2,128)(2,1)S(1)}, bf16[4,2,256]{2,1,0:T(2,128)(2,1)S(1)}, u32[]{:S(2)}, u32[]{:S(2)}) %collective-permute-start.9) | collective-permute-done | bytes 4128 | tf_op jit(solution)/shard_map/ppermute | solution.py:53
  78.8 17.9 %collective-permute-done.14 = bf16[1,8,320,256]{3,2,1,0:T(8,128)(2,1)S(1)} collective-permute-done((bf16[1,8,320,256]{3,2,1,0:T(8,128)(2,1)S(1)}, bf16[1,8,320,256]{3,2,1,0:T(8,128)(2,1)S(1)}, u32[]{:S(2)}, u32[]{:S(2)}) %collective-permute-start.14) | collective-permute-done | bytes 1310752 | tf_op jit(solution)/shard_map/ppermute | solution.py:53
  96.9 8.3 %collective-permute-done.17 = bf16[2,256,768]{2,1,0:T(8,128)(2,1)S(1)} collective-permute-done((bf16[2,256,768]{2,1,0:T(8,128)(2,1)S(1)}, bf16[2,256,768]{2,1,0:T(8,128)(2,1)S(1)}, u32[]{:S(2)}, u32[]{:S(2)}) %collective-permute-start.17) | collective-permute-done | bytes 786464 | tf_op jit(solution)/shard_map/ppermute | solution.py:53
  110.4 27.4 %collective-permute-done.21 = bf16[1,8,320,256]{3,2,1,0:T(8,128)(2,1)S(1)} collective-permute-done((bf16[1,8,320,256]{3,2,1,0:T(8,128)(2,1)S(1)}, bf16[1,8,320,256]{3,2,1,0:T(8,128)(2,1)S(1)}, u32[]{:S(2)}, u32[]{:S(2)}) %collective-permute-start.21) | collective-permute-done | bytes 1310752 | tf_op jit(solution)/shard_map/ppermute | solution.py:53
  154.1 12.7 %query.1 = (f32[4,256,320]{2,1,0:T(8,128)S(1)}, bf16[1,5,4,4,64,128]{5,4,3,2,1,0:T(8,128)(2,1)S(1)}) custom-call(bf16[256,2048]{1,0:T(8,128)(2,1)S(1)} %copy-done.17, bf16[4,8,320,256]{3,2,1,0:T(8,128)(2,1)} %copy-done.112, f32[256,64]{1,0:T(8,128)S(1)} %get-tuple-element.501.cos_ref, f32[256,64]{1,0:T(8,128)S(1)} %get-tuple-element.502.sin_ref, ...), custom_call_target="tpu_custom_call" | custom-call | flops 1000 | bytes 1000 | tf_op jit(solution)/shard_map/query/pallas_call | solution.py:922
  172.0 11.4 %collective-permute-done.27 = bf16[2,256,768]{2,1,0:T(8,128)(2,1)} collective-permute-done((bf16[2,256,768]{2,1,0:T(8,128)(2,1)}, bf16[2,256,768]{2,1,0:T(8,128)(2,1)}, u32[]{:S(2)}, u32[]{:S(2)}) %collective-permute-start.27) | collective-permute-done | bytes 786464 | tf_op jit(solution)/shard_map/ppermute | solution.py:53
  195.9 19.0 %attend.1.o_ref = bf16[1,5,4,4,64,128]{5,4,3,2,1,0:T(8,128)(2,1)S(1)} custom-call(bf16[1,5,4,4,64,128]{5,4,3,2,1,0:T(8,128)(2,1)S(1)} %copy-done.12, s32[1,4,1,256]{3,2,1,0:T(1,128)S(1)} %broadcast_in_dim.96.limit_ref, s32[1,2048,1]{2,1,0:T(8,128)S(1)} %copy-done.9, bf16[4,1,5,4,64,128]{5,4,3,2,1,0:T(8,128)(2,1)} %pad_maximum_fusion.12.low_ref, ...), custom_call_target="tpu_custom_call" | custom-call | flops 1000 | bytes 1000 | tf_op jit(solution)/shard_map/attend/pallas_call | solution.py:953
  214.9 7.8 %out.1 = (f32[256,2048]{1,0:T(8,128)}, bf16[256,2048]{1,0:T(8,128)(2,1)S(1)}, bf16[4,256,320]{2,1,0:T(8,128)(2,1)S(1)}) custom-call(bf16[1,5,4,4,64,128]{5,4,3,2,1,0:T(8,128)(2,1)S(1)} %attend.1.o_ref, bf16[2,8,320,256]{3,2,1,0:T(8,128)(2,1)} %pad_maximum_fusion.2.w_low, bf16[2,8,320,256]{3,2,1,0:T(8,128)(2,1)} %collective-permute-done.25.w_high, ...), custom_call_target="tpu_custom_call" | custom-call | flops 1000 | bytes 1000 | tf_op jit(solution)/shard_map/out/pallas_call | solution.py:968
  232.5 20.6 %collective-permute-done.32 = bf16[1,256,2048]{2,1,0:T(8,128)(2,1)S(1)} collective-permute-done((bf16[1,256,2048]{2,1,0:T(8,128)(2,1)S(1)}, bf16[1,256,2048]{2,1,0:T(8,128)(2,1)S(1)}, u32[]{:S(2)}, u32[]{:S(2)}) %collective-permute-start.32) | collective-permute-done | bytes 1048608 | tf_op jit(solution)/shard_map/ppermute | solution.py:53
  255.1 11.4 %collective-permute-done.35 = bf16[2,256,768]{2,1,0:T(8,128)(2,1)S(1)} collective-permute-done((bf16[2,256,768]{2,1,0:T(8,128)(2,1)S(1)}, bf16[2,256,768]{2,1,0:T(8,128)(2,1)S(1)}, u32[]{:S(2)}, u32[]{:S(2)}) %collective-permute-start.35) | collective-permute-done | bytes 786464 | tf_op jit(solution)/shard_map/ppermute | solution.py:53
  272.4 22.7 %collective-permute-done.40 = bf16[1,256,2048]{2,1,0:T(8,128)(2,1)S(1)} collective-permute-done((bf16[1,256,2048]{2,1,0:T(8,128)(2,1)S(1)}, bf16[1,256,2048]{2,1,0:T(8,128)(2,1)S(1)}, u32[]{:S(2)}, u32[]{:S(2)}) %collective-permute-start.40) | collective-permute-done | bytes 1048608 | tf_op jit(solution)/shard_map/ppermute | solution.py:53
  295.3 11.1 %collective-permute-done.39 = bf16[2,256,768]{2,1,0:T(8,128)(2,1)S(1)} collective-permute-done((bf16[2,256,768]{2,1,0:T(8,128)(2,1)S(1)}, bf16[2,256,768]{2,1,0:T(8,128)(2,1)S(1)}, u32[]{:S(2)}, u32[]{:S(2)}) %collective-permute-start.39) | collective-permute-done | bytes 786464 | tf_op jit(solution)/shard_map/ppermute | solution.py:53
  311.6 7.8 %hidden.6 = (bf16[1024,256]{1,0:T(8,128)(2,1)S(1)}, bf16[1024,512]{1,0:T(8,128)(2,1)S(1)}, bf16[768,1024]{1,0:T(8,128)(2,1)S(1)}) custom-call(bf16[512,2048]{1,0:T(8,128)(2,1)} %bitcast.202, bf16[512,2048]{1,0:T(8,128)(2,1)} %bitcast.238, bf16[512,2048]{1,0:T(8,128)(2,1)} %bitcast.214, bf16[512,2048]{1,0:T(8,128)(2,1)} %bitcast.226, ...), custom_call_target="tpu_custom_call" | custom-call | flops 1000 | bytes 1000 | tf_op jit(solution)/shard_map/hidden/pallas_call | solution.py:1010
  329.1 8.2 %hidden.8 = (bf16[1024,256]{1,0:T(8,128)(2,1)S(1)}, bf16[1024,512]{1,0:T(8,128)(2,1)S(1)}, bf16[768,1024]{1,0:T(8,128)(2,1)S(1)}) custom-call(bf16[512,2048]{1,0:T(8,128)(2,1)} %bitcast.204, bf16[512,2048]{1,0:T(8,128)(2,1)} %bitcast.240, bf16[512,2048]{1,0:T(8,128)(2,1)} %bitcast.216, bf16[512,2048]{1,0:T(8,128)(2,1)} %bitcast.228, ...), custom_call_target="tpu_custom_call" | custom-call | flops 1000 | bytes 1000 | tf_op jit(solution)/shard_map/hidden/pallas_call | solution.py:1010
  338.5 8.6 %hidden.7 = (bf16[1024,256]{1,0:T(8,128)(2,1)S(1)}, bf16[1024,512]{1,0:T(8,128)(2,1)S(1)}, bf16[768,1024]{1,0:T(8,128)(2,1)S(1)}) custom-call(bf16[512,2048]{1,0:T(8,128)(2,1)} %bitcast.205, bf16[512,2048]{1,0:T(8,128)(2,1)} %bitcast.241, bf16[512,2048]{1,0:T(8,128)(2,1)} %bitcast.217, bf16[512,2048]{1,0:T(8,128)(2,1)} %bitcast.229, ...), custom_call_target="tpu_custom_call" | custom-call | flops 1000 | bytes 1000 | tf_op jit(solution)/shard_map/hidden/pallas_call | solution.py:1010
  372.3 8.3 %hidden.9 = (bf16[1024,256]{1,0:T(8,128)(2,1)S(1)}, bf16[1024,512]{1,0:T(8,128)(2,1)S(1)}, bf16[768,1024]{1,0:T(8,128)(2,1)S(1)}) custom-call(bf16[512,2048]{1,0:T(8,128)(2,1)} %bitcast.208, bf16[512,2048]{1,0:T(8,128)(2,1)} %bitcast.244, bf16[512,2048]{1,0:T(8,128)(2,1)} %bitcast.220, bf16[512,2048]{1,0:T(8,128)(2,1)} %bitcast.232, ...), custom_call_target="tpu_custom_call" | custom-call | flops 1000 | bytes 1000 | tf_op jit(solution)/shard_map/hidden/pallas_call | solution.py:1010
  381.6 8.4 %hidden.10 = (bf16[1024,256]{1,0:T(8,128)(2,1)S(1)}, bf16[1024,512]{1,0:T(8,128)(2,1)S(1)}, bf16[768,1024]{1,0:T(8,128)(2,1)S(1)}) custom-call(bf16[512,2048]{1,0:T(8,128)(2,1)} %bitcast.209, bf16[512,2048]{1,0:T(8,128)(2,1)} %bitcast.245, bf16[512,2048]{1,0:T(8,128)(2,1)} %bitcast.221, bf16[512,2048]{1,0:T(8,128)(2,1)} %bitcast.233, ...), custom_call_target="tpu_custom_call" | custom-call | flops 1000 | bytes 1000 | tf_op jit(solution)/shard_map/hidden/pallas_call | solution.py:1010
  394.4 8.0 %hidden.11 = (bf16[1024,256]{1,0:T(8,128)(2,1)S(1)}, bf16[1024,512]{1,0:T(8,128)(2,1)S(1)}, bf16[768,1024]{1,0:T(8,128)(2,1)}) custom-call(bf16[512,2048]{1,0:T(8,128)(2,1)} %bitcast.210, bf16[512,2048]{1,0:T(8,128)(2,1)} %bitcast.246, bf16[512,2048]{1,0:T(8,128)(2,1)} %bitcast.222, bf16[512,2048]{1,0:T(8,128)(2,1)} %bitcast.234, ...), custom_call_target="tpu_custom_call" | custom-call | flops 1000 | bytes 1000 | tf_op jit(solution)/shard_map/hidden/pallas_call | solution.py:1010
  404.5 20.8 %back_sum.3 = (bf16[256,2048]{1,0:T(8,128)(2,1)S(1)}, bf16[256,2048]{1,0:T(8,128)(2,1)}, bf16[256,2048]{1,0:T(8,128)(2,1)}, bf16[256,2048]{1,0:T(8,128)(2,1)}) custom-call(bf16[1024,512]{1,0:T(8,128)(2,1)} %copy-done.64, bf16[1024,512]{1,0:T(8,128)(2,1)} %copy-done.66, bf16[1024,512]{1,0:T(8,128)(2,1)} %copy-done.65, bf16[1024,512]{1,0:T(8,128)(2,1)} %copy-done.67, ...), custom_call_target="tpu_custom_call" | custom-call | flops 1000 | bytes 1000 | tf_op jit(solution)/shard_map/back_sum/pallas_call | solution.py:1083
  436.1 12.1 %back_sum.2 = (bf16[512,2048]{1,0:T(8,128)(2,1)}, bf16[512,2048]{1,0:T(8,128)(2,1)}) custom-call(bf16[1024,256]{1,0:T(8,128)(2,1)S(1)} %get-tuple-element.287.refs_0_, bf16[1024,256]{1,0:T(8,128)(2,1)S(1)} %copy-done.84, bf16[1024,256]{1,0:T(8,128)(2,1)S(1)} %get-tuple-element.289.refs_2_, bf16[1024,256]{1,0:T(8,128)(2,1)S(1)} %get-tuple-element.291.refs_3_, ...), custom_call_target="tpu_custom_call" | custom-call | flops 1000 | bytes 1000 | tf_op jit(solution)/shard_map/back_sum/pallas_call | solution.py:1083
  455.9 8.1 %weight_grads.10 = (bf16[4,768,256]{2,1,0:T(8,128)(2,1)S(1)}, bf16[4,768,256]{2,1,0:T(8,128)(2,1)}) custom-call(bf16[512,2048]{1,0:T(8,128)(2,1)} %bitcast.212, bf16[512,2048]{1,0:T(8,128)(2,1)} %bitcast.248, bf16[512,2048]{1,0:T(8,128)(2,1)} %bitcast.224, bf16[512,2048]{1,0:T(8,128)(2,1)} %bitcast.236, bf16[768,1024]{1,0:T(8,128)(2,1)S(1)} %copy-done.57), custom_call_target="tpu_custom_call" | custom-call | flops 1000 | bytes 1000 | tf_op jit(solution)/shard_map/weight_grads/pallas_call | solution.py:1047
  464.0 8.4 %collective-permute-done.55.refs_6_ = bf16[2,768,256]{2,1,0:T(8,128)(2,1)} collective-permute-done((bf16[2,768,256]{2,1,0:T(8,128)(2,1)}, bf16[2,768,256]{2,1,0:T(8,128)(2,1)}, u32[]{:S(2)}, u32[]{:S(2)}) %collective-permute-start.55) | collective-permute-done | bytes 786464 | tf_op jit(solution)/shard_map/ppermute | solution.py:53
  501.4 19.0 %attend_back.2 = (f32[1,5,4,4,64,128]{5,4,3,2,1,0:T(8,128)}, bf16[4,1,5,4,64,128]{5,4,3,2,1,0:T(8,128)(2,1)S(1)}, bf16[4,1,5,4,64,128]{5,4,3,2,1,0:T(8,128)(2,1)}) custom-call(bf16[1,5,4,4,64,128]{5,4,3,2,1,0:T(8,128)(2,1)S(1)} %copy-done.13, bf16[1,5,4,4,64,128]{5,4,3,2,1,0:T(8,128)(2,1)} %copy-done.14, s32[1,4,1,256]{3,2,1,0:T(1,128)S(1)} %broadcast_in_dim.96.limit_ref, ...), custom_call_target="tpu_custom_call" | custom-call | flops 1000 | bytes 1000 | tf_op jit(solution)/shard_map/attend_back/pallas_call | solution.py:1150
  527.8 13.7 %attend_back.3 = (f32[1,5,4,4,64,128]{5,4,3,2,1,0:T(8,128)}, bf16[4,1,5,4,64,128]{5,4,3,2,1,0:T(8,128)(2,1)S(1)}, bf16[4,1,5,4,64,128]{5,4,3,2,1,0:T(8,128)(2,1)}) custom-call(bf16[1,5,4,4,64,128]{5,4,3,2,1,0:T(8,128)(2,1)S(1)} %copy-done.13, bf16[1,5,4,4,64,128]{5,4,3,2,1,0:T(8,128)(2,1)} %copy-done.14, ...), custom_call_target="tpu_custom_call", output_to_operand_aliasing={{0}: (6, {}), {1}: (7, {}), {2}: (8, {})} | custom-call | flops 1000 | bytes 1000 | tf_op jit(solution)/shard_map/attend_back/pallas_call | solution.py:1150
  551.3 8.4 %collective-permute-done.63.refs_14_ = bf16[2,768,256]{2,1,0:T(8,128)(2,1)S(1)} collective-permute-done((bf16[2,768,256]{2,1,0:T(8,128)(2,1)}, bf16[2,768,256]{2,1,0:T(8,128)(2,1)S(1)}, u32[]{:S(2)}, u32[]{:S(2)}) %collective-permute-start.63) | collective-permute-done | bytes 786464 | tf_op jit(solution)/shard_map/ppermute | solution.py:53
  581.6 9.6 %collective-permute-done.69.refs_15_ = bf16[1,768,256]{2,1,0:T(8,128)(2,1)} collective-permute-done((bf16[1,768,256]{2,1,0:T(8,128)(2,1)}, bf16[1,768,256]{2,1,0:T(8,128)(2,1)}, u32[]{:S(2)}, u32[]{:S(2)}) %collective-permute-start.69) | collective-permute-done | bytes 393248 | tf_op jit(solution)/shard_map/ppermute | solution.py:53
  591.2 10.9 %collective-permute-done.68.refs_18_ = bf16[2,768,256]{2,1,0:T(8,128)(2,1)} collective-permute-done((bf16[2,768,256]{2,1,0:T(8,128)(2,1)}, bf16[2,768,256]{2,1,0:T(8,128)(2,1)}, u32[]{:S(2)}, u32[]{:S(2)}) %collective-permute-start.68) | collective-permute-done | bytes 786464 | tf_op jit(solution)/shard_map/ppermute | solution.py:53
  618.3 11.2 %collective-permute-done.73.refs_19_ = bf16[1,768,256]{2,1,0:T(8,128)(2,1)S(1)} collective-permute-done((bf16[1,768,256]{2,1,0:T(8,128)(2,1)S(1)}, bf16[1,768,256]{2,1,0:T(8,128)(2,1)S(1)}, u32[]{:S(2)}, u32[]{:S(2)}) %collective-permute-start.73) | collective-permute-done | bytes 393248 | tf_op jit(solution)/shard_map/ppermute | solution.py:53
  629.5 7.8 %collective-permute-done.71 = bf16[2,1,5,4,64,128]{5,4,3,2,1,0:T(8,128)(2,1)S(1)} collective-permute-done((bf16[2,1,5,4,64,128]{5,4,3,2,1,0:T(8,128)(2,1)S(1)}, bf16[2,1,5,4,64,128]{5,4,3,2,1,0:T(8,128)(2,1)S(1)}, u32[]{:S(2)}, u32[]{:S(2)}) %collective-permute-start.71) | collective-permute-done | bytes 655392 | tf_op jit(solution)/shard_map/ppermute | solution.py:53
  653.8 8.5 %h_one_back.1 = (bf16[256,2048]{1,0:T(8,128)(2,1)S(1)}, f32[1,2048]{1,0:T(1,128)S(1)}) custom-call(bf16[4,256,320]{2,1,0:T(8,128)(2,1)S(1)} %copy-done.43, bf16[4,8,320,256]{3,2,1,0:T(8,128)(2,1)} %copy-done.112, bf16[256,640]{1,0:T(8,128)(2,1)S(1)} %get-tuple-element.410.dkv_ref, bf16[2048,640]{1,0:T(8,128)(2,1)} %bitcast.156, ...), custom_call_target="tpu_custom_call" | custom-call | flops 1000 | bytes 1000 | tf_op jit(solution)/shard_map/h_one_back/pallas_call | solution.py:1253
  711.5 7.7 %collective-permute-done.83 = bf16[2,320,256]{2,1,0:T(8,128)(2,1)S(1)} collective-permute-done((bf16[2,320,256]{2,1,0:T(8,128)(2,1)S(1)}, bf16[2,320,256]{2,1,0:T(8,128)(2,1)S(1)}, u32[]{:S(2)}, u32[]{:S(2)}) %collective-permute-start.83) | collective-permute-done | bytes 327712 | tf_op jit(solution)/shard_map/ppermute | solution.py:53
  (588 shorter events, 354.7 us)
Async XLA Ops:
  105.3 37.1 %collective-permute-start.19 = (bf16[2,8,320,256]{3,2,1,0:T(8,128)(2,1)S(1)}, bf16[2,8,320,256]{3,2,1,0:T(8,128)(2,1)S(1)}, u32[]{:S(2)}, u32[]{:S(2)}) collective-permute-start(bf16[2,8,320,256]{3,2,1,0:T(8,128)(2,1)S(1)} %pad_maximum_fusion), channel_id=1, source_target_pairs={{0,1},{1,0},{2,3},{3,2},{4,5},{5,4},{6,7},{7,6},{8,9},{9,8},{10,11... | collective-permute-start | bytes 7864328 | tf_op jit(solution)/shard_map/ppermute | solution.py:53
  142.3 43.8 %collective-permute-start.25 = (bf16[2,8,320,256]{3,2,1,0:T(8,128)(2,1)}, bf16[2,8,320,256]{3,2,1,0:T(8,128)(2,1)}, u32[]{:S(2)}, u32[]{:S(2)}) collective-permute-start(bf16[2,8,320,256]{3,2,1,0:T(8,128)(2,1)} %pad_maximum_fusion.2.w_low), channel_id=1, source_target_pairs={{0,1},{1,0},{2,3},{3,2},{4,5},{5,4},{6,7},{7,6},{8,9},{9,8},{10,11... | collective-permute-start | bytes 7864328 | tf_op jit(solution)/shard_map/ppermute | solution.py:53
  143.7 42.3 %collective-permute-start.24 = (bf16[4,1,5,4,64,128]{5,4,3,2,1,0:T(8,128)(2,1)}, bf16[4,1,5,4,64,128]{5,4,3,2,1,0:T(8,128)(2,1)}, u32[]{:S(2)}, u32[]{:S(2)}) collective-permute-start(bf16[4,1,5,4,64,128]{5,4,3,2,1,0:T(8,128)(2,1)} %pad_maximum_fusion.12.low_ref), channel_id=1, source_target_pairs={{0,4},{4,0},{8,12},{12,8},{16,20},{20,16},{24,28},{28,24},{1,5},{5... | collective-permute-start | bytes 3932168 | tf_op jit(solution)/shard_map/ppermute | solution.py:53
  144.3 41.8 %collective-permute-start.26 = (bf16[1,256,2048]{2,1,0:T(8,128)(2,1)}, bf16[1,256,2048]{2,1,0:T(8,128)(2,1)}, u32[]{:S(2)}, u32[]{:S(2)}) collective-permute-start(bf16[1,256,2048]{2,1,0:T(8,128)(2,1)} %bitcast.23), channel_id=1, source_target_pairs={{0,2},{1,3},{2,0},{3,1},{4,6},{5,7},{6,4},{7,5},{8,10},{9,11},{10,... | collective-permute-start | bytes 3145736 | tf_op jit(solution)/shard_map/ppermute | solution.py:53
  145.8 37.6 %collective-permute-start.27 = (bf16[2,256,768]{2,1,0:T(8,128)(2,1)}, bf16[2,256,768]{2,1,0:T(8,128)(2,1)}, u32[]{:S(2)}, u32[]{:S(2)}) collective-permute-start(bf16[2,256,768]{2,1,0:T(8,128)(2,1)} %pad_maximum_fusion.16), channel_id=1, source_target_pairs={{0,16},{4,20},{8,24},{12,28},{16,0},{20,4},{24,8},{28,12},{1,17},{... | collective-permute-start | bytes 2359304 | tf_op jit(solution)/shard_map/ppermute | solution.py:53
  186.1 39.5 %collective-permute-start.29 = (bf16[4,256,768]{2,1,0:T(8,128)(2,1)}, bf16[4,256,768]{2,1,0:T(8,128)(2,1)}, u32[]{:S(2)}, u32[]{:S(2)}) collective-permute-start(bf16[4,256,768]{2,1,0:T(8,128)(2,1)} %pad_maximum_fusion.7), channel_id=1, source_target_pairs={{0,4},{4,0},{8,12},{12,8},{16,20},{20,16},{24,28},{28,24},{1,5},{5... | collective-permute-start | bytes 4718600 | tf_op jit(solution)/shard_map/ppermute | solution.py:53
  225.6 40.8 %collective-permute-start.33 = (bf16[2,256,2048]{2,1,0:T(8,128)(2,1)S(1)}, bf16[2,256,2048]{2,1,0:T(8,128)(2,1)S(1)}, u32[]{:S(2)}, u32[]{:S(2)}) collective-permute-start(bf16[2,256,2048]{2,1,0:T(8,128)(2,1)S(1)} %constant_dynamic-update-slice_fusion.2), channel_id=1, source_target_pairs={{0,1},{1,0},{2,3},{3,2},{4,5},{5,4},{6,7},{7,6},{8,9},{9,8},{10,11... | collective-permute-start | bytes 6291464 | tf_op jit(solution)/shard_map/ppermute | solution.py:53
  227.2 39.3 %collective-permute-start.34 = (bf16[4,256,768]{2,1,0:T(8,128)(2,1)S(1)}, bf16[4,256,768]{2,1,0:T(8,128)(2,1)S(1)}, u32[]{:S(2)}, u32[]{:S(2)}) collective-permute-start(bf16[4,256,768]{2,1,0:T(8,128)(2,1)S(1)} %pad_maximum_fusion.8), channel_id=1, source_target_pairs={{0,4},{4,0},{8,12},{12,8},{16,20},{20,16},{24,28},{28,24},{1,5},{5... | collective-permute-start | bytes 4718600 | tf_op jit(solution)/shard_map/ppermute | solution.py:53
  229.4 37.1 %collective-permute-start.35 = (bf16[2,256,768]{2,1,0:T(8,128)(2,1)S(1)}, bf16[2,256,768]{2,1,0:T(8,128)(2,1)S(1)}, u32[]{:S(2)}, u32[]{:S(2)}) collective-permute-start(bf16[2,256,768]{2,1,0:T(8,128)(2,1)S(1)} %pad_maximum_fusion.18), channel_id=1, source_target_pairs={{0,16},{4,20},{8,24},{12,28},{16,0},{20,4},{24,8},{28,12},{1,17},{... | collective-permute-start | bytes 2359304 | tf_op jit(solution)/shard_map/ppermute | solution.py:53
  267.6 39.2 %collective-permute-start.37 = (bf16[2,256,2048]{2,1,0:T(8,128)(2,1)S(1)}, bf16[2,256,2048]{2,1,0:T(8,128)(2,1)S(1)}, u32[]{:S(2)}, u32[]{:S(2)}) collective-permute-start(bf16[2,256,2048]{2,1,0:T(8,128)(2,1)S(1)} %pad_maximum_fusion.3), channel_id=1, source_target_pairs={{0,1},{1,0},{2,3},{3,2},{4,5},{5,4},{6,7},{7,6},{8,9},{9,8},{10,11... | collective-permute-start | bytes 6291464 | tf_op jit(solution)/shard_map/ppermute | solution.py:53
  267.8 39.0 %collective-permute-start.38 = (bf16[4,256,768]{2,1,0:T(8,128)(2,1)S(1)}, bf16[4,256,768]{2,1,0:T(8,128)(2,1)S(1)}, u32[]{:S(2)}, u32[]{:S(2)}) collective-permute-start(bf16[4,256,768]{2,1,0:T(8,128)(2,1)S(1)} %pad_maximum_fusion.9), channel_id=1, source_target_pairs={{0,4},{4,0},{8,12},{12,8},{16,20},{20,16},{24,28},{28,24},{1,5},{5... | collective-permute-start | bytes 4718600 | tf_op jit(solution)/shard_map/ppermute | solution.py:53
  308.1 41.0 %collective-permute-start.44 = (bf16[2,256,2048]{2,1,0:T(8,128)(2,1)S(1)}, bf16[2,256,2048]{2,1,0:T(8,128)(2,1)}, u32[]{:S(2)}, u32[]{:S(2)}) collective-permute-start(bf16[2,256,2048]{2,1,0:T(8,128)(2,1)S(1)} %pad_maximum_fusion.4), channel_id=1, source_target_pairs={{0,1},{1,0},{2,3},{3,2},{4,5},{5,4},{6,7},{7,6},{8,9},{9,8},{10,11... | collective-permute-start | bytes 6291464 | tf_op jit(solution)/shard_map/ppermute | solution.py:53
  308.2 40.8 %collective-permute-start.42 = (bf16[4,256,768]{2,1,0:T(8,128)(2,1)S(1)}, bf16[4,256,768]{2,1,0:T(8,128)(2,1)}, u32[]{:S(2)}, u32[]{:S(2)}) collective-permute-start(bf16[4,256,768]{2,1,0:T(8,128)(2,1)S(1)} %pad_maximum_fusion.10), channel_id=1, source_target_pairs={{0,4},{4,0},{8,12},{12,8},{16,20},{20,16},{24,28},{28,24},{1,5},{5... | collective-permute-start | bytes 4718600 | tf_op jit(solution)/shard_map/ppermute | solution.py:53
  309.6 39.5 %collective-permute-start.43 = (bf16[2,256,768]{2,1,0:T(8,128)(2,1)S(1)}, bf16[2,256,768]{2,1,0:T(8,128)(2,1)S(1)}, u32[]{:S(2)}, u32[]{:S(2)}) collective-permute-start(bf16[2,256,768]{2,1,0:T(8,128)(2,1)S(1)} %pad_maximum_fusion.20), channel_id=1, source_target_pairs={{0,16},{4,20},{8,24},{12,28},{16,0},{20,4},{24,8},{28,12},{1,17},{... | collective-permute-start | bytes 2359304 | tf_op jit(solution)/shard_map/ppermute | solution.py:53
  310.6 38.5 %collective-permute-start.45 = (bf16[2,1,256,320]{3,2,0,1:T(8,128)(2,1)}, bf16[2,1,256,320]{3,2,0,1:T(8,128)(2,1)}, u32[]{:S(2)}, u32[]{:S(2)}) collective-permute-start(bf16[2,1,256,320]{3,2,0,1:T(8,128)(2,1)} %get-tuple-element.307), channel_id=1, source_target_pairs={{0,2},{1,3},{2,0},{3,1},{4,6},{5,7},{6,4},{7,5},{8,10},{9,11},{10,... | collective-permute-start | bytes 983048 | tf_op jit(solution)/shard_map/ppermute | solution.py:53
  349.1 42.1 %collective-permute-start.48 = (bf16[4,768,256]{2,1,0:T(8,128)(2,1)}, bf16[4,768,256]{2,1,0:T(8,128)(2,1)}, u32[]{:S(2)}, u32[]{:S(2)}) collective-permute-start(bf16[4,768,256]{2,1,0:T(8,128)(2,1)} %copy-done.104), channel_id=1, source_target_pairs={{0,4},{4,0},{8,12},{12,8},{16,20},{20,16},{24,28},{28,24},{1,5},{5... | collective-permute-start | bytes 4718600 | tf_op jit(solution)/shard_map/ppermute | solution.py:53
  350.4 40.8 %collective-permute-start.46 = (bf16[2,256,768]{2,1,0:T(8,128)(2,1)S(1)}, bf16[2,256,768]{2,1,0:T(8,128)(2,1)S(1)}, u32[]{:S(2)}, u32[]{:S(2)}) collective-permute-start(bf16[2,256,768]{2,1,0:T(8,128)(2,1)S(1)} %collective-permute-done.41), channel_id=1, source_target_pairs={{0,16},{4,20},{8,24},{12,28},{16,0},{20,4},{24,8},{28,12},{1,17},{... | collective-permute-start | bytes 2359304 | tf_op jit(solution)/shard_map/ppermute | solution.py:53
  391.2 40.3 %collective-permute-start.49 = (bf16[4,768,256]{2,1,0:T(8,128)(2,1)}, bf16[4,768,256]{2,1,0:T(8,128)(2,1)S(1)}, u32[]{:S(2)}, u32[]{:S(2)}) collective-permute-start(bf16[4,768,256]{2,1,0:T(8,128)(2,1)} %copy-done.105), channel_id=1, source_target_pairs={{0,4},{4,0},{8,12},{12,8},{16,20},{20,16},{24,28},{28,24},{1,5},{5... | collective-permute-start | bytes 4718600 | tf_op jit(solution)/shard_map/ppermute | solution.py:53
  394.0 37.5 %collective-permute-start.50 = (bf16[2,768,256]{2,1,0:T(8,128)(2,1)}, bf16[2,768,256]{2,1,0:T(8,128)(2,1)S(1)}, u32[]{:S(2)}, u32[]{:S(2)}) collective-permute-start(bf16[2,768,256]{2,1,0:T(8,128)(2,1)} %add_convert_fusion.5), channel_id=1, source_target_pairs={{0,16},{4,20},{8,24},{12,28},{16,0},{20,4},{24,8},{28,12},{1,17},{... | collective-permute-start | bytes 2359304 | tf_op jit(solution)/shard_map/ppermute | solution.py:53
  431.6 47.6 %collective-permute-start.54 = (bf16[4,768,256]{2,1,0:T(8,128)(2,1)S(1)}, bf16[4,768,256]{2,1,0:T(8,128)(2,1)}, u32[]{:S(2)}, u32[]{:S(2)}) collective-permute-start(bf16[4,768,256]{2,1,0:T(8,128)(2,1)S(1)} %copy-done.102), channel_id=1, source_target_pairs={{0,4},{4,0},{8,12},{12,8},{16,20},{20,16},{24,28},{28,24},{1,5},{5... | collective-permute-start | bytes 4718600 | tf_op jit(solution)/shard_map/ppermute | solution.py:53
  432.8 46.4 %collective-permute-start.51 = (bf16[256,2048]{1,0:T(8,128)(2,1)}, bf16[256,2048]{1,0:T(8,128)(2,1)}, u32[]{:S(2)}, u32[]{:S(2)}) collective-permute-start(bf16[256,2048]{1,0:T(8,128)(2,1)} %get-tuple-element.337), channel_id=1, source_target_pairs={{0,2},{1,3},{2,0},{3,1},{4,6},{5,7},{6,4},{7,5},{8,10},{9,11},{10,... | collective-permute-start | bytes 3145736 | tf_op jit(solution)/shard_map/ppermute | solution.py:53
  433.4 45.8 %collective-permute-start.52 = (bf16[256,2048]{1,0:T(8,128)(2,1)}, bf16[256,2048]{1,0:T(8,128)(2,1)}, u32[]{:S(2)}, u32[]{:S(2)}) collective-permute-start(bf16[256,2048]{1,0:T(8,128)(2,1)} %get-tuple-element.343), channel_id=1, source_target_pairs={{0,1},{1,0},{2,3},{3,2},{4,5},{5,4},{6,7},{7,6},{8,9},{9,8},{10,11... | collective-permute-start | bytes 3145736 | tf_op jit(solution)/shard_map/ppermute | solution.py:53
  433.4 45.8 %collective-permute-start.53 = (bf16[256,2048]{1,0:T(8,128)(2,1)}, bf16[256,2048]{1,0:T(8,128)(2,1)}, u32[]{:S(2)}, u32[]{:S(2)}) collective-permute-start(bf16[256,2048]{1,0:T(8,128)(2,1)} %get-tuple-element.345), channel_id=1, source_target_pairs={{0,3},{1,2},{2,1},{3,0},{4,7},{5,6},{6,5},{7,4},{8,11},{9,10},{10,... | collective-permute-start | bytes 3145736 | tf_op jit(solution)/shard_map/ppermute | solution.py:53
  479.2 41.8 %collective-permute-start.56 = (bf16[2,256,2048]{2,1,0:T(8,128)(2,1)}, bf16[2,256,2048]{2,1,0:T(8,128)(2,1)}, u32[]{:S(2)}, u32[]{:S(2)}) collective-permute-start(bf16[2,256,2048]{2,1,0:T(8,128)(2,1)} %bitcast.276), channel_id=1, source_target_pairs={{0,1},{1,0},{2,3},{3,2},{4,5},{5,4},{6,7},{7,6},{8,9},{9,8},{10,11... | collective-permute-start | bytes 6291464 | tf_op jit(solution)/shard_map/ppermute | solution.py:53
  480.3 40.7 %collective-permute-start.57 = (bf16[4,768,256]{2,1,0:T(8,128)(2,1)}, bf16[4,768,256]{2,1,0:T(8,128)(2,1)S(1)}, u32[]{:S(2)}, u32[]{:S(2)}) collective-permute-start(bf16[4,768,256]{2,1,0:T(8,128)(2,1)} %copy-done.103), channel_id=1, source_target_pairs={{0,4},{4,0},{8,12},{12,8},{16,20},{20,16},{24,28},{28,24},{1,5},{5... | collective-permute-start | bytes 4718600 | tf_op jit(solution)/shard_map/ppermute | solution.py:53
  483.4 37.6 %collective-permute-start.58 = (bf16[2,768,256]{2,1,0:T(8,128)(2,1)}, bf16[2,768,256]{2,1,0:T(8,128)(2,1)S(1)}, u32[]{:S(2)}, u32[]{:S(2)}) collective-permute-start(bf16[2,768,256]{2,1,0:T(8,128)(2,1)} %add_convert_fusion.3), channel_id=1, source_target_pairs={{0,16},{4,20},{8,24},{12,28},{16,0},{20,4},{24,8},{28,12},{1,17},{... | collective-permute-start | bytes 2359304 | tf_op jit(solution)/shard_map/ppermute | solution.py:53
  521.0 40.4 %collective-permute-start.62 = (bf16[4,768,256]{2,1,0:T(8,128)(2,1)}, bf16[4,768,256]{2,1,0:T(8,128)(2,1)}, u32[]{:S(2)}, u32[]{:S(2)}) collective-permute-start(bf16[4,768,256]{2,1,0:T(8,128)(2,1)} %get-tuple-element.374), channel_id=1, source_target_pairs={{0,4},{4,0},{8,12},{12,8},{16,20},{20,16},{24,28},{28,24},{1,5},{5... | collective-permute-start | bytes 4718600 | tf_op jit(solution)/shard_map/ppermute | solution.py:53
  522.2 37.5 %collective-permute-start.61 = (bf16[1,256,2048]{2,1,0:T(8,128)(2,1)S(1)}, bf16[1,256,2048]{2,1,0:T(8,128)(2,1)}, u32[]{:S(2)}, u32[]{:S(2)}) collective-permute-start(bf16[1,256,2048]{2,1,0:T(8,128)(2,1)S(1)} %bitcast.174), channel_id=1, source_target_pairs={{0,2},{1,3},{2,0},{3,1},{4,6},{5,7},{6,4},{7,5},{8,10},{9,11},{10,... | collective-permute-start | bytes 3145736 | tf_op jit(solution)/shard_map/ppermute | solution.py:53
  561.4 40.7 %collective-permute-start.66 = (bf16[2,256,2048]{2,1,0:T(8,128)(2,1)S(1)}, bf16[2,256,2048]{2,1,0:T(8,128)(2,1)}, u32[]{:S(2)}, u32[]{:S(2)}) collective-permute-start(bf16[2,256,2048]{2,1,0:T(8,128)(2,1)S(1)} %pad_maximum_fusion.5), channel_id=1, source_target_pairs={{0,1},{1,0},{2,3},{3,2},{4,5},{5,4},{6,7},{7,6},{8,9},{9,8},{10,11... | collective-permute-start | bytes 6291464 | tf_op jit(solution)/shard_map/ppermute | solution.py:53
  561.5 40.6 %collective-permute-start.67 = (bf16[4,1,5,4,64,128]{5,4,3,2,1,0:T(8,128)(2,1)}, bf16[4,1,5,4,64,128]{5,4,3,2,1,0:T(8,128)(2,1)}, u32[]{:S(2)}, u32[]{:S(2)}) collective-permute-start(bf16[4,1,5,4,64,128]{5,4,3,2,1,0:T(8,128)(2,1)} %get-tuple-element.389), channel_id=1, source_target_pairs={{0,4},{4,0},{8,12},{12,8},{16,20},{20,16},{24,28},{28,24},{1,5},{5... | collective-permute-start | bytes 3932168 | tf_op jit(solution)/shard_map/ppermute | solution.py:53
  565.0 37.1 %collective-permute-start.68 = (bf16[2,768,256]{2,1,0:T(8,128)(2,1)}, bf16[2,768,256]{2,1,0:T(8,128)(2,1)}, u32[]{:S(2)}, u32[]{:S(2)}) collective-permute-start(bf16[2,768,256]{2,1,0:T(8,128)(2,1)} %add_convert_fusion.1), channel_id=1, source_target_pairs={{0,16},{4,20},{8,24},{12,28},{16,0},{20,4},{24,8},{28,12},{1,17},{... | collective-permute-start | bytes 2359304 | tf_op jit(solution)/shard_map/ppermute | solution.py:53
  642.2 37.3 %collective-permute-start.77 = (bf16[2,768,256]{2,1,0:T(8,128)(2,1)}, bf16[2,768,256]{2,1,0:T(8,128)(2,1)}, u32[]{:S(2)}, u32[]{:S(2)}) collective-permute-start(bf16[2,768,256]{2,1,0:T(8,128)(2,1)} %add_convert_fusion), channel_id=1, source_target_pairs={{0,16},{4,20},{8,24},{12,28},{16,0},{20,4},{24,8},{28,12},{1,17},{... | collective-permute-start | bytes 2359304 | tf_op jit(solution)/shard_map/ppermute | solution.py:53
  (198 other events, 3421.7 us)

commit v7 on v6

--- a/solution.py
+++ b/solution.py
@@ -1113,7 +1113,8 @@
     t_ffn = TensorScatter(
         [x.reshape(n_tensor // 2, sp_rows, width) for x in back_sum(hiddens, True, 2)]
     )
-    link.go(t_back, s_ff[2], s_ff[1], during=[*t_ffn.sums, *sent[3:]])
+    back_got = t_back.advance(t_back.value())
+    link.go(s_ff[2], s_ff[1], during=[*t_ffn.sums, *sent[3:]], ends=back_got)
     first_spec = pl.BlockSpec((1, sp_rows, width), lambda i: (0, 0, 0))
     back_terms = t_back.terms()
     d_mixed, d_attn_own, d_gain_two = pl.pallas_call(
@@ -1334,10 +1335,11 @@
 
     s_kv = ScatterSoon(with_small(0), with_small(1))
     link.go(s_kv, s_query, s_out, s_ff[5])
+    s_kv.advance(s_kv.value())
+    t_sums = TensorAll(s_kv.result().astype(bf16))
+    t_sums.advance(t_sums.value())
     sum_in, sum_down = collect(FF_LAST, len(sizes), *early_sums)
-    link.go(s_kv, s_query, during=[sum_in, sum_down])
-    t_sums = TensorAll(s_kv.result().astype(bf16))
-    link.go(t_sums)
+    link.go(s_query, during=[sum_in, sum_down])
     stack = t_sums.stack
     small = jnp.sum(stack[:, kv_part:].astype(f32), axis=0)
     stack = stack[:, :kv_part]

time: 754 us -> 750 us (level)
    unnamed x277 -> x279, local copies, waits for them, and re-layouts: 40.3 us -> 40.3 us
  transfers between devices with their start and end apart: 94 -> 94, of which waited for: 40 -> 34; matrix products, arithmetic and copies ran while one was open for 10% -> 10% of each run, Pallas kernels for 35% -> 35%
where the time goes in v7:
time: 750 us; the launch traced here: 740 us
  waiting for transfers between devices  277 us (37%)
  Pallas kernels  257 us (34%)
  starting transfers between devices  92.6 us (12%)
  other arithmetic  60.7 us (8%)
  local copies, waits for them, and re-layouts  50 us (7%)
    ppermute x94, waiting for transfers between devices, swap(): return lax.ppermute(value, axis, [(i, i ^ mask) for i in range(size)])  277 us
    ppermute x94, starting transfers between devices, swap(): return lax.ppermute(value, axis, [(i, i ^ mask) for i in range(size)])  92.6 us
    pallas_call x6, Pallas kernels, hidden_part(): pl.pallas_call(functools.partial(hidden_kernel, [places for _, places in...  49.3 us
    pallas_call x6, Pallas kernels, grads_of(): pl.pallas_call(grads_kernel, grid=(grid,), in_specs=[block] * 4 + [whole(...  40.9 us
    unnamed x279, local copies, waits for them, and re-layouts  40.3 us
    pallas_call x2, Pallas kernels, back_sum(): pl.pallas_call(functools.partial(back_sum_kernel, [[places for _, places...  32.9 us
    pallas_call x2, Pallas kernels, attend_back(): pl.pallas_call(attend_back_kernel, grid=(rows, count), in_specs=[q_part,...  32.7 us
    convert_element_type x19, other arithmetic, plus(): return total.astype(kind)  26.3 us
  transfers between devices with their start and end apart: 94, of which 34 were waited for; matrix products, arithmetic and copies ran while one was open for 10% of the time, Pallas kernels for 35%

profile of v7, /device:TPU:0, one launch (start us, length us, event | category | flops | bytes accessed | tf_op | source)
XLA Modules:
  0.0 739.8 jit_solution(11749575352014660249)
XLA Ops:
  31.9 9.1 %collective-permute-done.6 = bf16[4,128,640]{2,1,0:T(8,128)(2,1)S(1)} collective-permute-done((bf16[4,128,640]{2,1,0:T(8,128)(2,1)S(1)}, bf16[4,128,640]{2,1,0:T(8,128)(2,1)S(1)}, u32[]{:S(2)}, u32[]{:S(2)}) %collective-permute-start.6) | collective-permute-done | bytes 655392 | tf_op jit(solution)/shard_map/ppermute | solution.py:53
  51.1 10.9 %collective-permute-done.9 = bf16[4,2,256]{2,1,0:T(2,128)(2,1)S(1)} collective-permute-done((bf16[4,2,256]{2,1,0:T(2,128)(2,1)S(1)}, bf16[4,2,256]{2,1,0:T(2,128)(2,1)S(1)}, u32[]{:S(2)}, u32[]{:S(2)}) %collective-permute-start.9) | collective-permute-done | bytes 4128 | tf_op jit(solution)/shard_map/ppermute | solution.py:53
  78.8 17.9 %collective-permute-done.14 = bf16[1,8,320,256]{3,2,1,0:T(8,128)(2,1)S(1)} collective-permute-done((bf16[1,8,320,256]{3,2,1,0:T(8,128)(2,1)S(1)}, bf16[1,8,320,256]{3,2,1,0:T(8,128)(2,1)S(1)}, u32[]{:S(2)}, u32[]{:S(2)}) %collective-permute-start.14) | collective-permute-done | bytes 1310752 | tf_op jit(solution)/shard_map/ppermute | solution.py:53
  96.9 8.3 %collective-permute-done.17 = bf16[2,256,768]{2,1,0:T(8,128)(2,1)S(1)} collective-permute-done((bf16[2,256,768]{2,1,0:T(8,128)(2,1)S(1)}, bf16[2,256,768]{2,1,0:T(8,128)(2,1)S(1)}, u32[]{:S(2)}, u32[]{:S(2)}) %collective-permute-start.17) | collective-permute-done | bytes 786464 | tf_op jit(solution)/shard_map/ppermute | solution.py:53
  110.4 27.4 %collective-permute-done.21 = bf16[1,8,320,256]{3,2,1,0:T(8,128)(2,1)S(1)} collective-permute-done((bf16[1,8,320,256]{3,2,1,0:T(8,128)(2,1)S(1)}, bf16[1,8,320,256]{3,2,1,0:T(8,128)(2,1)S(1)}, u32[]{:S(2)}, u32[]{:S(2)}) %collective-permute-start.21) | collective-permute-done | bytes 1310752 | tf_op jit(solution)/shard_map/ppermute | solution.py:53
  154.0 12.7 %query.1 = (f32[4,256,320]{2,1,0:T(8,128)S(1)}, bf16[1,5,4,4,64,128]{5,4,3,2,1,0:T(8,128)(2,1)S(1)}) custom-call(bf16[256,2048]{1,0:T(8,128)(2,1)S(1)} %copy-done.17, bf16[4,8,320,256]{3,2,1,0:T(8,128)(2,1)} %copy-done.112, f32[256,64]{1,0:T(8,128)S(1)} %get-tuple-element.481.cos_ref, f32[256,64]{1,0:T(8,128)S(1)} %get-tuple-element.482.sin_ref, ...), custom_call_target="tpu_custom_call" | custom-call | flops 1000 | bytes 1000 | tf_op jit(solution)/shard_map/query/pallas_call | solution.py:922
  172.0 11.4 %collective-permute-done.27 = bf16[2,256,768]{2,1,0:T(8,128)(2,1)} collective-permute-done((bf16[2,256,768]{2,1,0:T(8,128)(2,1)}, bf16[2,256,768]{2,1,0:T(8,128)(2,1)}, u32[]{:S(2)}, u32[]{:S(2)}) %collective-permute-start.27) | collective-permute-done | bytes 786464 | tf_op jit(solution)/shard_map/ppermute | solution.py:53
  195.9 19.0 %attend.1.o_ref = bf16[1,5,4,4,64,128]{5,4,3,2,1,0:T(8,128)(2,1)S(1)} custom-call(bf16[1,5,4,4,64,128]{5,4,3,2,1,0:T(8,128)(2,1)S(1)} %copy-done.12, s32[1,4,1,256]{3,2,1,0:T(1,128)S(1)} %broadcast_in_dim.96.limit_ref, s32[1,2048,1]{2,1,0:T(8,128)S(1)} %copy-done.9, bf16[4,1,5,4,64,128]{5,4,3,2,1,0:T(8,128)(2,1)} %pad_maximum_fusion.12.low_ref, ...), custom_call_target="tpu_custom_call" | custom-call | flops 1000 | bytes 1000 | tf_op jit(solution)/shard_map/attend/pallas_call | solution.py:953
  214.9 7.8 %out.1 = (f32[256,2048]{1,0:T(8,128)}, bf16[256,2048]{1,0:T(8,128)(2,1)S(1)}, bf16[4,256,320]{2,1,0:T(8,128)(2,1)S(1)}) custom-call(bf16[1,5,4,4,64,128]{5,4,3,2,1,0:T(8,128)(2,1)S(1)} %attend.1.o_ref, bf16[2,8,320,256]{3,2,1,0:T(8,128)(2,1)} %pad_maximum_fusion.2.w_low, bf16[2,8,320,256]{3,2,1,0:T(8,128)(2,1)} %collective-permute-done.25.w_high, ...), custom_call_target="tpu_custom_call" | custom-call | flops 1000 | bytes 1000 | tf_op jit(solution)/shard_map/out/pallas_call | solution.py:968
  232.5 20.6 %collective-permute-done.32 = bf16[1,256,2048]{2,1,0:T(8,128)(2,1)S(1)} collective-permute-done((bf16[1,256,2048]{2,1,0:T(8,128)(2,1)S(1)}, bf16[1,256,2048]{2,1,0:T(8,128)(2,1)S(1)}, u32[]{:S(2)}, u32[]{:S(2)}) %collective-permute-start.32) | collective-permute-done | bytes 1048608 | tf_op jit(solution)/shard_map/ppermute | solution.py:53
  255.1 11.4 %collective-permute-done.35 = bf16[2,256,768]{2,1,0:T(8,128)(2,1)S(1)} collective-permute-done((bf16[2,256,768]{2,1,0:T(8,128)(2,1)S(1)}, bf16[2,256,768]{2,1,0:T(8,128)(2,1)S(1)}, u32[]{:S(2)}, u32[]{:S(2)}) %collective-permute-start.35) | collective-permute-done | bytes 786464 | tf_op jit(solution)/shard_map/ppermute | solution.py:53
  272.4 22.7 %collective-permute-done.40 = bf16[1,256,2048]{2,1,0:T(8,128)(2,1)S(1)} collective-permute-done((bf16[1,256,2048]{2,1,0:T(8,128)(2,1)S(1)}, bf16[1,256,2048]{2,1,0:T(8,128)(2,1)S(1)}, u32[]{:S(2)}, u32[]{:S(2)}) %collective-permute-start.40) | collective-permute-done | bytes 1048608 | tf_op jit(solution)/shard_map/ppermute | solution.py:53
  295.3 11.1 %collective-permute-done.39 = bf16[2,256,768]{2,1,0:T(8,128)(2,1)S(1)} collective-permute-done((bf16[2,256,768]{2,1,0:T(8,128)(2,1)S(1)}, bf16[2,256,768]{2,1,0:T(8,128)(2,1)S(1)}, u32[]{:S(2)}, u32[]{:S(2)}) %collective-permute-start.39) | collective-permute-done | bytes 786464 | tf_op jit(solution)/shard_map/ppermute | solution.py:53
  311.6 7.8 %hidden.6 = (bf16[1024,256]{1,0:T(8,128)(2,1)S(1)}, bf16[1024,512]{1,0:T(8,128)(2,1)S(1)}, bf16[768,1024]{1,0:T(8,128)(2,1)S(1)}) custom-call(bf16[512,2048]{1,0:T(8,128)(2,1)} %bitcast.202, bf16[512,2048]{1,0:T(8,128)(2,1)} %bitcast.238, bf16[512,2048]{1,0:T(8,128)(2,1)} %bitcast.214, bf16[512,2048]{1,0:T(8,128)(2,1)} %bitcast.226, ...), custom_call_target="tpu_custom_call" | custom-call | flops 1000 | bytes 1000 | tf_op jit(solution)/shard_map/hidden/pallas_call | solution.py:1010
  329.1 8.2 %hidden.8 = (bf16[1024,256]{1,0:T(8,128)(2,1)S(1)}, bf16[1024,512]{1,0:T(8,128)(2,1)S(1)}, bf16[768,1024]{1,0:T(8,128)(2,1)S(1)}) custom-call(bf16[512,2048]{1,0:T(8,128)(2,1)} %bitcast.204, bf16[512,2048]{1,0:T(8,128)(2,1)} %bitcast.240, bf16[512,2048]{1,0:T(8,128)(2,1)} %bitcast.216, bf16[512,2048]{1,0:T(8,128)(2,1)} %bitcast.228, ...), custom_call_target="tpu_custom_call" | custom-call | flops 1000 | bytes 1000 | tf_op jit(solution)/shard_map/hidden/pallas_call | solution.py:1010
  338.4 8.6 %hidden.7 = (bf16[1024,256]{1,0:T(8,128)(2,1)S(1)}, bf16[1024,512]{1,0:T(8,128)(2,1)S(1)}, bf16[768,1024]{1,0:T(8,128)(2,1)S(1)}) custom-call(bf16[512,2048]{1,0:T(8,128)(2,1)} %bitcast.205, bf16[512,2048]{1,0:T(8,128)(2,1)} %bitcast.241, bf16[512,2048]{1,0:T(8,128)(2,1)} %bitcast.217, bf16[512,2048]{1,0:T(8,128)(2,1)} %bitcast.229, ...), custom_call_target="tpu_custom_call" | custom-call | flops 1000 | bytes 1000 | tf_op jit(solution)/shard_map/hidden/pallas_call | solution.py:1010
  372.3 8.3 %hidden.9 = (bf16[1024,256]{1,0:T(8,128)(2,1)S(1)}, bf16[1024,512]{1,0:T(8,128)(2,1)S(1)}, bf16[768,1024]{1,0:T(8,128)(2,1)S(1)}) custom-call(bf16[512,2048]{1,0:T(8,128)(2,1)} %bitcast.208, bf16[512,2048]{1,0:T(8,128)(2,1)} %bitcast.244, bf16[512,2048]{1,0:T(8,128)(2,1)} %bitcast.220, bf16[512,2048]{1,0:T(8,128)(2,1)} %bitcast.232, ...), custom_call_target="tpu_custom_call" | custom-call | flops 1000 | bytes 1000 | tf_op jit(solution)/shard_map/hidden/pallas_call | solution.py:1010
  381.6 8.4 %hidden.10 = (bf16[1024,256]{1,0:T(8,128)(2,1)S(1)}, bf16[1024,512]{1,0:T(8,128)(2,1)S(1)}, bf16[768,1024]{1,0:T(8,128)(2,1)S(1)}) custom-call(bf16[512,2048]{1,0:T(8,128)(2,1)} %bitcast.209, bf16[512,2048]{1,0:T(8,128)(2,1)} %bitcast.245, bf16[512,2048]{1,0:T(8,128)(2,1)} %bitcast.221, bf16[512,2048]{1,0:T(8,128)(2,1)} %bitcast.233, ...), custom_call_target="tpu_custom_call" | custom-call | flops 1000 | bytes 1000 | tf_op jit(solution)/shard_map/hidden/pallas_call | solution.py:1010
  394.3 8.0 %hidden.11 = (bf16[1024,256]{1,0:T(8,128)(2,1)S(1)}, bf16[1024,512]{1,0:T(8,128)(2,1)S(1)}, bf16[768,1024]{1,0:T(8,128)(2,1)}) custom-call(bf16[512,2048]{1,0:T(8,128)(2,1)} %bitcast.210, bf16[512,2048]{1,0:T(8,128)(2,1)} %bitcast.246, bf16[512,2048]{1,0:T(8,128)(2,1)} %bitcast.222, bf16[512,2048]{1,0:T(8,128)(2,1)} %bitcast.234, ...), custom_call_target="tpu_custom_call" | custom-call | flops 1000 | bytes 1000 | tf_op jit(solution)/shard_map/hidden/pallas_call | solution.py:1010
  404.4 20.8 %back_sum.3 = (bf16[256,2048]{1,0:T(8,128)(2,1)S(1)}, bf16[256,2048]{1,0:T(8,128)(2,1)}, bf16[256,2048]{1,0:T(8,128)(2,1)}, bf16[256,2048]{1,0:T(8,128)(2,1)}) custom-call(bf16[1024,512]{1,0:T(8,128)(2,1)} %copy-done.64, bf16[1024,512]{1,0:T(8,128)(2,1)} %copy-done.66, bf16[1024,512]{1,0:T(8,128)(2,1)} %copy-done.65, bf16[1024,512]{1,0:T(8,128)(2,1)} %copy-done.67, ...), custom_call_target="tpu_custom_call" | custom-call | flops 1000 | bytes 1000 | tf_op jit(solution)/shard_map/back_sum/pallas_call | solution.py:1083
  436.0 12.1 %back_sum.2 = (bf16[512,2048]{1,0:T(8,128)(2,1)}, bf16[512,2048]{1,0:T(8,128)(2,1)}) custom-call(bf16[1024,256]{1,0:T(8,128)(2,1)S(1)} %get-tuple-element.276.refs_0_, bf16[1024,256]{1,0:T(8,128)(2,1)S(1)} %copy-done.84, bf16[1024,256]{1,0:T(8,128)(2,1)S(1)} %get-tuple-element.278.refs_2_, bf16[1024,256]{1,0:T(8,128)(2,1)S(1)} %get-tuple-element.280.refs_3_, ...), custom_call_target="tpu_custom_call" | custom-call | flops 1000 | bytes 1000 | tf_op jit(solution)/shard_map/back_sum/pallas_call | solution.py:1083
  455.9 8.1 %weight_grads.10 = (bf16[4,768,256]{2,1,0:T(8,128)(2,1)S(1)}, bf16[4,768,256]{2,1,0:T(8,128)(2,1)}) custom-call(bf16[512,2048]{1,0:T(8,128)(2,1)} %bitcast.212, bf16[512,2048]{1,0:T(8,128)(2,1)} %bitcast.248, bf16[512,2048]{1,0:T(8,128)(2,1)} %bitcast.224, bf16[512,2048]{1,0:T(8,128)(2,1)} %bitcast.236, bf16[768,1024]{1,0:T(8,128)(2,1)S(1)} %copy-done.57), custom_call_target="tpu_custom_call" | custom-call | flops 1000 | bytes 1000 | tf_op jit(solution)/shard_map/weight_grads/pallas_call | solution.py:1047
  464.0 8.4 %collective-permute-done.55.refs_6_ = bf16[2,768,256]{2,1,0:T(8,128)(2,1)} collective-permute-done((bf16[2,768,256]{2,1,0:T(8,128)(2,1)}, bf16[2,768,256]{2,1,0:T(8,128)(2,1)}, u32[]{:S(2)}, u32[]{:S(2)}) %collective-permute-start.55) | collective-permute-done | bytes 786464 | tf_op jit(solution)/shard_map/ppermute | solution.py:53
  501.2 19.0 %attend_back.2 = (f32[1,5,4,4,64,128]{5,4,3,2,1,0:T(8,128)}, bf16[4,1,5,4,64,128]{5,4,3,2,1,0:T(8,128)(2,1)S(1)}, bf16[4,1,5,4,64,128]{5,4,3,2,1,0:T(8,128)(2,1)}) custom-call(bf16[1,5,4,4,64,128]{5,4,3,2,1,0:T(8,128)(2,1)S(1)} %copy-done.13, bf16[1,5,4,4,64,128]{5,4,3,2,1,0:T(8,128)(2,1)} %copy-done.14, s32[1,4,1,256]{3,2,1,0:T(1,128)S(1)} %broadcast_in_dim.96.limit_ref, ...), custom_call_target="tpu_custom_call" | custom-call | flops 1000 | bytes 1000 | tf_op jit(solution)/shard_map/attend_back/pallas_call | solution.py:1151
  527.6 13.7 %attend_back.3 = (f32[1,5,4,4,64,128]{5,4,3,2,1,0:T(8,128)}, bf16[4,1,5,4,64,128]{5,4,3,2,1,0:T(8,128)(2,1)S(1)}, bf16[4,1,5,4,64,128]{5,4,3,2,1,0:T(8,128)(2,1)}) custom-call(bf16[1,5,4,4,64,128]{5,4,3,2,1,0:T(8,128)(2,1)S(1)} %copy-done.13, bf16[1,5,4,4,64,128]{5,4,3,2,1,0:T(8,128)(2,1)} %copy-done.14, ...), custom_call_target="tpu_custom_call", output_to_operand_aliasing={{0}: (6, {}), {1}: (7, {}), {2}: (8, {})} | custom-call | flops 1000 | bytes 1000 | tf_op jit(solution)/shard_map/attend_back/pallas_call | solution.py:1151
  551.1 8.3 %collective-permute-done.63.refs_14_ = bf16[2,768,256]{2,1,0:T(8,128)(2,1)S(1)} collective-permute-done((bf16[2,768,256]{2,1,0:T(8,128)(2,1)}, bf16[2,768,256]{2,1,0:T(8,128)(2,1)S(1)}, u32[]{:S(2)}, u32[]{:S(2)}) %collective-permute-start.63) | collective-permute-done | bytes 786464 | tf_op jit(solution)/shard_map/ppermute | solution.py:53
  581.2 9.7 %collective-permute-done.69.refs_15_ = bf16[1,768,256]{2,1,0:T(8,128)(2,1)} collective-permute-done((bf16[1,768,256]{2,1,0:T(8,128)(2,1)}, bf16[1,768,256]{2,1,0:T(8,128)(2,1)}, u32[]{:S(2)}, u32[]{:S(2)}) %collective-permute-start.69) | collective-permute-done | bytes 393248 | tf_op jit(solution)/shard_map/ppermute | solution.py:53
  590.9 10.8 %collective-permute-done.68.refs_18_ = bf16[2,768,256]{2,1,0:T(8,128)(2,1)} collective-permute-done((bf16[2,768,256]{2,1,0:T(8,128)(2,1)}, bf16[2,768,256]{2,1,0:T(8,128)(2,1)}, u32[]{:S(2)}, u32[]{:S(2)}) %collective-permute-start.68) | collective-permute-done | bytes 786464 | tf_op jit(solution)/shard_map/ppermute | solution.py:53
  618.0 11.1 %collective-permute-done.73.refs_19_ = bf16[1,768,256]{2,1,0:T(8,128)(2,1)S(1)} collective-permute-done((bf16[1,768,256]{2,1,0:T(8,128)(2,1)S(1)}, bf16[1,768,256]{2,1,0:T(8,128)(2,1)S(1)}, u32[]{:S(2)}, u32[]{:S(2)}) %collective-permute-start.73) | collective-permute-done | bytes 393248 | tf_op jit(solution)/shard_map/ppermute | solution.py:53
  629.1 7.9 %collective-permute-done.71 = bf16[2,1,5,4,64,128]{5,4,3,2,1,0:T(8,128)(2,1)S(1)} collective-permute-done((bf16[2,1,5,4,64,128]{5,4,3,2,1,0:T(8,128)(2,1)S(1)}, bf16[2,1,5,4,64,128]{5,4,3,2,1,0:T(8,128)(2,1)S(1)}, u32[]{:S(2)}, u32[]{:S(2)}) %collective-permute-start.71) | collective-permute-done | bytes 655392 | tf_op jit(solution)/shard_map/ppermute | solution.py:53
  653.4 8.5 %h_one_back.1 = (bf16[256,2048]{1,0:T(8,128)(2,1)S(1)}, f32[1,2048]{1,0:T(1,128)S(1)}) custom-call(bf16[4,256,320]{2,1,0:T(8,128)(2,1)S(1)} %copy-done.43, bf16[4,8,320,256]{3,2,1,0:T(8,128)(2,1)} %copy-done.112, bf16[256,640]{1,0:T(8,128)(2,1)S(1)} %get-tuple-element.393.dkv_ref, bf16[2048,640]{1,0:T(8,128)(2,1)} %bitcast.156, ...), custom_call_target="tpu_custom_call" | custom-call | flops 1000 | bytes 1000 | tf_op jit(solution)/shard_map/h_one_back/pallas_call | solution.py:1254
  715.2 13.7 %collective-permute-done.88 = bf16[163,256]{1,0:T(8,128)(2,1)S(1)} collective-permute-done((bf16[163,256]{1,0:T(8,128)(2,1)S(1)}, bf16[163,256]{1,0:T(8,128)(2,1)S(1)}, u32[]{:S(2)}, u32[]{:S(2)}) %collective-permute-start.88) | collective-permute-done | bytes 83488 | tf_op jit(solution)/shard_map/ppermute | solution.py:53
  (589 shorter events, 345.5 us)
Async XLA Ops:
  105.3 37.1 %collective-permute-start.19 = (bf16[2,8,320,256]{3,2,1,0:T(8,128)(2,1)S(1)}, bf16[2,8,320,256]{3,2,1,0:T(8,128)(2,1)S(1)}, u32[]{:S(2)}, u32[]{:S(2)}) collective-permute-start(bf16[2,8,320,256]{3,2,1,0:T(8,128)(2,1)S(1)} %pad_maximum_fusion), channel_id=1, source_target_pairs={{0,1},{1,0},{2,3},{3,2},{4,5},{5,4},{6,7},{7,6},{8,9},{9,8},{10,11... | collective-permute-start | bytes 7864328 | tf_op jit(solution)/shard_map/ppermute | solution.py:53
  142.3 43.7 %collective-permute-start.25 = (bf16[2,8,320,256]{3,2,1,0:T(8,128)(2,1)}, bf16[2,8,320,256]{3,2,1,0:T(8,128)(2,1)}, u32[]{:S(2)}, u32[]{:S(2)}) collective-permute-start(bf16[2,8,320,256]{3,2,1,0:T(8,128)(2,1)} %pad_maximum_fusion.2.w_low), channel_id=1, source_target_pairs={{0,1},{1,0},{2,3},{3,2},{4,5},{5,4},{6,7},{7,6},{8,9},{9,8},{10,11... | collective-permute-start | bytes 7864328 | tf_op jit(solution)/shard_map/ppermute | solution.py:53
  143.7 42.3 %collective-permute-start.24 = (bf16[4,1,5,4,64,128]{5,4,3,2,1,0:T(8,128)(2,1)}, bf16[4,1,5,4,64,128]{5,4,3,2,1,0:T(8,128)(2,1)}, u32[]{:S(2)}, u32[]{:S(2)}) collective-permute-start(bf16[4,1,5,4,64,128]{5,4,3,2,1,0:T(8,128)(2,1)} %pad_maximum_fusion.12.low_ref), channel_id=1, source_target_pairs={{0,4},{4,0},{8,12},{12,8},{16,20},{20,16},{24,28},{28,24},{1,5},{5... | collective-permute-start | bytes 3932168 | tf_op jit(solution)/shard_map/ppermute | solution.py:53
  144.3 41.7 %collective-permute-start.26 = (bf16[1,256,2048]{2,1,0:T(8,128)(2,1)}, bf16[1,256,2048]{2,1,0:T(8,128)(2,1)}, u32[]{:S(2)}, u32[]{:S(2)}) collective-permute-start(bf16[1,256,2048]{2,1,0:T(8,128)(2,1)} %bitcast.23), channel_id=1, source_target_pairs={{0,2},{1,3},{2,0},{3,1},{4,6},{5,7},{6,4},{7,5},{8,10},{9,11},{10,... | collective-permute-start | bytes 3145736 | tf_op jit(solution)/shard_map/ppermute | solution.py:53
  145.8 37.6 %collective-permute-start.27 = (bf16[2,256,768]{2,1,0:T(8,128)(2,1)}, bf16[2,256,768]{2,1,0:T(8,128)(2,1)}, u32[]{:S(2)}, u32[]{:S(2)}) collective-permute-start(bf16[2,256,768]{2,1,0:T(8,128)(2,1)} %pad_maximum_fusion.16), channel_id=1, source_target_pairs={{0,16},{4,20},{8,24},{12,28},{16,0},{20,4},{24,8},{28,12},{1,17},{... | collective-permute-start | bytes 2359304 | tf_op jit(solution)/shard_map/ppermute | solution.py:53
  186.1 39.5 %collective-permute-start.29 = (bf16[4,256,768]{2,1,0:T(8,128)(2,1)}, bf16[4,256,768]{2,1,0:T(8,128)(2,1)}, u32[]{:S(2)}, u32[]{:S(2)}) collective-permute-start(bf16[4,256,768]{2,1,0:T(8,128)(2,1)} %pad_maximum_fusion.7), channel_id=1, source_target_pairs={{0,4},{4,0},{8,12},{12,8},{16,20},{20,16},{24,28},{28,24},{1,5},{5... | collective-permute-start | bytes 4718600 | tf_op jit(solution)/shard_map/ppermute | solution.py:53
  225.6 40.8 %collective-permute-start.33 = (bf16[2,256,2048]{2,1,0:T(8,128)(2,1)S(1)}, bf16[2,256,2048]{2,1,0:T(8,128)(2,1)S(1)}, u32[]{:S(2)}, u32[]{:S(2)}) collective-permute-start(bf16[2,256,2048]{2,1,0:T(8,128)(2,1)S(1)} %constant_dynamic-update-slice_fusion.2), channel_id=1, source_target_pairs={{0,1},{1,0},{2,3},{3,2},{4,5},{5,4},{6,7},{7,6},{8,9},{9,8},{10,11... | collective-permute-start | bytes 6291464 | tf_op jit(solution)/shard_map/ppermute | solution.py:53
  227.2 39.3 %collective-permute-start.34 = (bf16[4,256,768]{2,1,0:T(8,128)(2,1)S(1)}, bf16[4,256,768]{2,1,0:T(8,128)(2,1)S(1)}, u32[]{:S(2)}, u32[]{:S(2)}) collective-permute-start(bf16[4,256,768]{2,1,0:T(8,128)(2,1)S(1)} %pad_maximum_fusion.8), channel_id=1, source_target_pairs={{0,4},{4,0},{8,12},{12,8},{16,20},{20,16},{24,28},{28,24},{1,5},{5... | collective-permute-start | bytes 4718600 | tf_op jit(solution)/shard_map/ppermute | solution.py:53
  229.4 37.1 %collective-permute-start.35 = (bf16[2,256,768]{2,1,0:T(8,128)(2,1)S(1)}, bf16[2,256,768]{2,1,0:T(8,128)(2,1)S(1)}, u32[]{:S(2)}, u32[]{:S(2)}) collective-permute-start(bf16[2,256,768]{2,1,0:T(8,128)(2,1)S(1)} %pad_maximum_fusion.18), channel_id=1, source_target_pairs={{0,16},{4,20},{8,24},{12,28},{16,0},{20,4},{24,8},{28,12},{1,17},{... | collective-permute-start | bytes 2359304 | tf_op jit(solution)/shard_map/ppermute | solution.py:53
  267.6 39.2 %collective-permute-start.37 = (bf16[2,256,2048]{2,1,0:T(8,128)(2,1)S(1)}, bf16[2,256,2048]{2,1,0:T(8,128)(2,1)S(1)}, u32[]{:S(2)}, u32[]{:S(2)}) collective-permute-start(bf16[2,256,2048]{2,1,0:T(8,128)(2,1)S(1)} %pad_maximum_fusion.3), channel_id=1, source_target_pairs={{0,1},{1,0},{2,3},{3,2},{4,5},{5,4},{6,7},{7,6},{8,9},{9,8},{10,11... | collective-permute-start | bytes 6291464 | tf_op jit(solution)/shard_map/ppermute | solution.py:53
  267.8 39.0 %collective-permute-start.38 = (bf16[4,256,768]{2,1,0:T(8,128)(2,1)S(1)}, bf16[4,256,768]{2,1,0:T(8,128)(2,1)S(1)}, u32[]{:S(2)}, u32[]{:S(2)}) collective-permute-start(bf16[4,256,768]{2,1,0:T(8,128)(2,1)S(1)} %pad_maximum_fusion.9), channel_id=1, source_target_pairs={{0,4},{4,0},{8,12},{12,8},{16,20},{20,16},{24,28},{28,24},{1,5},{5... | collective-permute-start | bytes 4718600 | tf_op jit(solution)/shard_map/ppermute | solution.py:53
  308.1 40.9 %collective-permute-start.44 = (bf16[2,256,2048]{2,1,0:T(8,128)(2,1)S(1)}, bf16[2,256,2048]{2,1,0:T(8,128)(2,1)}, u32[]{:S(2)}, u32[]{:S(2)}) collective-permute-start(bf16[2,256,2048]{2,1,0:T(8,128)(2,1)S(1)} %pad_maximum_fusion.4), channel_id=1, source_target_pairs={{0,1},{1,0},{2,3},{3,2},{4,5},{5,4},{6,7},{7,6},{8,9},{9,8},{10,11... | collective-permute-start | bytes 6291464 | tf_op jit(solution)/shard_map/ppermute | solution.py:53
  308.2 40.7 %collective-permute-start.42 = (bf16[4,256,768]{2,1,0:T(8,128)(2,1)S(1)}, bf16[4,256,768]{2,1,0:T(8,128)(2,1)}, u32[]{:S(2)}, u32[]{:S(2)}) collective-permute-start(bf16[4,256,768]{2,1,0:T(8,128)(2,1)S(1)} %pad_maximum_fusion.10), channel_id=1, source_target_pairs={{0,4},{4,0},{8,12},{12,8},{16,20},{20,16},{24,28},{28,24},{1,5},{5... | collective-permute-start | bytes 4718600 | tf_op jit(solution)/shard_map/ppermute | solution.py:53
  309.6 39.4 %collective-permute-start.43 = (bf16[2,256,768]{2,1,0:T(8,128)(2,1)S(1)}, bf16[2,256,768]{2,1,0:T(8,128)(2,1)S(1)}, u32[]{:S(2)}, u32[]{:S(2)}) collective-permute-start(bf16[2,256,768]{2,1,0:T(8,128)(2,1)S(1)} %pad_maximum_fusion.20), channel_id=1, source_target_pairs={{0,16},{4,20},{8,24},{12,28},{16,0},{20,4},{24,8},{28,12},{1,17},{... | collective-permute-start | bytes 2359304 | tf_op jit(solution)/shard_map/ppermute | solution.py:53
  310.6 38.4 %collective-permute-start.45 = (bf16[2,1,256,320]{3,2,0,1:T(8,128)(2,1)}, bf16[2,1,256,320]{3,2,0,1:T(8,128)(2,1)}, u32[]{:S(2)}, u32[]{:S(2)}) collective-permute-start(bf16[2,1,256,320]{3,2,0,1:T(8,128)(2,1)} %get-tuple-element.296), channel_id=1, source_target_pairs={{0,2},{1,3},{2,0},{3,1},{4,6},{5,7},{6,4},{7,5},{8,10},{9,11},{10,... | collective-permute-start | bytes 983048 | tf_op jit(solution)/shard_map/ppermute | solution.py:53
  349.0 42.1 %collective-permute-start.51 = (bf16[4,768,256]{2,1,0:T(8,128)(2,1)}, bf16[4,768,256]{2,1,0:T(8,128)(2,1)}, u32[]{:S(2)}, u32[]{:S(2)}) collective-permute-start(bf16[4,768,256]{2,1,0:T(8,128)(2,1)} %copy-done.104), channel_id=1, source_target_pairs={{0,4},{4,0},{8,12},{12,8},{16,20},{20,16},{24,28},{28,24},{1,5},{5... | collective-permute-start | bytes 4718600 | tf_op jit(solution)/shard_map/ppermute | solution.py:53
  350.3 40.8 %collective-permute-start.46 = (bf16[2,256,768]{2,1,0:T(8,128)(2,1)S(1)}, bf16[2,256,768]{2,1,0:T(8,128)(2,1)S(1)}, u32[]{:S(2)}, u32[]{:S(2)}) collective-permute-start(bf16[2,256,768]{2,1,0:T(8,128)(2,1)S(1)} %collective-permute-done.41), channel_id=1, source_target_pairs={{0,16},{4,20},{8,24},{12,28},{16,0},{20,4},{24,8},{28,12},{1,17},{... | collective-permute-start | bytes 2359304 | tf_op jit(solution)/shard_map/ppermute | solution.py:53
  391.2 40.3 %collective-permute-start.52 = (bf16[4,768,256]{2,1,0:T(8,128)(2,1)}, bf16[4,768,256]{2,1,0:T(8,128)(2,1)S(1)}, u32[]{:S(2)}, u32[]{:S(2)}) collective-permute-start(bf16[4,768,256]{2,1,0:T(8,128)(2,1)} %copy-done.105), channel_id=1, source_target_pairs={{0,4},{4,0},{8,12},{12,8},{16,20},{20,16},{24,28},{28,24},{1,5},{5... | collective-permute-start | bytes 4718600 | tf_op jit(solution)/shard_map/ppermute | solution.py:53
  394.0 37.5 %collective-permute-start.53 = (bf16[2,768,256]{2,1,0:T(8,128)(2,1)}, bf16[2,768,256]{2,1,0:T(8,128)(2,1)S(1)}, u32[]{:S(2)}, u32[]{:S(2)}) collective-permute-start(bf16[2,768,256]{2,1,0:T(8,128)(2,1)} %add_convert_fusion.5), channel_id=1, source_target_pairs={{0,16},{4,20},{8,24},{12,28},{16,0},{20,4},{24,8},{28,12},{1,17},{... | collective-permute-start | bytes 2359304 | tf_op jit(solution)/shard_map/ppermute | solution.py:53
  431.5 40.9 %collective-permute-start.54 = (bf16[4,768,256]{2,1,0:T(8,128)(2,1)S(1)}, bf16[4,768,256]{2,1,0:T(8,128)(2,1)}, u32[]{:S(2)}, u32[]{:S(2)}) collective-permute-start(bf16[4,768,256]{2,1,0:T(8,128)(2,1)S(1)} %copy-done.102), channel_id=1, source_target_pairs={{0,4},{4,0},{8,12},{12,8},{16,20},{20,16},{24,28},{28,24},{1,5},{5... | collective-permute-start | bytes 4718600 | tf_op jit(solution)/shard_map/ppermute | solution.py:53
  432.8 39.6 %collective-permute-start.47 = (bf16[256,2048]{1,0:T(8,128)(2,1)}, bf16[256,2048]{1,0:T(8,128)(2,1)}, u32[]{:S(2)}, u32[]{:S(2)}) collective-permute-start(bf16[256,2048]{1,0:T(8,128)(2,1)} %get-tuple-element.313), channel_id=1, source_target_pairs={{0,2},{1,3},{2,0},{3,1},{4,6},{5,7},{6,4},{7,5},{8,10},{9,11},{10,... | collective-permute-start | bytes 3145736 | tf_op jit(solution)/shard_map/ppermute | solution.py:53
  433.4 39.0 %collective-permute-start.48 = (bf16[256,2048]{1,0:T(8,128)(2,1)}, bf16[256,2048]{1,0:T(8,128)(2,1)}, u32[]{:S(2)}, u32[]{:S(2)}) collective-permute-start(bf16[256,2048]{1,0:T(8,128)(2,1)} %get-tuple-element.314), channel_id=1, source_target_pairs={{0,1},{1,0},{2,3},{3,2},{4,5},{5,4},{6,7},{7,6},{8,9},{9,8},{10,11... | collective-permute-start | bytes 3145736 | tf_op jit(solution)/shard_map/ppermute | solution.py:53
  433.4 45.8 %collective-permute-start.49 = (bf16[256,2048]{1,0:T(8,128)(2,1)}, bf16[256,2048]{1,0:T(8,128)(2,1)}, u32[]{:S(2)}, u32[]{:S(2)}) collective-permute-start(bf16[256,2048]{1,0:T(8,128)(2,1)} %get-tuple-element.315), channel_id=1, source_target_pairs={{0,3},{1,2},{2,1},{3,0},{4,7},{5,6},{6,5},{7,4},{8,11},{9,10},{10,... | collective-permute-start | bytes 3145736 | tf_op jit(solution)/shard_map/ppermute | solution.py:53
  479.1 41.7 %collective-permute-start.56 = (bf16[2,256,2048]{2,1,0:T(8,128)(2,1)}, bf16[2,256,2048]{2,1,0:T(8,128)(2,1)}, u32[]{:S(2)}, u32[]{:S(2)}) collective-permute-start(bf16[2,256,2048]{2,1,0:T(8,128)(2,1)} %bitcast.276), channel_id=1, source_target_pairs={{0,1},{1,0},{2,3},{3,2},{4,5},{5,4},{6,7},{7,6},{8,9},{9,8},{10,11... | collective-permute-start | bytes 6291464 | tf_op jit(solution)/shard_map/ppermute | solution.py:53
  480.2 40.6 %collective-permute-start.57 = (bf16[4,768,256]{2,1,0:T(8,128)(2,1)}, bf16[4,768,256]{2,1,0:T(8,128)(2,1)S(1)}, u32[]{:S(2)}, u32[]{:S(2)}) collective-permute-start(bf16[4,768,256]{2,1,0:T(8,128)(2,1)} %copy-done.103), channel_id=1, source_target_pairs={{0,4},{4,0},{8,12},{12,8},{16,20},{20,16},{24,28},{28,24},{1,5},{5... | collective-permute-start | bytes 4718600 | tf_op jit(solution)/shard_map/ppermute | solution.py:53
  483.3 37.5 %collective-permute-start.58 = (bf16[2,768,256]{2,1,0:T(8,128)(2,1)}, bf16[2,768,256]{2,1,0:T(8,128)(2,1)S(1)}, u32[]{:S(2)}, u32[]{:S(2)}) collective-permute-start(bf16[2,768,256]{2,1,0:T(8,128)(2,1)} %add_convert_fusion.3), channel_id=1, source_target_pairs={{0,16},{4,20},{8,24},{12,28},{16,0},{20,4},{24,8},{28,12},{1,17},{... | collective-permute-start | bytes 2359304 | tf_op jit(solution)/shard_map/ppermute | solution.py:53
  520.8 40.3 %collective-permute-start.62 = (bf16[4,768,256]{2,1,0:T(8,128)(2,1)}, bf16[4,768,256]{2,1,0:T(8,128)(2,1)}, u32[]{:S(2)}, u32[]{:S(2)}) collective-permute-start(bf16[4,768,256]{2,1,0:T(8,128)(2,1)} %get-tuple-element.357), channel_id=1, source_target_pairs={{0,4},{4,0},{8,12},{12,8},{16,20},{20,16},{24,28},{28,24},{1,5},{5... | collective-permute-start | bytes 4718600 | tf_op jit(solution)/shard_map/ppermute | solution.py:53
  522.0 37.4 %collective-permute-start.61 = (bf16[1,256,2048]{2,1,0:T(8,128)(2,1)S(1)}, bf16[1,256,2048]{2,1,0:T(8,128)(2,1)}, u32[]{:S(2)}, u32[]{:S(2)}) collective-permute-start(bf16[1,256,2048]{2,1,0:T(8,128)(2,1)S(1)} %bitcast.174), channel_id=1, source_target_pairs={{0,2},{1,3},{2,0},{3,1},{4,6},{5,7},{6,4},{7,5},{8,10},{9,11},{10,... | collective-permute-start | bytes 3145736 | tf_op jit(solution)/shard_map/ppermute | solution.py:53
  561.1 40.6 %collective-permute-start.66 = (bf16[2,256,2048]{2,1,0:T(8,128)(2,1)S(1)}, bf16[2,256,2048]{2,1,0:T(8,128)(2,1)}, u32[]{:S(2)}, u32[]{:S(2)}) collective-permute-start(bf16[2,256,2048]{2,1,0:T(8,128)(2,1)S(1)} %pad_maximum_fusion.5), channel_id=1, source_target_pairs={{0,1},{1,0},{2,3},{3,2},{4,5},{5,4},{6,7},{7,6},{8,9},{9,8},{10,11... | collective-permute-start | bytes 6291464 | tf_op jit(solution)/shard_map/ppermute | solution.py:53
  561.2 40.5 %collective-permute-start.67 = (bf16[4,1,5,4,64,128]{5,4,3,2,1,0:T(8,128)(2,1)}, bf16[4,1,5,4,64,128]{5,4,3,2,1,0:T(8,128)(2,1)}, u32[]{:S(2)}, u32[]{:S(2)}) collective-permute-start(bf16[4,1,5,4,64,128]{5,4,3,2,1,0:T(8,128)(2,1)} %get-tuple-element.372), channel_id=1, source_target_pairs={{0,4},{4,0},{8,12},{12,8},{16,20},{20,16},{24,28},{28,24},{1,5},{5... | collective-permute-start | bytes 3932168 | tf_op jit(solution)/shard_map/ppermute | solution.py:53
  564.7 37.0 %collective-permute-start.68 = (bf16[2,768,256]{2,1,0:T(8,128)(2,1)}, bf16[2,768,256]{2,1,0:T(8,128)(2,1)}, u32[]{:S(2)}, u32[]{:S(2)}) collective-permute-start(bf16[2,768,256]{2,1,0:T(8,128)(2,1)} %add_convert_fusion.1), channel_id=1, source_target_pairs={{0,16},{4,20},{8,24},{12,28},{16,0},{20,4},{24,8},{28,12},{1,17},{... | collective-permute-start | bytes 2359304 | tf_op jit(solution)/shard_map/ppermute | solution.py:53
  641.9 37.3 %collective-permute-start.77 = (bf16[2,768,256]{2,1,0:T(8,128)(2,1)}, bf16[2,768,256]{2,1,0:T(8,128)(2,1)}, u32[]{:S(2)}, u32[]{:S(2)}) collective-permute-start(bf16[2,768,256]{2,1,0:T(8,128)(2,1)} %add_convert_fusion), channel_id=1, source_target_pairs={{0,16},{4,20},{8,24},{12,28},{16,0},{20,4},{24,8},{28,12},{1,17},{... | collective-permute-start | bytes 2359304 | tf_op jit(solution)/shard_map/ppermute | solution.py:53
  (199 other events, 3508.0 us)

commit v8 on v7

--- a/solution.py
+++ b/solution.py
@@ -294,22 +294,6 @@
 
     def terms(self):
         return [self.sums[0], *self.arrived]
-
-
-class TensorDirect(Item):
-    def __init__(self, parts):
-        self.parts = list(parts)
-
-    def value(self):
-        return self.parts
-
-    def advance(self, value):
-        order = order_of("tensor")
-        self.got = [self.bring(value[p], "tensor", order[p]) for p in range(1, len(order))]
-        return self.got
-
-    def terms(self):
-        return [x[None] for x in [self.parts[0], *self.got]]
 
 
 class TensorExchange(Item):
@@ -1106,15 +1090,17 @@
     add_grads(2)
     link.go(t_heads, s_ff[0], g_ff[5], during=[*turned[3:], *sent[1:]])
     hidden_part(g_ff[5], sizes[5])
-    t_back = TensorDirect(back_sum(d_gate_ups, False, n_tensor))
-    link.go(s_ff[1], s_ff[0], during=t_back.parts)
+    t_back = TensorScatter(
+        [x.reshape(n_tensor // 2, sp_rows, width) for x in back_sum(d_gate_ups, False, 2)]
+    )
+    link.go(s_ff[1], s_ff[0], during=t_back.sums)
+    t_back.advance(after(t_back.value(), *link.done))
     add_grads(3)
     add_grads(4)
     t_ffn = TensorScatter(
         [x.reshape(n_tensor // 2, sp_rows, width) for x in back_sum(hiddens, True, 2)]
     )
-    back_got = t_back.advance(t_back.value())
-    link.go(s_ff[2], s_ff[1], during=[*t_ffn.sums, *sent[3:]], ends=back_got)
+    link.go(t_back, s_ff[2], s_ff[1], during=[*t_ffn.sums, *sent[3:]])
     first_spec = pl.BlockSpec((1, sp_rows, width), lambda i: (0, 0, 0))
     back_terms = t_back.terms()
     d_mixed, d_attn_own, d_gain_two = pl.pallas_call(

time: 750 us -> 747 us (level)
    ppermute x94 -> x93, waiting for transfers between devices: 277 us -> 272 us  [swap(): return lax.ppermute(value, axis, [(i, i ^ mask) for i in range(size)])]
    unnamed x279 -> x291, local copies, waits for them, and re-layouts: 40.3 us -> 36 us
    convert_element_type x19 -> x20, other arithmetic: 26.3 us -> 29.5 us  [plus(): return total.astype(kind)]
    ppermute x94 -> x93, starting transfers between devices: 92.6 us -> 90.9 us  [swap(): return lax.ppermute(value, axis, [(i, i ^ mask) for i in range(size)])]
  transfers between devices with their start and end apart: 94 -> 93, of which waited for: 34 -> 34; matrix products, arithmetic and copies ran while one was open for 10% -> 11% of each run, Pallas kernels for 35% -> 35%
where the time goes in v8:
time: 747 us; the launch traced here: 736 us
  waiting for transfers between devices  272 us (36%)
  Pallas kernels  259 us (35%)
  starting transfers between devices  90.9 us (12%)
  other arithmetic  66.1 us (9%)
  local copies, waits for them, and re-layouts  45.7 us (6%)
    ppermute x93, waiting for transfers between devices, swap(): return lax.ppermute(value, axis, [(i, i ^ mask) for i in range(size)])  272 us
    ppermute x93, starting transfers between devices, swap(): return lax.ppermute(value, axis, [(i, i ^ mask) for i in range(size)])  90.9 us
    pallas_call x6, Pallas kernels, hidden_part(): pl.pallas_call(functools.partial(hidden_kernel, [places for _, places in...  49.1 us
    pallas_call x6, Pallas kernels, grads_of(): pl.pallas_call(grads_kernel, grid=(grid,), in_specs=[block] * 4 + [whole(...  43.7 us
    unnamed x291, local copies, waits for them, and re-layouts  36 us
    pallas_call x2, Pallas kernels, attend_back(): pl.pallas_call(attend_back_kernel, grid=(rows, count), in_specs=[q_part,...  32.9 us
    pallas_call x2, Pallas kernels, back_sum(): pl.pallas_call(functools.partial(back_sum_kernel, [[places for _, places...  32.9 us
    convert_element_type x20, other arithmetic, plus(): return total.astype(kind)  29.5 us
  transfers between devices with their start and end apart: 93, of which 34 were waited for; matrix products, arithmetic and copies ran while one was open for 11% of the time, Pallas kernels for 35%

profile of v8, /device:TPU:0, one launch (start us, length us, event | category | flops | bytes accessed | tf_op | source)
XLA Modules:
  0.0 736.3 jit_solution(1932674832380053393)
XLA Ops:
  30.3 9.4 %collective-permute-done.6 = bf16[4,128,640]{2,1,0:T(8,128)(2,1)S(1)} collective-permute-done((bf16[4,128,640]{2,1,0:T(8,128)(2,1)S(1)}, bf16[4,128,640]{2,1,0:T(8,128)(2,1)S(1)}, u32[]{:S(2)}, u32[]{:S(2)}) %collective-permute-start.6) | collective-permute-done | bytes 655392 | tf_op jit(solution)/shard_map/ppermute | solution.py:53
  49.8 10.9 %collective-permute-done.9 = bf16[4,2,256]{2,1,0:T(2,128)(2,1)S(1)} collective-permute-done((bf16[4,2,256]{2,1,0:T(2,128)(2,1)S(1)}, bf16[4,2,256]{2,1,0:T(2,128)(2,1)S(1)}, u32[]{:S(2)}, u32[]{:S(2)}) %collective-permute-start.9) | collective-permute-done | bytes 4128 | tf_op jit(solution)/shard_map/ppermute | solution.py:53
  78.5 16.9 %collective-permute-done.14 = bf16[1,8,320,256]{3,2,1,0:T(8,128)(2,1)} collective-permute-done((bf16[1,8,320,256]{3,2,1,0:T(8,128)(2,1)S(1)}, bf16[1,8,320,256]{3,2,1,0:T(8,128)(2,1)}, u32[]{:S(2)}, u32[]{:S(2)}) %collective-permute-start.14) | collective-permute-done | bytes 1310752 | tf_op jit(solution)/shard_map/ppermute | solution.py:53
  97.0 8.2 %collective-permute-done.17 = bf16[2,256,768]{2,1,0:T(8,128)(2,1)} collective-permute-done((bf16[2,256,768]{2,1,0:T(8,128)(2,1)S(1)}, bf16[2,256,768]{2,1,0:T(8,128)(2,1)}, u32[]{:S(2)}, u32[]{:S(2)}) %collective-permute-start.17) | collective-permute-done | bytes 786464 | tf_op jit(solution)/shard_map/ppermute | solution.py:53
  112.1 27.4 %collective-permute-done.21 = bf16[1,8,320,256]{3,2,1,0:T(8,128)(2,1)S(1)} collective-permute-done((bf16[1,8,320,256]{3,2,1,0:T(8,128)(2,1)S(1)}, bf16[1,8,320,256]{3,2,1,0:T(8,128)(2,1)S(1)}, u32[]{:S(2)}, u32[]{:S(2)}) %collective-permute-start.21) | collective-permute-done | bytes 1310752 | tf_op jit(solution)/shard_map/ppermute | solution.py:53
  155.1 12.7 %query.1 = (f32[4,256,320]{2,1,0:T(8,128)S(1)}, bf16[1,5,4,4,64,128]{5,4,3,2,1,0:T(8,128)(2,1)S(1)}) custom-call(bf16[256,2048]{1,0:T(8,128)(2,1)S(1)} %copy-done.17, bf16[4,8,320,256]{3,2,1,0:T(8,128)(2,1)} %copy-done.122, f32[256,64]{1,0:T(8,128)S(1)} %get-tuple-element.483.cos_ref, f32[256,64]{1,0:T(8,128)S(1)} %get-tuple-element.484.sin_ref, ...), custom_call_target="tpu_custom_call" | custom-call | flops 1000 | bytes 1000 | tf_op jit(solution)/shard_map/query/pallas_call | solution.py:906
  173.0 11.4 %collective-permute-done.27 = bf16[2,256,768]{2,1,0:T(8,128)(2,1)} collective-permute-done((bf16[2,256,768]{2,1,0:T(8,128)(2,1)}, bf16[2,256,768]{2,1,0:T(8,128)(2,1)}, u32[]{:S(2)}, u32[]{:S(2)}) %collective-permute-start.27) | collective-permute-done | bytes 786464 | tf_op jit(solution)/shard_map/ppermute | solution.py:53
  197.0 19.2 %attend.1.o_ref = bf16[1,5,4,4,64,128]{5,4,3,2,1,0:T(8,128)(2,1)S(1)} custom-call(bf16[1,5,4,4,64,128]{5,4,3,2,1,0:T(8,128)(2,1)S(1)} %copy-done.12, s32[1,4,1,256]{3,2,1,0:T(1,128)S(1)} %broadcast_in_dim.84.limit_ref, s32[1,2048,1]{2,1,0:T(8,128)S(1)} %copy-done.9, bf16[4,1,5,4,64,128]{5,4,3,2,1,0:T(8,128)(2,1)} %pad_maximum_fusion.12.low_ref, ...), custom_call_target="tpu_custom_call" | custom-call | flops 1000 | bytes 1000 | tf_op jit(solution)/shard_map/attend/pallas_call | solution.py:937
  216.2 7.8 %out.1 = (f32[256,2048]{1,0:T(8,128)}, bf16[256,2048]{1,0:T(8,128)(2,1)S(1)}, bf16[4,256,320]{2,1,0:T(8,128)(2,1)S(1)}) custom-call(bf16[1,5,4,4,64,128]{5,4,3,2,1,0:T(8,128)(2,1)S(1)} %attend.1.o_ref, bf16[2,8,320,256]{3,2,1,0:T(8,128)(2,1)} %pad_maximum_fusion.2.w_low, bf16[2,8,320,256]{3,2,1,0:T(8,128)(2,1)} %collective-permute-done.25.w_high, ...), custom_call_target="tpu_custom_call" | custom-call | flops 1000 | bytes 1000 | tf_op jit(solution)/shard_map/out/pallas_call | solution.py:952
  233.6 20.5 %collective-permute-done.32 = bf16[1,256,2048]{2,1,0:T(8,128)(2,1)S(1)} collective-permute-done((bf16[1,256,2048]{2,1,0:T(8,128)(2,1)S(1)}, bf16[1,256,2048]{2,1,0:T(8,128)(2,1)S(1)}, u32[]{:S(2)}, u32[]{:S(2)}) %collective-permute-start.32) | collective-permute-done | bytes 1048608 | tf_op jit(solution)/shard_map/ppermute | solution.py:53
  256.1 11.4 %collective-permute-done.35 = bf16[2,256,768]{2,1,0:T(8,128)(2,1)S(1)} collective-permute-done((bf16[2,256,768]{2,1,0:T(8,128)(2,1)S(1)}, bf16[2,256,768]{2,1,0:T(8,128)(2,1)S(1)}, u32[]{:S(2)}, u32[]{:S(2)}) %collective-permute-start.35) | collective-permute-done | bytes 786464 | tf_op jit(solution)/shard_map/ppermute | solution.py:53
  272.3 22.6 %collective-permute-done.40 = bf16[1,256,2048]{2,1,0:T(8,128)(2,1)S(1)} collective-permute-done((bf16[1,256,2048]{2,1,0:T(8,128)(2,1)S(1)}, bf16[1,256,2048]{2,1,0:T(8,128)(2,1)S(1)}, u32[]{:S(2)}, u32[]{:S(2)}) %collective-permute-start.40) | collective-permute-done | bytes 1048608 | tf_op jit(solution)/shard_map/ppermute | solution.py:53
  295.1 11.2 %collective-permute-done.39 = bf16[2,256,768]{2,1,0:T(8,128)(2,1)S(1)} collective-permute-done((bf16[2,256,768]{2,1,0:T(8,128)(2,1)S(1)}, bf16[2,256,768]{2,1,0:T(8,128)(2,1)S(1)}, u32[]{:S(2)}, u32[]{:S(2)}) %collective-permute-start.39) | collective-permute-done | bytes 786464 | tf_op jit(solution)/shard_map/ppermute | solution.py:53
  310.6 7.8 %hidden.6 = (bf16[1024,256]{1,0:T(8,128)(2,1)S(1)}, bf16[1024,512]{1,0:T(8,128)(2,1)S(1)}, bf16[768,1024]{1,0:T(8,128)(2,1)S(1)}) custom-call(bf16[512,2048]{1,0:T(8,128)(2,1)} %bitcast.202, bf16[512,2048]{1,0:T(8,128)(2,1)} %bitcast.238, bf16[512,2048]{1,0:T(8,128)(2,1)} %bitcast.214, bf16[512,2048]{1,0:T(8,128)(2,1)} %bitcast.226, ...), custom_call_target="tpu_custom_call" | custom-call | flops 1000 | bytes 1000 | tf_op jit(solution)/shard_map/hidden/pallas_call | solution.py:994
  328.7 8.2 %hidden.8 = (bf16[1024,256]{1,0:T(8,128)(2,1)S(1)}, bf16[1024,512]{1,0:T(8,128)(2,1)S(1)}, bf16[768,1024]{1,0:T(8,128)(2,1)S(1)}) custom-call(bf16[512,2048]{1,0:T(8,128)(2,1)} %bitcast.204, bf16[512,2048]{1,0:T(8,128)(2,1)} %bitcast.240, bf16[512,2048]{1,0:T(8,128)(2,1)} %bitcast.216, bf16[512,2048]{1,0:T(8,128)(2,1)} %bitcast.228, ...), custom_call_target="tpu_custom_call" | custom-call | flops 1000 | bytes 1000 | tf_op jit(solution)/shard_map/hidden/pallas_call | solution.py:994
  338.0 8.8 %hidden.7 = (bf16[1024,256]{1,0:T(8,128)(2,1)S(1)}, bf16[1024,512]{1,0:T(8,128)(2,1)S(1)}, bf16[768,1024]{1,0:T(8,128)(2,1)S(1)}) custom-call(bf16[512,2048]{1,0:T(8,128)(2,1)} %bitcast.205, bf16[512,2048]{1,0:T(8,128)(2,1)} %bitcast.241, bf16[512,2048]{1,0:T(8,128)(2,1)} %bitcast.217, bf16[512,2048]{1,0:T(8,128)(2,1)} %bitcast.229, ...), custom_call_target="tpu_custom_call" | custom-call | flops 1000 | bytes 1000 | tf_op jit(solution)/shard_map/hidden/pallas_call | solution.py:994
  362.7 7.9 %weight_grads.8 = (bf16[4,768,256]{2,1,0:T(8,128)(2,1)S(1)}, bf16[4,768,256]{2,1,0:T(8,128)(2,1)}) custom-call(bf16[512,2048]{1,0:T(8,128)(2,1)} %bitcast.207, bf16[512,2048]{1,0:T(8,128)(2,1)} %bitcast.243, bf16[512,2048]{1,0:T(8,128)(2,1)} %bitcast.219, bf16[512,2048]{1,0:T(8,128)(2,1)} %bitcast.231, bf16[768,1024]{1,0:T(8,128)(2,1)S(1)} %copy-done.60), custom_call_target="tpu_custom_call" | custom-call | flops 1000 | bytes 1000 | tf_op jit(solution)/shard_map/weight_grads/pallas_call | solution.py:1031
  380.5 8.4 %hidden.10 = (bf16[1024,256]{1,0:T(8,128)(2,1)S(1)}, bf16[1024,512]{1,0:T(8,128)(2,1)S(1)}, bf16[768,1024]{1,0:T(8,128)(2,1)S(1)}) custom-call(bf16[512,2048]{1,0:T(8,128)(2,1)} %bitcast.209, bf16[512,2048]{1,0:T(8,128)(2,1)} %bitcast.245, bf16[512,2048]{1,0:T(8,128)(2,1)} %bitcast.221, bf16[512,2048]{1,0:T(8,128)(2,1)} %bitcast.233, ...), custom_call_target="tpu_custom_call" | custom-call | flops 1000 | bytes 1000 | tf_op jit(solution)/shard_map/hidden/pallas_call | solution.py:994
  392.7 8.2 %hidden.11 = (bf16[1024,256]{1,0:T(8,128)(2,1)S(1)}, bf16[1024,512]{1,0:T(8,128)(2,1)S(1)}, bf16[768,1024]{1,0:T(8,128)(2,1)}) custom-call(bf16[512,2048]{1,0:T(8,128)(2,1)} %bitcast.210, bf16[512,2048]{1,0:T(8,128)(2,1)} %bitcast.246, bf16[512,2048]{1,0:T(8,128)(2,1)} %bitcast.222, bf16[512,2048]{1,0:T(8,128)(2,1)} %bitcast.234, ...), custom_call_target="tpu_custom_call" | custom-call | flops 1000 | bytes 1000 | tf_op jit(solution)/shard_map/hidden/pallas_call | solution.py:994
  403.0 20.7 %back_sum.3 = (bf16[512,2048]{1,0:T(8,128)(2,1)}, bf16[512,2048]{1,0:T(8,128)(2,1)}) custom-call(bf16[1024,512]{1,0:T(8,128)(2,1)S(1)} %copy-done.68, bf16[1024,512]{1,0:T(8,128)(2,1)S(1)} %copy-done.71, bf16[1024,512]{1,0:T(8,128)(2,1)} %copy-done.69, bf16[1024,512]{1,0:T(8,128)(2,1)} %copy-done.72, bf16[1024,512]{1,0:T(8,128)(2,1)} %copy-done.73, ...), custom_call_target="tpu_custom_call" | custom-call | flops 1000 | bytes 1000 | tf_op jit(solution)/shard_map/back_sum/pallas_call | solution.py:1067
  439.6 12.1 %back_sum.2 = (bf16[512,2048]{1,0:T(8,128)(2,1)}, bf16[512,2048]{1,0:T(8,128)(2,1)}) custom-call(bf16[1024,256]{1,0:T(8,128)(2,1)S(1)} %copy-done.85, bf16[1024,256]{1,0:T(8,128)(2,1)S(1)} %copy-done.89, bf16[1024,256]{1,0:T(8,128)(2,1)S(1)} %copy-done.87, bf16[1024,256]{1,0:T(8,128)(2,1)S(1)} %get-tuple-element.281.refs_3_, ...), custom_call_target="tpu_custom_call" | custom-call | flops 1000 | bytes 1000 | tf_op jit(solution)/shard_map/back_sum/pallas_call | solution.py:1067
  459.5 8.1 %weight_grads.10 = (bf16[4,768,256]{2,1,0:T(8,128)(2,1)S(1)}, bf16[4,768,256]{2,1,0:T(8,128)(2,1)}) custom-call(bf16[512,2048]{1,0:T(8,128)(2,1)} %bitcast.212, bf16[512,2048]{1,0:T(8,128)(2,1)} %bitcast.248, bf16[512,2048]{1,0:T(8,128)(2,1)} %bitcast.224, bf16[512,2048]{1,0:T(8,128)(2,1)} %bitcast.236, bf16[768,1024]{1,0:T(8,128)(2,1)S(1)} %copy-done.58), custom_call_target="tpu_custom_call" | custom-call | flops 1000 | bytes 1000 | tf_op jit(solution)/shard_map/weight_grads/pallas_call | solution.py:1031
  467.7 8.1 %collective-permute-done.54.refs_6_ = bf16[2,768,256]{2,1,0:T(8,128)(2,1)} collective-permute-done((bf16[2,768,256]{2,1,0:T(8,128)(2,1)S(1)}, bf16[2,768,256]{2,1,0:T(8,128)(2,1)}, u32[]{:S(2)}, u32[]{:S(2)}) %collective-permute-start.54) | collective-permute-done | bytes 786464 | tf_op jit(solution)/shard_map/ppermute | solution.py:53
  498.4 19.1 %attend_back.2 = (f32[1,5,4,4,64,128]{5,4,3,2,1,0:T(8,128)}, bf16[4,1,5,4,64,128]{5,4,3,2,1,0:T(8,128)(2,1)S(1)}, bf16[4,1,5,4,64,128]{5,4,3,2,1,0:T(8,128)(2,1)}) custom-call(bf16[1,5,4,4,64,128]{5,4,3,2,1,0:T(8,128)(2,1)S(1)} %copy-done.13, bf16[1,5,4,4,64,128]{5,4,3,2,1,0:T(8,128)(2,1)} %copy-done.14, s32[1,4,1,256]{3,2,1,0:T(1,128)S(1)} %copy-done.108, ...), custom_call_target="tpu_custom_call" | custom-call | flops 1000 | bytes 1000 | tf_op jit(solution)/shard_map/attend_back/pallas_call | solution.py:1137
  524.8 13.8 %attend_back.3 = (f32[1,5,4,4,64,128]{5,4,3,2,1,0:T(8,128)}, bf16[4,1,5,4,64,128]{5,4,3,2,1,0:T(8,128)(2,1)S(1)}, bf16[4,1,5,4,64,128]{5,4,3,2,1,0:T(8,128)(2,1)}) custom-call(bf16[1,5,4,4,64,128]{5,4,3,2,1,0:T(8,128)(2,1)S(1)} %copy-done.13, bf16[1,5,4,4,64,128]{5,4,3,2,1,0:T(8,128)(2,1)} %copy-done.14, ...), custom_call_target="tpu_custom_call", output_to_operand_aliasing={{0}: (6, {}), {1}: (7, {}), {2}: (8, {})} | custom-call | flops 1000 | bytes 1000 | tf_op jit(solution)/shard_map/attend_back/pallas_call | solution.py:1137
  548.0 9.5 %collective-permute-done.62.refs_14_ = bf16[2,768,256]{2,1,0:T(8,128)(2,1)S(1)} collective-permute-done((bf16[2,768,256]{2,1,0:T(8,128)(2,1)S(1)}, bf16[2,768,256]{2,1,0:T(8,128)(2,1)S(1)}, u32[]{:S(2)}, u32[]{:S(2)}) %collective-permute-start.62) | collective-permute-done | bytes 786464 | tf_op jit(solution)/shard_map/ppermute | solution.py:53
  578.6 10.1 %collective-permute-done.68.refs_15_ = bf16[1,768,256]{2,1,0:T(8,128)(2,1)} collective-permute-done((bf16[1,768,256]{2,1,0:T(8,128)(2,1)}, bf16[1,768,256]{2,1,0:T(8,128)(2,1)}, u32[]{:S(2)}, u32[]{:S(2)}) %collective-permute-start.68) | collective-permute-done | bytes 393248 | tf_op jit(solution)/shard_map/ppermute | solution.py:53
  588.8 10.4 %collective-permute-done.67.refs_18_ = bf16[2,768,256]{2,1,0:T(8,128)(2,1)} collective-permute-done((bf16[2,768,256]{2,1,0:T(8,128)(2,1)}, bf16[2,768,256]{2,1,0:T(8,128)(2,1)}, u32[]{:S(2)}, u32[]{:S(2)}) %collective-permute-start.67) | collective-permute-done | bytes 786464 | tf_op jit(solution)/shard_map/ppermute | solution.py:53
  616.0 10.6 %collective-permute-done.72.refs_19_ = bf16[1,768,256]{2,1,0:T(8,128)(2,1)S(1)} collective-permute-done((bf16[1,768,256]{2,1,0:T(8,128)(2,1)S(1)}, bf16[1,768,256]{2,1,0:T(8,128)(2,1)S(1)}, u32[]{:S(2)}, u32[]{:S(2)}) %collective-permute-start.72) | collective-permute-done | bytes 393248 | tf_op jit(solution)/shard_map/ppermute | solution.py:53
  626.6 8.3 %collective-permute-done.70 = bf16[2,1,5,4,64,128]{5,4,3,2,1,0:T(8,128)(2,1)S(1)} collective-permute-done((bf16[2,1,5,4,64,128]{5,4,3,2,1,0:T(8,128)(2,1)S(1)}, bf16[2,1,5,4,64,128]{5,4,3,2,1,0:T(8,128)(2,1)S(1)}, u32[]{:S(2)}, u32[]{:S(2)}) %collective-permute-start.70) | collective-permute-done | bytes 655392 | tf_op jit(solution)/shard_map/ppermute | solution.py:53
  650.9 8.5 %h_one_back.1 = (bf16[256,2048]{1,0:T(8,128)(2,1)S(1)}, f32[1,2048]{1,0:T(1,128)S(1)}) custom-call(bf16[4,256,320]{2,1,0:T(8,128)(2,1)S(1)} %copy-done.43, bf16[4,8,320,256]{3,2,1,0:T(8,128)(2,1)} %copy-done.122, bf16[256,640]{1,0:T(8,128)(2,1)S(1)} %get-tuple-element.395.dkv_ref, bf16[2048,640]{1,0:T(8,128)(2,1)} %bitcast.157, ...), custom_call_target="tpu_custom_call" | custom-call | flops 1000 | bytes 1000 | tf_op jit(solution)/shard_map/h_one_back/pallas_call | solution.py:1240
  713.1 13.4 %collective-permute-done.87 = bf16[163,256]{1,0:T(8,128)(2,1)S(1)} collective-permute-done((bf16[163,256]{1,0:T(8,128)(2,1)S(1)}, bf16[163,256]{1,0:T(8,128)(2,1)S(1)}, u32[]{:S(2)}, u32[]{:S(2)}) %collective-permute-start.87) | collective-permute-done | bytes 83488 | tf_op jit(solution)/shard_map/ppermute | solution.py:53
  (600 shorter events, 341.5 us)
Async XLA Ops:
  105.2 38.2 %collective-permute-start.19 = (bf16[2,8,320,256]{3,2,1,0:T(8,128)(2,1)S(1)}, bf16[2,8,320,256]{3,2,1,0:T(8,128)(2,1)S(1)}, u32[]{:S(2)}, u32[]{:S(2)}) collective-permute-start(bf16[2,8,320,256]{3,2,1,0:T(8,128)(2,1)S(1)} %pad_maximum_fusion), channel_id=1, source_target_pairs={{0,1},{1,0},{2,3},{3,2},{4,5},{5,4},{6,7},{7,6},{8,9},{9,8},{10,11... | collective-permute-start | bytes 7864328 | tf_op jit(solution)/shard_map/ppermute | solution.py:53
  106.5 36.9 %collective-permute-start.22 = (bf16[4,256,768]{2,1,0:T(8,128)(2,1)S(1)}, bf16[4,256,768]{2,1,0:T(8,128)(2,1)S(1)}, u32[]{:S(2)}, u32[]{:S(2)}) collective-permute-start(bf16[4,256,768]{2,1,0:T(8,128)(2,1)S(1)} %pad_maximum_fusion.6), channel_id=1, source_target_pairs={{0,4},{4,0},{8,12},{12,8},{16,20},{20,16},{24,28},{28,24},{1,5},{5... | collective-permute-start | bytes 4718600 | tf_op jit(solution)/shard_map/ppermute | solution.py:53
  143.3 43.8 %collective-permute-start.25 = (bf16[2,8,320,256]{3,2,1,0:T(8,128)(2,1)}, bf16[2,8,320,256]{3,2,1,0:T(8,128)(2,1)}, u32[]{:S(2)}, u32[]{:S(2)}) collective-permute-start(bf16[2,8,320,256]{3,2,1,0:T(8,128)(2,1)} %pad_maximum_fusion.2.w_low), channel_id=1, source_target_pairs={{0,1},{1,0},{2,3},{3,2},{4,5},{5,4},{6,7},{7,6},{8,9},{9,8},{10,11... | collective-permute-start | bytes 7864328 | tf_op jit(solution)/shard_map/ppermute | solution.py:53
  144.7 42.4 %collective-permute-start.24 = (bf16[4,1,5,4,64,128]{5,4,3,2,1,0:T(8,128)(2,1)}, bf16[4,1,5,4,64,128]{5,4,3,2,1,0:T(8,128)(2,1)}, u32[]{:S(2)}, u32[]{:S(2)}) collective-permute-start(bf16[4,1,5,4,64,128]{5,4,3,2,1,0:T(8,128)(2,1)} %pad_maximum_fusion.12.low_ref), channel_id=1, source_target_pairs={{0,4},{4,0},{8,12},{12,8},{16,20},{20,16},{24,28},{28,24},{1,5},{5... | collective-permute-start | bytes 3932168 | tf_op jit(solution)/shard_map/ppermute | solution.py:53
  145.2 41.9 %collective-permute-start.26 = (bf16[1,256,2048]{2,1,0:T(8,128)(2,1)}, bf16[1,256,2048]{2,1,0:T(8,128)(2,1)}, u32[]{:S(2)}, u32[]{:S(2)}) collective-permute-start(bf16[1,256,2048]{2,1,0:T(8,128)(2,1)} %bitcast.23), channel_id=1, source_target_pairs={{0,2},{1,3},{2,0},{3,1},{4,6},{5,7},{6,4},{7,5},{8,10},{9,11},{10,... | collective-permute-start | bytes 3145736 | tf_op jit(solution)/shard_map/ppermute | solution.py:53
  146.8 37.7 %collective-permute-start.27 = (bf16[2,256,768]{2,1,0:T(8,128)(2,1)}, bf16[2,256,768]{2,1,0:T(8,128)(2,1)}, u32[]{:S(2)}, u32[]{:S(2)}) collective-permute-start(bf16[2,256,768]{2,1,0:T(8,128)(2,1)} %pad_maximum_fusion.16), channel_id=1, source_target_pairs={{0,16},{4,20},{8,24},{12,28},{16,0},{20,4},{24,8},{28,12},{1,17},{... | collective-permute-start | bytes 2359304 | tf_op jit(solution)/shard_map/ppermute | solution.py:53
  187.1 39.5 %collective-permute-start.29 = (bf16[4,256,768]{2,1,0:T(8,128)(2,1)}, bf16[4,256,768]{2,1,0:T(8,128)(2,1)}, u32[]{:S(2)}, u32[]{:S(2)}) collective-permute-start(bf16[4,256,768]{2,1,0:T(8,128)(2,1)} %pad_maximum_fusion.7), channel_id=1, source_target_pairs={{0,4},{4,0},{8,12},{12,8},{16,20},{20,16},{24,28},{28,24},{1,5},{5... | collective-permute-start | bytes 4718600 | tf_op jit(solution)/shard_map/ppermute | solution.py:53
  226.7 40.8 %collective-permute-start.33 = (bf16[2,256,2048]{2,1,0:T(8,128)(2,1)S(1)}, bf16[2,256,2048]{2,1,0:T(8,128)(2,1)S(1)}, u32[]{:S(2)}, u32[]{:S(2)}) collective-permute-start(bf16[2,256,2048]{2,1,0:T(8,128)(2,1)S(1)} %constant_dynamic-update-slice_fusion.2), channel_id=1, source_target_pairs={{0,1},{1,0},{2,3},{3,2},{4,5},{5,4},{6,7},{7,6},{8,9},{9,8},{10,11... | collective-permute-start | bytes 6291464 | tf_op jit(solution)/shard_map/ppermute | solution.py:53
  228.2 39.3 %collective-permute-start.34 = (bf16[4,256,768]{2,1,0:T(8,128)(2,1)S(1)}, bf16[4,256,768]{2,1,0:T(8,128)(2,1)S(1)}, u32[]{:S(2)}, u32[]{:S(2)}) collective-permute-start(bf16[4,256,768]{2,1,0:T(8,128)(2,1)S(1)} %pad_maximum_fusion.8), channel_id=1, source_target_pairs={{0,4},{4,0},{8,12},{12,8},{16,20},{20,16},{24,28},{28,24},{1,5},{5... | collective-permute-start | bytes 4718600 | tf_op jit(solution)/shard_map/ppermute | solution.py:53
  230.3 37.2 %collective-permute-start.35 = (bf16[2,256,768]{2,1,0:T(8,128)(2,1)S(1)}, bf16[2,256,768]{2,1,0:T(8,128)(2,1)S(1)}, u32[]{:S(2)}, u32[]{:S(2)}) collective-permute-start(bf16[2,256,768]{2,1,0:T(8,128)(2,1)S(1)} %pad_maximum_fusion.18), channel_id=1, source_target_pairs={{0,16},{4,20},{8,24},{12,28},{16,0},{20,4},{24,8},{28,12},{1,17},{... | collective-permute-start | bytes 2359304 | tf_op jit(solution)/shard_map/ppermute | solution.py:53
  267.5 39.2 %collective-permute-start.37 = (bf16[2,256,2048]{2,1,0:T(8,128)(2,1)S(1)}, bf16[2,256,2048]{2,1,0:T(8,128)(2,1)S(1)}, u32[]{:S(2)}, u32[]{:S(2)}) collective-permute-start(bf16[2,256,2048]{2,1,0:T(8,128)(2,1)S(1)} %pad_maximum_fusion.3), channel_id=1, source_target_pairs={{0,1},{1,0},{2,3},{3,2},{4,5},{5,4},{6,7},{7,6},{8,9},{9,8},{10,11... | collective-permute-start | bytes 6291464 | tf_op jit(solution)/shard_map/ppermute | solution.py:53
  267.8 38.9 %collective-permute-start.38 = (bf16[4,256,768]{2,1,0:T(8,128)(2,1)S(1)}, bf16[4,256,768]{2,1,0:T(8,128)(2,1)S(1)}, u32[]{:S(2)}, u32[]{:S(2)}) collective-permute-start(bf16[4,256,768]{2,1,0:T(8,128)(2,1)S(1)} %pad_maximum_fusion.9), channel_id=1, source_target_pairs={{0,4},{4,0},{8,12},{12,8},{16,20},{20,16},{24,28},{28,24},{1,5},{5... | collective-permute-start | bytes 4718600 | tf_op jit(solution)/shard_map/ppermute | solution.py:53
  306.7 42.1 %collective-permute-start.44 = (bf16[2,256,2048]{2,1,0:T(8,128)(2,1)S(1)}, bf16[2,256,2048]{2,1,0:T(8,128)(2,1)}, u32[]{:S(2)}, u32[]{:S(2)}) collective-permute-start(bf16[2,256,2048]{2,1,0:T(8,128)(2,1)S(1)} %pad_maximum_fusion.4), channel_id=1, source_target_pairs={{0,1},{1,0},{2,3},{3,2},{4,5},{5,4},{6,7},{7,6},{8,9},{9,8},{10,11... | collective-permute-start | bytes 6291464 | tf_op jit(solution)/shard_map/ppermute | solution.py:53
  307.0 41.9 %collective-permute-start.42 = (bf16[4,256,768]{2,1,0:T(8,128)(2,1)S(1)}, bf16[4,256,768]{2,1,0:T(8,128)(2,1)}, u32[]{:S(2)}, u32[]{:S(2)}) collective-permute-start(bf16[4,256,768]{2,1,0:T(8,128)(2,1)S(1)} %pad_maximum_fusion.10), channel_id=1, source_target_pairs={{0,4},{4,0},{8,12},{12,8},{16,20},{20,16},{24,28},{28,24},{1,5},{5... | collective-permute-start | bytes 4718600 | tf_op jit(solution)/shard_map/ppermute | solution.py:53
  308.3 40.5 %collective-permute-start.43 = (bf16[2,256,768]{2,1,0:T(8,128)(2,1)S(1)}, bf16[2,256,768]{2,1,0:T(8,128)(2,1)S(1)}, u32[]{:S(2)}, u32[]{:S(2)}) collective-permute-start(bf16[2,256,768]{2,1,0:T(8,128)(2,1)S(1)} %pad_maximum_fusion.20), channel_id=1, source_target_pairs={{0,16},{4,20},{8,24},{12,28},{16,0},{20,4},{24,8},{28,12},{1,17},{... | collective-permute-start | bytes 2359304 | tf_op jit(solution)/shard_map/ppermute | solution.py:53
  309.4 39.4 %collective-permute-start.45 = (bf16[2,1,256,320]{3,2,0,1:T(8,128)(2,1)}, bf16[2,1,256,320]{3,2,0,1:T(8,128)(2,1)}, u32[]{:S(2)}, u32[]{:S(2)}) collective-permute-start(bf16[2,1,256,320]{3,2,0,1:T(8,128)(2,1)} %get-tuple-element.297), channel_id=1, source_target_pairs={{0,2},{1,3},{2,0},{3,1},{4,6},{5,7},{6,4},{7,5},{8,10},{9,11},{10,... | collective-permute-start | bytes 983048 | tf_op jit(solution)/shard_map/ppermute | solution.py:53
  348.8 41.3 %collective-permute-start.48 = (bf16[4,768,256]{2,1,0:T(8,128)(2,1)}, bf16[4,768,256]{2,1,0:T(8,128)(2,1)}, u32[]{:S(2)}, u32[]{:S(2)}) collective-permute-start(bf16[4,768,256]{2,1,0:T(8,128)(2,1)} %get-tuple-element.318), channel_id=1, source_target_pairs={{0,4},{4,0},{8,12},{12,8},{16,20},{20,16},{24,28},{28,24},{1,5},{5... | collective-permute-start | bytes 4718600 | tf_op jit(solution)/shard_map/ppermute | solution.py:53
  350.0 40.1 %collective-permute-start.46 = (bf16[2,256,768]{2,1,0:T(8,128)(2,1)S(1)}, bf16[2,256,768]{2,1,0:T(8,128)(2,1)S(1)}, u32[]{:S(2)}, u32[]{:S(2)}) collective-permute-start(bf16[2,256,768]{2,1,0:T(8,128)(2,1)S(1)} %collective-permute-done.41), channel_id=1, source_target_pairs={{0,16},{4,20},{8,24},{12,28},{16,0},{20,4},{24,8},{28,12},{1,17},{... | collective-permute-start | bytes 2359304 | tf_op jit(solution)/shard_map/ppermute | solution.py:53
  390.1 39.6 %collective-permute-start.49 = (bf16[4,768,256]{2,1,0:T(8,128)(2,1)}, bf16[4,768,256]{2,1,0:T(8,128)(2,1)}, u32[]{:S(2)}, u32[]{:S(2)}) collective-permute-start(bf16[4,768,256]{2,1,0:T(8,128)(2,1)} %get-tuple-element.320), channel_id=1, source_target_pairs={{0,4},{4,0},{8,12},{12,8},{16,20},{20,16},{24,28},{28,24},{1,5},{5... | collective-permute-start | bytes 4718600 | tf_op jit(solution)/shard_map/ppermute | solution.py:53
  392.4 37.3 %collective-permute-start.50 = (bf16[2,768,256]{2,1,0:T(8,128)(2,1)S(1)}, bf16[2,768,256]{2,1,0:T(8,128)(2,1)S(1)}, u32[]{:S(2)}, u32[]{:S(2)}) collective-permute-start(bf16[2,768,256]{2,1,0:T(8,128)(2,1)S(1)} %add_convert_fusion.5), channel_id=1, source_target_pairs={{0,16},{4,20},{8,24},{12,28},{16,0},{20,4},{24,8},{28,12},{1,17},{... | collective-permute-start | bytes 2359304 | tf_op jit(solution)/shard_map/ppermute | solution.py:53
  429.8 46.0 %collective-permute-start.53 = (bf16[4,768,256]{2,1,0:T(8,128)(2,1)}, bf16[4,768,256]{2,1,0:T(8,128)(2,1)}, u32[]{:S(2)}, u32[]{:S(2)}) collective-permute-start(bf16[4,768,256]{2,1,0:T(8,128)(2,1)} %get-tuple-element.332), channel_id=1, source_target_pairs={{0,4},{4,0},{8,12},{12,8},{16,20},{20,16},{24,28},{28,24},{1,5},{5... | collective-permute-start | bytes 4718600 | tf_op jit(solution)/shard_map/ppermute | solution.py:53
  437.4 38.3 %collective-permute-start.52 = (bf16[1,256,2048]{2,1,0:T(8,128)(2,1)}, bf16[1,256,2048]{2,1,0:T(8,128)(2,1)}, u32[]{:S(2)}, u32[]{:S(2)}) collective-permute-start(bf16[1,256,2048]{2,1,0:T(8,128)(2,1)} %fusion.4), channel_id=1, source_target_pairs={{0,2},{1,3},{2,0},{3,1},{4,6},{5,7},{6,4},{7,5},{8,10},{9,11},{10,... | collective-permute-start | bytes 3145736 | tf_op jit(solution)/shard_map/ppermute | solution.py:53
  475.8 41.8 %collective-permute-start.55 = (bf16[2,256,2048]{2,1,0:T(8,128)(2,1)}, bf16[2,256,2048]{2,1,0:T(8,128)(2,1)}, u32[]{:S(2)}, u32[]{:S(2)}) collective-permute-start(bf16[2,256,2048]{2,1,0:T(8,128)(2,1)} %bitcast.275), channel_id=1, source_target_pairs={{0,1},{1,0},{2,3},{3,2},{4,5},{5,4},{6,7},{7,6},{8,9},{9,8},{10,11... | collective-permute-start | bytes 6291464 | tf_op jit(solution)/shard_map/ppermute | solution.py:53
  475.8 41.8 %collective-permute-start.56 = (bf16[4,768,256]{2,1,0:T(8,128)(2,1)}, bf16[4,768,256]{2,1,0:T(8,128)(2,1)}, u32[]{:S(2)}, u32[]{:S(2)}) collective-permute-start(bf16[4,768,256]{2,1,0:T(8,128)(2,1)} %copy-done.115), channel_id=1, source_target_pairs={{0,4},{4,0},{8,12},{12,8},{16,20},{20,16},{24,28},{28,24},{1,5},{5... | collective-permute-start | bytes 4718600 | tf_op jit(solution)/shard_map/ppermute | solution.py:53
  479.0 38.6 %collective-permute-start.57 = (bf16[2,768,256]{2,1,0:T(8,128)(2,1)}, bf16[2,768,256]{2,1,0:T(8,128)(2,1)S(1)}, u32[]{:S(2)}, u32[]{:S(2)}) collective-permute-start(bf16[2,768,256]{2,1,0:T(8,128)(2,1)} %add_convert_fusion.3), channel_id=1, source_target_pairs={{0,16},{4,20},{8,24},{12,28},{16,0},{20,4},{24,8},{28,12},{1,17},{... | collective-permute-start | bytes 2359304 | tf_op jit(solution)/shard_map/ppermute | solution.py:53
  480.4 37.1 %collective-permute-start.59 = (bf16[1,768,256]{2,1,0:T(8,128)(2,1)S(1)}, bf16[1,768,256]{2,1,0:T(8,128)(2,1)S(1)}, u32[]{:S(2)}, u32[]{:S(2)}) collective-permute-start(bf16[1,768,256]{2,1,0:T(8,128)(2,1)S(1)} %add_convert_fusion.11), channel_id=1, source_target_pairs={{0,8},{4,12},{8,0},{12,4},{16,24},{20,28},{24,16},{28,20},{1,9},{5... | collective-permute-start | bytes 1179656 | tf_op jit(solution)/shard_map/ppermute | solution.py:53
  517.6 41.7 %collective-permute-start.61 = (bf16[4,768,256]{2,1,0:T(8,128)(2,1)}, bf16[4,768,256]{2,1,0:T(8,128)(2,1)}, u32[]{:S(2)}, u32[]{:S(2)}) collective-permute-start(bf16[4,768,256]{2,1,0:T(8,128)(2,1)} %get-tuple-element.359), channel_id=1, source_target_pairs={{0,4},{4,0},{8,12},{12,8},{16,20},{20,16},{24,28},{28,24},{1,5},{5... | collective-permute-start | bytes 4718600 | tf_op jit(solution)/shard_map/ppermute | solution.py:53
  518.7 38.8 %collective-permute-start.60 = (bf16[1,256,2048]{2,1,0:T(8,128)(2,1)S(1)}, bf16[1,256,2048]{2,1,0:T(8,128)(2,1)}, u32[]{:S(2)}, u32[]{:S(2)}) collective-permute-start(bf16[1,256,2048]{2,1,0:T(8,128)(2,1)S(1)} %bitcast.175), channel_id=1, source_target_pairs={{0,2},{1,3},{2,0},{3,1},{4,6},{5,7},{6,4},{7,5},{8,10},{9,11},{10,... | collective-permute-start | bytes 3145736 | tf_op jit(solution)/shard_map/ppermute | solution.py:53
  559.3 39.9 %collective-permute-start.65 = (bf16[2,256,2048]{2,1,0:T(8,128)(2,1)S(1)}, bf16[2,256,2048]{2,1,0:T(8,128)(2,1)}, u32[]{:S(2)}, u32[]{:S(2)}) collective-permute-start(bf16[2,256,2048]{2,1,0:T(8,128)(2,1)S(1)} %pad_maximum_fusion.5), channel_id=1, source_target_pairs={{0,1},{1,0},{2,3},{3,2},{4,5},{5,4},{6,7},{7,6},{8,9},{9,8},{10,11... | collective-permute-start | bytes 6291464 | tf_op jit(solution)/shard_map/ppermute | solution.py:53
  559.4 39.8 %collective-permute-start.66 = (bf16[4,1,5,4,64,128]{5,4,3,2,1,0:T(8,128)(2,1)}, bf16[4,1,5,4,64,128]{5,4,3,2,1,0:T(8,128)(2,1)}, u32[]{:S(2)}, u32[]{:S(2)}) collective-permute-start(bf16[4,1,5,4,64,128]{5,4,3,2,1,0:T(8,128)(2,1)} %get-tuple-element.374), channel_id=1, source_target_pairs={{0,4},{4,0},{8,12},{12,8},{16,20},{20,16},{24,28},{28,24},{1,5},{5... | collective-permute-start | bytes 3932168 | tf_op jit(solution)/shard_map/ppermute | solution.py:53
  599.1 36.9 %collective-permute-start.71 = (bf16[4,768,256]{2,1,0:T(8,128)(2,1)S(1)}, bf16[4,768,256]{2,1,0:T(8,128)(2,1)S(1)}, u32[]{:S(2)}, u32[]{:S(2)}) collective-permute-start(bf16[4,768,256]{2,1,0:T(8,128)(2,1)S(1)} %get-tuple-element.388), channel_id=1, source_target_pairs={{0,4},{4,0},{8,12},{12,8},{16,20},{20,16},{24,28},{28,24},{1,5},{5... | collective-permute-start | bytes 4718600 | tf_op jit(solution)/shard_map/ppermute | solution.py:53
  640.0 37.3 %collective-permute-start.76 = (bf16[2,768,256]{2,1,0:T(8,128)(2,1)}, bf16[2,768,256]{2,1,0:T(8,128)(2,1)}, u32[]{:S(2)}, u32[]{:S(2)}) collective-permute-start(bf16[2,768,256]{2,1,0:T(8,128)(2,1)} %add_convert_fusion), channel_id=1, source_target_pairs={{0,16},{4,20},{8,24},{12,28},{16,0},{20,4},{24,8},{28,12},{1,17},{... | collective-permute-start | bytes 2359304 | tf_op jit(solution)/shard_map/ppermute | solution.py:53
  (204 other events, 3724.9 us)
